TPU v7x, 32 devices: a whole 2x2x4 slice. The times are simulated.
32 devices in a mesh: dev: 32 (over z, y, x, core).
Axes of the slice: x: 2, y: 2, z: 4, core: 2. Of those that a mesh axis runs over, the one named last changes fastest.
Arguments:
- tokens: bfloat16 [8192, 1088], P('dev'), may hold values from -6 to 6
- attn_weight: bfloat16 [4352, 1088], P('dev')
- mlp_weight: bfloat16 [8704, 1088], P('dev'), may hold values from -0.1875 to 0.1875
- vectors: bfloat16 [13056], P('dev')
- cotangent: bfloat16 [8192, 1088], P('dev'), may hold values from -6 to 6
- seq_lengths: int32 [32], replicated, may hold values from 128 to 256, as said below
- seq_device: int32 [32], replicated, may hold values from 0 to 31, as said below
- seq_offset: int32 [32], replicated, may hold values from 0 to 128, as said below
Outputs:
- output: bfloat16 [8192, 1088], P('dev')
- grad_tokens: float32 [8192, 1088], P('dev')
- grad_attn: float32 [4352, 1088], P('dev')
- grad_mlp: float32 [8704, 1088], P('dev')
- grad_vectors: float32 [13056], P('dev')
Inputs may be any that keep to these rules, and one draw needn't show every extreme that they name: Sequence j has seq_lengths[j] tokens; some sequence has exactly 256 and some exactly 128. `seq_device`: A permutation: each device holds exactly one sequence. Sequence j fills slots seq_offset[j] to seq_offset[j] + seq_lengths[j] - 1 of its device; the other slots are empty.
All inputs are finite; a program needn't handle non-finite values.
Results may differ from a plain program's by a relative error of at most 0.01.
Values may be sent and summed in bfloat16 or wider, within the bound.
No kernel may reach another device: no remote copies, remote signals or barrier semaphores. Data moves between devices by JAX's collectives and lax.ppermute only.
A program may use at most 256 MiB of HBM per device.

v0:
```python
import jax
import jax.numpy as jnp
from jax import lax
from jax.sharding import PartitionSpec as P

D = 1088
HEADS = 17
HEAD_SIZE = 64
FF = 4352


epsilon = 1e-05
neg_large = -1e30


def normalize(values, gain, shift):
    centre = values - jnp.mean(values, axis=-1, keepdims=True)
    spread = jnp.mean(centre * centre, axis=-1, keepdims=True)
    factor = lax.rsqrt(spread + epsilon)
    normed = centre * factor
    return (normed * gain + shift, normed, factor)


def normalize_back(grad_out, normed, factor, gain):
    inner = grad_out * gain
    return factor * (
        inner
        - jnp.mean(inner, axis=-1, keepdims=True)
        - normed * jnp.mean(inner * normed, axis=-1, keepdims=True)
    )


def split_vectors(whole_vec):
    width = D
    pieces = [
        whole_vec[number * width : (number + 1) * width].astype(jnp.float32) for number in range(8)
    ]
    return pieces + [whole_vec[8 * width :].astype(jnp.float32)]


def gelu_exact(values):
    return jax.nn.gelu(values, approximate=False)


def block_scores(query_block, keys, keep, start, scale):
    span = query_block.shape[0]
    query_pos = start + jnp.arange(span, dtype=jnp.int32)
    key_pos = jnp.arange(keys.shape[0], dtype=jnp.int32)
    allowed = (key_pos[None, :] <= query_pos[:, None]) & (keep[None, :] == keep[:, None])
    scores = (
        jnp.einsum("qhd,khd->hqk", query_block, keys, preferred_element_type=jnp.float32) * scale
    )
    return jnp.where(allowed[None], scores, neg_large)


def block_layout(queries):
    total_rows = queries.shape[0]
    count = total_rows // total_rows
    starts = jnp.arange(count, dtype=jnp.int32) * total_rows
    return (count, total_rows, starts)


def attend(queries, keys, values, keep, scale):
    count, span, starts = block_layout(queries)
    query_blocks = queries.reshape((count, span) + queries.shape[1:])

    def one_block(item):
        query_block, start = item
        scores = block_scores(query_block, keys, keep, start, scale)
        top = jnp.max(scores, axis=-1, keepdims=True)
        expo = jnp.exp(scores - top)
        total = jnp.sum(expo, axis=-1, keepdims=True)
        weights = (expo / total).astype(jnp.bfloat16)
        mixed = jnp.einsum("hqk,khd->qhd", weights, values, preferred_element_type=jnp.float32)
        return (mixed, top + jnp.log(total))

    mixed, log_total = lax.map(one_block, (query_blocks, starts))
    return (mixed.reshape(queries.shape), log_total)


def attend_back(queries, keys, values, keep, scale, grad_mixed, log_total):
    count, span, starts = block_layout(queries)
    query_blocks = queries.reshape((count, span) + queries.shape[1:])
    grad_blocks = grad_mixed.reshape((count, span) + queries.shape[1:])

    def one_block(carry, item):
        grad_keys, grad_values = carry
        query_block, grad_block, block_total, start = item
        scores = block_scores(query_block, keys, keep, start, scale)
        probs = jnp.exp(scores - block_total)
        grad_values = grad_values + jnp.einsum(
            "hqk,qhd->khd",
            probs.astype(jnp.bfloat16),
            grad_block,
            preferred_element_type=jnp.float32,
        )
        grad_probs = jnp.einsum(
            "qhd,khd->hqk", grad_block, values, preferred_element_type=jnp.float32
        )
        inner = jnp.sum(probs * grad_probs, axis=-1, keepdims=True)
        grad_scores = (probs * (grad_probs - inner)).astype(jnp.bfloat16)
        grad_query = (
            jnp.einsum("hqk,khd->qhd", grad_scores, keys, preferred_element_type=jnp.float32)
            * scale
        )
        grad_keys = (
            grad_keys
            + jnp.einsum(
                "hqk,qhd->khd", grad_scores, query_block, preferred_element_type=jnp.float32
            )
            * scale
        )
        return ((grad_keys, grad_values), grad_query)

    zeros = jnp.zeros(keys.shape, jnp.float32)
    sums, grad_queries = lax.scan(
        one_block, (zeros, zeros), (query_blocks, grad_blocks, log_total, starts)
    )
    return (grad_queries.reshape(queries.shape), sums[0], sums[1])


def shards(
    tokens, attn_weight, mlp_weight, vectors, cotangent, seq_lengths, seq_device, seq_offset
):
    total_rows = tokens.shape[0]
    width = D
    hidden = FF
    scale = HEAD_SIZE ** (-0.5)
    devices = lax.axis_size("dev")
    here = lax.axis_index("dev")
    chosen = (seq_device == here).astype(jnp.int32)
    begin = jnp.sum(chosen * seq_offset)
    finish = begin + jnp.sum(chosen * seq_lengths)
    positions = jnp.arange(total_rows, dtype=jnp.int32)
    keep = ((positions >= begin) & (positions < finish)).astype(jnp.int32)
    live = keep[:, None] == 1
    head_shape = (total_rows, HEADS, HEAD_SIZE)
    full_attn, full_mlp, full_vec = (
        lax.all_gather(attn_weight, "dev", axis=0, tiled=True),
        lax.all_gather(mlp_weight, "dev", axis=0, tiled=True),
        lax.all_gather(vectors, "dev", axis=0, tiled=True),
    )
    (
        gain_one,
        shift_one,
        query_bias,
        value_bias,
        out_bias,
        gain_two,
        shift_two,
        down_bias,
        up_bias,
    ) = split_vectors(full_vec)
    inputs = tokens.astype(jnp.float32)
    first_out, normed_one, factor_one = normalize(inputs, gain_one, shift_one)
    first_low = first_out.astype(jnp.bfloat16)
    projected = jnp.einsum(
        "rd,od->ro", first_low, full_attn[: 3 * width], preferred_element_type=jnp.float32
    )
    queries = (projected[:, :width] + query_bias).astype(jnp.bfloat16).reshape(head_shape)
    keys = projected[:, width : 2 * width].astype(jnp.bfloat16).reshape(head_shape)
    values = (projected[:, 2 * width :] + value_bias).astype(jnp.bfloat16).reshape(head_shape)
    mixed, log_total = attend(queries, keys, values, keep, scale)
    mixed_low = mixed.reshape(total_rows, width).astype(jnp.bfloat16)
    branch = (
        jnp.einsum(
            "rd,od->ro", mixed_low, full_attn[3 * width :], preferred_element_type=jnp.float32
        )
        + out_bias
    )
    middle = inputs + branch
    second_out, normed_two, factor_two = normalize(middle, gain_two, shift_two)
    second_low = second_out.astype(jnp.bfloat16)
    up_sum = (
        jnp.einsum("rd,fd->rf", second_low, full_mlp[:hidden], preferred_element_type=jnp.float32)
        + up_bias
    )
    activated, gelu_back = jax.vjp(gelu_exact, up_sum)
    act_low = activated.astype(jnp.bfloat16)
    down = jnp.dot(act_low, full_mlp[hidden:], preferred_element_type=jnp.float32) + down_bias
    output = jnp.where(live, middle + down, 0.0).astype(jnp.bfloat16)
    back_attn, back_mlp, back_vec = (
        lax.all_gather(attn_weight, "dev", axis=0, tiled=True),
        lax.all_gather(mlp_weight, "dev", axis=0, tiled=True),
        lax.all_gather(vectors, "dev", axis=0, tiled=True),
    )
    back_pieces = split_vectors(back_vec)
    gain_one_back = back_pieces[0]
    gain_two_back = back_pieces[5]
    grad_down = jnp.where(live, cotangent, jnp.zeros_like(cotangent))
    grad_down_weight = jnp.einsum(
        "rf,rd->fd", act_low, grad_down, preferred_element_type=jnp.float32
    )
    grad_down_bias = jnp.sum(grad_down.astype(jnp.float32), axis=0)
    grad_act = jnp.einsum(
        "rd,fd->rf", grad_down, back_mlp[hidden:], preferred_element_type=jnp.float32
    )
    grad_up = gelu_back(grad_act)[0].astype(jnp.bfloat16)
    grad_up_weight = jnp.einsum(
        "rf,rd->fd", grad_up, second_low, preferred_element_type=jnp.float32
    )
    grad_up_bias = jnp.sum(grad_up.astype(jnp.float32), axis=0)
    grad_second = jnp.dot(grad_up, back_mlp[:hidden], preferred_element_type=jnp.float32)
    grad_gain_two = jnp.sum(grad_second * normed_two, axis=0)
    grad_shift_two = jnp.sum(grad_second, axis=0)
    grad_middle = grad_down.astype(jnp.float32) + normalize_back(
        grad_second, normed_two, factor_two, gain_two_back
    )
    grad_mlp = jnp.concatenate([grad_up_weight, grad_down_weight], axis=0)
    mlp_rows = grad_mlp.shape[0] // devices
    grad_branch = grad_middle.astype(jnp.bfloat16)
    grad_out_weight = jnp.einsum(
        "ro,rd->od", grad_branch, mixed_low, preferred_element_type=jnp.float32
    )
    grad_out_bias = jnp.sum(grad_branch.astype(jnp.float32), axis=0)
    grad_mixed = jnp.dot(grad_branch, back_attn[3 * width :], preferred_element_type=jnp.float32)
    grad_mixed_low = grad_mixed.astype(jnp.bfloat16).reshape(head_shape)
    grad_queries, grad_keys, grad_values = attend_back(
        queries, keys, values, keep, scale, grad_mixed_low, log_total
    )
    grad_projected = jnp.concatenate(
        [
            grad_queries.reshape(total_rows, width),
            grad_keys.reshape(total_rows, width),
            grad_values.reshape(total_rows, width),
        ],
        axis=1,
    ).astype(jnp.bfloat16)
    grad_proj_weight = jnp.einsum(
        "ro,rd->od", grad_projected, first_low, preferred_element_type=jnp.float32
    )
    grad_columns = jnp.sum(grad_projected.astype(jnp.float32), axis=0)
    grad_query_bias = grad_columns[:width]
    grad_value_bias = grad_columns[2 * width :]
    grad_first = jnp.dot(grad_projected, back_attn[: 3 * width], preferred_element_type=jnp.float32)
    grad_gain_one = jnp.sum(grad_first * normed_one, axis=0)
    grad_shift_one = jnp.sum(grad_first, axis=0)
    grad_inputs = grad_middle + normalize_back(grad_first, normed_one, factor_one, gain_one_back)
    grad_attn = jnp.concatenate([grad_proj_weight, grad_out_weight], axis=0)
    attn_rows = grad_attn.shape[0] // devices
    grad_vec = jnp.concatenate(
        [
            grad_gain_one,
            grad_shift_one,
            grad_query_bias,
            grad_value_bias,
            grad_out_bias,
            grad_gain_two,
            grad_shift_two,
            grad_down_bias,
            grad_up_bias,
        ],
        axis=0,
    )
    stacked = jnp.concatenate(
        [grad_attn.reshape(devices, attn_rows, width), grad_mlp.reshape(devices, mlp_rows, width)],
        axis=1,
    )
    stacked = stacked.reshape(devices * (attn_rows + mlp_rows), width)
    both_share = lax.psum_scatter(stacked, "dev", scatter_dimension=0, tiled=True)
    attn_share = both_share[:attn_rows]
    mlp_share = both_share[attn_rows:]
    vec_share = lax.psum_scatter(grad_vec, "dev", scatter_dimension=0, tiled=True)
    return (output, grad_inputs, attn_share, mlp_share, vec_share)


def solution(mesh):
    return jax.shard_map(
        shards,
        mesh=mesh,
        in_specs=(
            P("dev", None),
            P("dev", None),
            P("dev", None),
            P("dev"),
            P("dev", None),
            P(),
            P(),
            P(),
        ),
        out_specs=(P("dev", None), P("dev", None), P("dev", None), P("dev", None), P("dev")),
        check_vma=False,
    )
```

profile of v0, /device:TPU:8, one launch (start us, length us, event | category | flops | bytes accessed | tf_op | source)
XLA Modules:
  0.0 1283.5 jit_solution(5339280874241848930)
XLA Ops:
  8.7 1.3 fusion.71
  12.2 41.0 %all-reduce = bf16[13056]{0:T(1024)(128)(2,1)S(1)} all-reduce(bf16[13056]{0:T(1024)(128)(2,1)S(1)} %dynamic-update-slice), channel_id=1, replica_groups=mesh['dev'=32] {'dev'}, use_global_device_ids=true, to_apply=%add | all-reduce | flops 13056 | bytes 52224
  54.5 1.2 convert_reduce_fusion.2
  55.7 1.3 fusion.63
  57.8 39.3 %all-gather.3.cloned.1.call-done = bf16[4352,1088]{1,0:T(8,128)(2,1)} async-done(((bf16[136,1088]{1,0:T(8,128)(2,1)}), bf16[4352,1088]{1,0:T(8,128)(2,1)}) %all-gather.3.cloned.1.call-update) | async-done | bytes 9469968 | tf_op jit(solution)/shard_map/all_gather | solution.py:139
  97.1 5.8 fusion.13
  107.2 2.9 fusion.84
  110.3 117.0 %all-gather.5.cloned.1.call-done = bf16[8704,1088]{1,0:T(8,128)(2,1)} async-done(((bf16[272,1088]{1,0:T(8,128)(2,1)}), bf16[8704,1088]{1,0:T(8,128)(2,1)}) %all-gather.5.cloned.1.call-update) | async-done | bytes 18939920 | tf_op jit(solution)/shard_map/all_gather | solution.py:140
  227.3 16.1 %multiply_convert_fusion.1 = (bf16[256,4352]{1,0:T(8,128)(2,1)}, f32[256,4352]{1,0:T(8,128)S(1)}, f32[256,4352]{1,0:T(8,128)S(1)}) fusion(f32[4352]{0:T(1024)S(1)} %slice_convert_fusion.1, bf16[8704,1088]{1,0:T(8,128)(2,1)} %all-gather.5.cloned.1.call-done, f32[256,1088]{0,1:T(8,128)S(1)} %get-tuple-element.86, f32[1088]{0:T(1024)S(1)} %get-tuple-element.74, ...), kind=kOutput, calls=%fused_computation.23 | convolution fusion | flops 2499231744 | bytes 22310400 | tf_op jit(solution)/shard_map/rd,fd->rf/dot_general | solution.py:175
  243.4 7.1 convert_reduce_fusion
  250.5 8.9 multiply_reduce_fusion.1
  259.5 1.3 convert_reduce_fusion.4
  260.8 2.9 convolution_convert_fusion
  264.6 1.1 multiply_reduce_fusion
  265.7 1.1 multiply_convert_fusion
  268.1 0.9 fusion.72
  269.1 8.3 fusion.80
  277.4 2.2 fusion.77
  279.6 7.5 pad_maximum_fusion.2
  287.1 21.4 %copy.28 = f32[4352,1088]{1,0:T(8,128)} copy(f32[4352,1088]{0,1:T(8,128)} %pad_maximum_fusion.2) | data formatting | bytes 37879808 | tf_op jit(solution)/shard_map/concatenate | solution.py:239
  308.5 10.8 fusion.66
  319.3 27.1 %pad_maximum_fusion.1 = f32[8704,1088]{0,1:T(8,128)} fusion(f32[4352,1088]{0,1:T(8,128)} %fusion.66, f32[4352,1088]{0,1:T(8,128)} %fusion.80), kind=kLoop, calls=%fused_computation.1 | loop fusion | flops 9469952 | bytes 75759616 | tf_op jit(solution)/shard_map/concatenate | solution.py:209
  346.3 37.8 %copy.29 = f32[8704,1088]{1,0:T(8,128)} copy(f32[8704,1088]{0,1:T(8,128)} %pad_maximum_fusion.1) | data formatting | bytes 75759616 | tf_op jit(solution)/shard_map/concatenate | solution.py:209
  384.2 40.8 %pad_maximum_fusion = f32[32,408,1088]{2,1,0:T(8,128)} fusion(f32[32,272,1088]{2,1,0:T(8,128)} %bitcast.36, f32[32,136,1088]{2,1,0:T(8,128)} %bitcast.39), kind=kLoop, calls=%fused_computation | loop fusion | flops 14204928 | bytes 113639424 | tf_op jit(solution)/shard_map/concatenate | solution.py:255
  425.0 1.7 convert_reduce_fusion.1
  426.8 7.7 fusion.62
  434.6 43.6 %all-reduce.2 = f32[13056]{0:T(1024)S(1)} all-reduce(f32[13056]{0:T(1024)S(1)} %concatenate.20), channel_id=3, replica_groups=mesh['dev'=32] {'dev'}, use_global_device_ids=true, to_apply=%region_22.23.clone | all-reduce | flops 13056 | bytes 104448
  478.8 2.8 fusion.61
  481.6 10.0 fusion.35
  491.6 780.5 %all-reduce.5.cloned.1.call-done = f32[13056,1088]{1,0:T(8,128)} async-done(((f32[13056,1088]{1,0:T(8,128)}), f32[13056,1088]{1,0:T(8,128)}) %all-reduce.5.cloned.1.call-update) | async-done | bytes 56819728
  1272.2 1.9 constant_dynamic-slice_fusion
  1274.1 2.4 constant_dynamic-slice_fusion.1
  (72 shorter events, 11.9 us)
Async XLA Ops:
  7.2 90.0 %all-gather.3.cloned.1.call-start = ((), (), s32[]{:S(2)}) async-start(), calls=%async_computation | async-start | bytes 10340352 | tf_op jit(solution)/shard_map/all_gather | solution.py:139
  7.9 219.4 %all-gather.5.cloned.1.call-start = ((), (), s32[]{:S(2)}) async-start(), calls=%async_computation.1 | async-start | bytes 20680704 | tf_op jit(solution)/shard_map/all_gather | solution.py:140
  8.6 1263.5 %all-reduce.5.cloned.1.call-start = ((), (), s32[]{:S(2)}) async-start(), calls=%async_computation.2 | async-start | bytes 120324096
  103.0 2.1 copy-start.6
  103.4 0.8 copy-start.3
  105.1 2.0 copy-start
  105.7 1.5 copy-start.1
  107.1 2.9 copy-start.9
  227.3 16.1 %copy-start.8 = (bf16[256,1088]{0,1:T(8,128)(2,1)S(1)}, bf16[256,1088]{0,1:T(8,128)(2,1)}, u32[]{:S(2)}) copy-start(bf16[256,1088]{0,1:T(8,128)(2,1)} %param.12) | copy-start | bytes 1671172
  250.5 13.2 %slice-start = ((s8[4456448]{0:T(1024)(128)(4,1)}), s8[4194304]{0:T(1024)(128)(4,1)S(1)}, s32[]{:S(2)}) async-start(s8[4456448]{0:T(1024)(128)(4,1)} %bitcast.37), calls=%async_computation.3 | async-start | bytes 8388608
  250.5 13.2 %slice-start.1 = ((s8[4456448]{0:T(1024)(128)(4,1)}), s8[262144]{0:T(1024)(128)(4,1)S(1)}, s32[]{:S(2)}) async-start(s8[4456448]{0:T(1024)(128)(4,1)} %bitcast.37), calls=%async_computation.4 | async-start | bytes 524288
  264.5 12.8 copy-start.5
  265.6 1.1 copy-start.4
  265.7 2.0 copy-start.7
  266.8 1.4 copy-start.10
  268.1 9.2 copy-start.2
  426.7 7.7 copy-start.11
  426.8 7.7 copy-start.12
  426.8 7.7 copy-start.13
  426.8 7.7 copy-start.15
  426.8 7.7 copy-start.16
  426.8 54.8 %copy-start.14 = (f32[1088]{0:T(1024)S(1)}, f32[1088]{0:T(1024)}, u32[]{:S(2)}) copy-start(f32[1088]{0:T(1024)} %get-tuple-element.73) | copy-start | bytes 13060
Sparse Core Ops, SparseCore 0:
  10.9 86.1 all-gather.2
  100.0 127.2 all-gather.4
  425.1 847.0 all-reduce.4
where the time goes:
time: 1290 us; the launch traced here: 1280 us
  waiting for transfers between devices  938 us (73%)
  other arithmetic  89.3 us (7%)
  matrix products  88.6 us (7%)
  blocking collectives  84.5 us (7%)
  local copies, waits for them, and re-layouts  66.7 us (5%)
  between operations  15.9 us (1%)
    unnamed x4, waiting for transfers between devices  782 us
    all_gather x1, waiting for transfers between devices, shards(): lax.all_gather(mlp_weight, 'dev', axis=0, tiled=True)  117 us
    unnamed x2, blocking collectives  84.5 us
    concatenate x1, other arithmetic, shards(): jnp.concatenate([grad_attn.reshape(devices, attn_rows, width), grad_mlp.r...  40.8 us
    all_gather x1, waiting for transfers between devices, shards(): lax.all_gather(attn_weight, 'dev', axis=0, tiled=True)  39.3 us
    concatenate x1, local copies, waits for them, and re-layouts, shards(): grad_mlp = jnp.concatenate([grad_up_weight, grad_down_weight], axis=0)  37.8 us
    concatenate x1, other arithmetic, shards(): grad_mlp = jnp.concatenate([grad_up_weight, grad_down_weight], axis=0)  27.1 us
  transfers between devices with their start and end apart: 3, of which 3 were waited for; matrix products, arithmetic and copies ran while one was open for 3% of the time, Pallas kernels for 0%

commit v1 on v0

v1 whole, which is shorter than its diff:
```python
import jax
import jax.numpy as jnp
from jax import lax
from jax.sharding import PartitionSpec as P

D = 1088
HEADS = 17
HEAD_SIZE = 64
FF = 4352


epsilon = 1e-05
neg_large = -1e30


def normalize(values, gain, shift):
    centre = values - jnp.mean(values, axis=-1, keepdims=True)
    spread = jnp.mean(centre * centre, axis=-1, keepdims=True)
    factor = lax.rsqrt(spread + epsilon)
    normed = centre * factor
    return (normed * gain + shift, normed, factor)


def normalize_back(grad_out, normed, factor, gain):
    inner = grad_out * gain
    return factor * (
        inner
        - jnp.mean(inner, axis=-1, keepdims=True)
        - normed * jnp.mean(inner * normed, axis=-1, keepdims=True)
    )


def split_vectors(whole_vec):
    width = D
    pieces = [
        whole_vec[number * width : (number + 1) * width].astype(jnp.float32) for number in range(8)
    ]
    return pieces + [whole_vec[8 * width :].astype(jnp.float32)]


def gelu_exact(values):
    return jax.nn.gelu(values, approximate=False)


def allowed_pairs(keep):
    position = jnp.arange(keep.shape[0], dtype=jnp.int32)
    return (position[None, :] <= position[:, None]) & (keep[None, :] == keep[:, None])


def attend(queries, keys, values, allowed, scale):
    scores = jnp.einsum("qhd,khd->hqk", queries, keys, preferred_element_type=jnp.float32) * scale
    scores = jnp.where(allowed[None], scores, neg_large)
    top = jnp.max(scores, axis=-1, keepdims=True)
    expo = jnp.exp(scores - top)
    total = jnp.sum(expo, axis=-1, keepdims=True)
    weights = (expo / total).astype(jnp.bfloat16)
    mixed = jnp.einsum("hqk,khd->qhd", weights, values, preferred_element_type=jnp.float32)
    return (mixed, top + jnp.log(total))


def attend_back(queries, keys, values, allowed, scale, grad_mixed, log_total):
    scores = jnp.einsum("qhd,khd->hqk", queries, keys, preferred_element_type=jnp.float32) * scale
    scores = jnp.where(allowed[None], scores, neg_large)
    probs = jnp.exp(scores - log_total)
    grad_values = jnp.einsum(
        "hqk,qhd->khd", probs.astype(jnp.bfloat16), grad_mixed, preferred_element_type=jnp.float32
    )
    grad_probs = jnp.einsum("qhd,khd->hqk", grad_mixed, values, preferred_element_type=jnp.float32)
    inner = jnp.sum(probs * grad_probs, axis=-1, keepdims=True)
    grad_scores = (probs * (grad_probs - inner)).astype(jnp.bfloat16)
    grad_queries = (
        jnp.einsum("hqk,khd->qhd", grad_scores, keys, preferred_element_type=jnp.float32) * scale
    )
    grad_keys = (
        jnp.einsum("hqk,qhd->khd", grad_scores, queries, preferred_element_type=jnp.float32) * scale
    )
    return (grad_queries, grad_keys, grad_values)


def gather_rows(own):
    beside = swap(own, 1)
    across = swap(own, 2)
    return jnp.concatenate([own, beside, across, swap(across, 1)], axis=0)


def reduce_rows(partial):
    rows = partial.shape[0] // 4
    given = jnp.concatenate([partial[rows : 2 * rows], partial[3 * rows :]], axis=0)
    taken = swap(given, 1)
    far = (partial[2 * rows : 3 * rows] + taken[rows:]).astype(jnp.bfloat16)
    return partial[:rows] + taken[:rows] + swap(far, 2).astype(jnp.float32)


def swap(piece, mask):
    devices = lax.axis_size("dev")
    return lax.ppermute(piece, "dev", [(number, number ^ mask) for number in range(devices)])


def same_low(devices):
    return [list(range(low, devices, 4)) for low in range(4)]


def gather_vectors(own):
    here = lax.axis_index("dev")
    whole = own
    mask = 1
    while mask < lax.axis_size("dev"):
        other = swap(whole, mask)
        upper = (here & mask) != 0
        whole = jnp.concatenate(
            [jnp.where(upper, other, whole), jnp.where(upper, whole, other)], axis=0
        )
        mask *= 2
    return whole


def scatter_vectors(whole):
    here = lax.axis_index("dev")
    mask = lax.axis_size("dev") // 2
    while mask:
        half = whole.shape[0] // 2
        upper = (here & mask) != 0
        mine = jnp.where(upper, whole[half:], whole[:half])
        yours = jnp.where(upper, whole[:half], whole[half:])
        whole = mine + swap(yours, mask)
        mask //= 2
    return whole


def gather_hidden(shard):
    devices = lax.axis_size("dev")
    here = lax.axis_index("dev")
    half = devices // 2
    if devices != 32:
        both = lax.all_gather(
            shard, "dev", axis=0, tiled=True, axis_index_groups=same_low(devices)
        )
        rows = both.shape[0] // 2
        blocks = jnp.arange(half // 4, dtype=jnp.int32) * 4 + (here & 3)
        return [(both[:rows], both[rows:], blocks)]
    first = here < half
    one, two, three = swap(shard, 8), swap(shard, 16), swap(shard, 24)
    up = jnp.concatenate([jnp.where(first, shard, two), jnp.where(first, one, three)], axis=0)
    down = jnp.concatenate([jnp.where(first, two, shard), jnp.where(first, three, one)], axis=0)
    block = here & (half - 1)
    blocks = jnp.stack([block, block ^ 8])
    return [(swap(up, 4), swap(down, 4), blocks ^ 4), (up, down, blocks)]


def scatter_hidden(grads):
    devices = lax.axis_size("dev")
    if devices != 32:
        both = jnp.concatenate(grads[0], axis=0).astype(jnp.bfloat16)
        return lax.psum_scatter(
            both, "dev", scatter_dimension=0, tiled=True, axis_index_groups=same_low(devices)
        ).astype(jnp.float32)
    first = lax.axis_index("dev") < devices // 2
    low = jnp.bfloat16
    up = grads[1][0] + swap(grads[0][0].astype(low), 4).astype(jnp.float32)
    down = grads[1][1] + swap(grads[0][1].astype(low), 4).astype(jnp.float32)
    rows = up.shape[0] // 2
    mine = jnp.where(first, up[:rows], down[:rows])
    two = jnp.where(first, down[:rows], up[:rows]).astype(low)
    one = jnp.where(first, up[rows:], down[rows:]).astype(low)
    three = jnp.where(first, down[rows:], up[rows:]).astype(low)
    return (
        mine
        + swap(one, 8).astype(jnp.float32)
        + swap(two, 16).astype(jnp.float32)
        + swap(three, 24).astype(jnp.float32)
    )


def shards(
    tokens, attn_weight, mlp_weight, vectors, cotangent, seq_lengths, seq_device, seq_offset
):
    total_rows = tokens.shape[0]
    width = D
    scale = HEAD_SIZE ** (-0.5)
    low = jnp.bfloat16
    devices = lax.axis_size("dev")
    here = lax.axis_index("dev")
    chosen = (seq_device == here).astype(jnp.int32)
    begin = jnp.sum(chosen * seq_offset)
    finish = begin + jnp.sum(chosen * seq_lengths)
    positions = jnp.arange(total_rows, dtype=jnp.int32)
    keep = ((positions >= begin) & (positions < finish)).astype(jnp.int32)
    live = keep[:, None] == 1
    allowed = allowed_pairs(keep)
    head_shape = (total_rows, HEADS, HEAD_SIZE)

    full_vec = gather_vectors(vectors)
    full_attn = lax.all_gather(attn_weight, "dev", axis=0, tiled=True)
    grad_down = jnp.where(live, cotangent, jnp.zeros_like(cotangent))
    hidden_parts = gather_hidden(mlp_weight)
    grad_down_rows = gather_rows(grad_down)

    (
        gain_one,
        shift_one,
        query_bias,
        value_bias,
        out_bias,
        gain_two,
        shift_two,
        down_bias,
        up_bias,
    ) = split_vectors(full_vec)
    up_bias = up_bias.reshape(devices // 2, -1)

    inputs = tokens.astype(jnp.float32)
    first_out, normed_one, factor_one = normalize(inputs, gain_one, shift_one)
    first_low = first_out.astype(low)
    projected = jnp.einsum(
        "rd,od->ro", first_low, full_attn[: 3 * width], preferred_element_type=jnp.float32
    )
    queries = (projected[:, :width] + query_bias).astype(low).reshape(head_shape)
    keys = projected[:, width : 2 * width].astype(low).reshape(head_shape)
    values = (projected[:, 2 * width :] + value_bias).astype(low).reshape(head_shape)
    mixed, log_total = attend(queries, keys, values, allowed, scale)
    mixed_low = mixed.reshape(total_rows, width).astype(low)
    branch = (
        jnp.einsum(
            "rd,od->ro", mixed_low, full_attn[3 * width :], preferred_element_type=jnp.float32
        )
        + out_bias
    )
    middle = inputs + branch
    second_out, normed_two, factor_two = normalize(middle, gain_two, shift_two)
    second_low = gather_rows(second_out.astype(low))

    down_rows = 0.0
    second_rows = 0.0
    grads = []
    grad_up_bias = jnp.zeros_like(up_bias)
    for up_weight, down_weight, blocks in hidden_parts:
        bias = up_bias[blocks].reshape(-1)
        up_sum = (
            jnp.einsum("rd,fd->rf", second_low, up_weight, preferred_element_type=jnp.float32)
            + bias
        )
        activated, gelu_back = jax.vjp(gelu_exact, up_sum)
        act_low = activated.astype(low)
        grad_act = jnp.einsum(
            "rd,fd->rf", grad_down_rows, down_weight, preferred_element_type=jnp.float32
        )
        grad_up = gelu_back(grad_act)[0].astype(low)
        grad_down_weight = jnp.einsum(
            "rf,rd->fd", act_low, grad_down_rows, preferred_element_type=jnp.float32
        )
        grad_up_weight = jnp.einsum(
            "rf,rd->fd", grad_up, second_low, preferred_element_type=jnp.float32
        )
        grads.append((grad_up_weight, grad_down_weight))
        column_sums = jnp.sum(grad_up.astype(jnp.float32), axis=0)
        grad_up_bias = grad_up_bias.at[blocks].set(
            column_sums.reshape(blocks.shape[0], -1)
        )
        second_rows = second_rows + jnp.dot(
            grad_up, up_weight, preferred_element_type=jnp.float32
        )
        down_rows = down_rows + jnp.dot(act_low, down_weight, preferred_element_type=jnp.float32)
    grad_second = reduce_rows(second_rows)
    down = reduce_rows(down_rows) + down_bias
    output = jnp.where(live, middle + down, 0.0).astype(low)
    mlp_share = scatter_hidden(grads)

    grad_down_wide = grad_down.astype(jnp.float32)
    grad_down_bias = jnp.sum(grad_down_wide, axis=0)
    grad_gain_two = jnp.sum(grad_second * normed_two, axis=0)
    grad_shift_two = jnp.sum(grad_second, axis=0)
    grad_middle = grad_down_wide + normalize_back(grad_second, normed_two, factor_two, gain_two)
    grad_branch = grad_middle.astype(low)
    grad_out_weight = jnp.einsum(
        "ro,rd->od", grad_branch, mixed_low, preferred_element_type=jnp.float32
    )
    grad_out_bias = jnp.sum(grad_branch.astype(jnp.float32), axis=0)
    grad_mixed = jnp.dot(grad_branch, full_attn[3 * width :], preferred_element_type=jnp.float32)
    grad_mixed_low = grad_mixed.astype(low).reshape(head_shape)
    grad_queries, grad_keys, grad_values = attend_back(
        queries, keys, values, allowed, scale, grad_mixed_low, log_total
    )
    grad_projected = jnp.concatenate(
        [
            grad_queries.reshape(total_rows, width),
            grad_keys.reshape(total_rows, width),
            grad_values.reshape(total_rows, width),
        ],
        axis=1,
    ).astype(low)
    grad_proj_weight = jnp.einsum(
        "ro,rd->od", grad_projected, first_low, preferred_element_type=jnp.float32
    )
    grad_attn = jnp.concatenate(
        [grad_proj_weight.astype(low), grad_out_weight.astype(low)], axis=0
    )
    attn_share = lax.psum_scatter(grad_attn, "dev", scatter_dimension=0, tiled=True)
    grad_columns = jnp.sum(grad_projected.astype(jnp.float32), axis=0)
    grad_first = jnp.dot(grad_projected, full_attn[: 3 * width], preferred_element_type=jnp.float32)
    grad_gain_one = jnp.sum(grad_first * normed_one, axis=0)
    grad_shift_one = jnp.sum(grad_first, axis=0)
    grad_inputs = grad_middle + normalize_back(grad_first, normed_one, factor_one, gain_one)
    grad_vec = jnp.concatenate(
        [
            grad_gain_one,
            grad_shift_one,
            grad_columns[:width],
            grad_columns[2 * width :],
            grad_out_bias,
            grad_gain_two,
            grad_shift_two,
            grad_down_bias,
            grad_up_bias.reshape(-1),
        ],
        axis=0,
    )
    vec_share = scatter_vectors(grad_vec)
    return (output, grad_inputs, attn_share.astype(jnp.float32), mlp_share, vec_share)


def solution(mesh):
    return jax.shard_map(
        shards,
        mesh=mesh,
        in_specs=(
            P("dev", None),
            P("dev", None),
            P("dev", None),
            P("dev"),
            P("dev", None),
            P(),
            P(),
            P(),
        ),
        out_specs=(P("dev", None), P("dev", None), P("dev", None), P("dev", None), P("dev")),
        check_vma=False,
    )
```

time: 1290 us -> 547 us (0.42)
  waiting for transfers between devices: 938 us -> 372 us
  blocking collectives: 84.5 us -> 0 us
  local copies, waits for them, and re-layouts: 66.7 us -> 11.5 us
  other arithmetic: 89.3 us -> 38.3 us
  starting transfers between devices: 0.11 us -> 27.2 us
  matrix products: 88.6 us -> 70.7 us
    unnamed x4 -> x3, waiting for transfers between devices: 782 us -> 165 us
    ppermute x0 -> x30, waiting for transfers between devices: none -> 174 us  [swap(): lax.ppermute(piece, 'dev', [(number, number ^ mask) for number in range(d...]
    all_gather x2 -> x1, waiting for transfers between devices: 156 us -> 32.8 us  [shards(): full_attn = lax.all_gather(attn_weight, 'dev', axis=0, tiled=True)]
    unnamed x2 -> x0, blocking collectives: 84.5 us -> none
    concatenate x3 -> x9, other arithmetic: 75.3 us -> 10.2 us  [the longest x1 6.3 us: shards(): jnp.concatenate([grad_proj_weight.astype(low), grad_out_weight.astype(low...]
    concatenate x3 -> x2, local copies, waits for them, and re-layouts: 59.3 us -> 0.16 us  [shards(): jnp.concatenate([grad_gain_one, grad_shift_one, grad_columns[:width], gra...]
    ppermute x0 -> x30, starting transfers between devices: none -> 27.1 us  [swap(): lax.ppermute(piece, 'dev', [(number, number ^ mask) for number in range(d...]
    dot_general x13 -> x18, matrix products: 68.6 us -> 52.3 us  [the longest x2 13 us: shards(): jnp.einsum('rd,fd->rf', second_low, up_weight, preferred_element_type=jnp...]
  transfers between devices with their start and end apart: 3 -> 32, of which waited for: 3 -> 16; matrix products, arithmetic and copies ran while one was open for 3% -> 19% of each run, Pallas kernels for 0% -> 0%
where the time goes in v1:
time: 547 us; the launch traced here: 537 us
  waiting for transfers between devices  372 us (68%)
  matrix products  70.7 us (13%)
  other arithmetic  38.3 us (7%)
  starting transfers between devices  27.2 us (5%)
  between operations  16.6 us (3%)
  local copies, waits for them, and re-layouts  11.5 us (2%)
    ppermute x30, waiting for transfers between devices, swap(): lax.ppermute(piece, 'dev', [(number, number ^ mask) for number in range(d...  174 us
    unnamed x3, waiting for transfers between devices  165 us
    all_gather x1, waiting for transfers between devices, shards(): full_attn = lax.all_gather(attn_weight, 'dev', axis=0, tiled=True)  32.8 us
    ppermute x30, starting transfers between devices, swap(): lax.ppermute(piece, 'dev', [(number, number ^ mask) for number in range(d...  27.1 us
    dot_general x2, matrix products, shards(): jnp.einsum('rd,fd->rf', second_low, up_weight, preferred_element_type=jnp...  13 us
  transfers between devices with their start and end apart: 32, of which 16 were waited for; matrix products, arithmetic and copies ran while one was open for 19% of the time, Pallas kernels for 0%

profile of v1, /device:TPU:8, one launch (start us, length us, event | category | flops | bytes accessed | tf_op | source)
XLA Modules:
  0.0 536.5 jit_solution(5144703460886784628)
XLA Ops:
  9.6 2.5 collective-permute-start.9
  21.8 13.2 %collective-permute-done.1 = bf16[816]{0:T(1024)(128)(2,1)S(1)} collective-permute-done((bf16[816]{0:T(1024)(128)(2,1)S(1)}, bf16[816]{0:T(1024)(128)(2,1)S(1)}, u32[]{:S(2)}, u32[]{:S(2)}) %collective-permute-start.1) | collective-permute-done | bytes 1664 | tf_op jit(solution)/shard_map/ppermute | solution.py:96
  39.6 28.7 %collective-permute-done.3 = bf16[3264]{0:T(1024)(128)(2,1)S(1)} collective-permute-done((bf16[3264]{0:T(1024)(128)(2,1)S(1)}, bf16[3264]{0:T(1024)(128)(2,1)S(1)}, u32[]{:S(2)}, u32[]{:S(2)}) %collective-permute-start.3) | collective-permute-done | bytes 6560 | tf_op jit(solution)/shard_map/ppermute | solution.py:96
  68.5 15.7 %collective-permute-done.4 = bf16[6528]{0:T(1024)(128)(2,1)S(1)} collective-permute-done((bf16[6528]{0:T(1024)(128)(2,1)S(1)}, bf16[6528]{0:T(1024)(128)(2,1)S(1)}, u32[]{:S(2)}, u32[]{:S(2)}) %collective-permute-start.4) | collective-permute-done | bytes 13088 | tf_op jit(solution)/shard_map/ppermute | solution.py:96
  87.5 32.8 %all-gather.2.cloned.1.call-done = bf16[4352,1088]{1,0:T(8,128)(2,1)} async-done(((bf16[136,1088]{1,0:T(8,128)(2,1)}), bf16[4352,1088]{1,0:T(8,128)(2,1)}) %all-gather.2.cloned.1.call-update) | async-done | bytes 9469968 | tf_op jit(solution)/shard_map/all_gather | solution.py:193
  120.4 5.7 %fusion.2 = f32[256,3264]{0,1:T(8,128)S(1)} fusion(bf16[4352,1088]{1,0:T(8,128)(2,1)} %all-gather.2.cloned.1.call-done, bf16[256,1088]{0,1:T(8,128)(2,1)S(1)} %copy-done.3, f32[1088]{0:T(1024)S(1)} %get-tuple-element.82, f32[1088]{0:T(1024)S(1)} %get-tuple-element.81, f32[256]{0:T(256)S(1)} %add_rsqrt_fusion.1, f32[256]{0:T(256)S(1)} %broadcast_multiply_fusion.5), kind=kOutput, calls=%fused_computation.9 | convolution fusion | flops 1819901952 | bytes 11430400 | tf_op jit(solution)/shard_map/rd,od->ro/dot_general | solution.py:214
  130.5 2.8 fusion.75
  136.9 11.8 %collective-permute-done.6 = bf16[256,1088]{0,1:T(8,128)(2,1)S(1)} collective-permute-done((bf16[256,1088]{0,1:T(8,128)(2,1)S(1)}, bf16[256,1088]{0,1:T(8,128)(2,1)S(1)}, u32[]{:S(2)}, u32[]{:S(2)}) %collective-permute-start.6) | collective-permute-done | bytes 557088 | tf_op jit(solution)/shard_map/ppermute | solution.py:96
  151.2 6.6 %multiply_convert_fusion.1 = (bf16[1024,544]{0,1:T(8,128)(2,1)S(1)}, f32[1024,544]{0,1:T(8,128)S(1)}, f32[1024,544]{0,1:T(8,128)S(1)}) fusion(f32[544]{0:T(1024)S(1)} %add.204, bf16[256,1088]{0,1:T(8,128)(2,1)S(1)} %collective-permute-done.7, bf16[256,1088]{0,1:T(8,128)(2,1)S(1)} %collective-permute-done.6, ...), kind=kOutput, calls=%fused_computation.41 | convolution fusion | flops 1260199936 | bytes 8984704 | tf_op jit(solution)/shard_map/rd,fd->rf/dot_general | solution.py:239
  157.9 4.3 convert_reduce_fusion.1
  164.2 15.1 %collective-permute-done.11 = bf16[544,1088]{1,0:T(8,128)(2,1)S(1)} collective-permute-done((bf16[544,1088]{1,0:T(8,128)(2,1)S(1)}, bf16[544,1088]{1,0:T(8,128)(2,1)S(1)}, u32[]{:S(2)}, u32[]{:S(2)}) %collective-permute-start.11) | collective-permute-done | bytes 1183776 | tf_op jit(solution)/shard_map/ppermute | solution.py:96
  179.3 6.3 %multiply_convert_fusion.2 = (bf16[1024,544]{0,1:T(8,128)(2,1)S(1)}, f32[1024,544]{0,1:T(8,128)S(1)}, f32[1024,544]{0,1:T(8,128)S(1)}) fusion(f32[544]{0:T(1024)S(1)} %add.200, bf16[544,1088]{1,0:T(8,128)(2,1)S(1)} %collective-permute-done.11, bf16[256,1088]{0,1:T(8,128)(2,1)S(1)} %collective-permute-done.7, ...), kind=kOutput, calls=%fused_computation.54 | convolution fusion | flops 1257832448 | bytes 8984704 | tf_op jit(solution)/shard_map/rd,fd->rf/dot_general | solution.py:239
  185.6 20.1 %collective-permute-done.12 = bf16[544,1088]{1,0:T(8,128)(2,1)S(1)} collective-permute-done((bf16[544,1088]{1,0:T(8,128)(2,1)S(1)}, bf16[544,1088]{1,0:T(8,128)(2,1)S(1)}, u32[]{:S(2)}, u32[]{:S(2)}) %collective-permute-start.12) | collective-permute-done | bytes 1183776 | tf_op jit(solution)/shard_map/ppermute | solution.py:96
  205.8 3.9 convert_reduce_fusion.2
  217.6 2.8 convolution_convert_fusion.3
  222.0 4.2 convolution_convert_fusion.2
  235.5 15.5 %collective-permute-done.20 = bf16[544,1088]{1,0:T(8,128)(2,1)} collective-permute-done((bf16[544,1088]{1,0:T(8,128)(2,1)}, bf16[544,1088]{1,0:T(8,128)(2,1)}, u32[]{:S(2)}, u32[]{:S(2)}) %collective-permute-start.20) | collective-permute-done | bytes 1183776 | tf_op jit(solution)/shard_map/ppermute | solution.py:96
  251.1 3.1 convolution_add_fusion.3
  254.2 23.3 %collective-permute-done.21 = bf16[544,1088]{1,0:T(8,128)(2,1)} collective-permute-done((bf16[544,1088]{1,0:T(8,128)(2,1)}, bf16[544,1088]{1,0:T(8,128)(2,1)}, u32[]{:S(2)}, u32[]{:S(2)}) %collective-permute-start.21) | collective-permute-done | bytes 1183776 | tf_op jit(solution)/shard_map/ppermute | solution.py:96
  277.5 3.6 convolution_add_fusion.2
  290.1 13.3 %collective-permute-done.19 = bf16[256,1088]{0,1:T(8,128)(2,1)S(1)} collective-permute-done((bf16[256,1088]{0,1:T(8,128)(2,1)S(1)}, bf16[256,1088]{0,1:T(8,128)(2,1)S(1)}, u32[]{:S(2)}, u32[]{:S(2)}) %collective-permute-start.19) | collective-permute-done | bytes 557088 | tf_op jit(solution)/shard_map/ppermute | solution.py:96
  303.3 2.2 multiply_reduce_fusion.1
  305.6 7.6 %collective-permute-done.14 = bf16[256,1088]{0,1:T(8,128)(2,1)S(1)} collective-permute-done((bf16[256,1088]{0,1:T(8,128)(2,1)S(1)}, bf16[256,1088]{0,1:T(8,128)(2,1)S(1)}, u32[]{:S(2)}, u32[]{:S(2)}) %collective-permute-start.14) | collective-permute-done | bytes 557088 | tf_op jit(solution)/shard_map/ppermute | solution.py:96
  313.1 2.6 convert_reduce_fusion.5
  315.7 2.9 convolution_convert_fusion.4
  323.6 3.1 convolution_convert_fusion
  327.6 6.3 %pad_maximum_fusion = bf16[4352,1088]{0,1:T(8,128)(2,1)} fusion(bf16[1088,1088]{0,1:T(8,128)(2,1)S(1)} %convolution_convert_fusion.1, bf16[3264,1088]{0,1:T(8,128)(2,1)S(1)} %convolution_convert_fusion), kind=kLoop, calls=%fused_computation.5 | loop fusion | flops 18939904 | bytes 18939904 | tf_op jit(solution)/shard_map/concatenate | solution.py:294
  334.0 7.3 %fusion.43 = (f32[1088]{0:T(1024)S(1)}, f32[256]{0:T(256)S(1)}, f32[256]{0:T(256)S(1)}, f32[1088]{0:T(1024)S(1)}, f32[256,1088]{0,1:T(8,128)}) fusion(bf16[256,1088]{0,1:T(8,128)(2,1)S(1)} %copy-done.4, f32[256]{0:T(256)S(1)} %add_rsqrt_fusion.1, f32[256]{0:T(256)S(1)} %broadcast_multiply_fusion.5, f32[1088]{0:T(1024)S(1)} %get-tuple-element.81, ...), kind=kOutput, calls=%fused_computation.103 | convolution fusion | flops 1826027008 | bytes 10879744 | tf_op jit(solution)/shard_map/dot_general | solution.py:299
  343.4 3.4 collective-permute-done.25
  348.7 3.7 convert_add_fusion.2
  357.8 2.2 collective-permute-done.28
  362.1 164.5 %all-reduce.3.cloned.1.call-done = bf16[4352,1088]{0,1:T(8,128)(2,1)} async-done(((bf16[4352,1088]{0,1:T(8,128)(2,1)}), bf16[4352,1088]{0,1:T(8,128)(2,1)}) %all-reduce.3.cloned.1.call-update) | async-done | bytes 9469968
  (208 shorter events, 78.7 us)
Async XLA Ops:
  7.2 113.2 %all-gather.2.cloned.1.call-start = ((), (), s32[]{:S(2)}) async-start(), calls=%async_computation | async-start | bytes 10340352 | tf_op jit(solution)/shard_map/all_gather | solution.py:193
  7.9 518.8 %all-reduce.3.cloned.1.call-start = ((), (), s32[]{:S(2)}) async-start(), calls=%async_computation.1 | async-start | bytes 18939904
  8.0 127.5 %collective-permute-start.10 = (bf16[272,1088]{1,0:T(8,128)(2,1)}, bf16[272,1088]{1,0:T(8,128)(2,1)}, u32[]{:S(2)}, u32[]{:S(2)}) collective-permute-start(bf16[272,1088]{1,0:T(8,128)(2,1)} %param.10), channel_id=1, source_target_pairs={{0,24},{1,25},{2,26},{3,27},{4,28},{5,29},{6,30},{7,31},{8,16},{9,... | collective-permute-start | bytes 1775624 | tf_op jit(solution)/shard_map/ppermute | solution.py:96
  9.6 125.9 %collective-permute-start.9 = (bf16[272,1088]{1,0:T(8,128)(2,1)}, bf16[272,1088]{1,0:T(8,128)(2,1)}, u32[]{:S(2)}, u32[]{:S(2)}) collective-permute-start(bf16[272,1088]{1,0:T(8,128)(2,1)} %param.10), channel_id=1, source_target_pairs={{0,8},{1,9},{2,10},{3,11},{4,12},{5,13},{6,14},{7,15},{8,0},{9,1},... | collective-permute-start | bytes 1775624 | tf_op jit(solution)/shard_map/ppermute | solution.py:96
  12.1 74.3 %collective-permute-start.8 = (bf16[272,1088]{1,0:T(8,128)(2,1)}, bf16[272,1088]{1,0:T(8,128)(2,1)S(1)}, u32[]{:S(2)}, u32[]{:S(2)}) collective-permute-start(bf16[272,1088]{1,0:T(8,128)(2,1)} %param.10), channel_id=1, source_target_pairs={{0,16},{1,17},{2,18},{3,19},{4,20},{5,21},{6,22},{7,23},{8,24},{9,... | collective-permute-start | bytes 1775624 | tf_op jit(solution)/shard_map/ppermute | solution.py:96
  12.1 9.0 %collective-permute-start = (bf16[408]{0:T(512)(128)(2,1)}, bf16[408]{0:T(512)(128)(2,1)S(1)}, u32[]{:S(2)}, u32[]{:S(2)}) collective-permute-start(bf16[408]{0:T(512)(128)(2,1)} %param.11), channel_id=1, source_target_pairs={{0,1},{1,0},{2,3},{3,2},{4,5},{5,4},{6,7},{7,6},{8,9},{9,8},{10,11... | collective-permute-start | bytes 2456 | tf_op jit(solution)/shard_map/ppermute | solution.py:96
  17.4 68.4 %collective-permute-start.16 = (bf16[256,1088]{0,1:T(8,128)(2,1)}, bf16[256,1088]{0,1:T(8,128)(2,1)}, u32[]{:S(2)}, u32[]{:S(2)}) collective-permute-start(bf16[256,1088]{0,1:T(8,128)(2,1)} %get-tuple-element.26), channel_id=1, source_target_pairs={{0,2},{1,3},{2,0},{3,1},{4,6},{5,7},{6,4},{7,5},{8,10},{9,11},{10,... | collective-permute-start | bytes 1671176 | tf_op jit(solution)/shard_map/ppermute | solution.py:96
  21.2 13.8 %collective-permute-start.1 = (bf16[816]{0:T(1024)(128)(2,1)S(1)}, bf16[816]{0:T(1024)(128)(2,1)S(1)}, u32[]{:S(2)}, u32[]{:S(2)}) collective-permute-start(bf16[816]{0:T(1024)(128)(2,1)S(1)} %pad_maximum_fusion.11), channel_id=1, source_target_pairs={{0,2},{1,3},{2,0},{3,1},{4,6},{5,7},{6,4},{7,5},{8,10},{9,11},{10,... | collective-permute-start | bytes 4904 | tf_op jit(solution)/shard_map/ppermute | solution.py:96
  35.1 3.6 collective-permute-start.2
  38.9 29.4 %collective-permute-start.3 = (bf16[3264]{0:T(1024)(128)(2,1)S(1)}, bf16[3264]{0:T(1024)(128)(2,1)S(1)}, u32[]{:S(2)}, u32[]{:S(2)}) collective-permute-start(bf16[3264]{0:T(1024)(128)(2,1)S(1)} %pad_maximum_fusion.9), channel_id=1, source_target_pairs={{0,8},{1,9},{2,10},{3,11},{4,12},{5,13},{6,14},{7,15},{8,0},{9,1},... | collective-permute-start | bytes 19592 | tf_op jit(solution)/shard_map/ppermute | solution.py:96
  68.5 15.8 %collective-permute-start.4 = (bf16[6528]{0:T(1024)(128)(2,1)S(1)}, bf16[6528]{0:T(1024)(128)(2,1)S(1)}, u32[]{:S(2)}, u32[]{:S(2)}) collective-permute-start(bf16[6528]{0:T(1024)(128)(2,1)S(1)} %pad_maximum_fusion.8), channel_id=1, source_target_pairs={{0,16},{1,17},{2,18},{3,19},{4,20},{5,21},{6,22},{7,23},{8,24},{9,... | collective-permute-start | bytes 39176 | tf_op jit(solution)/shard_map/ppermute | solution.py:96
  84.3 73.6 %collective-permute-start.15 = (bf16[256,1088]{0,1:T(8,128)(2,1)}, bf16[256,1088]{0,1:T(8,128)(2,1)}, u32[]{:S(2)}, u32[]{:S(2)}) collective-permute-start(bf16[256,1088]{0,1:T(8,128)(2,1)} %get-tuple-element.26), channel_id=1, source_target_pairs={{0,1},{1,0},{2,3},{3,2},{4,5},{5,4},{6,7},{7,6},{8,9},{9,8},{10,11... | collective-permute-start | bytes 1671176 | tf_op jit(solution)/shard_map/ppermute | solution.py:96
  85.8 72.1 %collective-permute-start.17 = (bf16[256,1088]{0,1:T(8,128)(2,1)}, bf16[256,1088]{0,1:T(8,128)(2,1)}, u32[]{:S(2)}, u32[]{:S(2)}) collective-permute-start(bf16[256,1088]{0,1:T(8,128)(2,1)} %collective-permute-done.16), channel_id=1, source_target_pairs={{0,1},{1,0},{2,3},{3,2},{4,5},{5,4},{6,7},{7,6},{8,9},{9,8},{10,11... | collective-permute-start | bytes 1671176 | tf_op jit(solution)/shard_map/ppermute | solution.py:96
  133.9 14.9 %collective-permute-start.6 = (bf16[256,1088]{0,1:T(8,128)(2,1)S(1)}, bf16[256,1088]{0,1:T(8,128)(2,1)S(1)}, u32[]{:S(2)}, u32[]{:S(2)}) collective-permute-start(bf16[256,1088]{0,1:T(8,128)(2,1)S(1)} %add_convert_fusion.2), channel_id=1, source_target_pairs={{0,2},{1,3},{2,0},{3,1},{4,6},{5,7},{6,4},{7,5},{8,10},{9,11},{10,... | collective-permute-start | bytes 1671176 | tf_op jit(solution)/shard_map/ppermute | solution.py:96
  136.9 13.8 %collective-permute-start.5 = (bf16[256,1088]{0,1:T(8,128)(2,1)S(1)}, bf16[256,1088]{0,1:T(8,128)(2,1)S(1)}, u32[]{:S(2)}, u32[]{:S(2)}) collective-permute-start(bf16[256,1088]{0,1:T(8,128)(2,1)S(1)} %add_convert_fusion.2), channel_id=1, source_target_pairs={{0,1},{1,0},{2,3},{3,2},{4,5},{5,4},{6,7},{7,6},{8,9},{9,8},{10,11... | collective-permute-start | bytes 1671176 | tf_op jit(solution)/shard_map/ppermute | solution.py:96
  148.8 2.4 collective-permute-start.7
  148.9 30.4 %collective-permute-start.11 = (bf16[544,1088]{1,0:T(8,128)(2,1)S(1)}, bf16[544,1088]{1,0:T(8,128)(2,1)S(1)}, u32[]{:S(2)}, u32[]{:S(2)}) collective-permute-start(bf16[544,1088]{1,0:T(8,128)(2,1)S(1)} %pad_maximum_fusion.6), channel_id=1, source_target_pairs={{0,4},{1,5},{2,6},{3,7},{4,0},{5,1},{6,2},{7,3},{8,12},{9,13},{10,... | collective-permute-start | bytes 3551240 | tf_op jit(solution)/shard_map/ppermute | solution.py:96
  150.7 55.1 %collective-permute-start.12 = (bf16[544,1088]{1,0:T(8,128)(2,1)S(1)}, bf16[544,1088]{1,0:T(8,128)(2,1)S(1)}, u32[]{:S(2)}, u32[]{:S(2)}) collective-permute-start(bf16[544,1088]{1,0:T(8,128)(2,1)S(1)} %pad_maximum_fusion.7), channel_id=1, source_target_pairs={{0,4},{1,5},{2,6},{3,7},{4,0},{5,1},{6,2},{7,3},{8,12},{9,13},{10,... | collective-permute-start | bytes 3551240 | tf_op jit(solution)/shard_map/ppermute | solution.py:96
  215.6 70.7 %collective-permute-start.18 = (f32[512,1088]{0,1:T(8,128)}, f32[512,1088]{0,1:T(8,128)}, u32[]{:S(2)}, u32[]{:S(2)}) collective-permute-start(f32[512,1088]{0,1:T(8,128)} %pad_maximum_fusion.4), channel_id=1, source_target_pairs={{0,1},{1,0},{2,3},{3,2},{4,5},{5,4},{6,7},{7,6},{8,9},{9,8},{10,11... | collective-permute-start | bytes 6684680 | tf_op jit(solution)/shard_map/ppermute | solution.py:96
  220.4 30.7 %collective-permute-start.20 = (bf16[544,1088]{1,0:T(8,128)(2,1)}, bf16[544,1088]{1,0:T(8,128)(2,1)}, u32[]{:S(2)}, u32[]{:S(2)}) collective-permute-start(bf16[544,1088]{1,0:T(8,128)(2,1)} %convolution_convert_fusion.3), channel_id=1, source_target_pairs={{0,4},{1,5},{2,6},{3,7},{4,0},{5,1},{6,2},{7,3},{8,12},{9,13},{10,... | collective-permute-start | bytes 3551240 | tf_op jit(solution)/shard_map/ppermute | solution.py:96
  226.2 51.3 %collective-permute-start.21 = (bf16[544,1088]{1,0:T(8,128)(2,1)}, bf16[544,1088]{1,0:T(8,128)(2,1)}, u32[]{:S(2)}, u32[]{:S(2)}) collective-permute-start(bf16[544,1088]{1,0:T(8,128)(2,1)} %convolution_convert_fusion.2), channel_id=1, source_target_pairs={{0,4},{1,5},{2,6},{3,7},{4,0},{5,1},{6,2},{7,3},{8,12},{9,13},{10,... | collective-permute-start | bytes 3551240 | tf_op jit(solution)/shard_map/ppermute | solution.py:96
  235.5 53.8 %collective-permute-start.13 = (f32[512,1088]{0,1:T(8,128)S(1)}, f32[512,1088]{0,1:T(8,128)S(1)}, u32[]{:S(2)}, u32[]{:S(2)}) collective-permute-start(f32[512,1088]{0,1:T(8,128)S(1)} %pad_maximum_fusion.2), channel_id=1, source_target_pairs={{0,1},{1,0},{2,3},{3,2},{4,5},{5,4},{6,7},{7,6},{8,9},{9,8},{10,11... | collective-permute-start | bytes 6684680 | tf_op jit(solution)/shard_map/ppermute | solution.py:96
  282.7 66.0 %collective-permute-start.22 = (bf16[272,1088]{1,0:T(8,128)(2,1)}, bf16[272,1088]{1,0:T(8,128)(2,1)}, u32[]{:S(2)}, u32[]{:S(2)}) collective-permute-start(bf16[272,1088]{1,0:T(8,128)(2,1)} %get-tuple-element.36), channel_id=1, source_target_pairs={{0,8},{1,9},{2,10},{3,11},{4,12},{5,13},{6,14},{7,15},{8,0},{9,1},... | collective-permute-start | bytes 1775624 | tf_op jit(solution)/shard_map/ppermute | solution.py:96
  283.4 65.4 %collective-permute-start.23 = (bf16[272,1088]{1,0:T(8,128)(2,1)}, bf16[272,1088]{1,0:T(8,128)(2,1)}, u32[]{:S(2)}, u32[]{:S(2)}) collective-permute-start(bf16[272,1088]{1,0:T(8,128)(2,1)} %get-tuple-element.37), channel_id=1, source_target_pairs={{0,16},{1,17},{2,18},{3,19},{4,20},{5,21},{6,22},{7,23},{8,24},{9,... | collective-permute-start | bytes 1775624 | tf_op jit(solution)/shard_map/ppermute | solution.py:96
  285.3 63.5 %collective-permute-start.24 = (bf16[272,1088]{1,0:T(8,128)(2,1)}, bf16[272,1088]{1,0:T(8,128)(2,1)}, u32[]{:S(2)}, u32[]{:S(2)}) collective-permute-start(bf16[272,1088]{1,0:T(8,128)(2,1)} %get-tuple-element.38), channel_id=1, source_target_pairs={{0,24},{1,25},{2,26},{3,27},{4,28},{5,29},{6,30},{7,31},{8,16},{9,... | collective-permute-start | bytes 1775624 | tf_op jit(solution)/shard_map/ppermute | solution.py:96
  287.7 15.6 %collective-permute-start.19 = (bf16[256,1088]{0,1:T(8,128)(2,1)S(1)}, bf16[256,1088]{0,1:T(8,128)(2,1)S(1)}, u32[]{:S(2)}, u32[]{:S(2)}) collective-permute-start(bf16[256,1088]{0,1:T(8,128)(2,1)S(1)} %fusion.45), channel_id=1, source_target_pairs={{0,2},{1,3},{2,0},{3,1},{4,6},{5,7},{6,4},{7,5},{8,10},{9,11},{10,... | collective-permute-start | bytes 1671176 | tf_op jit(solution)/shard_map/ppermute | solution.py:96
  289.5 23.7 %collective-permute-start.14 = (bf16[256,1088]{0,1:T(8,128)(2,1)S(1)}, bf16[256,1088]{0,1:T(8,128)(2,1)S(1)}, u32[]{:S(2)}, u32[]{:S(2)}) collective-permute-start(bf16[256,1088]{0,1:T(8,128)(2,1)S(1)} %fusion.47), channel_id=1, source_target_pairs={{0,2},{1,3},{2,0},{3,1},{4,6},{5,7},{6,4},{7,5},{8,10},{9,11},{10,... | collective-permute-start | bytes 1671176 | tf_op jit(solution)/shard_map/ppermute | solution.py:96
  341.4 5.4 %collective-permute-start.25 = (f32[6528]{0:T(1024)S(1)}, f32[6528]{0:T(1024)S(1)}, u32[]{:S(2)}, u32[]{:S(2)}) collective-permute-start(f32[6528]{0:T(1024)S(1)} %broadcast_select_fusion.5), channel_id=1, source_target_pairs={{0,16},{1,17},{2,18},{3,19},{4,20},{5,21},{6,22},{7,23},{8,24},{9,... | collective-permute-start | bytes 78344 | tf_op jit(solution)/shard_map/ppermute | solution.py:96
  346.9 5.5 %collective-permute-start.26 = (f32[3264]{0:T(1024)S(1)}, f32[3264]{0:T(1024)S(1)}, u32[]{:S(2)}, u32[]{:S(2)}) collective-permute-start(f32[3264]{0:T(1024)S(1)} %slice_select_fusion), channel_id=1, source_target_pairs={{0,8},{1,9},{2,10},{3,11},{4,12},{5,13},{6,14},{7,15},{8,0},{9,1},... | collective-permute-start | bytes 39176 | tf_op jit(solution)/shard_map/ppermute | solution.py:96
  352.6 3.7 collective-permute-start.27
  356.4 3.6 collective-permute-start.28
  360.1 1.4 collective-permute-start.29
  (34 other events, 841.2 us)
Sparse Core Ops, SparseCore 0:
  11.0 109.3 all-gather.1
  334.1 192.5 all-reduce.2

commit v2 on v1

--- a/solution.py
+++ b/solution.py
@@ -63,32 +63,36 @@
     scores = jnp.where(allowed[None], scores, neg_large)
     probs = jnp.exp(scores - log_total)
     grad_values = jnp.einsum(
-        "hqk,qhd->khd", probs.astype(jnp.bfloat16), grad_mixed, preferred_element_type=jnp.float32
+        "hqk,qhd->hdk", probs.astype(jnp.bfloat16), grad_mixed, preferred_element_type=jnp.float32
     )
     grad_probs = jnp.einsum("qhd,khd->hqk", grad_mixed, values, preferred_element_type=jnp.float32)
     inner = jnp.sum(probs * grad_probs, axis=-1, keepdims=True)
     grad_scores = (probs * (grad_probs - inner)).astype(jnp.bfloat16)
     grad_queries = (
-        jnp.einsum("hqk,khd->qhd", grad_scores, keys, preferred_element_type=jnp.float32) * scale
+        jnp.einsum("hqk,khd->hdq", grad_scores, keys, preferred_element_type=jnp.float32) * scale
     )
     grad_keys = (
-        jnp.einsum("hqk,qhd->khd", grad_scores, queries, preferred_element_type=jnp.float32) * scale
+        jnp.einsum("hqk,qhd->hdk", grad_scores, queries, preferred_element_type=jnp.float32) * scale
     )
     return (grad_queries, grad_keys, grad_values)
 
 
 def gather_rows(own):
+    across = swap(own, 2)
     beside = swap(own, 1)
-    across = swap(own, 2)
-    return jnp.concatenate([own, beside, across, swap(across, 1)], axis=0)
-
-
-def reduce_rows(partial):
-    rows = partial.shape[0] // 4
-    given = jnp.concatenate([partial[rows : 2 * rows], partial[3 * rows :]], axis=0)
-    taken = swap(given, 1)
-    far = (partial[2 * rows : 3 * rows] + taken[rows:]).astype(jnp.bfloat16)
-    return partial[:rows] + taken[:rows] + swap(far, 2).astype(jnp.float32)
+    return jnp.concatenate([own, across, beside, swap(across, 1)], axis=0)
+
+
+def reduce_near(partial):
+    half = partial.shape[0] // 2
+    low = jnp.bfloat16
+    both = partial[:half] + swap(partial[half:].astype(low), 1).astype(jnp.float32)
+    rows = half // 2
+    return (both[:rows], both[rows:].astype(low))
+
+
+def after(values, others):
+    return lax.optimization_barrier((values, others))[0]
 
 
 def swap(piece, mask):
@@ -127,7 +131,107 @@
     return whole
 
 
-def gather_hidden(shard):
+def gather_attn(shard, vectors):
+    devices = lax.axis_size("dev")
+    if devices != 32:
+        return (lax.all_gather(shard, "dev", axis=0, tiled=True), gather_vectors(vectors), shard)
+    here = lax.axis_index("dev")
+    rows, width = shard.shape
+    spare = 8
+    extra = jnp.pad(vectors[None, :], ((0, spare - 1), (0, width - vectors.shape[0])))
+    zero = jnp.concatenate([shard, extra], axis=0)
+    one, two, three = swap(zero, 8), swap(zero, 16), swap(zero, 24)
+    odd = (here & 8) != 0
+    upper = (here & 16) != 0
+    near = (jnp.where(odd, one, zero), jnp.where(odd, zero, one))
+    far = (jnp.where(odd, three, two), jnp.where(odd, two, three))
+    top = jnp.stack([jnp.where(upper, far[0], near[0]), jnp.where(upper, far[1], near[1])])
+    bottom = jnp.stack([jnp.where(upper, near[0], far[0]), jnp.where(upper, near[1], far[1])])
+    ready = (one, two, three)
+    pieces = {(0, 0): top, (0, 1): bottom}
+    pieces[4, 0] = swap(top, 4)
+    pieces[2, 1] = swap(bottom, 2)
+    pieces[2, 0] = swap(top, 2)
+    pieces[4, 1] = swap(bottom, 4)
+    pieces[6, 0] = swap(pieces[4, 0], 2)
+    pieces[6, 1] = swap(pieces[2, 1], 4)
+    for place in list(pieces):
+        pieces[place[0] ^ 1, place[1]] = swap(pieces[place], 1)
+    whole = jnp.zeros((4, 8, rows, width), shard.dtype)
+    vector = jnp.zeros((4, 8, 1, vectors.shape[0]), vectors.dtype)
+    for (mask, half), piece in pieces.items():
+        start = (2 * half, (here & 7) ^ mask, 0, 0)
+        whole = lax.dynamic_update_slice(whole, piece[:, None, :rows], start)
+        vector = lax.dynamic_update_slice(
+            vector, piece[:, None, rows : rows + 1, : vectors.shape[0]], start
+        )
+    return (whole.reshape(-1, width), vector.reshape(-1), (ready, (pieces[6, 0], pieces[6, 1])))
+
+
+def scatter_attn(grads, sources):
+    devices = lax.axis_size("dev")
+    low = jnp.bfloat16
+    first, mixed = sources
+    own, width = first[0].shape
+    if devices != 32:
+        product = jnp.concatenate(
+            [
+                jnp.dot(grads[: 3 * width], first[0], preferred_element_type=jnp.float32),
+                jnp.dot(grads[3 * width :], mixed[0], preferred_element_type=jnp.float32),
+            ],
+            axis=0,
+        ).astype(low)
+        return lax.psum_scatter(product, "dev", scatter_dimension=0, tiled=True).astype(jnp.float32)
+    here = lax.axis_index("dev")
+    block = here & 7
+    grads = grads.reshape(4, 8, -1, own)
+    rows = grads.shape[2]
+    order = (6, 2, 4, 0)
+    mine = jnp.stack([lax.dynamic_index_in_dim(grads, block ^ mask, 1, False) for mask in order])
+    yours = jnp.stack(
+        [lax.dynamic_index_in_dim(grads, block ^ mask ^ 1, 1, False) for mask in order]
+    )
+    both = jnp.concatenate([mine, swap(yours, 1)], axis=-1)
+    first = jnp.concatenate(first, axis=0)
+    mixed = jnp.concatenate(mixed, axis=0)
+
+    def upper_part(place):
+        left = both[place, :2].reshape(2 * rows, 2 * own)
+        return jnp.dot(left, first, preferred_element_type=jnp.float32)
+
+    def lower_part(place):
+        return jnp.concatenate(
+            [
+                jnp.dot(both[place, 2], first, preferred_element_type=jnp.float32),
+                jnp.dot(both[place, 3], mixed, preferred_element_type=jnp.float32),
+            ],
+            axis=0,
+        )
+
+    def wide(value):
+        return value.astype(jnp.float32)
+
+    across_diagonal = swap(upper_part(0).astype(low), 2)
+    along_diagonal = swap(lower_part(0).astype(low), 4)
+    across_upper = swap(upper_part(1).astype(low), 2)
+    along_lower = swap(lower_part(2).astype(low), 4)
+    across_lower = swap((lower_part(1) + wide(along_diagonal)).astype(low), 2)
+    along_upper = swap((upper_part(2) + wide(across_diagonal)).astype(low), 4)
+    upper = upper_part(3) + wide(across_upper) + wide(along_upper)
+    lower = lower_part(3) + wide(across_lower) + wide(along_lower)
+    total = jnp.concatenate([upper, lower], axis=0).reshape(4, rows, width)
+    layer = here >> 3
+
+    def part(mask):
+        return lax.dynamic_index_in_dim(total, layer ^ mask, 0, False)
+
+    result = part(0)
+    for mask in (1, 2, 3):
+        result = result + wide(swap(part(mask).astype(low), 8 * mask))
+    return result
+
+
+def gather_hidden(shard, attn_ready):
     devices = lax.axis_size("dev")
     here = lax.axis_index("dev")
     half = devices // 2
@@ -138,16 +242,22 @@
         rows = both.shape[0] // 2
         blocks = jnp.arange(half // 4, dtype=jnp.int32) * 4 + (here & 3)
         return [(both[:rows], both[rows:], blocks)]
+    layers_ready, all_ready = attn_ready
+    held = [shard] + [swap(after(shard, layers_ready), 8 * mask) for mask in (1, 2, 3)]
+    moved = [swap(shard, 4)] + [swap(after(piece, all_ready), 4) for piece in held[1:]]
     first = here < half
-    one, two, three = swap(shard, 8), swap(shard, 16), swap(shard, 24)
-    up = jnp.concatenate([jnp.where(first, shard, two), jnp.where(first, one, three)], axis=0)
-    down = jnp.concatenate([jnp.where(first, two, shard), jnp.where(first, three, one)], axis=0)
     block = here & (half - 1)
     blocks = jnp.stack([block, block ^ 8])
-    return [(swap(up, 4), swap(down, 4), blocks ^ 4), (up, down, blocks)]
-
-
-def scatter_hidden(grads):
+    parts = []
+    for pieces, numbers in ((held, blocks), (moved, blocks ^ 4)):
+        zero, one, two, three = pieces
+        up = jnp.concatenate([jnp.where(first, zero, two), jnp.where(first, one, three)], axis=0)
+        down = jnp.concatenate([jnp.where(first, two, zero), jnp.where(first, three, one)], axis=0)
+        parts.append((up, down, numbers))
+    return parts
+
+
+def scatter_hidden(grads, others):
     devices = lax.axis_size("dev")
     if devices != 32:
         both = jnp.concatenate(grads[0], axis=0).astype(jnp.bfloat16)
@@ -156,8 +266,9 @@
         ).astype(jnp.float32)
     first = lax.axis_index("dev") < devices // 2
     low = jnp.bfloat16
-    up = grads[1][0] + swap(grads[0][0].astype(low), 4).astype(jnp.float32)
-    down = grads[1][1] + swap(grads[0][1].astype(low), 4).astype(jnp.float32)
+    moved = [swap(part.astype(low), 4) for part in grads[1]]
+    moved = after(moved, others)
+    up, down = [own + part.astype(jnp.float32) for own, part in zip(grads[0], moved)]
     rows = up.shape[0] // 2
     mine = jnp.where(first, up[:rows], down[:rows])
     two = jnp.where(first, down[:rows], up[:rows]).astype(low)
@@ -189,10 +300,9 @@
     allowed = allowed_pairs(keep)
     head_shape = (total_rows, HEADS, HEAD_SIZE)
 
-    full_vec = gather_vectors(vectors)
-    full_attn = lax.all_gather(attn_weight, "dev", axis=0, tiled=True)
+    full_attn, full_vec, attn_ready = gather_attn(attn_weight, vectors)
     grad_down = jnp.where(live, cotangent, jnp.zeros_like(cotangent))
-    hidden_parts = gather_hidden(mlp_weight)
+    hidden_parts = gather_hidden(mlp_weight, attn_ready)
     grad_down_rows = gather_rows(grad_down)
 
     (
@@ -211,6 +321,7 @@
     inputs = tokens.astype(jnp.float32)
     first_out, normed_one, factor_one = normalize(inputs, gain_one, shift_one)
     first_low = first_out.astype(low)
+    first_beside = swap(first_low, 1)
     projected = jnp.einsum(
         "rd,od->ro", first_low, full_attn[: 3 * width], preferred_element_type=jnp.float32
     )
@@ -219,6 +330,7 @@
     values = (projected[:, 2 * width :] + value_bias).astype(low).reshape(head_shape)
     mixed, log_total = attend(queries, keys, values, allowed, scale)
     mixed_low = mixed.reshape(total_rows, width).astype(low)
+    mixed_beside = swap(mixed_low, 1)
     branch = (
         jnp.einsum(
             "rd,od->ro", mixed_low, full_attn[3 * width :], preferred_element_type=jnp.float32
@@ -229,9 +341,8 @@
     second_out, normed_two, factor_two = normalize(middle, gain_two, shift_two)
     second_low = gather_rows(second_out.astype(low))
 
-    down_rows = 0.0
     second_rows = 0.0
-    grads = []
+    kept = []
     grad_up_bias = jnp.zeros_like(up_bias)
     for up_weight, down_weight, blocks in hidden_parts:
         bias = up_bias[blocks].reshape(-1)
@@ -245,25 +356,28 @@
             "rd,fd->rf", grad_down_rows, down_weight, preferred_element_type=jnp.float32
         )
         grad_up = gelu_back(grad_act)[0].astype(low)
-        grad_down_weight = jnp.einsum(
-            "rf,rd->fd", act_low, grad_down_rows, preferred_element_type=jnp.float32
-        )
-        grad_up_weight = jnp.einsum(
-            "rf,rd->fd", grad_up, second_low, preferred_element_type=jnp.float32
-        )
-        grads.append((grad_up_weight, grad_down_weight))
-        column_sums = jnp.sum(grad_up.astype(jnp.float32), axis=0)
-        grad_up_bias = grad_up_bias.at[blocks].set(
-            column_sums.reshape(blocks.shape[0], -1)
-        )
         second_rows = second_rows + jnp.dot(
             grad_up, up_weight, preferred_element_type=jnp.float32
         )
-        down_rows = down_rows + jnp.dot(act_low, down_weight, preferred_element_type=jnp.float32)
-    grad_second = reduce_rows(second_rows)
-    down = reduce_rows(down_rows) + down_bias
+        column_sums = jnp.sum(grad_up.astype(jnp.float32), axis=0)
+        grad_up_bias = grad_up_bias.at[blocks].set(column_sums.reshape(blocks.shape[0], -1))
+        kept.append((act_low, grad_up))
+    grad_second, far = reduce_near(second_rows)
+    grad_second = grad_second + swap(far, 2).astype(jnp.float32)
+    kept = after(kept, far)
+    grads = [
+        (
+            jnp.einsum("rf,rd->fd", grad_up, second_low, preferred_element_type=jnp.float32),
+            jnp.einsum("rf,rd->fd", act_low, grad_down_rows, preferred_element_type=jnp.float32),
+        )
+        for act_low, grad_up in kept
+    ]
+    down = 0.0
+    for (act_low, grad_up), (up_weight, down_weight, blocks) in zip(kept, hidden_parts):
+        down = down + jnp.dot(act_low, down_weight, preferred_element_type=jnp.float32)
+    down, far = reduce_near(down)
+    down = down + swap(far, 2).astype(jnp.float32) + down_bias
     output = jnp.where(live, middle + down, 0.0).astype(low)
-    mlp_share = scatter_hidden(grads)
 
     grad_down_wide = grad_down.astype(jnp.float32)
     grad_down_bias = jnp.sum(grad_down_wide, axis=0)
@@ -271,32 +385,30 @@
     grad_shift_two = jnp.sum(grad_second, axis=0)
     grad_middle = grad_down_wide + normalize_back(grad_second, normed_two, factor_two, gain_two)
     grad_branch = grad_middle.astype(low)
-    grad_out_weight = jnp.einsum(
-        "ro,rd->od", grad_branch, mixed_low, preferred_element_type=jnp.float32
-    )
     grad_out_bias = jnp.sum(grad_branch.astype(jnp.float32), axis=0)
     grad_mixed = jnp.dot(grad_branch, full_attn[3 * width :], preferred_element_type=jnp.float32)
     grad_mixed_low = grad_mixed.astype(low).reshape(head_shape)
     grad_queries, grad_keys, grad_values = attend_back(
         queries, keys, values, allowed, scale, grad_mixed_low, log_total
     )
-    grad_projected = jnp.concatenate(
+    grad_features = jnp.concatenate(
         [
-            grad_queries.reshape(total_rows, width),
-            grad_keys.reshape(total_rows, width),
-            grad_values.reshape(total_rows, width),
+            grad_queries.reshape(width, total_rows).astype(low),
+            grad_keys.reshape(width, total_rows).astype(low),
+            grad_values.reshape(width, total_rows).astype(low),
+            grad_branch.T,
         ],
-        axis=1,
-    ).astype(low)
-    grad_proj_weight = jnp.einsum(
-        "ro,rd->od", grad_projected, first_low, preferred_element_type=jnp.float32
-    )
-    grad_attn = jnp.concatenate(
-        [grad_proj_weight.astype(low), grad_out_weight.astype(low)], axis=0
-    )
-    attn_share = lax.psum_scatter(grad_attn, "dev", scatter_dimension=0, tiled=True)
-    grad_columns = jnp.sum(grad_projected.astype(jnp.float32), axis=0)
-    grad_first = jnp.dot(grad_projected, full_attn[: 3 * width], preferred_element_type=jnp.float32)
+        axis=0,
+    )
+    attn_share = scatter_attn(
+        grad_features, ((first_low, first_beside), (mixed_low, mixed_beside))
+    )
+    mlp_share = scatter_hidden(grads, grad_features)
+    grad_projected = grad_features[: 3 * width]
+    grad_columns = jnp.sum(grad_projected.astype(jnp.float32), axis=1)
+    grad_first = jnp.einsum(
+        "fr,fd->rd", grad_projected, full_attn[: 3 * width], preferred_element_type=jnp.float32
+    )
     grad_gain_one = jnp.sum(grad_first * normed_one, axis=0)
     grad_shift_one = jnp.sum(grad_first, axis=0)
     grad_inputs = grad_middle + normalize_back(grad_first, normed_one, factor_one, gain_one)
@@ -315,7 +427,7 @@
         axis=0,
     )
     vec_share = scatter_vectors(grad_vec)
-    return (output, grad_inputs, attn_share.astype(jnp.float32), mlp_share, vec_share)
+    return (output, grad_inputs, attn_share, mlp_share, vec_share)
 
 
 def solution(mesh):

time: 547 us -> 472 us (0.86)
  waiting for transfers between devices: 372 us -> 230 us
  local copies, waits for them, and re-layouts: 11.5 us -> 64.3 us
  starting transfers between devices: 27.2 us -> 50.8 us
  between operations: 16.6 us -> 3.86 us
    unnamed x3 -> x0, waiting for transfers between devices: 165 us -> none
    ppermute x30 -> x56, waiting for transfers between devices: 174 us -> 230 us  [swap(): lax.ppermute(piece, 'dev', [(number, number ^ mask) for number in range(d...]
    all_gather x1 -> x0, waiting for transfers between devices: 32.8 us -> none  [shards(): full_attn = lax.all_gather(attn_weight, 'dev', axis=0, tiled=True)]
    dynamic_update_slice x0 -> x30, local copies, waits for them, and re-layouts: none -> 25.3 us  [the longest x14 24.5 us: gather_attn(): whole = lax.dynamic_update_slice(whole, piece[:, None, :rows], start)]
    ppermute x30 -> x56, starting transfers between devices: 27.1 us -> 50.8 us  [swap(): lax.ppermute(piece, 'dev', [(number, number ^ mask) for number in range(d...]
    slice x2 -> x8, local copies, waits for them, and re-layouts: 1.5 us -> 14.6 us  [the longest x1 6.75 us: shards(): full_attn[:3 * width]]
    broadcast_in_dim x0 -> x17, local copies, waits for them, and re-layouts: none -> 12.6 us  [the longest x14 7.25 us: gather_attn(): piece[:, None, rows:rows + 1, :vectors.shape[0]]]
    concatenate x9 -> x6, other arithmetic: 10.2 us -> 1.93 us  [the longest x1 1 us: gather_attn(): zero = jnp.concatenate([shard, extra], axis=0)]
  transfers between devices with their start and end apart: 32 -> 56, of which waited for: 16 -> 20; matrix products, arithmetic and copies ran while one was open for 19% -> 32% of each run, Pallas kernels for 0% -> 0%
where the time goes in v2:
time: 472 us; the launch traced here: 465 us
  waiting for transfers between devices  230 us (49%)
  matrix products  75.5 us (16%)
  local copies, waits for them, and re-layouts  64.3 us (14%)
  starting transfers between devices  50.8 us (11%)
  other arithmetic  40.1 us (8%)
    ppermute x56, waiting for transfers between devices, swap(): lax.ppermute(piece, 'dev', [(number, number ^ mask) for number in range(d...  230 us
    ppermute x56, starting transfers between devices, swap(): lax.ppermute(piece, 'dev', [(number, number ^ mask) for number in range(d...  50.8 us
    dynamic_update_slice x14, local copies, waits for them, and re-layouts, gather_attn(): whole = lax.dynamic_update_slice(whole, piece[:, None, :rows], start)  24.5 us
    dot_general x2, matrix products, shards(): jnp.einsum('rd,fd->rf', second_low, up_weight, preferred_element_type=jnp...  18.2 us
  transfers between devices with their start and end apart: 56, of which 20 were waited for; matrix products, arithmetic and copies ran while one was open for 32% of the time, Pallas kernels for 0%

profile of v2, /device:TPU:8, one launch (start us, length us, event | category | flops | bytes accessed | tf_op | source)
XLA Modules:
  0.0 464.9 jit_solution(12239712634582634578)
XLA Ops:
  17.3 9.9 %collective-permute-done = bf16[144,1088]{1,0:T(8,128)(2,1)S(1)} collective-permute-done((bf16[144,1088]{1,0:T(8,128)(2,1)S(1)}, bf16[144,1088]{1,0:T(8,128)(2,1)S(1)}, u32[]{:S(2)}, u32[]{:S(2)}) %collective-permute-start) | collective-permute-done | bytes 313376 | tf_op jit(solution)/shard_map/ppermute | solution.py:100
  27.2 5.2 %collective-permute-done.1 = bf16[144,1088]{1,0:T(8,128)(2,1)S(1)} collective-permute-done((bf16[144,1088]{1,0:T(8,128)(2,1)S(1)}, bf16[144,1088]{1,0:T(8,128)(2,1)S(1)}, u32[]{:S(2)}, u32[]{:S(2)}) %collective-permute-start.1) | collective-permute-done | bytes 313376 | tf_op jit(solution)/shard_map/ppermute | solution.py:100
  37.6 4.6 broadcast_in_dim.196
  44.3 44.9 %collective-permute-done.20 = bf16[272,1088]{1,0:T(8,128)(2,1)} collective-permute-done((bf16[272,1088]{1,0:T(8,128)(2,1)}, bf16[272,1088]{1,0:T(8,128)(2,1)}, u32[]{:S(2)}, u32[]{:S(2)}) %collective-permute-start.20) | collective-permute-done | bytes 591904 | tf_op jit(solution)/shard_map/ppermute | solution.py:100
  97.8 6.5 %collective-permute-done.3 = bf16[2,144,1088]{2,1,0:T(8,128)(2,1)} collective-permute-done((bf16[2,144,1088]{2,1,0:T(8,128)(2,1)S(1)}, bf16[2,144,1088]{2,1,0:T(8,128)(2,1)}, u32[]{:S(2)}, u32[]{:S(2)}) %collective-permute-start.3) | collective-permute-done | bytes 626720 | tf_op jit(solution)/shard_map/ppermute | solution.py:100
  106.6 15.3 %collective-permute-done.4 = bf16[2,144,1088]{2,1,0:T(8,128)(2,1)} collective-permute-done((bf16[2,144,1088]{2,1,0:T(8,128)(2,1)S(1)}, bf16[2,144,1088]{2,1,0:T(8,128)(2,1)}, u32[]{:S(2)}, u32[]{:S(2)}) %collective-permute-start.4) | collective-permute-done | bytes 626720 | tf_op jit(solution)/shard_map/ppermute | solution.py:100
  136.1 5.7 %collective-permute-done.7 = bf16[2,144,1088]{2,1,0:T(8,128)(2,1)S(1)} collective-permute-done((bf16[2,144,1088]{2,1,0:T(8,128)(2,1)}, bf16[2,144,1088]{2,1,0:T(8,128)(2,1)S(1)}, u32[]{:S(2)}, u32[]{:S(2)}) %collective-permute-start.7) | collective-permute-done | bytes 626720 | tf_op jit(solution)/shard_map/ppermute | solution.py:100
  141.8 7.2 %collective-permute-done.8 = bf16[2,144,1088]{2,1,0:T(8,128)(2,1)S(1)} collective-permute-done((bf16[2,144,1088]{2,1,0:T(8,128)(2,1)}, bf16[2,144,1088]{2,1,0:T(8,128)(2,1)S(1)}, u32[]{:S(2)}, u32[]{:S(2)}) %collective-permute-start.8) | collective-permute-done | bytes 626720 | tf_op jit(solution)/shard_map/ppermute | solution.py:100
  172.2 6.7 %slice.382 = bf16[3,8,136,1088]{3,2,1,0:T(8,128)(2,1)} slice(bf16[4,8,136,1088]{3,2,1,0:T(8,128)(2,1)} %fusion.63), slice={[0:3], [0:8], [0:136], [0:1088]} | slice | bytes 14204928 | tf_op jit(solution)/shard_map/slice | solution.py:326
  184.3 5.5 %fusion.187 = f32[256,3264]{0,1:T(8,128)S(1)} fusion(bf16[3264,1088]{1,0:T(8,128)(2,1)} %bitcast.261, bf16[256,1088]{0,1:T(8,128)(2,1)S(1)} %fusion.36), kind=kOutput, calls=%fused_computation.394 | convolution fusion | flops 1818230784 | bytes 11001856 | tf_op jit(solution)/shard_map/rd,od->ro/dot_general | solution.py:325
  200.1 11.8 %collective-permute-done.17 = bf16[256,1088]{0,1:T(8,128)(2,1)} collective-permute-done((bf16[256,1088]{0,1:T(8,128)(2,1)S(1)}, bf16[256,1088]{0,1:T(8,128)(2,1)}, u32[]{:S(2)}, u32[]{:S(2)}) %collective-permute-start.17) | collective-permute-done | bytes 557088 | tf_op jit(solution)/shard_map/ppermute | solution.py:100
  216.0 9.4 %multiply_convert_fusion.1 = (bf16[1024,544]{0,1:T(8,128)(2,1)}, f32[1024,544]{0,1:T(8,128)S(1)}, f32[1024,544]{0,1:T(8,128)S(1)}) fusion(f32[544]{0:T(1024)S(1)} %add.309, bf16[256,1088]{0,1:T(8,128)(2,1)} %collective-permute-done.19, bf16[256,1088]{0,1:T(8,128)(2,1)} %collective-permute-done.18, bf16[256,1088]{0,1:T(8,128)(2,1)} %collective-permute-done.17, ...), kind=kOutput, calls=%fused_computation.50 | convolution fusion | flops 1260199936 | bytes 8984704 | tf_op jit(solution)/shard_map/rd,fd->rf/dot_general | solution.py:350
  225.5 3.9 convert_reduce_fusion.1
  231.5 8.7 %multiply_convert_fusion.2 = (bf16[1024,544]{0,1:T(8,128)(2,1)}, f32[1024,544]{0,1:T(8,128)S(1)}, f32[1024,544]{0,1:T(8,128)S(1)}) fusion(f32[544]{0:T(1024)S(1)} %add.305, bf16[256,1088]{0,1:T(8,128)(2,1)} %collective-permute-done.19, bf16[256,1088]{0,1:T(8,128)(2,1)} %collective-permute-done.18, bf16[256,1088]{0,1:T(8,128)(2,1)} %collective-permute-done.17, ...), kind=kOutput, calls=%fused_computation.64 | convolution fusion | flops 1260199936 | bytes 8984704 | tf_op jit(solution)/shard_map/rd,fd->rf/dot_general | solution.py:350
  240.2 3.9 convert_reduce_fusion.2
  267.7 4.7 %convolution_convert_fusion.1 = bf16[544,1088]{1,0:T(8,128)(2,1)} fusion(bf16[1024,544]{0,1:T(8,128)(2,1)} %copy-done.60, bf16[256,1088]{0,1:T(8,128)(2,1)} %collective-permute-done.19, bf16[256,1088]{0,1:T(8,128)(2,1)} %collective-permute-done.18, bf16[256,1088]{0,1:T(8,128)(2,1)} %collective-permute-done.17, bf16[256,1088]{0,1:T(8,128)(2,1)} %copy-done.43), kind=kOutput, calls=%fused_computation.20 | convolution fusion | flops 1221658624 | bytes 4526080 | tf_op jit(solution)/shard_map/rf,rd->fd/dot_general | solution.py:370
  273.9 4.1 convolution_convert_fusion
  283.6 12.7 %collective-permute-done.32 = bf16[256,1088]{0,1:T(8,128)(2,1)} collective-permute-done((bf16[256,1088]{0,1:T(8,128)(2,1)}, bf16[256,1088]{0,1:T(8,128)(2,1)}, u32[]{:S(2)}, u32[]{:S(2)}) %collective-permute-start.32) | collective-permute-done | bytes 557088 | tf_op jit(solution)/shard_map/ppermute | solution.py:100
  296.3 3.7 convert_reduce_fusion.5
  300.0 3.3 convolution_convert_fusion.4
  308.4 4.5 fusion.41
  313.0 3.4 collective-permute-start.51
  316.5 3.4 convert_bitcast_fusion
  320.3 8.6 %collective-permute-done.47 = bf16[544,1088]{1,0:T(8,128)(2,1)} collective-permute-done((bf16[544,1088]{1,0:T(8,128)(2,1)}, bf16[544,1088]{1,0:T(8,128)(2,1)}, u32[]{:S(2)}, u32[]{:S(2)}) %collective-permute-start.47) | collective-permute-done | bytes 1183776 | tf_op jit(solution)/shard_map/ppermute | solution.py:100
  331.8 3.5 convolution_add_fusion.2
  336.9 3.5 convolution_add_fusion.3
  352.1 23.3 %collective-permute-done.37 = bf16[272,1088]{1,0:T(8,128)(2,1)S(1)} collective-permute-done((bf16[272,1088]{1,0:T(8,128)(2,1)S(1)}, bf16[272,1088]{1,0:T(8,128)(2,1)S(1)}, u32[]{:S(2)}, u32[]{:S(2)}) %collective-permute-start.37) | collective-permute-done | bytes 591904 | tf_op jit(solution)/shard_map/ppermute | solution.py:100
  382.6 22.1 %collective-permute-done.38 = bf16[272,1088]{1,0:T(8,128)(2,1)S(1)} collective-permute-done((bf16[272,1088]{1,0:T(8,128)(2,1)S(1)}, bf16[272,1088]{1,0:T(8,128)(2,1)S(1)}, u32[]{:S(2)}, u32[]{:S(2)}) %collective-permute-start.38) | collective-permute-done | bytes 591904 | tf_op jit(solution)/shard_map/ppermute | solution.py:100
  410.6 12.7 %collective-permute-done.49 = bf16[272,1088]{1,0:T(8,128)(2,1)S(1)} collective-permute-done((bf16[272,1088]{1,0:T(8,128)(2,1)S(1)}, bf16[272,1088]{1,0:T(8,128)(2,1)S(1)}, u32[]{:S(2)}, u32[]{:S(2)}) %collective-permute-start.49) | collective-permute-done | bytes 591904 | tf_op jit(solution)/shard_map/ppermute | solution.py:100
  423.3 28.1 %collective-permute-done.50 = bf16[272,1088]{1,0:T(8,128)(2,1)S(1)} collective-permute-done((bf16[272,1088]{1,0:T(8,128)(2,1)S(1)}, bf16[272,1088]{1,0:T(8,128)(2,1)S(1)}, u32[]{:S(2)}, u32[]{:S(2)}) %collective-permute-start.50) | collective-permute-done | bytes 591904 | tf_op jit(solution)/shard_map/ppermute | solution.py:100
  452.8 4.1 collective-permute-done.44
  456.8 6.6 %collective-permute-done.45 = bf16[136,1088]{1,0:T(8,128)(2,1)S(1)} collective-permute-done((bf16[136,1088]{1,0:T(8,128)(2,1)S(1)}, bf16[136,1088]{1,0:T(8,128)(2,1)S(1)}, u32[]{:S(2)}, u32[]{:S(2)}) %collective-permute-start.45) | collective-permute-done | bytes 295968 | tf_op jit(solution)/shard_map/ppermute | solution.py:100
  (388 shorter events, 159.4 us)
Async XLA Ops:
  2.4 24.8 %collective-permute-start = (bf16[144,1088]{1,0:T(8,128)(2,1)S(1)}, bf16[144,1088]{1,0:T(8,128)(2,1)S(1)}, u32[]{:S(2)}, u32[]{:S(2)}) collective-permute-start(bf16[144,1088]{1,0:T(8,128)(2,1)S(1)} %fusion.79), channel_id=1, source_target_pairs={{0,24},{1,25},{2,26},{3,27},{4,28},{5,29},{6,30},{7,31},{8,16},{9,... | collective-permute-start | bytes 940040 | tf_op jit(solution)/shard_map/ppermute | solution.py:100
  4.1 28.4 %collective-permute-start.1 = (bf16[144,1088]{1,0:T(8,128)(2,1)S(1)}, bf16[144,1088]{1,0:T(8,128)(2,1)S(1)}, u32[]{:S(2)}, u32[]{:S(2)}) collective-permute-start(bf16[144,1088]{1,0:T(8,128)(2,1)S(1)} %fusion.79), channel_id=1, source_target_pairs={{0,16},{1,17},{2,18},{3,19},{4,20},{5,21},{6,22},{7,23},{8,24},{9,... | collective-permute-start | bytes 940040 | tf_op jit(solution)/shard_map/ppermute | solution.py:100
  5.1 27.3 %collective-permute-start.2 = (bf16[144,1088]{1,0:T(8,128)(2,1)S(1)}, bf16[144,1088]{1,0:T(8,128)(2,1)S(1)}, u32[]{:S(2)}, u32[]{:S(2)}) collective-permute-start(bf16[144,1088]{1,0:T(8,128)(2,1)S(1)} %fusion.79), channel_id=1, source_target_pairs={{0,8},{1,9},{2,10},{3,11},{4,12},{5,13},{6,14},{7,15},{8,0},{9,1},... | collective-permute-start | bytes 940040 | tf_op jit(solution)/shard_map/ppermute | solution.py:100
  11.7 184.8 %collective-permute-start.23 = (bf16[256,1088]{0,1:T(8,128)(2,1)S(1)}, bf16[256,1088]{0,1:T(8,128)(2,1)}, u32[]{:S(2)}, u32[]{:S(2)}) collective-permute-start(bf16[256,1088]{0,1:T(8,128)(2,1)S(1)} %get-tuple-element.36), channel_id=1, source_target_pairs={{0,2},{1,3},{2,0},{3,1},{4,6},{5,7},{6,4},{7,5},{8,10},{9,11},{10,... | collective-permute-start | bytes 1671176 | tf_op jit(solution)/shard_map/ppermute | solution.py:100
  13.2 186.9 %collective-permute-start.26 = (bf16[272,1088]{1,0:T(8,128)(2,1)}, bf16[272,1088]{1,0:T(8,128)(2,1)}, u32[]{:S(2)}, u32[]{:S(2)}) collective-permute-start(bf16[272,1088]{1,0:T(8,128)(2,1)} %param.10), channel_id=1, source_target_pairs={{0,4},{1,5},{2,6},{3,7},{4,0},{5,1},{6,2},{7,3},{8,12},{9,13},{10,... | collective-permute-start | bytes 1775624 | tf_op jit(solution)/shard_map/ppermute | solution.py:100
  32.4 60.8 %collective-permute-start.21 = (bf16[272,1088]{1,0:T(8,128)(2,1)}, bf16[272,1088]{1,0:T(8,128)(2,1)}, u32[]{:S(2)}, u32[]{:S(2)}) collective-permute-start(bf16[272,1088]{1,0:T(8,128)(2,1)} %param.10), channel_id=1, source_target_pairs={{0,8},{1,9},{2,10},{3,11},{4,12},{5,13},{6,14},{7,15},{8,0},{9,1},... | collective-permute-start | bytes 1775624 | tf_op jit(solution)/shard_map/ppermute | solution.py:100
  34.8 59.9 %collective-permute-start.22 = (bf16[272,1088]{1,0:T(8,128)(2,1)}, bf16[272,1088]{1,0:T(8,128)(2,1)}, u32[]{:S(2)}, u32[]{:S(2)}) collective-permute-start(bf16[272,1088]{1,0:T(8,128)(2,1)} %param.10), channel_id=1, source_target_pairs={{0,24},{1,25},{2,26},{3,27},{4,28},{5,29},{6,30},{7,31},{8,16},{9,... | collective-permute-start | bytes 1775624 | tf_op jit(solution)/shard_map/ppermute | solution.py:100
  36.4 52.8 %collective-permute-start.20 = (bf16[272,1088]{1,0:T(8,128)(2,1)}, bf16[272,1088]{1,0:T(8,128)(2,1)}, u32[]{:S(2)}, u32[]{:S(2)}) collective-permute-start(bf16[272,1088]{1,0:T(8,128)(2,1)} %param.10), channel_id=1, source_target_pairs={{0,16},{1,17},{2,18},{3,19},{4,20},{5,21},{6,22},{7,23},{8,24},{9,... | collective-permute-start | bytes 1775624 | tf_op jit(solution)/shard_map/ppermute | solution.py:100
  93.2 29.4 %collective-permute-start.5 = (bf16[2,144,1088]{2,1,0:T(8,128)(2,1)S(1)}, bf16[2,144,1088]{2,1,0:T(8,128)(2,1)}, u32[]{:S(2)}, u32[]{:S(2)}) collective-permute-start(bf16[2,144,1088]{2,1,0:T(8,128)(2,1)S(1)} %pad_maximum_fusion.13), channel_id=1, source_target_pairs={{0,2},{1,3},{2,0},{3,1},{4,6},{5,7},{6,4},{7,5},{8,10},{9,11},{10,... | collective-permute-start | bytes 1880072 | tf_op jit(solution)/shard_map/ppermute | solution.py:100
  94.7 27.1 %collective-permute-start.4 = (bf16[2,144,1088]{2,1,0:T(8,128)(2,1)S(1)}, bf16[2,144,1088]{2,1,0:T(8,128)(2,1)}, u32[]{:S(2)}, u32[]{:S(2)}) collective-permute-start(bf16[2,144,1088]{2,1,0:T(8,128)(2,1)S(1)} %pad_maximum_fusion.14), channel_id=1, source_target_pairs={{0,2},{1,3},{2,0},{3,1},{4,6},{5,7},{6,4},{7,5},{8,10},{9,11},{10,... | collective-permute-start | bytes 1880072 | tf_op jit(solution)/shard_map/ppermute | solution.py:100
  150.0 46.7 %collective-permute-start.28 = (bf16[272,1088]{1,0:T(8,128)(2,1)}, bf16[272,1088]{1,0:T(8,128)(2,1)}, u32[]{:S(2)}, u32[]{:S(2)}) collective-permute-start(bf16[272,1088]{1,0:T(8,128)(2,1)} %collective-permute-done.21), channel_id=1, source_target_pairs={{0,4},{1,5},{2,6},{3,7},{4,0},{5,1},{6,2},{7,3},{8,12},{9,13},{10,... | collective-permute-start | bytes 1775624 | tf_op jit(solution)/shard_map/ppermute | solution.py:100
  167.2 29.9 %collective-permute-start.29 = (bf16[272,1088]{1,0:T(8,128)(2,1)}, bf16[272,1088]{1,0:T(8,128)(2,1)}, u32[]{:S(2)}, u32[]{:S(2)}) collective-permute-start(bf16[272,1088]{1,0:T(8,128)(2,1)} %collective-permute-done.22), channel_id=1, source_target_pairs={{0,4},{1,5},{2,6},{3,7},{4,0},{5,1},{6,2},{7,3},{8,12},{9,13},{10,... | collective-permute-start | bytes 1775624 | tf_op jit(solution)/shard_map/ppermute | solution.py:100
  170.7 41.2 %collective-permute-start.27 = (bf16[272,1088]{1,0:T(8,128)(2,1)}, bf16[272,1088]{1,0:T(8,128)(2,1)}, u32[]{:S(2)}, u32[]{:S(2)}) collective-permute-start(bf16[272,1088]{1,0:T(8,128)(2,1)} %collective-permute-done.20), channel_id=1, source_target_pairs={{0,4},{1,5},{2,6},{3,7},{4,0},{5,1},{6,2},{7,3},{8,12},{9,13},{10,... | collective-permute-start | bytes 1775624 | tf_op jit(solution)/shard_map/ppermute | solution.py:100
  196.6 28.9 %collective-permute-start.24 = (bf16[256,1088]{0,1:T(8,128)(2,1)S(1)}, bf16[256,1088]{0,1:T(8,128)(2,1)}, u32[]{:S(2)}, u32[]{:S(2)}) collective-permute-start(bf16[256,1088]{0,1:T(8,128)(2,1)S(1)} %get-tuple-element.36), channel_id=1, source_target_pairs={{0,1},{1,0},{2,3},{3,2},{4,5},{5,4},{6,7},{7,6},{8,9},{9,8},{10,11... | collective-permute-start | bytes 1671176 | tf_op jit(solution)/shard_map/ppermute | solution.py:100
  196.6 28.8 %collective-permute-start.25 = (bf16[256,1088]{0,1:T(8,128)(2,1)}, bf16[256,1088]{0,1:T(8,128)(2,1)}, u32[]{:S(2)}, u32[]{:S(2)}) collective-permute-start(bf16[256,1088]{0,1:T(8,128)(2,1)} %collective-permute-done.23), channel_id=1, source_target_pairs={{0,1},{1,0},{2,3},{3,2},{4,5},{5,4},{6,7},{7,6},{8,9},{9,8},{10,11... | collective-permute-start | bytes 1671176 | tf_op jit(solution)/shard_map/ppermute | solution.py:100
  250.1 94.9 %collective-permute-start.35 = (bf16[256,1088]{0,1:T(8,128)(2,1)S(1)}, bf16[256,1088]{0,1:T(8,128)(2,1)S(1)}, u32[]{:S(2)}, u32[]{:S(2)}) collective-permute-start(bf16[256,1088]{0,1:T(8,128)(2,1)S(1)} %fusion.36), channel_id=1, source_target_pairs={{0,1},{1,0},{2,3},{3,2},{4,5},{5,4},{6,7},{7,6},{8,9},{9,8},{10,11... | collective-permute-start | bytes 1671176 | tf_op jit(solution)/shard_map/ppermute | solution.py:100
  250.1 98.6 %collective-permute-start.39 = (bf16[256,1088]{0,1:T(8,128)(2,1)S(1)}, bf16[256,1088]{0,1:T(8,128)(2,1)S(1)}, u32[]{:S(2)}, u32[]{:S(2)}) collective-permute-start(bf16[256,1088]{0,1:T(8,128)(2,1)S(1)} %bitcast.255), channel_id=1, source_target_pairs={{0,1},{1,0},{2,3},{3,2},{4,5},{5,4},{6,7},{7,6},{8,9},{9,8},{10,11... | collective-permute-start | bytes 1671176 | tf_op jit(solution)/shard_map/ppermute | solution.py:100
  272.4 47.9 %collective-permute-start.46 = (bf16[544,1088]{1,0:T(8,128)(2,1)}, bf16[544,1088]{1,0:T(8,128)(2,1)}, u32[]{:S(2)}, u32[]{:S(2)}) collective-permute-start(bf16[544,1088]{1,0:T(8,128)(2,1)} %convolution_convert_fusion.1), channel_id=1, source_target_pairs={{0,4},{1,5},{2,6},{3,7},{4,0},{5,1},{6,2},{7,3},{8,12},{9,13},{10,... | collective-permute-start | bytes 3551240 | tf_op jit(solution)/shard_map/ppermute | solution.py:100
  277.9 51.0 %collective-permute-start.47 = (bf16[544,1088]{1,0:T(8,128)(2,1)}, bf16[544,1088]{1,0:T(8,128)(2,1)}, u32[]{:S(2)}, u32[]{:S(2)}) collective-permute-start(bf16[544,1088]{1,0:T(8,128)(2,1)} %convolution_convert_fusion), channel_id=1, source_target_pairs={{0,4},{1,5},{2,6},{3,7},{4,0},{5,1},{6,2},{7,3},{8,12},{9,13},{10,... | collective-permute-start | bytes 3551240 | tf_op jit(solution)/shard_map/ppermute | solution.py:100
  342.3 67.1 %collective-permute-start.48 = (bf16[272,1088]{1,0:T(8,128)(2,1)S(1)}, bf16[272,1088]{1,0:T(8,128)(2,1)S(1)}, u32[]{:S(2)}, u32[]{:S(2)}) collective-permute-start(bf16[272,1088]{1,0:T(8,128)(2,1)S(1)} %get-tuple-element.43), channel_id=1, source_target_pairs={{0,8},{1,9},{2,10},{3,11},{4,12},{5,13},{6,14},{7,15},{8,0},{9,1},... | collective-permute-start | bytes 1775624 | tf_op jit(solution)/shard_map/ppermute | solution.py:100
  344.3 34.0 %collective-permute-start.55 = (f32[408]{0:T(512)S(1)}, f32[408]{0:T(512)S(1)}, u32[]{:S(2)}, u32[]{:S(2)}) collective-permute-start(f32[408]{0:T(512)S(1)} %slice_select_fusion.3), channel_id=1, source_target_pairs={{0,1},{1,0},{2,3},{3,2},{4,5},{5,4},{6,7},{7,6},{8,9},{9,8},{10,11... | collective-permute-start | bytes 4904 | tf_op jit(solution)/shard_map/ppermute | solution.py:100
  345.5 36.1 %collective-permute-start.36 = (bf16[272,1088]{1,0:T(8,128)(2,1)S(1)}, bf16[272,1088]{1,0:T(8,128)(2,1)S(1)}, u32[]{:S(2)}, u32[]{:S(2)}) collective-permute-start(bf16[272,1088]{1,0:T(8,128)(2,1)S(1)} %convolution_convert_fusion.3), channel_id=1, source_target_pairs={{0,2},{1,3},{2,0},{3,1},{4,6},{5,7},{6,4},{7,5},{8,10},{9,11},{10,... | collective-permute-start | bytes 1775624 | tf_op jit(solution)/shard_map/ppermute | solution.py:100
  347.6 27.9 %collective-permute-start.37 = (bf16[272,1088]{1,0:T(8,128)(2,1)S(1)}, bf16[272,1088]{1,0:T(8,128)(2,1)S(1)}, u32[]{:S(2)}, u32[]{:S(2)}) collective-permute-start(bf16[272,1088]{1,0:T(8,128)(2,1)S(1)} %convolution_convert_fusion.2), channel_id=1, source_target_pairs={{0,2},{1,3},{2,0},{3,1},{4,6},{5,7},{6,4},{7,5},{8,10},{9,11},{10,... | collective-permute-start | bytes 1775624 | tf_op jit(solution)/shard_map/ppermute | solution.py:100
  349.3 27.4 %collective-permute-start.40 = (bf16[272,1088]{1,0:T(8,128)(2,1)S(1)}, bf16[272,1088]{1,0:T(8,128)(2,1)S(1)}, u32[]{:S(2)}, u32[]{:S(2)}) collective-permute-start(bf16[272,1088]{1,0:T(8,128)(2,1)S(1)} %pad_maximum_fusion.28), channel_id=1, source_target_pairs={{0,4},{1,5},{2,6},{3,7},{4,0},{5,1},{6,2},{7,3},{8,12},{9,13},{10,... | collective-permute-start | bytes 1775624 | tf_op jit(solution)/shard_map/ppermute | solution.py:100
  375.5 31.0 %collective-permute-start.42 = (bf16[272,1088]{1,0:T(8,128)(2,1)S(1)}, bf16[272,1088]{1,0:T(8,128)(2,1)S(1)}, u32[]{:S(2)}, u32[]{:S(2)}) collective-permute-start(bf16[272,1088]{1,0:T(8,128)(2,1)S(1)} %pad_maximum_fusion.29), channel_id=1, source_target_pairs={{0,4},{1,5},{2,6},{3,7},{4,0},{5,1},{6,2},{7,3},{8,12},{9,13},{10,... | collective-permute-start | bytes 1775624 | tf_op jit(solution)/shard_map/ppermute | solution.py:100
  376.7 28.0 %collective-permute-start.38 = (bf16[272,1088]{1,0:T(8,128)(2,1)S(1)}, bf16[272,1088]{1,0:T(8,128)(2,1)S(1)}, u32[]{:S(2)}, u32[]{:S(2)}) collective-permute-start(bf16[272,1088]{1,0:T(8,128)(2,1)S(1)} %fusion.4), channel_id=1, source_target_pairs={{0,4},{1,5},{2,6},{3,7},{4,0},{5,1},{6,2},{7,3},{8,12},{9,13},{10,... | collective-permute-start | bytes 1775624 | tf_op jit(solution)/shard_map/ppermute | solution.py:100
  378.3 28.2 %collective-permute-start.41 = (bf16[272,1088]{1,0:T(8,128)(2,1)S(1)}, bf16[272,1088]{1,0:T(8,128)(2,1)S(1)}, u32[]{:S(2)}, u32[]{:S(2)}) collective-permute-start(bf16[272,1088]{1,0:T(8,128)(2,1)S(1)} %fusion.34), channel_id=1, source_target_pairs={{0,2},{1,3},{2,0},{3,1},{4,6},{5,7},{6,4},{7,5},{8,10},{9,11},{10,... | collective-permute-start | bytes 1775624 | tf_op jit(solution)/shard_map/ppermute | solution.py:100
  381.6 41.7 %collective-permute-start.49 = (bf16[272,1088]{1,0:T(8,128)(2,1)S(1)}, bf16[272,1088]{1,0:T(8,128)(2,1)S(1)}, u32[]{:S(2)}, u32[]{:S(2)}) collective-permute-start(bf16[272,1088]{1,0:T(8,128)(2,1)S(1)} %get-tuple-element.44), channel_id=1, source_target_pairs={{0,16},{1,17},{2,18},{3,19},{4,20},{5,21},{6,22},{7,23},{8,24},{9,... | collective-permute-start | bytes 1775624 | tf_op jit(solution)/shard_map/ppermute | solution.py:100
  404.7 46.7 %collective-permute-start.50 = (bf16[272,1088]{1,0:T(8,128)(2,1)S(1)}, bf16[272,1088]{1,0:T(8,128)(2,1)S(1)}, u32[]{:S(2)}, u32[]{:S(2)}) collective-permute-start(bf16[272,1088]{1,0:T(8,128)(2,1)S(1)} %get-tuple-element.45), channel_id=1, source_target_pairs={{0,24},{1,25},{2,26},{3,27},{4,28},{5,29},{6,30},{7,31},{8,16},{9,... | collective-permute-start | bytes 1775624 | tf_op jit(solution)/shard_map/ppermute | solution.py:100
  407.0 45.7 %collective-permute-start.43 = (bf16[136,1088]{1,0:T(8,128)(2,1)S(1)}, bf16[136,1088]{1,0:T(8,128)(2,1)S(1)}, u32[]{:S(2)}, u32[]{:S(2)}) collective-permute-start(bf16[136,1088]{1,0:T(8,128)(2,1)S(1)} %get-tuple-element.48), channel_id=1, source_target_pairs={{0,8},{1,9},{2,10},{3,11},{4,12},{5,13},{6,14},{7,15},{8,0},{9,1},... | collective-permute-start | bytes 887816 | tf_op jit(solution)/shard_map/ppermute | solution.py:100
  408.3 48.6 %collective-permute-start.44 = (bf16[136,1088]{1,0:T(8,128)(2,1)S(1)}, bf16[136,1088]{1,0:T(8,128)(2,1)S(1)}, u32[]{:S(2)}, u32[]{:S(2)}) collective-permute-start(bf16[136,1088]{1,0:T(8,128)(2,1)S(1)} %get-tuple-element.50), channel_id=1, source_target_pairs={{0,16},{1,17},{2,18},{3,19},{4,20},{5,21},{6,22},{7,23},{8,24},{9,... | collective-permute-start | bytes 887816 | tf_op jit(solution)/shard_map/ppermute | solution.py:100
  409.4 54.1 %collective-permute-start.45 = (bf16[136,1088]{1,0:T(8,128)(2,1)S(1)}, bf16[136,1088]{1,0:T(8,128)(2,1)S(1)}, u32[]{:S(2)}, u32[]{:S(2)}) collective-permute-start(bf16[136,1088]{1,0:T(8,128)(2,1)S(1)} %get-tuple-element.49), channel_id=1, source_target_pairs={{0,24},{1,25},{2,26},{3,27},{4,28},{5,29},{6,30},{7,31},{8,16},{9,... | collective-permute-start | bytes 887816 | tf_op jit(solution)/shard_map/ppermute | solution.py:100
  (91 other events, 1233.6 us)

commit v3 on v2

--- a/solution.py
+++ b/solution.py
@@ -1,6 +1,8 @@
 import jax
 import jax.numpy as jnp
 from jax import lax
+from jax.experimental import pallas as pl
+from jax.experimental.pallas import tpu as pltpu
 from jax.sharding import PartitionSpec as P
 
 D = 1088
@@ -38,8 +40,10 @@
     return pieces + [whole_vec[8 * width :].astype(jnp.float32)]
 
 
-def gelu_exact(values):
-    return jax.nn.gelu(values, approximate=False)
+def gelu_parts(values):
+    share = 0.5 + 0.5 * lax.erf(values * (0.5**0.5))
+    density = jnp.exp(-0.5 * values * values) * ((2.0 * jnp.pi) ** (-0.5))
+    return (values * share, share + values * density)
 
 
 def allowed_pairs(keep):
@@ -83,12 +87,21 @@
     return jnp.concatenate([own, across, beside, swap(across, 1)], axis=0)
 
 
-def reduce_near(partial):
-    half = partial.shape[0] // 2
+def row_products(left_parts, right_parts, start, stop):
+    total = 0.0
+    for left, right in zip(left_parts, right_parts):
+        total = total + jnp.dot(left[start:stop], right, preferred_element_type=jnp.float32)
+    return total
+
+
+def reduce_near(left_parts, right_parts):
     low = jnp.bfloat16
-    both = partial[:half] + swap(partial[half:].astype(low), 1).astype(jnp.float32)
-    rows = half // 2
-    return (both[:rows], both[rows:].astype(low))
+    rows = left_parts[0].shape[0] // 4
+    given = row_products(left_parts, right_parts, 2 * rows, 4 * rows).astype(low)
+    taken = swap(given, 1).astype(jnp.float32)
+    far = row_products(left_parts, right_parts, rows, 2 * rows) + taken[rows:]
+    near = row_products(left_parts, right_parts, 0, rows) + taken[:rows]
+    return (near, far.astype(low))
 
 
 def after(values, others):
@@ -131,41 +144,73 @@
     return whole
 
 
-def gather_attn(shard, vectors):
+def z_groups(devices):
+    return [list(range(low, devices, 8)) for low in range(8)]
+
+
+def gather_z(shard):
+    devices = lax.axis_size("dev")
+    return lax.all_gather(shard, "dev", axis=0, tiled=False, axis_index_groups=z_groups(devices))
+
+
+def place_blocks(pieces, held):
+    block = (lax.axis_index("dev") & 7).astype(jnp.int32).reshape(1)
+    arrays = [piece[0] for piece in pieces]
+    rows, width = arrays[0].shape[1:]
+    count = sum(array.shape[0] for array in arrays)
+
+    def body(block_ref, *refs):
+        piece_refs = refs[: len(arrays)]
+        three_ref, last_ref, sems = refs[-3:]
+        copies = []
+        for ref, (array, mask, begin) in zip(piece_refs, pieces):
+            target = block_ref[0] ^ mask
+            for number in range(array.shape[0]):
+                matrix = begin + number
+                goal = last_ref.at[target] if matrix == 3 else three_ref.at[matrix, target]
+                copies.append(
+                    pltpu.make_async_copy(ref.at[number], goal, sems.at[len(copies)])
+                )
+                copies[-1].start()
+        for copy in copies:
+            copy.wait()
+
+    anywhere = pl.BlockSpec(memory_space=pl.ANY)
+    kind = arrays[0].dtype
+    return pl.pallas_call(
+        body,
+        out_shape=(
+            jax.ShapeDtypeStruct((3, 8, rows, width), kind),
+            jax.ShapeDtypeStruct((8, rows, width), kind),
+        ),
+        in_specs=[pl.BlockSpec(memory_space=pltpu.SMEM)]
+        + [anywhere] * (len(arrays) + len(held)),
+        out_specs=(anywhere, anywhere),
+        scratch_shapes=[pltpu.SemaphoreType.DMA((count,))],
+        input_output_aliases={1 + len(arrays) + number: number for number in range(len(held))},
+        cost_estimate=pl.CostEstimate(
+            flops=0, bytes_accessed=4 * count * rows * width, transcendentals=0
+        ),
+    )(block, *arrays, *held)
+
+
+def gather_attn(shard):
     devices = lax.axis_size("dev")
     if devices != 32:
-        return (lax.all_gather(shard, "dev", axis=0, tiled=True), gather_vectors(vectors), shard)
-    here = lax.axis_index("dev")
-    rows, width = shard.shape
-    spare = 8
-    extra = jnp.pad(vectors[None, :], ((0, spare - 1), (0, width - vectors.shape[0])))
-    zero = jnp.concatenate([shard, extra], axis=0)
-    one, two, three = swap(zero, 8), swap(zero, 16), swap(zero, 24)
-    odd = (here & 8) != 0
-    upper = (here & 16) != 0
-    near = (jnp.where(odd, one, zero), jnp.where(odd, zero, one))
-    far = (jnp.where(odd, three, two), jnp.where(odd, two, three))
-    top = jnp.stack([jnp.where(upper, far[0], near[0]), jnp.where(upper, far[1], near[1])])
-    bottom = jnp.stack([jnp.where(upper, near[0], far[0]), jnp.where(upper, near[1], far[1])])
-    ready = (one, two, three)
-    pieces = {(0, 0): top, (0, 1): bottom}
-    pieces[4, 0] = swap(top, 4)
-    pieces[2, 1] = swap(bottom, 2)
-    pieces[2, 0] = swap(top, 2)
-    pieces[4, 1] = swap(bottom, 4)
-    pieces[6, 0] = swap(pieces[4, 0], 2)
-    pieces[6, 1] = swap(pieces[2, 1], 4)
-    for place in list(pieces):
-        pieces[place[0] ^ 1, place[1]] = swap(pieces[place], 1)
-    whole = jnp.zeros((4, 8, rows, width), shard.dtype)
-    vector = jnp.zeros((4, 8, 1, vectors.shape[0]), vectors.dtype)
-    for (mask, half), piece in pieces.items():
-        start = (2 * half, (here & 7) ^ mask, 0, 0)
-        whole = lax.dynamic_update_slice(whole, piece[:, None, :rows], start)
-        vector = lax.dynamic_update_slice(
-            vector, piece[:, None, rows : rows + 1, : vectors.shape[0]], start
-        )
-    return (whole.reshape(-1, width), vector.reshape(-1), (ready, (pieces[6, 0], pieces[6, 1])))
+        whole = lax.all_gather(shard, "dev", axis=0, tiled=True)
+        width = shard.shape[1]
+        return (whole[: 3 * width], whole[3 * width :], shard)
+    own = gather_z(shard)
+    along, across = swap(own, 4), swap(own, 2)
+    beside = swap(own, 1)
+    upper, lower = swap(along[:2], 2), swap(across[2:], 4)
+    pieces = [(own, 0, 0), (beside, 1, 0), (along, 4, 0), (across, 2, 0)]
+    pieces += [(swap(along, 1), 5, 0), (swap(across, 1), 3, 0)]
+    held = place_blocks(pieces, ())
+    pieces = [(upper, 6, 0), (lower, 6, 2), (swap(upper, 1), 7, 0), (swap(lower, 1), 7, 2)]
+    three, last = place_blocks(pieces, held)
+    width = shard.shape[1]
+    return (three.reshape(3 * width, width), last.reshape(width, width), (upper, lower))
 
 
 def scatter_attn(grads, sources):
@@ -220,66 +265,69 @@
     upper = upper_part(3) + wide(across_upper) + wide(along_upper)
     lower = lower_part(3) + wide(across_lower) + wide(along_lower)
     total = jnp.concatenate([upper, lower], axis=0).reshape(4, rows, width)
-    layer = here >> 3
-
-    def part(mask):
-        return lax.dynamic_index_in_dim(total, layer ^ mask, 0, False)
-
-    result = part(0)
-    for mask in (1, 2, 3):
-        result = result + wide(swap(part(mask).astype(low), 8 * mask))
-    return result
-
-
-def gather_hidden(shard, attn_ready):
-    devices = lax.axis_size("dev")
-    here = lax.axis_index("dev")
-    half = devices // 2
+    return scatter_z(total, here >> 3)
+
+
+def gather_hidden(shard, near_ready):
+    devices = lax.axis_size("dev")
     if devices != 32:
         both = lax.all_gather(
             shard, "dev", axis=0, tiled=True, axis_index_groups=same_low(devices)
         )
-        rows = both.shape[0] // 2
+        return (both, None)
+    cut = 128
+    one, two = gather_z(shard[:cut]), gather_z(shard[cut:])
+    one = after(one, near_ready)
+    return ((one, swap(one, 4)), two)
+
+
+def hidden_parts(gathered, here, devices, ready):
+    half = devices // 2
+    one, two = gathered
+    if devices != 32:
+        rows = one.shape[0] // 2
         blocks = jnp.arange(half // 4, dtype=jnp.int32) * 4 + (here & 3)
-        return [(both[:rows], both[rows:], blocks)]
-    layers_ready, all_ready = attn_ready
-    held = [shard] + [swap(after(shard, layers_ready), 8 * mask) for mask in (1, 2, 3)]
-    moved = [swap(shard, 4)] + [swap(after(piece, all_ready), 4) for piece in held[1:]]
-    first = here < half
-    block = here & (half - 1)
-    blocks = jnp.stack([block, block ^ 8])
+        return [(one[:rows], one[rows:], blocks, 0, rows // (half // 4))]
+    two = after(two, ready)
+    blocks = jnp.stack([here & 7, (here & 7) + 8])
     parts = []
-    for pieces, numbers in ((held, blocks), (moved, blocks ^ 4)):
-        zero, one, two, three = pieces
-        up = jnp.concatenate([jnp.where(first, zero, two), jnp.where(first, one, three)], axis=0)
-        down = jnp.concatenate([jnp.where(first, two, zero), jnp.where(first, three, one)], axis=0)
-        parts.append((up, down, numbers))
+    for pieces, numbers in (((one[0], two), blocks), ((one[1], swap(two, 4)), blocks ^ 4)):
+        start = 0
+        for piece in pieces:
+            rows, width = piece.shape[1:]
+            up, down = piece[:2].reshape(2 * rows, width), piece[2:].reshape(2 * rows, width)
+            parts.append((up, down, numbers, start, start + rows))
+            start += rows
     return parts
 
 
 def scatter_hidden(grads, others):
     devices = lax.axis_size("dev")
+    low = jnp.bfloat16
     if devices != 32:
-        both = jnp.concatenate(grads[0], axis=0).astype(jnp.bfloat16)
+        both = jnp.concatenate(grads[0], axis=0).astype(low)
         return lax.psum_scatter(
             both, "dev", scatter_dimension=0, tiled=True, axis_index_groups=same_low(devices)
         ).astype(jnp.float32)
-    first = lax.axis_index("dev") < devices // 2
+    layer = lax.axis_index("dev") >> 3
+    moved = [[swap(part.astype(low), 4) for part in pair] for pair in grads[2:]]
+    shares = []
+    for own, other in zip(grads[:2], moved):
+        other = after(other, others)
+        total = jnp.concatenate(
+            [mine + part.astype(jnp.float32) for mine, part in zip(own, other)], axis=0
+        )
+        shares.append(scatter_z(total.reshape(4, -1, total.shape[1]), layer))
+    return jnp.concatenate(shares, axis=0)
+
+
+def scatter_z(total, layer):
     low = jnp.bfloat16
-    moved = [swap(part.astype(low), 4) for part in grads[1]]
-    moved = after(moved, others)
-    up, down = [own + part.astype(jnp.float32) for own, part in zip(grads[0], moved)]
-    rows = up.shape[0] // 2
-    mine = jnp.where(first, up[:rows], down[:rows])
-    two = jnp.where(first, down[:rows], up[:rows]).astype(low)
-    one = jnp.where(first, up[rows:], down[rows:]).astype(low)
-    three = jnp.where(first, down[rows:], up[rows:]).astype(low)
-    return (
-        mine
-        + swap(one, 8).astype(jnp.float32)
-        + swap(two, 16).astype(jnp.float32)
-        + swap(three, 24).astype(jnp.float32)
-    )
+    result = lax.dynamic_index_in_dim(total, layer, 0, False)
+    for mask in (1, 2, 3):
+        part = lax.dynamic_index_in_dim(total, layer ^ mask, 0, False).astype(low)
+        result = result + swap(part, 8 * mask).astype(jnp.float32)
+    return result
 
 
 def shards(
@@ -300,9 +348,10 @@
     allowed = allowed_pairs(keep)
     head_shape = (total_rows, HEADS, HEAD_SIZE)
 
-    full_attn, full_vec, attn_ready = gather_attn(attn_weight, vectors)
+    full_vec = gather_vectors(vectors)
     grad_down = jnp.where(live, cotangent, jnp.zeros_like(cotangent))
-    hidden_parts = gather_hidden(mlp_weight, attn_ready)
+    full_proj, full_out, attn_ready = gather_attn(attn_weight)
+    gathered = gather_hidden(mlp_weight, attn_ready)
     grad_down_rows = gather_rows(grad_down)
 
     (
@@ -323,7 +372,7 @@
     first_low = first_out.astype(low)
     first_beside = swap(first_low, 1)
     projected = jnp.einsum(
-        "rd,od->ro", first_low, full_attn[: 3 * width], preferred_element_type=jnp.float32
+        "rd,od->ro", first_low, full_proj, preferred_element_type=jnp.float32
     )
     queries = (projected[:, :width] + query_bias).astype(low).reshape(head_shape)
     keys = projected[:, width : 2 * width].astype(low).reshape(head_shape)
@@ -333,36 +382,35 @@
     mixed_beside = swap(mixed_low, 1)
     branch = (
         jnp.einsum(
-            "rd,od->ro", mixed_low, full_attn[3 * width :], preferred_element_type=jnp.float32
+            "rd,od->ro", mixed_low, full_out, preferred_element_type=jnp.float32
         )
         + out_bias
     )
     middle = inputs + branch
     second_out, normed_two, factor_two = normalize(middle, gain_two, shift_two)
-    second_low = gather_rows(second_out.astype(low))
-
-    second_rows = 0.0
+    second_own = second_out.astype(low)
+    second_low = gather_rows(second_own)
+    parts = hidden_parts(gathered, here, devices, second_own)
+
     kept = []
     grad_up_bias = jnp.zeros_like(up_bias)
-    for up_weight, down_weight, blocks in hidden_parts:
-        bias = up_bias[blocks].reshape(-1)
+    for up_weight, down_weight, blocks, start, stop in parts:
+        bias = up_bias[:, start:stop][blocks].reshape(-1)
         up_sum = (
             jnp.einsum("rd,fd->rf", second_low, up_weight, preferred_element_type=jnp.float32)
             + bias
         )
-        activated, gelu_back = jax.vjp(gelu_exact, up_sum)
-        act_low = activated.astype(low)
+        activated, slope = gelu_parts(up_sum)
         grad_act = jnp.einsum(
             "rd,fd->rf", grad_down_rows, down_weight, preferred_element_type=jnp.float32
         )
-        grad_up = gelu_back(grad_act)[0].astype(low)
-        second_rows = second_rows + jnp.dot(
-            grad_up, up_weight, preferred_element_type=jnp.float32
-        )
+        grad_up = (grad_act * slope).astype(low)
         column_sums = jnp.sum(grad_up.astype(jnp.float32), axis=0)
-        grad_up_bias = grad_up_bias.at[blocks].set(column_sums.reshape(blocks.shape[0], -1))
-        kept.append((act_low, grad_up))
-    grad_second, far = reduce_near(second_rows)
+        grad_up_bias = grad_up_bias.at[blocks, start:stop].set(
+            column_sums.reshape(blocks.shape[0], -1)
+        )
+        kept.append((activated.astype(low), grad_up))
+    grad_second, far = reduce_near([pair[1] for pair in kept], [part[0] for part in parts])
     grad_second = grad_second + swap(far, 2).astype(jnp.float32)
     kept = after(kept, far)
     grads = [
@@ -372,12 +420,7 @@
         )
         for act_low, grad_up in kept
     ]
-    down = 0.0
-    for (act_low, grad_up), (up_weight, down_weight, blocks) in zip(kept, hidden_parts):
-        down = down + jnp.dot(act_low, down_weight, preferred_element_type=jnp.float32)
-    down, far = reduce_near(down)
-    down = down + swap(far, 2).astype(jnp.float32) + down_bias
-    output = jnp.where(live, middle + down, 0.0).astype(low)
+    down, down_far = reduce_near([pair[0] for pair in kept], [part[1] for part in parts])
 
     grad_down_wide = grad_down.astype(jnp.float32)
     grad_down_bias = jnp.sum(grad_down_wide, axis=0)
@@ -386,7 +429,7 @@
     grad_middle = grad_down_wide + normalize_back(grad_second, normed_two, factor_two, gain_two)
     grad_branch = grad_middle.astype(low)
     grad_out_bias = jnp.sum(grad_branch.astype(jnp.float32), axis=0)
-    grad_mixed = jnp.dot(grad_branch, full_attn[3 * width :], preferred_element_type=jnp.float32)
+    grad_mixed = jnp.dot(grad_branch, full_out, preferred_element_type=jnp.float32)
     grad_mixed_low = grad_mixed.astype(low).reshape(head_shape)
     grad_queries, grad_keys, grad_values = attend_back(
         queries, keys, values, allowed, scale, grad_mixed_low, log_total
@@ -404,10 +447,12 @@
         grad_features, ((first_low, first_beside), (mixed_low, mixed_beside))
     )
     mlp_share = scatter_hidden(grads, grad_features)
+    down_far = after(swap(down_far, 2), grad_features).astype(jnp.float32)
+    output = jnp.where(live, middle + (down + down_far + down_bias), 0.0).astype(low)
     grad_projected = grad_features[: 3 * width]
     grad_columns = jnp.sum(grad_projected.astype(jnp.float32), axis=1)
     grad_first = jnp.einsum(
-        "fr,fd->rd", grad_projected, full_attn[: 3 * width], preferred_element_type=jnp.float32
+        "fr,fd->rd", grad_projected, full_proj, preferred_element_type=jnp.float32
     )
     grad_gain_one = jnp.sum(grad_first * normed_one, axis=0)
     grad_shift_one = jnp.sum(grad_first, axis=0)

time: 472 us -> 822 us (1.74)
  Pallas kernels: 0 us -> 306 us
  waiting for transfers between devices: 230 us -> 182 us
  other arithmetic: 40.1 us -> 75.2 us
  matrix products: 75.5 us -> 108 us
  local copies, waits for them, and re-layouts: 64.3 us -> 82.7 us
  between operations: 3.86 us -> 17.1 us
    pallas_call x0 -> x2, Pallas kernels: none -> 306 us  [place_blocks(): pl.pallas_call(body, out_shape=(jax.ShapeDtypeStruct((3, 8, rows, width),...]
    ppermute x56 -> x53, waiting for transfers between devices: 230 us -> 159 us  [swap(): lax.ppermute(piece, 'dev', [(number, number ^ mask) for number in range(d...]
    scatter x0 -> x16, other arithmetic: none -> 44 us
    scatter x2 -> x24, local copies, waits for them, and re-layouts: 1.6 us -> 29 us  [shards(): grad_up_bias.at[blocks].set(column_sums.reshape(blocks.shape[0], -1))]
    dynamic_update_slice x30 -> x0, local copies, waits for them, and re-layouts: 25.3 us -> none  [the longest x14 24.5 us: gather_attn(): whole = lax.dynamic_update_slice(whole, piece[:, None, :rows], start)]
    all_gather x0 -> x3, waiting for transfers between devices: none -> 21.9 us  [gather_z(): lax.all_gather(shard, 'dev', axis=0, tiled=False, axis_index_groups=z_gro...]
    dot_general x8 -> x28, matrix products: 22.3 us -> 43.5 us  [the longest x24 31.4 us: row_products(): jnp.dot(left[start:stop], right, preferred_element_type=jnp.float32)]
    broadcast_in_dim x17 -> x1, local copies, waits for them, and re-layouts: 12.6 us -> 0.6 us  [shards(): grad_up_bias = jnp.zeros_like(up_bias)]
  transfers between devices with their start and end apart: 56 -> 56, of which waited for: 20 -> 17; matrix products, arithmetic and copies ran while one was open for 32% -> 30% of each run, Pallas kernels for 0% -> 38%
where the time goes in v3:
time: 822 us; the launch traced here: 817 us
  Pallas kernels  306 us (37%)
  waiting for transfers between devices  182 us (22%)
  matrix products  108 us (13%)
  local copies, waits for them, and re-layouts  82.7 us (10%)
  other arithmetic  75.2 us (9%)
  starting transfers between devices  45.2 us (5%)
  between operations  17.1 us (2%)
    pallas_call x2, Pallas kernels, place_blocks(): pl.pallas_call(body, out_shape=(jax.ShapeDtypeStruct((3, 8, rows, width),...  306 us
    ppermute x53, waiting for transfers between devices, swap(): lax.ppermute(piece, 'dev', [(number, number ^ mask) for number in range(d...  159 us
    ppermute x53, starting transfers between devices, swap(): lax.ppermute(piece, 'dev', [(number, number ^ mask) for number in range(d...  45.1 us
    scatter x16, other arithmetic  44 us
    dot_general x24, matrix products, row_products(): jnp.dot(left[start:stop], right, preferred_element_type=jnp.float32)  31.4 us
    scatter x24, local copies, waits for them, and re-layouts  29 us
    all_gather x3, waiting for transfers between devices, gather_z(): lax.all_gather(shard, 'dev', axis=0, tiled=False, axis_index_groups=z_gro...  21.9 us
  transfers between devices with their start and end apart: 56, of which 17 were waited for; matrix products, arithmetic and copies ran while one was open for 30% of the time, Pallas kernels for 38%

profile of v3, /device:TPU:8, one launch (start us, length us, event | category | flops | bytes accessed | tf_op | source)
XLA Modules:
  0.0 816.5 jit_solution(208438004253504497)
XLA Ops:
  20.0 21.9 %all-gather.7.cloned.1.call-done = bf16[544,1088]{1,0:T(8,128)(2,1)} async-done(((bf16[136,1088]{1,0:T(8,128)(2,1)}), bf16[544,1088]{1,0:T(8,128)(2,1)}) %all-gather.7.cloned.1.call-update) | async-done | bytes 1183760 | tf_op jit(solution)/shard_map/all_gather | solution.py:153
  45.6 25.7 %collective-permute-done.2 = bf16[1632]{0:T(1024)(128)(2,1)S(1)} collective-permute-done((bf16[1632]{0:T(1024)(128)(2,1)S(1)}, bf16[1632]{0:T(1024)(128)(2,1)S(1)}, u32[]{:S(2)}, u32[]{:S(2)}) %collective-permute-start.2) | collective-permute-done | bytes 3296 | tf_op jit(solution)/shard_map/ppermute | solution.py:113
  84.4 7.5 collective-permute-done.8.refs_1_
  103.3 229.1 %shard_map.119 = (bf16[3,8,136,1088]{3,2,1,0:T(8,128)(2,1)}, bf16[8,136,1088]{2,1,0:T(8,128)(2,1)}) custom-call(s32[1]{0:T(128)} %bitcast.block_ref, bf16[4,136,1088]{2,1,0:T(8,128)(2,1)} %bitcast.1.refs_0_, bf16[4,136,1088]{2,1,0:T(8,128)(2,1)} %collective-permute-done.11.refs_1_, bf16[4,136,1088]{2,1,0:T(8,128)(2,1)} %copy-done.34, ...), custom_call_target="tpu_custom_call" | custom-call | bytes 14204928 | tf_op jit(solution)/shard_map/pallas_call | solution.py:180
  333.3 77.1 %shard_map.120 = (bf16[3,8,136,1088]{3,2,1,0:T(8,128)(2,1)}, bf16[8,136,1088]{2,1,0:T(8,128)(2,1)}) custom-call(s32[1]{0:T(128)} %bitcast.block_ref, bf16[2,136,1088]{2,1,0:T(8,128)(2,1)} %collective-permute-done.6.refs_0_, bf16[2,136,1088]{2,1,0:T(8,128)(2,1)} %collective-permute-done.8.refs_1_, ...), custom_call_target="tpu_custom_call", output_to_operand_aliasing={{0}: (5, {}), {1}: (6, {})} | custom-call | bytes 4734976 | tf_op jit(solution)/shard_map/pallas_call | solution.py:180
  410.4 5.5 fusion.219
  427.5 11.0 %collective-permute-done.14 = bf16[256,1088]{0,1:T(8,128)(2,1)} collective-permute-done((bf16[256,1088]{0,1:T(8,128)(2,1)}, bf16[256,1088]{0,1:T(8,128)(2,1)}, u32[]{:S(2)}, u32[]{:S(2)}) %collective-permute-start.14) | collective-permute-done | bytes 557088 | tf_op jit(solution)/shard_map/ppermute | solution.py:113
  447.9 3.5 multiply_convert_fusion.4
  457.5 3.4 multiply_convert_fusion.2
  460.9 4.6 convert_reduce_fusion.4
  467.4 19.3 %while.4 = (s32[]{:T(128)}, f32[16,272]{1,0:T(8,128)}, s32[2,2]{1,0:T(2,128)}, f32[2,128]{1,0:T(2,128)}, s32[]{:T(128)}, /*index=5*/s32[2]{0:T(128)}) while((s32[]{:T(128)}, f32[16,272]{1,0:T(8,128)}, s32[2,2]{1,0:T(2,128)}, f32[2,128]{1,0:T(2,128)}, s32[]{:T(128)}, /*index=5*/s32[2]{0:T(128)}) %tuple.165), condition=%wide.while_cond, body=%wide.while_body.sunk | while | flops 139 | bytes 2699 | solution.py:409
  486.7 19.1 %while.5 = (s32[]{:T(128)}, f32[16,272]{1,0:T(8,128)}, s32[2,2]{1,0:T(2,128)}, f32[2,144]{1,0:T(2,128)}, s32[]{:T(128)}, /*index=5*/s32[2]{0:T(128)}) while((s32[]{:T(128)}, f32[16,272]{1,0:T(8,128)}, s32[2,2]{1,0:T(2,128)}, f32[2,144]{1,0:T(2,128)}, s32[]{:T(128)}, /*index=5*/s32[2]{0:T(128)}) %tuple.148), condition=%wide.while_cond.1, body=%wide.while_body.1.sunk | while | flops 155 | bytes 3019 | solution.py:409
  514.2 3.5 convert_reduce_fusion.6
  519.6 15.7 %while.6 = (s32[]{:T(128)}, f32[16,272]{1,0:T(8,128)}, s32[2,2]{1,0:T(2,128)S(1)}, f32[2,128]{1,0:T(2,128)S(1)}, s32[]{:T(128)}, /*index=5*/s32[2]{0:T(128)S(1)}) while((s32[]{:T(128)}, f32[16,272]{1,0:T(8,128)}, s32[2,2]{1,0:T(2,128)S(1)}, f32[2,128]{1,0:T(2,128)S(1)}, s32[]{:T(128)}, /*index=5*/s32[2]{0:T(128)S(1)}) %tuple.167), condition=%wide.while_cond.2, body=%wide.while_body.2.sunk | while | flops 139 | bytes 2699 | solution.py:409
  536.7 3.6 multiply_convert_fusion.1
  540.3 4.1 convert_reduce_fusion.3
  550.6 19.0 %while.7 = (s32[]{:T(128)}, f32[16,272]{1,0:T(8,128)}, s32[2,2]{1,0:T(2,128)}, f32[2,144]{1,0:T(2,128)}, s32[]{:T(128)}, /*index=5*/s32[2]{0:T(128)}) while((s32[]{:T(128)}, f32[16,272]{1,0:T(8,128)}, s32[2,2]{1,0:T(2,128)}, f32[2,144]{1,0:T(2,128)}, s32[]{:T(128)}, /*index=5*/s32[2]{0:T(128)}) %tuple.163), condition=%wide.while_cond.3, body=%wide.while_body.3.sunk | while | flops 155 | bytes 3019 | solution.py:409
  589.4 3.4 convolution_convert_fusion.1
  593.4 3.4 convolution_convert_fusion
  615.4 4.2 fusion.61
  619.9 3.4 fusion.60
  632.8 3.3 reshape.385
  637.0 5.7 constant_dynamic-slice_fusion.6
  673.1 10.7 %collective-permute-done.41 = bf16[128,1088]{1,0:T(8,128)(2,1)S(1)} collective-permute-done((bf16[128,1088]{1,0:T(8,128)(2,1)}, bf16[128,1088]{1,0:T(8,128)(2,1)S(1)}, u32[]{:S(2)}, u32[]{:S(2)}) %collective-permute-start.41) | collective-permute-done | bytes 278560 | tf_op jit(solution)/shard_map/ppermute | solution.py:113
  687.1 18.3 %collective-permute-done.42 = bf16[128,1088]{1,0:T(8,128)(2,1)S(1)} collective-permute-done((bf16[128,1088]{1,0:T(8,128)(2,1)}, bf16[128,1088]{1,0:T(8,128)(2,1)S(1)}, u32[]{:S(2)}, u32[]{:S(2)}) %collective-permute-start.42) | collective-permute-done | bytes 278560 | tf_op jit(solution)/shard_map/ppermute | solution.py:113
  708.0 3.4 collective-permute-done.46
  711.4 7.9 collective-permute-done.47
  731.8 31.5 %collective-permute-done.29 = bf16[272,1088]{1,0:T(8,128)(2,1)S(1)} collective-permute-done((bf16[272,1088]{1,0:T(8,128)(2,1)S(1)}, bf16[272,1088]{1,0:T(8,128)(2,1)S(1)}, u32[]{:S(2)}, u32[]{:S(2)}) %collective-permute-start.29) | collective-permute-done | bytes 591904 | tf_op jit(solution)/shard_map/ppermute | solution.py:113
  767.4 11.4 %collective-permute-done.30 = bf16[272,1088]{1,0:T(8,128)(2,1)S(1)} collective-permute-done((bf16[272,1088]{1,0:T(8,128)(2,1)S(1)}, bf16[272,1088]{1,0:T(8,128)(2,1)S(1)}, u32[]{:S(2)}, u32[]{:S(2)}) %collective-permute-start.30) | collective-permute-done | bytes 591904 | tf_op jit(solution)/shard_map/ppermute | solution.py:113
  785.0 5.3 collective-permute-done.35
  790.3 13.3 %collective-permute-done.36 = bf16[136,1088]{1,0:T(8,128)(2,1)S(1)} collective-permute-done((bf16[136,1088]{1,0:T(8,128)(2,1)S(1)}, bf16[136,1088]{1,0:T(8,128)(2,1)S(1)}, u32[]{:S(2)}, u32[]{:S(2)}) %collective-permute-start.36) | collective-permute-done | bytes 295968 | tf_op jit(solution)/shard_map/ppermute | solution.py:113
  803.7 4.9 collective-permute-done.37
  (467 shorter events, 268.7 us)
Async XLA Ops:
  7.2 34.7 %all-gather.7.cloned.1.call-start = ((), (), s32[]{:S(2)}) async-start(), calls=%async_computation | async-start | bytes 1566720 | tf_op jit(solution)/shard_map/all_gather | solution.py:153
  7.9 91.6 %all-gather.9.cloned.1.call-start = ((), (), s32[]{:S(2)}) async-start(), calls=%async_computation.1 | async-start | bytes 1474560 | tf_op jit(solution)/shard_map/all_gather | solution.py:153
  9.7 416.3 %all-gather.11.cloned.1.call-start = ((), (), s32[]{:S(2)}) async-start(), calls=%async_computation.2 | async-start | bytes 1658880 | tf_op jit(solution)/shard_map/all_gather | solution.py:153
  15.7 67.2 %collective-permute-start.17 = (bf16[256,1088]{0,1:T(8,128)(2,1)}, bf16[256,1088]{0,1:T(8,128)(2,1)}, u32[]{:S(2)}, u32[]{:S(2)}) collective-permute-start(bf16[256,1088]{0,1:T(8,128)(2,1)} %get-tuple-element.118), channel_id=1, source_target_pairs={{0,2},{1,3},{2,0},{3,1},{4,6},{5,7},{6,4},{7,5},{8,10},{9,11},{10,... | collective-permute-start | bytes 1671176 | tf_op jit(solution)/shard_map/ppermute | solution.py:113
  19.3 25.5 %collective-permute-start.1 = (bf16[816]{0:T(1024)(128)(2,1)S(1)}, bf16[816]{0:T(1024)(128)(2,1)S(1)}, u32[]{:S(2)}, u32[]{:S(2)}) collective-permute-start(bf16[816]{0:T(1024)(128)(2,1)S(1)} %pad_maximum_fusion.18), channel_id=1, source_target_pairs={{0,2},{1,3},{2,0},{3,1},{4,6},{5,7},{6,4},{7,5},{8,10},{9,11},{10,... | collective-permute-start | bytes 4904 | tf_op jit(solution)/shard_map/ppermute | solution.py:113
  41.9 37.5 %collective-permute-start.5 = (bf16[4,136,1088]{2,1,0:T(8,128)(2,1)}, bf16[4,136,1088]{2,1,0:T(8,128)(2,1)S(1)}, u32[]{:S(2)}, u32[]{:S(2)}) collective-permute-start(bf16[4,136,1088]{2,1,0:T(8,128)(2,1)} %bitcast.1.refs_0_), channel_id=1, source_target_pairs={{0,4},{1,5},{2,6},{3,7},{4,0},{5,1},{6,2},{7,3},{8,12},{9,13},{10,... | collective-permute-start | bytes 3551240 | tf_op jit(solution)/shard_map/ppermute | solution.py:113
  43.4 33.2 %collective-permute-start.7 = (bf16[4,136,1088]{2,1,0:T(8,128)(2,1)}, bf16[4,136,1088]{2,1,0:T(8,128)(2,1)}, u32[]{:S(2)}, u32[]{:S(2)}) collective-permute-start(bf16[4,136,1088]{2,1,0:T(8,128)(2,1)} %bitcast.1.refs_0_), channel_id=1, source_target_pairs={{0,2},{1,3},{2,0},{3,1},{4,6},{5,7},{6,4},{7,5},{8,10},{9,11},{10,... | collective-permute-start | bytes 3551240 | tf_op jit(solution)/shard_map/ppermute | solution.py:113
  45.0 26.3 %collective-permute-start.2 = (bf16[1632]{0:T(1024)(128)(2,1)S(1)}, bf16[1632]{0:T(1024)(128)(2,1)S(1)}, u32[]{:S(2)}, u32[]{:S(2)}) collective-permute-start(bf16[1632]{0:T(1024)(128)(2,1)S(1)} %pad_maximum_fusion.17), channel_id=1, source_target_pairs={{0,4},{1,5},{2,6},{3,7},{4,0},{5,1},{6,2},{7,3},{8,12},{9,13},{10,... | collective-permute-start | bytes 9800 | tf_op jit(solution)/shard_map/ppermute | solution.py:113
  91.9 240.5 %collective-permute-start.10 = (bf16[2,136,1088]{2,1,0:T(8,128)(2,1)}, bf16[2,136,1088]{2,1,0:T(8,128)(2,1)S(1)}, u32[]{:S(2)}, u32[]{:S(2)}) collective-permute-start(bf16[2,136,1088]{2,1,0:T(8,128)(2,1)} %collective-permute-done.8.refs_1_), channel_id=1, source_target_pairs={{0,1},{1,0},{2,3},{3,2},{4,5},{5,4},{6,7},{7,6},{8,9},{9,8},{10,11... | collective-permute-start | bytes 1775624 | tf_op jit(solution)/shard_map/ppermute | solution.py:113
  94.3 238.2 %collective-permute-start.9 = (bf16[2,136,1088]{2,1,0:T(8,128)(2,1)}, bf16[2,136,1088]{2,1,0:T(8,128)(2,1)}, u32[]{:S(2)}, u32[]{:S(2)}) collective-permute-start(bf16[2,136,1088]{2,1,0:T(8,128)(2,1)} %collective-permute-done.6.refs_0_), channel_id=1, source_target_pairs={{0,1},{1,0},{2,3},{3,2},{4,5},{5,4},{6,7},{7,6},{8,9},{9,8},{10,11... | collective-permute-start | bytes 1775624 | tf_op jit(solution)/shard_map/ppermute | solution.py:113
  102.1 349.3 %collective-permute-start.18 = (bf16[256,1088]{0,1:T(8,128)(2,1)}, bf16[256,1088]{0,1:T(8,128)(2,1)}, u32[]{:S(2)}, u32[]{:S(2)}) collective-permute-start(bf16[256,1088]{0,1:T(8,128)(2,1)} %get-tuple-element.118), channel_id=1, source_target_pairs={{0,1},{1,0},{2,3},{3,2},{4,5},{5,4},{6,7},{7,6},{8,9},{9,8},{10,11... | collective-permute-start | bytes 1671176 | tf_op jit(solution)/shard_map/ppermute | solution.py:113
  102.7 348.7 %collective-permute-start.19 = (bf16[256,1088]{0,1:T(8,128)(2,1)}, bf16[256,1088]{0,1:T(8,128)(2,1)}, u32[]{:S(2)}, u32[]{:S(2)}) collective-permute-start(bf16[256,1088]{0,1:T(8,128)(2,1)} %collective-permute-done.17), channel_id=1, source_target_pairs={{0,1},{1,0},{2,3},{3,2},{4,5},{5,4},{6,7},{7,6},{8,9},{9,8},{10,11... | collective-permute-start | bytes 1671176 | tf_op jit(solution)/shard_map/ppermute | solution.py:113
  102.8 337.0 %collective-permute-start.20 = (bf16[4,128,1088]{1,2,0:T(8,128)(2,1)}, bf16[4,128,1088]{1,2,0:T(8,128)(2,1)}, u32[]{:S(2)}, u32[]{:S(2)}) collective-permute-start(bf16[4,128,1088]{1,2,0:T(8,128)(2,1)} %copy.40), channel_id=1, source_target_pairs={{0,4},{1,5},{2,6},{3,7},{4,0},{5,1},{6,2},{7,3},{8,12},{9,13},{10,... | collective-permute-start | bytes 3342344 | tf_op jit(solution)/shard_map/ppermute | solution.py:113
  439.8 95.5 %collective-permute-start.21 = (bf16[4,144,1088]{2,1,0:T(8,128)(2,1)}, bf16[4,144,1088]{2,1,0:T(8,128)(2,1)}, u32[]{:S(2)}, u32[]{:S(2)}) collective-permute-start(bf16[4,144,1088]{2,1,0:T(8,128)(2,1)} %bitcast.15), channel_id=1, source_target_pairs={{0,4},{1,5},{2,6},{3,7},{4,0},{5,1},{6,2},{7,3},{8,12},{9,13},{10,... | collective-permute-start | bytes 3760136 | tf_op jit(solution)/shard_map/ppermute | solution.py:113
  550.4 24.0 %collective-permute-start.22 = (bf16[512,1088]{0,1:T(8,128)(2,1)}, bf16[512,1088]{0,1:T(8,128)(2,1)}, u32[]{:S(2)}, u32[]{:S(2)}) collective-permute-start(bf16[512,1088]{0,1:T(8,128)(2,1)} %fusion.5), channel_id=1, source_target_pairs={{0,1},{1,0},{2,3},{3,2},{4,5},{5,4},{6,7},{7,6},{8,9},{9,8},{10,11... | collective-permute-start | bytes 3342344 | tf_op jit(solution)/shard_map/ppermute | solution.py:113
  576.5 29.2 %collective-permute-start.25 = (bf16[256,1088]{0,1:T(8,128)(2,1)S(1)}, bf16[256,1088]{0,1:T(8,128)(2,1)S(1)}, u32[]{:S(2)}, u32[]{:S(2)}) collective-permute-start(bf16[256,1088]{0,1:T(8,128)(2,1)S(1)} %fusion.23), channel_id=1, source_target_pairs={{0,2},{1,3},{2,0},{3,1},{4,6},{5,7},{6,4},{7,5},{8,10},{9,11},{10,... | collective-permute-start | bytes 1671176 | tf_op jit(solution)/shard_map/ppermute | solution.py:113
  584.3 40.5 %collective-permute-start.38 = (bf16[256,1088]{0,1:T(8,128)(2,1)}, bf16[256,1088]{0,1:T(8,128)(2,1)}, u32[]{:S(2)}, u32[]{:S(2)}) collective-permute-start(bf16[256,1088]{0,1:T(8,128)(2,1)} %convolution_convert_fusion.5), channel_id=1, source_target_pairs={{0,4},{1,5},{2,6},{3,7},{4,0},{5,1},{6,2},{7,3},{8,12},{9,13},{10,... | collective-permute-start | bytes 1671176 | tf_op jit(solution)/shard_map/ppermute | solution.py:113
  588.0 38.2 %collective-permute-start.39 = (bf16[256,1088]{0,1:T(8,128)(2,1)}, bf16[256,1088]{0,1:T(8,128)(2,1)}, u32[]{:S(2)}, u32[]{:S(2)}) collective-permute-start(bf16[256,1088]{0,1:T(8,128)(2,1)} %convolution_convert_fusion.4), channel_id=1, source_target_pairs={{0,4},{1,5},{2,6},{3,7},{4,0},{5,1},{6,2},{7,3},{8,12},{9,13},{10,... | collective-permute-start | bytes 1671176 | tf_op jit(solution)/shard_map/ppermute | solution.py:113
  592.8 71.4 %collective-permute-start.43 = (bf16[288,1088]{1,0:T(8,128)(2,1)}, bf16[288,1088]{1,0:T(8,128)(2,1)}, u32[]{:S(2)}, u32[]{:S(2)}) collective-permute-start(bf16[288,1088]{1,0:T(8,128)(2,1)} %convolution_convert_fusion.1), channel_id=1, source_target_pairs={{0,4},{1,5},{2,6},{3,7},{4,0},{5,1},{6,2},{7,3},{8,12},{9,13},{10,... | collective-permute-start | bytes 1880072 | tf_op jit(solution)/shard_map/ppermute | solution.py:113
  596.8 68.1 %collective-permute-start.44 = (bf16[288,1088]{1,0:T(8,128)(2,1)}, bf16[288,1088]{1,0:T(8,128)(2,1)}, u32[]{:S(2)}, u32[]{:S(2)}) collective-permute-start(bf16[288,1088]{1,0:T(8,128)(2,1)} %convolution_convert_fusion), channel_id=1, source_target_pairs={{0,4},{1,5},{2,6},{3,7},{4,0},{5,1},{6,2},{7,3},{8,12},{9,13},{10,... | collective-permute-start | bytes 1880072 | tf_op jit(solution)/shard_map/ppermute | solution.py:113
  605.7 113.8 %collective-permute-start.23 = (bf16[512,1088]{0,1:T(8,128)(2,1)}, bf16[512,1088]{0,1:T(8,128)(2,1)}, u32[]{:S(2)}, u32[]{:S(2)}) collective-permute-start(bf16[512,1088]{0,1:T(8,128)(2,1)} %fusion.4), channel_id=1, source_target_pairs={{0,1},{1,0},{2,3},{3,2},{4,5},{5,4},{6,7},{7,6},{8,9},{9,8},{10,11... | collective-permute-start | bytes 3342344 | tf_op jit(solution)/shard_map/ppermute | solution.py:113
  644.4 26.5 %collective-permute-start.40 = (bf16[128,1088]{1,0:T(8,128)(2,1)}, bf16[128,1088]{1,0:T(8,128)(2,1)}, u32[]{:S(2)}, u32[]{:S(2)}) collective-permute-start(bf16[128,1088]{1,0:T(8,128)(2,1)} %bitcast.135), channel_id=1, source_target_pairs={{0,8},{1,9},{2,10},{3,11},{4,12},{5,13},{6,14},{7,15},{8,0},{9,1},... | collective-permute-start | bytes 835592 | tf_op jit(solution)/shard_map/ppermute | solution.py:113
  664.2 41.2 %collective-permute-start.42 = (bf16[128,1088]{1,0:T(8,128)(2,1)}, bf16[128,1088]{1,0:T(8,128)(2,1)S(1)}, u32[]{:S(2)}, u32[]{:S(2)}) collective-permute-start(bf16[128,1088]{1,0:T(8,128)(2,1)} %bitcast.299), channel_id=1, source_target_pairs={{0,24},{1,25},{2,26},{3,27},{4,28},{5,29},{6,30},{7,31},{8,16},{9,... | collective-permute-start | bytes 835592 | tf_op jit(solution)/shard_map/ppermute | solution.py:113
  664.9 57.8 %collective-permute-start.26 = (bf16[4,4,136,256]{3,2,1,0:T(8,128)(2,1)}, bf16[4,4,136,256]{3,2,1,0:T(8,128)(2,1)S(1)}, u32[]{:S(2)}, u32[]{:S(2)}) collective-permute-start(bf16[4,4,136,256]{3,2,1,0:T(8,128)(2,1)} %pad_maximum_fusion.9), channel_id=1, source_target_pairs={{0,1},{1,0},{2,3},{3,2},{4,5},{5,4},{6,7},{7,6},{8,9},{9,8},{10,11... | collective-permute-start | bytes 3342344 | tf_op jit(solution)/shard_map/ppermute | solution.py:113
  670.9 37.0 %collective-permute-start.45 = (bf16[144,1088]{1,0:T(8,128)(2,1)S(1)}, bf16[144,1088]{1,0:T(8,128)(2,1)S(1)}, u32[]{:S(2)}, u32[]{:S(2)}) collective-permute-start(bf16[144,1088]{1,0:T(8,128)(2,1)S(1)} %get-tuple-element.135), channel_id=1, source_target_pairs={{0,8},{1,9},{2,10},{3,11},{4,12},{5,13},{6,14},{7,15},{8,0},{9,1},... | collective-permute-start | bytes 940040 | tf_op jit(solution)/shard_map/ppermute | solution.py:113
  683.8 27.5 %collective-permute-start.46 = (bf16[144,1088]{1,0:T(8,128)(2,1)S(1)}, bf16[144,1088]{1,0:T(8,128)(2,1)S(1)}, u32[]{:S(2)}, u32[]{:S(2)}) collective-permute-start(bf16[144,1088]{1,0:T(8,128)(2,1)S(1)} %get-tuple-element.137), channel_id=1, source_target_pairs={{0,16},{1,17},{2,18},{3,19},{4,20},{5,21},{6,22},{7,23},{8,24},{9,... | collective-permute-start | bytes 940040 | tf_op jit(solution)/shard_map/ppermute | solution.py:113
  722.1 44.3 %collective-permute-start.24 = (bf16[256,1088]{0,1:T(8,128)(2,1)S(1)}, bf16[256,1088]{0,1:T(8,128)(2,1)S(1)}, u32[]{:S(2)}, u32[]{:S(2)}) collective-permute-start(bf16[256,1088]{0,1:T(8,128)(2,1)S(1)} %fusion.22), channel_id=1, source_target_pairs={{0,2},{1,3},{2,0},{3,1},{4,6},{5,7},{6,4},{7,5},{8,10},{9,11},{10,... | collective-permute-start | bytes 1671176 | tf_op jit(solution)/shard_map/ppermute | solution.py:113
  723.6 43.8 %collective-permute-start.28 = (bf16[272,1088]{1,0:T(8,128)(2,1)S(1)}, bf16[272,1088]{1,0:T(8,128)(2,1)S(1)}, u32[]{:S(2)}, u32[]{:S(2)}) collective-permute-start(bf16[272,1088]{1,0:T(8,128)(2,1)S(1)} %convolution_convert_fusion.3), channel_id=1, source_target_pairs={{0,2},{1,3},{2,0},{3,1},{4,6},{5,7},{6,4},{7,5},{8,10},{9,11},{10,... | collective-permute-start | bytes 1775624 | tf_op jit(solution)/shard_map/ppermute | solution.py:113
  725.7 37.5 %collective-permute-start.29 = (bf16[272,1088]{1,0:T(8,128)(2,1)S(1)}, bf16[272,1088]{1,0:T(8,128)(2,1)S(1)}, u32[]{:S(2)}, u32[]{:S(2)}) collective-permute-start(bf16[272,1088]{1,0:T(8,128)(2,1)S(1)} %convolution_convert_fusion.2), channel_id=1, source_target_pairs={{0,2},{1,3},{2,0},{3,1},{4,6},{5,7},{6,4},{7,5},{8,10},{9,11},{10,... | collective-permute-start | bytes 1775624 | tf_op jit(solution)/shard_map/ppermute | solution.py:113
  727.4 37.0 %collective-permute-start.32 = (bf16[272,1088]{1,0:T(8,128)(2,1)S(1)}, bf16[272,1088]{1,0:T(8,128)(2,1)S(1)}, u32[]{:S(2)}, u32[]{:S(2)}) collective-permute-start(bf16[272,1088]{1,0:T(8,128)(2,1)S(1)} %pad_maximum_fusion.13), channel_id=1, source_target_pairs={{0,4},{1,5},{2,6},{3,7},{4,0},{5,1},{6,2},{7,3},{8,12},{9,13},{10,... | collective-permute-start | bytes 1775624 | tf_op jit(solution)/shard_map/ppermute | solution.py:113
  729.2 50.1 %collective-permute-start.34 = (bf16[272,1088]{1,0:T(8,128)(2,1)S(1)}, bf16[272,1088]{1,0:T(8,128)(2,1)S(1)}, u32[]{:S(2)}, u32[]{:S(2)}) collective-permute-start(bf16[272,1088]{1,0:T(8,128)(2,1)S(1)} %pad_maximum_fusion.14), channel_id=1, source_target_pairs={{0,4},{1,5},{2,6},{3,7},{4,0},{5,1},{6,2},{7,3},{8,12},{9,13},{10,... | collective-permute-start | bytes 1775624 | tf_op jit(solution)/shard_map/ppermute | solution.py:113
  782.8 25.8 %collective-permute-start.37 = (bf16[136,1088]{1,0:T(8,128)(2,1)S(1)}, bf16[136,1088]{1,0:T(8,128)(2,1)S(1)}, u32[]{:S(2)}, u32[]{:S(2)}) collective-permute-start(bf16[136,1088]{1,0:T(8,128)(2,1)S(1)} %get-tuple-element.139), channel_id=1, source_target_pairs={{0,24},{1,25},{2,26},{3,27},{4,28},{5,29},{6,30},{7,31},{8,16},{9,... | collective-permute-start | bytes 887816 | tf_op jit(solution)/shard_map/ppermute | solution.py:113
  (108 other events, 1388.3 us)
Sparse Core Ops, SparseCore 0:
  9.6 32.2 all-gather.6
  44.0 29.6 all-gather.8
  75.3 31.9 all-gather.10

commit v4 on v3

--- a/solution.py
+++ b/solution.py
@@ -9,6 +9,7 @@
 HEADS = 17
 HEAD_SIZE = 64
 FF = 4352
+VMEM_LIMIT = 32 * 1024 * 1024
 
 
 epsilon = 1e-05
@@ -153,7 +154,7 @@
     return lax.all_gather(shard, "dev", axis=0, tiled=False, axis_index_groups=z_groups(devices))
 
 
-def place_blocks(pieces, held):
+def place_blocks(pieces):
     block = (lax.axis_index("dev") & 7).astype(jnp.int32).reshape(1)
     arrays = [piece[0] for piece in pieces]
     rows, width = arrays[0].shape[1:]
@@ -161,7 +162,7 @@
 
     def body(block_ref, *refs):
         piece_refs = refs[: len(arrays)]
-        three_ref, last_ref, sems = refs[-3:]
+        three_ref, last_ref, sems = refs[len(arrays) :]
         copies = []
         for ref, (array, mask, begin) in zip(piece_refs, pieces):
             target = block_ref[0] ^ mask
@@ -175,7 +176,6 @@
         for copy in copies:
             copy.wait()
 
-    anywhere = pl.BlockSpec(memory_space=pl.ANY)
     kind = arrays[0].dtype
     return pl.pallas_call(
         body,
@@ -184,14 +184,14 @@
             jax.ShapeDtypeStruct((8, rows, width), kind),
         ),
         in_specs=[pl.BlockSpec(memory_space=pltpu.SMEM)]
-        + [anywhere] * (len(arrays) + len(held)),
-        out_specs=(anywhere, anywhere),
+        + [pl.BlockSpec(memory_space=pl.ANY)] * len(arrays),
+        out_specs=(pl.BlockSpec(memory_space=pltpu.VMEM), pl.BlockSpec(memory_space=pltpu.VMEM)),
         scratch_shapes=[pltpu.SemaphoreType.DMA((count,))],
-        input_output_aliases={1 + len(arrays) + number: number for number in range(len(held))},
+        compiler_params=pltpu.CompilerParams(vmem_limit_bytes=VMEM_LIMIT),
         cost_estimate=pl.CostEstimate(
             flops=0, bytes_accessed=4 * count * rows * width, transcendentals=0
         ),
-    )(block, *arrays, *held)
+    )(block, *arrays)
 
 
 def gather_attn(shard):
@@ -206,9 +206,8 @@
     upper, lower = swap(along[:2], 2), swap(across[2:], 4)
     pieces = [(own, 0, 0), (beside, 1, 0), (along, 4, 0), (across, 2, 0)]
     pieces += [(swap(along, 1), 5, 0), (swap(across, 1), 3, 0)]
-    held = place_blocks(pieces, ())
-    pieces = [(upper, 6, 0), (lower, 6, 2), (swap(upper, 1), 7, 0), (swap(lower, 1), 7, 2)]
-    three, last = place_blocks(pieces, held)
+    pieces += [(upper, 6, 0), (lower, 6, 2), (swap(upper, 1), 7, 0), (swap(lower, 1), 7, 2)]
+    three, last = place_blocks(pieces)
     width = shard.shape[1]
     return (three.reshape(3 * width, width), last.reshape(width, width), (upper, lower))
 
@@ -226,46 +225,63 @@
             ],
             axis=0,
         ).astype(low)
-        return lax.psum_scatter(product, "dev", scatter_dimension=0, tiled=True).astype(jnp.float32)
-    here = lax.axis_index("dev")
-    block = here & 7
-    grads = grads.reshape(4, 8, -1, own)
-    rows = grads.shape[2]
-    order = (6, 2, 4, 0)
-    mine = jnp.stack([lax.dynamic_index_in_dim(grads, block ^ mask, 1, False) for mask in order])
-    yours = jnp.stack(
-        [lax.dynamic_index_in_dim(grads, block ^ mask ^ 1, 1, False) for mask in order]
-    )
-    both = jnp.concatenate([mine, swap(yours, 1)], axis=-1)
-    first = jnp.concatenate(first, axis=0)
-    mixed = jnp.concatenate(mixed, axis=0)
-
-    def upper_part(place):
-        left = both[place, :2].reshape(2 * rows, 2 * own)
-        return jnp.dot(left, first, preferred_element_type=jnp.float32)
-
-    def lower_part(place):
-        return jnp.concatenate(
-            [
-                jnp.dot(both[place, 2], first, preferred_element_type=jnp.float32),
-                jnp.dot(both[place, 3], mixed, preferred_element_type=jnp.float32),
-            ],
-            axis=0,
-        )
-
-    def wide(value):
-        return value.astype(jnp.float32)
-
-    across_diagonal = swap(upper_part(0).astype(low), 2)
-    along_diagonal = swap(lower_part(0).astype(low), 4)
-    across_upper = swap(upper_part(1).astype(low), 2)
-    along_lower = swap(lower_part(2).astype(low), 4)
-    across_lower = swap((lower_part(1) + wide(along_diagonal)).astype(low), 2)
-    along_upper = swap((upper_part(2) + wide(across_diagonal)).astype(low), 4)
-    upper = upper_part(3) + wide(across_upper) + wide(along_upper)
-    lower = lower_part(3) + wide(across_lower) + wide(along_lower)
-    total = jnp.concatenate([upper, lower], axis=0).reshape(4, rows, width)
-    return scatter_z(total, here >> 3)
+        share = lax.psum_scatter(product, "dev", scatter_dimension=0, tiled=True)
+        return (lambda: share.astype(jnp.float32), grads)
+    pairs = (jnp.stack([first[0], mixed[0]]), jnp.stack([first[1], mixed[1]]))
+    blocks = grads.reshape(4, 8, -1, own)
+    diagonal, across, along, mine = attn_products(blocks, swap(blocks, 1), pairs)
+
+    across_upper = swap(across[0], 2)
+    along_lower = swap(along[1], 4)
+    along_diagonal = swap(diagonal[1], 4).astype(jnp.float32)
+    across_diagonal = swap(diagonal[0], 2).astype(jnp.float32)
+    across_lower = swap((across[1] + along_diagonal).astype(low), 2)
+    along_upper = swap((along[0] + across_diagonal).astype(low), 4)
+
+    def finish():
+        return scatter_z(mine, ((across_upper, along_upper), (across_lower, along_lower)))
+
+    return (finish, (across[1], along[0]))
+
+
+def attn_products(mine, beside, pairs):
+    block = (lax.axis_index("dev") & 7).astype(jnp.int32).reshape(1)
+    rows = mine.shape[2]
+    width = pairs[0].shape[2]
+    low, wide = jnp.bfloat16, jnp.float32
+    kinds = (low, low, low, wide, wide, low, wide, wide)
+
+    def body(block_ref, mine_ref, beside_ref, pair_ref, other_ref, *outs):
+        for place, mask in enumerate((6, 2, 4, 0)):
+            target = block_ref[0] ^ mask
+            for half in range(2):
+                out = outs[2 * place + half]
+
+                @pl.loop(0, 2)
+                def _(number):
+                    side = number if half else 0
+                    matrix = 2 * half + number
+                    value = jnp.dot(
+                        mine_ref[matrix, target], pair_ref[side], preferred_element_type=wide
+                    ) + jnp.dot(
+                        beside_ref[matrix, target], other_ref[side], preferred_element_type=wide
+                    )
+                    out[number] = value.astype(out.dtype)
+
+    vmem = pl.BlockSpec(memory_space=pltpu.VMEM)
+    outs = pl.pallas_call(
+        body,
+        out_shape=[jax.ShapeDtypeStruct((2, rows, width), kind) for kind in kinds],
+        in_specs=[pl.BlockSpec(memory_space=pltpu.SMEM)] + [vmem] * 4,
+        out_specs=[vmem] * 8,
+        compiler_params=pltpu.CompilerParams(vmem_limit_bytes=VMEM_LIMIT),
+        cost_estimate=pl.CostEstimate(
+            flops=64 * rows * mine.shape[3] * width,
+            bytes_accessed=30 * 1024 * 1024,
+            transcendentals=0,
+        ),
+    )(block, mine, beside, *pairs)
+    return [outs[2 * place : 2 * place + 2] for place in range(4)]
 
 
 def gather_hidden(shard, near_ready):
@@ -281,22 +297,29 @@
     return ((one, swap(one, 4)), two)
 
 
+def pick_blocks(bias, blocks, start, stop):
+    picked = lax.dynamic_index_in_dim(bias, blocks, 1, False)
+    return picked[:, start:stop].reshape(-1)
+
+
+def put_blocks(bias, blocks, start, stop, values):
+    values = values.reshape(bias.shape[0], 1, stop - start)
+    return lax.dynamic_update_slice(bias, values, (0, blocks, start))
+
+
 def hidden_parts(gathered, here, devices, ready):
-    half = devices // 2
     one, two = gathered
     if devices != 32:
         rows = one.shape[0] // 2
-        blocks = jnp.arange(half // 4, dtype=jnp.int32) * 4 + (here & 3)
-        return [(one[:rows], one[rows:], blocks, 0, rows // (half // 4))]
+        return [(one[:rows], one[rows:], here & 3, 0, rows // (devices // 8))]
     two = after(two, ready)
-    blocks = jnp.stack([here & 7, (here & 7) + 8])
     parts = []
-    for pieces, numbers in (((one[0], two), blocks), ((one[1], swap(two, 4)), blocks ^ 4)):
+    for pieces, number in (((one[0], two), here & 7), ((one[1], swap(two, 4)), (here & 7) ^ 4)):
         start = 0
         for piece in pieces:
             rows, width = piece.shape[1:]
             up, down = piece[:2].reshape(2 * rows, width), piece[2:].reshape(2 * rows, width)
-            parts.append((up, down, numbers, start, start + rows))
+            parts.append((up, down, number, start, start + rows))
             start += rows
     return parts
 
@@ -309,25 +332,60 @@
         return lax.psum_scatter(
             both, "dev", scatter_dimension=0, tiled=True, axis_index_groups=same_low(devices)
         ).astype(jnp.float32)
-    layer = lax.axis_index("dev") >> 3
     moved = [[swap(part.astype(low), 4) for part in pair] for pair in grads[2:]]
     shares = []
     for own, other in zip(grads[:2], moved):
         other = after(other, others)
-        total = jnp.concatenate(
-            [mine + part.astype(jnp.float32) for mine, part in zip(own, other)], axis=0
-        )
-        shares.append(scatter_z(total.reshape(4, -1, total.shape[1]), layer))
+        rows = own[0].shape[0] // 2
+        own = [part.reshape(2, rows, -1) for part in own]
+        other = [(part.reshape(2, rows, -1),) for part in other]
+        shares.append(scatter_z(own, other))
     return jnp.concatenate(shares, axis=0)
 
 
-def scatter_z(total, layer):
-    low = jnp.bfloat16
-    result = lax.dynamic_index_in_dim(total, layer, 0, False)
-    for mask in (1, 2, 3):
-        part = lax.dynamic_index_in_dim(total, layer ^ mask, 0, False).astype(low)
-        result = result + swap(part, 8 * mask).astype(jnp.float32)
-    return result
+def scatter_z(own, others):
+    mine, one, two, three = route_z(own, others)
+    wide = jnp.float32
+    return (
+        mine
+        + swap(two, 16).astype(wide)
+        + swap(three, 24).astype(wide)
+        + swap(one, 8).astype(wide)
+    )
+
+
+def route_z(own, others):
+    layer = (lax.axis_index("dev") >> 3).astype(jnp.int32).reshape(1)
+    rows, width = own[0].shape[1:]
+    count = len(others[0])
+
+    def body(layer_ref, *refs):
+        outs = refs[-4:]
+        for mask, out in enumerate(outs):
+            goal = layer_ref[0] ^ mask
+            number = goal & 1
+            for half in range(2):
+                sources = refs[half * (count + 1) : (half + 1) * (count + 1)]
+
+                @pl.when((goal >> 1) == half)
+                def _():
+                    total = sources[0][number]
+                    for source in sources[1:]:
+                        total = total + source[number].astype(jnp.float32)
+                    out[...] = total.astype(out.dtype)
+
+    vmem = pl.BlockSpec(memory_space=pltpu.VMEM)
+    kinds = (jnp.float32, jnp.bfloat16, jnp.bfloat16, jnp.bfloat16)
+    return pl.pallas_call(
+        body,
+        out_shape=[jax.ShapeDtypeStruct((rows, width), kind) for kind in kinds],
+        in_specs=[pl.BlockSpec(memory_space=pltpu.SMEM)] + [vmem] * (2 * count + 2),
+        out_specs=[vmem] * 4,
+        compiler_params=pltpu.CompilerParams(vmem_limit_bytes=VMEM_LIMIT),
+        cost_estimate=pl.CostEstimate(
+            flops=4 * rows * width, bytes_accessed=30 * rows * width, transcendentals=0
+        ),
+    )(layer, own[0], *others[0], own[1], *others[1])
 
 
 def shards(
@@ -365,7 +423,8 @@
         down_bias,
         up_bias,
     ) = split_vectors(full_vec)
-    up_bias = up_bias.reshape(devices // 2, -1)
+    low_count = 8 if devices == 32 else 4
+    up_bias = up_bias.reshape(devices // 2 // low_count, low_count, -1)
 
     inputs = tokens.astype(jnp.float32)
     first_out, normed_one, factor_one = normalize(inputs, gain_one, shift_one)
@@ -395,7 +454,7 @@
     kept = []
     grad_up_bias = jnp.zeros_like(up_bias)
     for up_weight, down_weight, blocks, start, stop in parts:
-        bias = up_bias[:, start:stop][blocks].reshape(-1)
+        bias = pick_blocks(up_bias, blocks, start, stop)
         up_sum = (
             jnp.einsum("rd,fd->rf", second_low, up_weight, preferred_element_type=jnp.float32)
             + bias
@@ -406,9 +465,7 @@
         )
         grad_up = (grad_act * slope).astype(low)
         column_sums = jnp.sum(grad_up.astype(jnp.float32), axis=0)
-        grad_up_bias = grad_up_bias.at[blocks, start:stop].set(
-            column_sums.reshape(blocks.shape[0], -1)
-        )
+        grad_up_bias = put_blocks(grad_up_bias, blocks, start, stop, column_sums)
         kept.append((activated.astype(low), grad_up))
     grad_second, far = reduce_near([pair[1] for pair in kept], [part[0] for part in parts])
     grad_second = grad_second + swap(far, 2).astype(jnp.float32)
@@ -443,11 +500,13 @@
         ],
         axis=0,
     )
-    attn_share = scatter_attn(
+    attn_finish, attn_sent = scatter_attn(
         grad_features, ((first_low, first_beside), (mixed_low, mixed_beside))
     )
-    mlp_share = scatter_hidden(grads, grad_features)
-    down_far = after(swap(down_far, 2), grad_features).astype(jnp.float32)
+    mlp_share = scatter_hidden(grads, attn_sent)
+    attn_share = attn_finish()
+    grad_features = after(grad_features, attn_sent)
+    down_far = after(swap(down_far, 2), attn_sent).astype(jnp.float32)
     output = jnp.where(live, middle + (down + down_far + down_bias), 0.0).astype(low)
     grad_projected = grad_features[: 3 * width]
     grad_columns = jnp.sum(grad_projected.astype(jnp.float32), axis=1)

time: 822 us -> 430 us (0.52)
  Pallas kernels: 306 us -> 14.9 us
  waiting for transfers between devices: 182 us -> 114 us
  other arithmetic: 75.2 us -> 30 us
    pallas_call x2 -> x1, Pallas kernels: 306 us -> 3.47 us  [place_blocks(): pl.pallas_call(body, out_shape=(jax.ShapeDtypeStruct((3, 8, rows, width),...]
    ppermute x53, waiting for transfers between devices: 159 us -> 113 us  [swap(): lax.ppermute(piece, 'dev', [(number, number ^ mask) for number in range(d...]
    scatter x16 -> x0, other arithmetic: 44 us -> none
    scatter x24 -> x0, local copies, waits for them, and re-layouts: 29 us -> none
    ppermute x0 -> x11, local copies, waits for them, and re-layouts: none -> 23.4 us  [swap(): lax.ppermute(piece, 'dev', [(number, number ^ mask) for number in range(d...]
    all_gather x3, waiting for transfers between devices: 21.9 us -> 0.01 us  [gather_z(): lax.all_gather(shard, 'dev', axis=0, tiled=False, axis_index_groups=z_gro...]
    dot_general x24, matrix products: 31.4 us -> 48.8 us  [row_products(): jnp.dot(left[start:stop], right, preferred_element_type=jnp.float32)]
    pallas_call x0 -> x4, Pallas kernels: none -> 11.4 us  [the longest x1 7.98 us: attn_products(): pl.pallas_call(body, out_shape=[jax.ShapeDtypeStruct((2, rows, width), ki...]
  transfers between devices with their start and end apart: 56 -> 56, of which waited for: 17 -> 18; matrix products, arithmetic and copies ran while one was open for 30% -> 43% of each run, Pallas kernels for 38% -> 4%
where the time goes in v4:
time: 430 us; the launch traced here: 423 us
  waiting for transfers between devices  114 us (27%)
  matrix products  108 us (25%)
  local copies, waits for them, and re-layouts  89.7 us (21%)
  starting transfers between devices  49.6 us (12%)
  other arithmetic  30 us (7%)
  between operations  17.2 us (4%)
  Pallas kernels  14.9 us (3%)
    ppermute x53, waiting for transfers between devices, swap(): lax.ppermute(piece, 'dev', [(number, number ^ mask) for number in range(d...  113 us
    ppermute x53, starting transfers between devices, swap(): lax.ppermute(piece, 'dev', [(number, number ^ mask) for number in range(d...  49.5 us
    dot_general x24, matrix products, row_products(): jnp.dot(left[start:stop], right, preferred_element_type=jnp.float32)  48.8 us
    ppermute x11, local copies, waits for them, and re-layouts, swap(): lax.ppermute(piece, 'dev', [(number, number ^ mask) for number in range(d...  23.4 us
    unnamed x291, local copies, waits for them, and re-layouts  20.7 us
    dot_general x4, matrix products, shards(): jnp.einsum('rd,fd->rf', grad_down_rows, down_weight, preferred_element_ty...  16.4 us
    dot_general x1, matrix products, shards(): jnp.einsum('fr,fd->rd', grad_projected, full_proj, preferred_element_type...  9.41 us
    dot_general x4, matrix products, shards(): jnp.einsum('rd,fd->rf', second_low, up_weight, preferred_element_type=jnp...  8.94 us
  transfers between devices with their start and end apart: 56, of which 18 were waited for; matrix products, arithmetic and copies ran while one was open for 43% of the time, Pallas kernels for 4%

profile of v4, /device:TPU:8, one launch (start us, length us, event | category | flops | bytes accessed | tf_op | source)
XLA Modules:
  0.0 423.1 jit_solution(8538093536471080373)
XLA Ops:
  19.8 10.7 %collective-permute-done.1 = bf16[816]{0:T(1024)(128)(2,1)S(1)} collective-permute-done((bf16[816]{0:T(1024)(128)(2,1)S(1)}, bf16[816]{0:T(1024)(128)(2,1)S(1)}, u32[]{:S(2)}, u32[]{:S(2)}) %collective-permute-start.1) | collective-permute-done | bytes 1664 | tf_op jit(solution)/shard_map/ppermute | solution.py:114
  34.9 3.3 collective-permute-done.3
  38.3 3.1 collective-permute-start.4
  50.9 20.6 %collective-permute-done.6.refs_2_ = bf16[4,136,1088]{2,1,0:T(8,128)(2,1)S(1)} collective-permute-done((bf16[4,136,1088]{2,1,0:T(8,128)(2,1)}, bf16[4,136,1088]{2,1,0:T(8,128)(2,1)S(1)}, u32[]{:S(2)}, u32[]{:S(2)}) %collective-permute-start.6) | collective-permute-done | bytes 1183776 | tf_op jit(solution)/shard_map/ppermute | solution.py:114
  77.6 8.5 %collective-permute-done.10.refs_6_ = bf16[2,136,1088]{2,1,0:T(8,128)(2,1)S(1)} collective-permute-done((bf16[2,136,1088]{2,1,0:T(8,128)(2,1)S(1)}, bf16[2,136,1088]{2,1,0:T(8,128)(2,1)S(1)}, u32[]{:S(2)}, u32[]{:S(2)}) %collective-permute-start.10) | collective-permute-done | bytes 591904 | tf_op jit(solution)/shard_map/ppermute | solution.py:114
  101.8 3.5 shard_map.119
  123.7 7.0 %collective-permute-done.14 = bf16[256,1088]{0,1:T(8,128)(2,1)} collective-permute-done((bf16[256,1088]{0,1:T(8,128)(2,1)}, bf16[256,1088]{0,1:T(8,128)(2,1)}, u32[]{:S(2)}, u32[]{:S(2)}) %collective-permute-start.14) | collective-permute-done | bytes 557088 | tf_op jit(solution)/shard_map/ppermute | solution.py:114
  146.4 3.6 multiply_convert_fusion.2
  151.8 5.0 %convert_reduce_fusion.5 = (f32[288]{0:T(512)S(1)}, bf16[1024,288]{0,1:T(8,128)(2,1)}) fusion(f32[1024,288]{0,1:T(8,128)S(1)} %get-tuple-element.158, bf16[288,1088]{1,0:T(8,128)(2,1)S(1)} %bitcast.122, bf16[256,1088]{1,0:T(8,128)(2,1)S(1)} %copy-done.93, bf16[256,1088]{1,0:T(8,128)(2,1)S(1)} %copy-done.88, bf16[256,1088]{1,0:T(8,128)(2,1)S(1)} %copy-done.83, ...), kind=kOutput, calls=%fused_computation.111 | convolution fusion | flops 654180096 | bytes 4625536 | tf_op jit(solution)/shard_map/rd,fd->rf/dot_general | solution.py:463
  156.8 3.7 convert_reduce_fusion.7
  162.3 3.7 convert_reduce_fusion.6
  176.4 3.9 convert_reduce_fusion.4
  186.7 2.7 fusion.84
  204.2 3.2 fusion.75
  229.8 3.7 multiply_reduce_fusion.1
  242.5 3.5 concatenate.37
  246.0 3.1 copy.260
  249.3 4.0 fusion.4
  256.2 2.7 copy.244
  259.0 3.2 convolution_add_fusion.9
  282.1 8.0 %shard_map.120 = (bf16[2,136,1088]{2,1,0:T(8,128)(2,1)S(1)}, bf16[2,136,1088]{2,1,0:T(8,128)(2,1)S(1)}, bf16[2,136,1088]{2,1,0:T(8,128)(2,1)S(1)}, f32[2,136,108...) custom-call(s32[1]{0:T(128)} %bitcast.block_ref, ...), custom_call_target="tpu_custom_call" | custom-call | flops 2424307712 | bytes 31457280 | tf_op jit(solution)/shard_map/pallas_call | solution.py:272
  291.1 9.4 %fusion.122 = (f32[1088]{0:T(1024)S(1)}, f32[256,1088]{0,1:T(8,128)}) fusion(bf16[3264,1088]{1,0:T(8,128)(2,1)} %bitcast.119, bf16[4352,256]{0,1:T(8,128)(2,1)S(1)} %copy-done.33), kind=kOutput, calls=%fused_computation.250 | convolution fusion | flops 1818508288 | bytes 9924864 | tf_op jit(solution)/shard_map/fr,fd->rd/dot_general | solution.py:513
  311.5 2.8 collective-permute-start.40
  315.5 6.9 %collective-permute-done.49 = f32[3264]{0:T(1024)S(1)} collective-permute-done((f32[3264]{0:T(1024)S(1)}, f32[3264]{0:T(1024)S(1)}, u32[]{:S(2)}, u32[]{:S(2)}) %collective-permute-start.49) | collective-permute-done | bytes 13088 | tf_op jit(solution)/shard_map/ppermute | solution.py:114
  330.0 3.9 fusion.21
  345.0 13.5 %collective-permute-done.30 = bf16[2,136,1088]{2,1,0:T(8,128)(2,1)S(1)} collective-permute-done((bf16[2,136,1088]{2,1,0:T(8,128)(2,1)S(1)}, bf16[2,136,1088]{2,1,0:T(8,128)(2,1)S(1)}, u32[]{:S(2)}, u32[]{:S(2)}) %collective-permute-start.30) | collective-permute-done | bytes 591904 | tf_op jit(solution)/shard_map/ppermute | solution.py:114
  362.2 3.1 collective-permute-start.45
  365.3 6.6 %collective-permute-done.29.refs_1_ = bf16[2,136,1088]{2,1,0:T(8,128)(2,1)S(1)} collective-permute-done((bf16[2,136,1088]{2,1,0:T(8,128)(2,1)S(1)}, bf16[2,136,1088]{2,1,0:T(8,128)(2,1)S(1)}, u32[]{:S(2)}, u32[]{:S(2)}) %collective-permute-start.29) | collective-permute-done | bytes 591904 | tf_op jit(solution)/shard_map/ppermute | solution.py:114
  377.1 4.5 %collective-permute-done.33.refs_4_ = bf16[2,136,1088]{2,1,0:T(8,128)(2,1)S(1)} collective-permute-done((bf16[2,136,1088]{2,1,0:T(8,128)(2,1)S(1)}, bf16[2,136,1088]{2,1,0:T(8,128)(2,1)S(1)}, u32[]{:S(2)}, u32[]{:S(2)}) %collective-permute-start.33) | collective-permute-done | bytes 591904 | tf_op jit(solution)/shard_map/ppermute | solution.py:114
  388.7 16.6 %collective-permute-done.46 = bf16[144,1088]{1,0:T(8,128)(2,1)S(1)} collective-permute-done((bf16[144,1088]{1,0:T(8,128)(2,1)S(1)}, bf16[144,1088]{1,0:T(8,128)(2,1)S(1)}, u32[]{:S(2)}, u32[]{:S(2)}) %collective-permute-start.46) | collective-permute-done | bytes 313376 | tf_op jit(solution)/shard_map/ppermute | solution.py:114
  406.5 4.4 %collective-permute-done.35 = bf16[136,1088]{1,0:T(8,128)(2,1)S(1)} collective-permute-done((bf16[136,1088]{1,0:T(8,128)(2,1)S(1)}, bf16[136,1088]{1,0:T(8,128)(2,1)S(1)}, u32[]{:S(2)}, u32[]{:S(2)}) %collective-permute-start.35) | collective-permute-done | bytes 295968 | tf_op jit(solution)/shard_map/ppermute | solution.py:114
  410.9 4.2 collective-permute-done.36
  (546 shorter events, 219.4 us)
Async XLA Ops:
  7.2 36.0 %all-gather.7.cloned.1.call-start = ((), (), s32[]{:S(2)}) async-start(), calls=%async_computation | async-start | bytes 1566720 | tf_op jit(solution)/shard_map/all_gather | solution.py:154
  8.0 87.5 %all-gather.9.cloned.1.call-start = ((), (), s32[]{:S(2)}) async-start(), calls=%async_computation.1 | async-start | bytes 1474560 | tf_op jit(solution)/shard_map/all_gather | solution.py:154
  9.8 106.6 %all-gather.11.cloned.1.call-start = ((), (), s32[]{:S(2)}) async-start(), calls=%async_computation.2 | async-start | bytes 1658880 | tf_op jit(solution)/shard_map/all_gather | solution.py:154
  15.7 34.6 %collective-permute-start.17 = (bf16[256,1088]{0,1:T(8,128)(2,1)}, bf16[256,1088]{0,1:T(8,128)(2,1)}, u32[]{:S(2)}, u32[]{:S(2)}) collective-permute-start(bf16[256,1088]{0,1:T(8,128)(2,1)} %copy.226), channel_id=1, source_target_pairs={{0,2},{1,3},{2,0},{3,1},{4,6},{5,7},{6,4},{7,5},{8,10},{9,11},{10,... | collective-permute-start | bytes 1671176 | tf_op jit(solution)/shard_map/ppermute | solution.py:114
  17.2 57.5 %collective-permute-start.18 = (bf16[256,1088]{0,1:T(8,128)(2,1)}, bf16[256,1088]{0,1:T(8,128)(2,1)}, u32[]{:S(2)}, u32[]{:S(2)}) collective-permute-start(bf16[256,1088]{0,1:T(8,128)(2,1)} %copy.226), channel_id=1, source_target_pairs={{0,1},{1,0},{2,3},{3,2},{4,5},{5,4},{6,7},{7,6},{8,9},{9,8},{10,11... | collective-permute-start | bytes 1671176 | tf_op jit(solution)/shard_map/ppermute | solution.py:114
  43.2 28.3 %collective-permute-start.6 = (bf16[4,136,1088]{2,1,0:T(8,128)(2,1)}, bf16[4,136,1088]{2,1,0:T(8,128)(2,1)S(1)}, u32[]{:S(2)}, u32[]{:S(2)}) collective-permute-start(bf16[4,136,1088]{2,1,0:T(8,128)(2,1)} %bitcast.1.refs_0_), channel_id=1, source_target_pairs={{0,4},{1,5},{2,6},{3,7},{4,0},{5,1},{6,2},{7,3},{8,12},{9,13},{10,... | collective-permute-start | bytes 3551240 | tf_op jit(solution)/shard_map/ppermute | solution.py:114
  44.8 28.6 %collective-permute-start.7 = (bf16[4,136,1088]{2,1,0:T(8,128)(2,1)}, bf16[4,136,1088]{2,1,0:T(8,128)(2,1)S(1)}, u32[]{:S(2)}, u32[]{:S(2)}) collective-permute-start(bf16[4,136,1088]{2,1,0:T(8,128)(2,1)} %bitcast.1.refs_0_), channel_id=1, source_target_pairs={{0,2},{1,3},{2,0},{3,1},{4,6},{5,7},{6,4},{7,5},{8,10},{9,11},{10,... | collective-permute-start | bytes 3551240 | tf_op jit(solution)/shard_map/ppermute | solution.py:114
  50.3 24.4 %collective-permute-start.27 = (bf16[256,1088]{0,1:T(8,128)(2,1)}, bf16[256,1088]{0,1:T(8,128)(2,1)S(1)}, u32[]{:S(2)}, u32[]{:S(2)}) collective-permute-start(bf16[256,1088]{0,1:T(8,128)(2,1)} %copy.262), channel_id=1, source_target_pairs={{0,1},{1,0},{2,3},{3,2},{4,5},{5,4},{6,7},{7,6},{8,9},{9,8},{10,11... | collective-permute-start | bytes 1671176 | tf_op jit(solution)/shard_map/ppermute | solution.py:114
  50.4 24.9 %collective-permute-start.19 = (bf16[256,1088]{0,1:T(8,128)(2,1)}, bf16[256,1088]{0,1:T(8,128)(2,1)S(1)}, u32[]{:S(2)}, u32[]{:S(2)}) collective-permute-start(bf16[256,1088]{0,1:T(8,128)(2,1)} %collective-permute-done.17), channel_id=1, source_target_pairs={{0,1},{1,0},{2,3},{3,2},{4,5},{5,4},{6,7},{7,6},{8,9},{9,8},{10,11... | collective-permute-start | bytes 1671176 | tf_op jit(solution)/shard_map/ppermute | solution.py:114
  74.7 25.7 %collective-permute-start.5 = (bf16[4,136,1088]{2,1,0:T(8,128)(2,1)}, bf16[4,136,1088]{2,1,0:T(8,128)(2,1)}, u32[]{:S(2)}, u32[]{:S(2)}) collective-permute-start(bf16[4,136,1088]{2,1,0:T(8,128)(2,1)} %bitcast.1.refs_0_), channel_id=1, source_target_pairs={{0,1},{1,0},{2,3},{3,2},{4,5},{5,4},{6,7},{7,6},{8,9},{9,8},{10,11... | collective-permute-start | bytes 3551240 | tf_op jit(solution)/shard_map/ppermute | solution.py:114
  74.7 27.0 %collective-permute-start.8 = (bf16[4,136,1088]{2,1,0:T(8,128)(2,1)S(1)}, bf16[4,136,1088]{2,1,0:T(8,128)(2,1)}, u32[]{:S(2)}, u32[]{:S(2)}) collective-permute-start(bf16[4,136,1088]{2,1,0:T(8,128)(2,1)S(1)} %collective-permute-done.6.refs_2_), channel_id=1, source_target_pairs={{0,1},{1,0},{2,3},{3,2},{4,5},{5,4},{6,7},{7,6},{8,9},{9,8},{10,11... | collective-permute-start | bytes 3551240 | tf_op jit(solution)/shard_map/ppermute | solution.py:114
  75.2 26.5 %collective-permute-start.9 = (bf16[4,136,1088]{2,1,0:T(8,128)(2,1)S(1)}, bf16[4,136,1088]{2,1,0:T(8,128)(2,1)}, u32[]{:S(2)}, u32[]{:S(2)}) collective-permute-start(bf16[4,136,1088]{2,1,0:T(8,128)(2,1)S(1)} %collective-permute-done.7.refs_3_), channel_id=1, source_target_pairs={{0,1},{1,0},{2,3},{3,2},{4,5},{5,4},{6,7},{7,6},{8,9},{9,8},{10,11... | collective-permute-start | bytes 3551240 | tf_op jit(solution)/shard_map/ppermute | solution.py:114
  100.4 30.3 %collective-permute-start.20 = (bf16[4,128,1088]{1,2,0:T(8,128)(2,1)}, bf16[4,128,1088]{1,2,0:T(8,128)(2,1)}, u32[]{:S(2)}, u32[]{:S(2)}) collective-permute-start(bf16[4,128,1088]{1,2,0:T(8,128)(2,1)} %copy.231), channel_id=1, source_target_pairs={{0,4},{1,5},{2,6},{3,7},{4,0},{5,1},{6,2},{7,3},{8,12},{9,13},{10,... | collective-permute-start | bytes 3342344 | tf_op jit(solution)/shard_map/ppermute | solution.py:114
  116.3 21.3 %collective-permute-start.15 = (bf16[256,1088]{0,1:T(8,128)(2,1)}, bf16[256,1088]{0,1:T(8,128)(2,1)}, u32[]{:S(2)}, u32[]{:S(2)}) collective-permute-start(bf16[256,1088]{0,1:T(8,128)(2,1)} %copy.220), channel_id=1, source_target_pairs={{0,1},{1,0},{2,3},{3,2},{4,5},{5,4},{6,7},{7,6},{8,9},{9,8},{10,11... | collective-permute-start | bytes 1671176 | tf_op jit(solution)/shard_map/ppermute | solution.py:114
  117.7 54.8 %collective-permute-start.21 = (bf16[4,144,1088]{2,1,0:T(8,128)(2,1)}, bf16[4,144,1088]{2,1,0:T(8,128)(2,1)}, u32[]{:S(2)}, u32[]{:S(2)}) collective-permute-start(bf16[4,144,1088]{2,1,0:T(8,128)(2,1)} %bitcast.13), channel_id=1, source_target_pairs={{0,4},{1,5},{2,6},{3,7},{4,0},{5,1},{6,2},{7,3},{8,12},{9,13},{10,... | collective-permute-start | bytes 3760136 | tf_op jit(solution)/shard_map/ppermute | solution.py:114
  215.8 89.0 %collective-permute-start.38 = (bf16[256,1088]{0,1:T(8,128)(2,1)}, bf16[256,1088]{0,1:T(8,128)(2,1)}, u32[]{:S(2)}, u32[]{:S(2)}) collective-permute-start(bf16[256,1088]{0,1:T(8,128)(2,1)} %convolution_convert_fusion.3), channel_id=1, source_target_pairs={{0,4},{1,5},{2,6},{3,7},{4,0},{5,1},{6,2},{7,3},{8,12},{9,13},{10,... | collective-permute-start | bytes 1671176 | tf_op jit(solution)/shard_map/ppermute | solution.py:114
  218.6 86.4 %collective-permute-start.39 = (bf16[256,1088]{0,1:T(8,128)(2,1)}, bf16[256,1088]{0,1:T(8,128)(2,1)}, u32[]{:S(2)}, u32[]{:S(2)}) collective-permute-start(bf16[256,1088]{0,1:T(8,128)(2,1)} %convolution_convert_fusion.2), channel_id=1, source_target_pairs={{0,4},{1,5},{2,6},{3,7},{4,0},{5,1},{6,2},{7,3},{8,12},{9,13},{10,... | collective-permute-start | bytes 1671176 | tf_op jit(solution)/shard_map/ppermute | solution.py:114
  221.5 112.3 %collective-permute-start.43 = (bf16[288,1088]{1,0:T(8,128)(2,1)}, bf16[288,1088]{1,0:T(8,128)(2,1)}, u32[]{:S(2)}, u32[]{:S(2)}) collective-permute-start(bf16[288,1088]{1,0:T(8,128)(2,1)} %convolution_convert_fusion.1), channel_id=1, source_target_pairs={{0,4},{1,5},{2,6},{3,7},{4,0},{5,1},{6,2},{7,3},{8,12},{9,13},{10,... | collective-permute-start | bytes 1880072 | tf_op jit(solution)/shard_map/ppermute | solution.py:114
  249.2 29.0 %collective-permute-start.26 = (bf16[4,8,136,256]{3,2,1,0:T(8,128)(2,1)S(1)}, bf16[4,8,136,256]{3,2,1,0:T(8,128)(2,1)}, u32[]{:S(2)}, u32[]{:S(2)}) collective-permute-start(bf16[4,8,136,256]{3,2,1,0:T(8,128)(2,1)S(1)} %bitcast.112), channel_id=1, source_target_pairs={{0,1},{1,0},{2,3},{3,2},{4,5},{5,4},{6,7},{7,6},{8,9},{9,8},{10,11... | collective-permute-start | bytes 6684680 | tf_op jit(solution)/shard_map/ppermute | solution.py:114
  267.5 66.9 %collective-permute-start.44 = (bf16[288,1088]{1,0:T(8,128)(2,1)}, bf16[288,1088]{1,0:T(8,128)(2,1)}, u32[]{:S(2)}, u32[]{:S(2)}) collective-permute-start(bf16[288,1088]{1,0:T(8,128)(2,1)} %convolution_convert_fusion), channel_id=1, source_target_pairs={{0,4},{1,5},{2,6},{3,7},{4,0},{5,1},{6,2},{7,3},{8,12},{9,13},{10,... | collective-permute-start | bytes 1880072 | tf_op jit(solution)/shard_map/ppermute | solution.py:114
  278.2 47.5 %collective-permute-start.24 = (bf16[256,1088]{0,1:T(8,128)(2,1)}, bf16[256,1088]{0,1:T(8,128)(2,1)}, u32[]{:S(2)}, u32[]{:S(2)}) collective-permute-start(bf16[256,1088]{0,1:T(8,128)(2,1)} %copy.247), channel_id=1, source_target_pairs={{0,2},{1,3},{2,0},{3,1},{4,6},{5,7},{6,4},{7,5},{8,10},{9,11},{10,... | collective-permute-start | bytes 1671176 | tf_op jit(solution)/shard_map/ppermute | solution.py:114
  311.5 48.6 %collective-permute-start.40 = (bf16[128,1088]{1,0:T(8,128)(2,1)}, bf16[128,1088]{1,0:T(8,128)(2,1)}, u32[]{:S(2)}, u32[]{:S(2)}) collective-permute-start(bf16[128,1088]{1,0:T(8,128)(2,1)} %get-tuple-element.70), channel_id=1, source_target_pairs={{0,16},{1,17},{2,18},{3,19},{4,20},{5,21},{6,22},{7,23},{8,24},{9,... | collective-permute-start | bytes 835592 | tf_op jit(solution)/shard_map/ppermute | solution.py:114
  333.8 26.9 %collective-permute-start.41 = (bf16[128,1088]{1,0:T(8,128)(2,1)}, bf16[128,1088]{1,0:T(8,128)(2,1)}, u32[]{:S(2)}, u32[]{:S(2)}) collective-permute-start(bf16[128,1088]{1,0:T(8,128)(2,1)} %get-tuple-element.71), channel_id=1, source_target_pairs={{0,24},{1,25},{2,26},{3,27},{4,28},{5,29},{6,30},{7,31},{8,16},{9,... | collective-permute-start | bytes 835592 | tf_op jit(solution)/shard_map/ppermute | solution.py:114
  334.4 27.8 %collective-permute-start.42 = (bf16[128,1088]{1,0:T(8,128)(2,1)}, bf16[128,1088]{1,0:T(8,128)(2,1)}, u32[]{:S(2)}, u32[]{:S(2)}) collective-permute-start(bf16[128,1088]{1,0:T(8,128)(2,1)} %get-tuple-element.72), channel_id=1, source_target_pairs={{0,8},{1,9},{2,10},{3,11},{4,12},{5,13},{6,14},{7,15},{8,0},{9,1},... | collective-permute-start | bytes 835592 | tf_op jit(solution)/shard_map/ppermute | solution.py:114
  343.7 28.2 %collective-permute-start.29 = (bf16[2,136,1088]{2,1,0:T(8,128)(2,1)S(1)}, bf16[2,136,1088]{2,1,0:T(8,128)(2,1)S(1)}, u32[]{:S(2)}, u32[]{:S(2)}) collective-permute-start(bf16[2,136,1088]{2,1,0:T(8,128)(2,1)S(1)} %copy-done.21), channel_id=1, source_target_pairs={{0,2},{1,3},{2,0},{3,1},{4,6},{5,7},{6,4},{7,5},{8,10},{9,11},{10,... | collective-permute-start | bytes 1775624 | tf_op jit(solution)/shard_map/ppermute | solution.py:114
  360.1 21.5 %collective-permute-start.33 = (bf16[2,136,1088]{2,1,0:T(8,128)(2,1)S(1)}, bf16[2,136,1088]{2,1,0:T(8,128)(2,1)S(1)}, u32[]{:S(2)}, u32[]{:S(2)}) collective-permute-start(bf16[2,136,1088]{2,1,0:T(8,128)(2,1)S(1)} %add_convert_fusion), channel_id=1, source_target_pairs={{0,2},{1,3},{2,0},{3,1},{4,6},{5,7},{6,4},{7,5},{8,10},{9,11},{10,... | collective-permute-start | bytes 1775624 | tf_op jit(solution)/shard_map/ppermute | solution.py:114
  362.2 24.5 %collective-permute-start.45 = (bf16[144,1088]{1,0:T(8,128)(2,1)S(1)}, bf16[144,1088]{1,0:T(8,128)(2,1)S(1)}, u32[]{:S(2)}, u32[]{:S(2)}) collective-permute-start(bf16[144,1088]{1,0:T(8,128)(2,1)S(1)} %get-tuple-element.78), channel_id=1, source_target_pairs={{0,16},{1,17},{2,18},{3,19},{4,20},{5,21},{6,22},{7,23},{8,24},{9,... | collective-permute-start | bytes 940040 | tf_op jit(solution)/shard_map/ppermute | solution.py:114
  371.9 33.3 %collective-permute-start.46 = (bf16[144,1088]{1,0:T(8,128)(2,1)S(1)}, bf16[144,1088]{1,0:T(8,128)(2,1)S(1)}, u32[]{:S(2)}, u32[]{:S(2)}) collective-permute-start(bf16[144,1088]{1,0:T(8,128)(2,1)S(1)} %get-tuple-element.79), channel_id=1, source_target_pairs={{0,24},{1,25},{2,26},{3,27},{4,28},{5,29},{6,30},{7,31},{8,16},{9,... | collective-permute-start | bytes 940040 | tf_op jit(solution)/shard_map/ppermute | solution.py:114
  373.9 31.4 %collective-permute-start.47 = (bf16[144,1088]{1,0:T(8,128)(2,1)S(1)}, bf16[144,1088]{1,0:T(8,128)(2,1)S(1)}, u32[]{:S(2)}, u32[]{:S(2)}) collective-permute-start(bf16[144,1088]{1,0:T(8,128)(2,1)S(1)} %get-tuple-element.80), channel_id=1, source_target_pairs={{0,8},{1,9},{2,10},{3,11},{4,12},{5,13},{6,14},{7,15},{8,0},{9,1},... | collective-permute-start | bytes 940040 | tf_op jit(solution)/shard_map/ppermute | solution.py:114
  382.1 28.8 %collective-permute-start.35 = (bf16[136,1088]{1,0:T(8,128)(2,1)S(1)}, bf16[136,1088]{1,0:T(8,128)(2,1)S(1)}, u32[]{:S(2)}, u32[]{:S(2)}) collective-permute-start(bf16[136,1088]{1,0:T(8,128)(2,1)S(1)} %get-tuple-element.62), channel_id=1, source_target_pairs={{0,16},{1,17},{2,18},{3,19},{4,20},{5,21},{6,22},{7,23},{8,24},{9,... | collective-permute-start | bytes 887816 | tf_op jit(solution)/shard_map/ppermute | solution.py:114
  384.7 30.4 %collective-permute-start.36 = (bf16[136,1088]{1,0:T(8,128)(2,1)S(1)}, bf16[136,1088]{1,0:T(8,128)(2,1)S(1)}, u32[]{:S(2)}, u32[]{:S(2)}) collective-permute-start(bf16[136,1088]{1,0:T(8,128)(2,1)S(1)} %get-tuple-element.63), channel_id=1, source_target_pairs={{0,24},{1,25},{2,26},{3,27},{4,28},{5,29},{6,30},{7,31},{8,16},{9,... | collective-permute-start | bytes 887816 | tf_op jit(solution)/shard_map/ppermute | solution.py:114
  386.7 28.4 %collective-permute-start.37 = (bf16[136,1088]{1,0:T(8,128)(2,1)S(1)}, bf16[136,1088]{1,0:T(8,128)(2,1)S(1)}, u32[]{:S(2)}, u32[]{:S(2)}) collective-permute-start(bf16[136,1088]{1,0:T(8,128)(2,1)S(1)} %get-tuple-element.64), channel_id=1, source_target_pairs={{0,8},{1,9},{2,10},{3,11},{4,12},{5,13},{6,14},{7,15},{8,0},{9,1},... | collective-permute-start | bytes 887816 | tf_op jit(solution)/shard_map/ppermute | solution.py:114
  (167 other events, 1363.3 us)
Sparse Core Ops, SparseCore 0:
  9.6 32.5 all-gather.6
  44.4 29.5 all-gather.8
  75.6 31.8 all-gather.10

commit v5 on v4

--- a/solution.py
+++ b/solution.py
@@ -63,46 +63,168 @@
     return (mixed, top + jnp.log(total))
 
 
-def attend_back(queries, keys, values, allowed, scale, grad_mixed, log_total):
-    scores = jnp.einsum("qhd,khd->hqk", queries, keys, preferred_element_type=jnp.float32) * scale
-    scores = jnp.where(allowed[None], scores, neg_large)
-    probs = jnp.exp(scores - log_total)
-    grad_values = jnp.einsum(
-        "hqk,qhd->hdk", probs.astype(jnp.bfloat16), grad_mixed, preferred_element_type=jnp.float32
-    )
-    grad_probs = jnp.einsum("qhd,khd->hqk", grad_mixed, values, preferred_element_type=jnp.float32)
-    inner = jnp.sum(probs * grad_probs, axis=-1, keepdims=True)
-    grad_scores = (probs * (grad_probs - inner)).astype(jnp.bfloat16)
-    grad_queries = (
-        jnp.einsum("hqk,khd->hdq", grad_scores, keys, preferred_element_type=jnp.float32) * scale
-    )
-    grad_keys = (
-        jnp.einsum("hqk,qhd->hdk", grad_scores, queries, preferred_element_type=jnp.float32) * scale
-    )
-    return (grad_queries, grad_keys, grad_values)
+VMEM = pl.BlockSpec(memory_space=pltpu.VMEM)
+SMEM = pl.BlockSpec(memory_space=pltpu.SMEM)
+
+
+def local_kernel(body, outs, operands, flops, specs=None):
+    outs = [jax.ShapeDtypeStruct(shape, kind) for shape, kind in outs]
+    moved = sum(array.size * array.dtype.itemsize for array in (*outs, *operands))
+    return pl.pallas_call(
+        body,
+        out_shape=outs,
+        in_specs=specs or [VMEM] * len(operands),
+        out_specs=[VMEM] * len(outs),
+        compiler_params=pltpu.CompilerParams(vmem_limit_bytes=VMEM_LIMIT),
+        cost_estimate=pl.CostEstimate(flops=flops, bytes_accessed=moved, transcendentals=0),
+    )(*operands)
+
+
+def product(left, right, left_axis, right_axis):
+    return lax.dot_general(
+        left, right, (((left_axis,), (right_axis,)), ((), ())), preferred_element_type=jnp.float32
+    )
+
+
+def attend_back(queries, keys, values, span, scale, grad_mixed, log_total):
+    width, rows = queries.shape
+    low = jnp.bfloat16
+
+    def body(span_ref, q_ref, k_ref, v_ref, do_ref, log_ref, out_ref):
+        begin, finish = span_ref[0], span_ref[1]
+
+        def inside(axis):
+            position = lax.broadcasted_iota(jnp.int32, (rows, rows), axis)
+            return (position, (position >= begin) & (position < finish))
+
+        key_pos, key_live = inside(0)
+        query_pos, query_live = inside(1)
+        allowed = (key_pos <= query_pos) & (key_live == query_live)
+
+        @pl.loop(0, HEADS)
+        def _(head):
+            part = pl.ds(pl.multiple_of(head * HEAD_SIZE, HEAD_SIZE), HEAD_SIZE)
+            q, k, v, do = q_ref[part, :], k_ref[part, :], v_ref[part, :], do_ref[part, :]
+            scores = jnp.where(allowed, product(k, q, 0, 0) * scale, neg_large)
+            probs = jnp.exp(scores - log_ref[head])
+            out_ref[2, part, :] = product(do, probs.astype(low), 1, 1).astype(low)
+            grad_probs = product(v, do, 0, 0)
+            inner = jnp.sum(probs * grad_probs, axis=0, keepdims=True)
+            grad_scores = (probs * (grad_probs - inner)).astype(low)
+            out_ref[0, part, :] = (product(k, grad_scores, 1, 0) * scale).astype(low)
+            out_ref[1, part, :] = (product(q, grad_scores, 1, 1) * scale).astype(low)
+
+    return local_kernel(
+        body,
+        [((3, width, rows), low)],
+        (span, queries, keys, values, grad_mixed, log_total),
+        10 * rows * rows * width,
+        [SMEM] + [VMEM] * 5,
+    )[0]
+
+
+def mlp_block(row_pair, grad_pair, weights, biases, before, last):
+    rows, width = row_pair[0].shape
+    low, wide = jnp.bfloat16, jnp.float32
+    hidden = [2 * weight.shape[1] for weight in weights]
+    outs = []
+    for count in hidden:
+        outs += [((2, rows, count), low), ((2, rows, count), low), ((1, count), wide)]
+    sums = len(outs)
+    if last:
+        outs += [((rows, width), wide), ((rows, width), low)]
+    else:
+        outs += [((2, rows, width), wide)]
+    number = len(weights)
+
+    def body(*refs):
+        row_refs, grad_refs = refs[:2], refs[2:4]
+        weight_refs, bias_refs = refs[4 : 4 + number], refs[4 + number : 4 + 2 * number]
+        out_refs = refs[-len(outs) :]
+        for side in range(2):
+            total = None if before is None else refs[4 + 2 * number][side]
+            for place in range(number):
+                weight, count = weight_refs[place], hidden[place]
+                up = weight[0:2].reshape(count, width)
+                down = weight[2:4].reshape(count, width)
+                up_sum = product(row_refs[side][...], up, 1, 1) + bias_refs[place][...]
+                activated, slope = gelu_parts(up_sum)
+                grad_act = product(grad_refs[side][...], down, 1, 1)
+                grad_up = (grad_act * slope).astype(low)
+                act_ref, up_ref, sum_ref = out_refs[3 * place : 3 * place + 3]
+                act_ref[side] = activated.astype(low)
+                up_ref[side] = grad_up
+                columns = jnp.sum(grad_up.astype(wide), axis=0, keepdims=True)
+                sum_ref[...] = columns if side == 0 else sum_ref[...] + columns
+                term = product(grad_up, up, 1, 0)
+                total = term if total is None else total + term
+            if last:
+                out = out_refs[sums + side]
+                out[...] = total.astype(out.dtype)
+            else:
+                out_refs[sums][side] = total
+
+    operands = (*row_pair, *grad_pair, *weights, *biases)
+    operands += () if before is None else (before,)
+    result = local_kernel(body, outs, operands, 12 * rows * width * sum(hidden))
+    return ([result[3 * place : 3 * place + 3] for place in range(number)], result[sums:])
+
+
+def mlp_weight_grads(blocks, rows, grads, kind):
+    width = rows[0].shape[1]
+    operands, outs, number = [], [], len(rows)
+    for near, far in blocks:
+        operands += [near[0], far[0], near[1], far[1]]
+        count = near[0].shape[2]
+        outs += [((2, count // 2, width), kind)] * 2
+
+    def body(*refs):
+        row_refs = refs[len(operands) : len(operands) + number]
+        grad_refs = refs[len(operands) + number : len(operands) + 2 * number]
+        out_refs = refs[-len(outs) :]
+        for place in range(len(blocks)):
+            sources = refs[4 * place : 4 * place + 4]
+            for out, pair, others in (
+                (out_refs[2 * place], sources[2:], row_refs),
+                (out_refs[2 * place + 1], sources[:2], grad_refs),
+            ):
+                total = None
+                for which in range(number):
+                    term = product(pair[which // 2][which % 2], others[which][...], 0, 0)
+                    total = term if total is None else total + term
+                out[...] = total.reshape(out.shape).astype(kind)
+
+    flops = sum(16 * rows[0].shape[0] * near[0].shape[2] * width for near, far in blocks)
+    result = local_kernel(body, outs, (*operands, *rows, *grads), flops)
+    return [tuple(result[2 * place : 2 * place + 2]) for place in range(len(blocks))]
+
+
+def mlp_outputs(blocks, weights):
+    rows, width = blocks[0][0][0].shape[1], weights[0].shape[2]
+    number = len(weights)
+    operands = [near[0] for near, far in blocks] + [far[0] for near, far in blocks]
+
+    def body(*refs):
+        weight_refs, out_refs = refs[2 * number : 3 * number], refs[-2:]
+        for group in range(2):
+            for side in range(2):
+                total = None
+                for place in range(number):
+                    weight = weight_refs[place]
+                    down = weight[2:4].reshape(2 * weight.shape[1], width)
+                    term = product(refs[group * number + place][side], down, 1, 0)
+                    total = term if total is None else total + term
+                out_refs[side][group] = total.astype(out_refs[side].dtype)
+
+    outs = [((2, rows, width), jnp.float32), ((2, rows, width), jnp.bfloat16)]
+    flops = 16 * rows * width * sum(weight.shape[1] for weight in weights)
+    return local_kernel(body, outs, (*operands, *weights), flops)
 
 
 def gather_rows(own):
     across = swap(own, 2)
     beside = swap(own, 1)
-    return jnp.concatenate([own, across, beside, swap(across, 1)], axis=0)
-
-
-def row_products(left_parts, right_parts, start, stop):
-    total = 0.0
-    for left, right in zip(left_parts, right_parts):
-        total = total + jnp.dot(left[start:stop], right, preferred_element_type=jnp.float32)
-    return total
-
-
-def reduce_near(left_parts, right_parts):
-    low = jnp.bfloat16
-    rows = left_parts[0].shape[0] // 4
-    given = row_products(left_parts, right_parts, 2 * rows, 4 * rows).astype(low)
-    taken = swap(given, 1).astype(jnp.float32)
-    far = row_products(left_parts, right_parts, rows, 2 * rows) + taken[rows:]
-    near = row_products(left_parts, right_parts, 0, rows) + taken[:rows]
-    return (near, far.astype(low))
+    return ((own, beside), (across, swap(across, 1)))
 
 
 def after(values, others):
@@ -220,16 +342,16 @@
     if devices != 32:
         product = jnp.concatenate(
             [
-                jnp.dot(grads[: 3 * width], first[0], preferred_element_type=jnp.float32),
-                jnp.dot(grads[3 * width :], mixed[0], preferred_element_type=jnp.float32),
+                jnp.dot(grads[0].reshape(3 * width, own), first[0], preferred_element_type=jnp.float32),
+                jnp.dot(grads[1], mixed[0], preferred_element_type=jnp.float32),
             ],
             axis=0,
         ).astype(low)
         share = lax.psum_scatter(product, "dev", scatter_dimension=0, tiled=True)
         return (lambda: share.astype(jnp.float32), grads)
     pairs = (jnp.stack([first[0], mixed[0]]), jnp.stack([first[1], mixed[1]]))
-    blocks = grads.reshape(4, 8, -1, own)
-    diagonal, across, along, mine = attn_products(blocks, swap(blocks, 1), pairs)
+    grads = [part.reshape(-1, 8, width // 8, own) for part in grads]
+    diagonal, across, along, mine = attn_products(grads, [swap(part, 1) for part in grads], pairs)
 
     across_upper = swap(across[0], 2)
     along_lower = swap(along[1], 4)
@@ -246,41 +368,37 @@
 
 def attn_products(mine, beside, pairs):
     block = (lax.axis_index("dev") & 7).astype(jnp.int32).reshape(1)
-    rows = mine.shape[2]
+    rows = mine[0].shape[2]
     width = pairs[0].shape[2]
     low, wide = jnp.bfloat16, jnp.float32
     kinds = (low, low, low, wide, wide, low, wide, wide)
 
-    def body(block_ref, mine_ref, beside_ref, pair_ref, other_ref, *outs):
+    def body(block_ref, *refs):
+        (three, last), (three_beside, last_beside) = refs[:2], refs[2:4]
+        pair_ref, other_ref = refs[4:6]
+        outs = refs[6:]
         for place, mask in enumerate((6, 2, 4, 0)):
             target = block_ref[0] ^ mask
             for half in range(2):
                 out = outs[2 * place + half]
-
-                @pl.loop(0, 2)
-                def _(number):
-                    side = number if half else 0
+                for number in range(2):
                     matrix = 2 * half + number
-                    value = jnp.dot(
-                        mine_ref[matrix, target], pair_ref[side], preferred_element_type=wide
-                    ) + jnp.dot(
-                        beside_ref[matrix, target], other_ref[side], preferred_element_type=wide
+                    left = last[0, target] if matrix == 3 else three[matrix, target]
+                    left_beside = (
+                        last_beside[0, target] if matrix == 3 else three_beside[matrix, target]
                     )
+                    side = 1 if matrix == 3 else 0
+                    value = product(left, pair_ref[side], 1, 0)
+                    value = value + product(left_beside, other_ref[side], 1, 0)
                     out[number] = value.astype(out.dtype)
 
-    vmem = pl.BlockSpec(memory_space=pltpu.VMEM)
-    outs = pl.pallas_call(
+    outs = local_kernel(
         body,
-        out_shape=[jax.ShapeDtypeStruct((2, rows, width), kind) for kind in kinds],
-        in_specs=[pl.BlockSpec(memory_space=pltpu.SMEM)] + [vmem] * 4,
-        out_specs=[vmem] * 8,
-        compiler_params=pltpu.CompilerParams(vmem_limit_bytes=VMEM_LIMIT),
-        cost_estimate=pl.CostEstimate(
-            flops=64 * rows * mine.shape[3] * width,
-            bytes_accessed=30 * 1024 * 1024,
-            transcendentals=0,
-        ),
-    )(block, mine, beside, *pairs)
+        [((2, rows, width), kind) for kind in kinds],
+        (block, *mine, *beside, *pairs),
+        64 * rows * mine[0].shape[3] * width,
+        [SMEM] + [VMEM] * 6,
+    )
     return [outs[2 * place : 2 * place + 2] for place in range(4)]
 
 
@@ -310,36 +428,31 @@
 def hidden_parts(gathered, here, devices, ready):
     one, two = gathered
     if devices != 32:
-        rows = one.shape[0] // 2
-        return [(one[:rows], one[rows:], here & 3, 0, rows // (devices // 8))]
+        rows = one.shape[0] // 4
+        return [[(one.reshape(4, rows, -1), here & 3, 0, rows // (devices // 16))]]
     two = after(two, ready)
-    parts = []
-    for pieces, number in (((one[0], two), here & 7), ((one[1], swap(two, 4)), (here & 7) ^ 4)):
-        start = 0
-        for piece in pieces:
-            rows, width = piece.shape[1:]
-            up, down = piece[:2].reshape(2 * rows, width), piece[2:].reshape(2 * rows, width)
-            parts.append((up, down, number, start, start + rows))
-            start += rows
-    return parts
-
-
-def scatter_hidden(grads, others):
+    cut, end = one[0].shape[1], one[0].shape[1] + two.shape[1]
+    own, other = here & 7, (here & 7) ^ 4
+    return [
+        [(one[0], own, 0, cut), (two, own, cut, end)],
+        [(one[1], other, 0, cut), (swap(two, 4), other, cut, end)],
+    ]
+
+
+def scatter_hidden(own, others, ready):
     devices = lax.axis_size("dev")
     low = jnp.bfloat16
     if devices != 32:
-        both = jnp.concatenate(grads[0], axis=0).astype(low)
+        width = own[0][0].shape[2]
+        both = jnp.concatenate([part.reshape(-1, width) for part in own[0]], axis=0).astype(low)
         return lax.psum_scatter(
             both, "dev", scatter_dimension=0, tiled=True, axis_index_groups=same_low(devices)
         ).astype(jnp.float32)
-    moved = [[swap(part.astype(low), 4) for part in pair] for pair in grads[2:]]
-    shares = []
-    for own, other in zip(grads[:2], moved):
-        other = after(other, others)
-        rows = own[0].shape[0] // 2
-        own = [part.reshape(2, rows, -1) for part in own]
-        other = [(part.reshape(2, rows, -1),) for part in other]
-        shares.append(scatter_z(own, other))
+    moved = [[swap(part, 4) for part in pair] for pair in others]
+    shares = [
+        scatter_z(mine, [(part,) for part in after(other, ready)])
+        for mine, other in zip(own, moved)
+    ]
     return jnp.concatenate(shares, axis=0)
 
 
@@ -448,36 +561,36 @@
     middle = inputs + branch
     second_out, normed_two, factor_two = normalize(middle, gain_two, shift_two)
     second_own = second_out.astype(low)
-    second_low = gather_rows(second_own)
+    near, far = gather_rows(second_own)
     parts = hidden_parts(gathered, here, devices, second_own)
-
-    kept = []
+    near_grads, far_grads = grad_down_rows
+
+    sides = []
+    near_sum = far_sum = None
     grad_up_bias = jnp.zeros_like(up_bias)
-    for up_weight, down_weight, blocks, start, stop in parts:
-        bias = pick_blocks(up_bias, blocks, start, stop)
-        up_sum = (
-            jnp.einsum("rd,fd->rf", second_low, up_weight, preferred_element_type=jnp.float32)
-            + bias
-        )
-        activated, slope = gelu_parts(up_sum)
-        grad_act = jnp.einsum(
-            "rd,fd->rf", grad_down_rows, down_weight, preferred_element_type=jnp.float32
-        )
-        grad_up = (grad_act * slope).astype(low)
-        column_sums = jnp.sum(grad_up.astype(jnp.float32), axis=0)
-        grad_up_bias = put_blocks(grad_up_bias, blocks, start, stop, column_sums)
-        kept.append((activated.astype(low), grad_up))
-    grad_second, far = reduce_near([pair[1] for pair in kept], [part[0] for part in parts])
-    grad_second = grad_second + swap(far, 2).astype(jnp.float32)
-    kept = after(kept, far)
-    grads = [
-        (
-            jnp.einsum("rf,rd->fd", grad_up, second_low, preferred_element_type=jnp.float32),
-            jnp.einsum("rf,rd->fd", act_low, grad_down_rows, preferred_element_type=jnp.float32),
-        )
-        for act_low, grad_up in kept
-    ]
-    down, down_far = reduce_near([pair[0] for pair in kept], [part[1] for part in parts])
+    for place, side in enumerate(parts):
+        weights = [part[0] for part in side]
+        biases = [pick_blocks(up_bias, *part[1:]).reshape(1, -1) for part in side]
+        last = place == len(parts) - 1
+        near_blocks, near_sum = mlp_block(near, near_grads, weights, biases, near_sum, last)
+        far_blocks, far_sum = mlp_block(far, far_grads, weights, biases, far_sum, last)
+        if not last:
+            near_sum, far_sum = near_sum[0], far_sum[0]
+        for part, one, two in zip(side, near_blocks, far_blocks):
+            grad_up_bias = put_blocks(grad_up_bias, *part[1:], (one[2] + two[2]).reshape(-1))
+        sides.append([(one[:2], two[:2]) for one, two in zip(near_blocks, far_blocks)])
+    far_total = (far_sum[0] + swap(far_sum[1], 1).astype(jnp.float32)).astype(low)
+    near_taken = swap(near_sum[1], 1)
+    grad_second = near_sum[0] + near_taken.astype(jnp.float32)
+    sides = after(sides, far_total)
+    grad_second = grad_second + swap(far_total, 2).astype(jnp.float32)
+    all_rows, all_grads = near + far, near_grads + far_grads
+    other_grads = [mlp_weight_grads(side, all_rows, all_grads, low) for side in sides[1:]]
+    own_grads = mlp_weight_grads(sides[0], all_rows, all_grads, jnp.float32)
+    down_keep, down_give = mlp_outputs(sum(sides, []), [part[0] for side in parts for part in side])
+    down_taken = swap(down_give, 1).astype(jnp.float32)
+    down = down_keep[0] + down_taken[0]
+    down_far = (down_keep[1] + down_taken[1]).astype(low)
 
     grad_down_wide = grad_down.astype(jnp.float32)
     grad_down_bias = jnp.sum(grad_down_wide, axis=0)
@@ -487,31 +600,27 @@
     grad_branch = grad_middle.astype(low)
     grad_out_bias = jnp.sum(grad_branch.astype(jnp.float32), axis=0)
     grad_mixed = jnp.dot(grad_branch, full_out, preferred_element_type=jnp.float32)
-    grad_mixed_low = grad_mixed.astype(low).reshape(head_shape)
-    grad_queries, grad_keys, grad_values = attend_back(
-        queries, keys, values, allowed, scale, grad_mixed_low, log_total
-    )
-    grad_features = jnp.concatenate(
-        [
-            grad_queries.reshape(width, total_rows).astype(low),
-            grad_keys.reshape(width, total_rows).astype(low),
-            grad_values.reshape(width, total_rows).astype(low),
-            grad_branch.T,
-        ],
-        axis=0,
+    grad_mixed_low = grad_mixed.astype(low)
+    grad_features = attend_back(
+        queries.reshape(total_rows, width).T,
+        keys.reshape(total_rows, width).T,
+        values.reshape(total_rows, width).T,
+        jnp.stack([begin, finish]),
+        scale,
+        grad_mixed_low.T,
+        log_total.reshape(HEADS, 1, total_rows),
     )
     attn_finish, attn_sent = scatter_attn(
-        grad_features, ((first_low, first_beside), (mixed_low, mixed_beside))
-    )
-    mlp_share = scatter_hidden(grads, attn_sent)
+        (grad_features, grad_branch.T), ((first_low, first_beside), (mixed_low, mixed_beside))
+    )
+    mlp_share = scatter_hidden(own_grads, sum(other_grads, []), attn_sent)
     attn_share = attn_finish()
-    grad_features = after(grad_features, attn_sent)
+    grad_features = after(grad_features, attn_sent).reshape(3 * width, total_rows)
     down_far = after(swap(down_far, 2), attn_sent).astype(jnp.float32)
     output = jnp.where(live, middle + (down + down_far + down_bias), 0.0).astype(low)
-    grad_projected = grad_features[: 3 * width]
-    grad_columns = jnp.sum(grad_projected.astype(jnp.float32), axis=1)
+    grad_columns = jnp.sum(grad_features.astype(jnp.float32), axis=1)
     grad_first = jnp.einsum(
-        "fr,fd->rd", grad_projected, full_proj, preferred_element_type=jnp.float32
+        "fr,fd->rd", grad_features, full_proj, preferred_element_type=jnp.float32
     )
     grad_gain_one = jnp.sum(grad_first * normed_one, axis=0)
     grad_shift_one = jnp.sum(grad_first, axis=0)

time: 430 us -> 435 us (1.012)
  matrix products: 108 us -> 17.3 us
  local copies, waits for them, and re-layouts: 89.7 us -> 153 us
  Pallas kernels: 14.9 us -> 46.1 us
  other arithmetic: 30 us -> 34.5 us
    dot_general x45 -> x1, matrix products: 101 us -> 8.72 us  [shards(): jnp.einsum('fr,fd->rd', grad_features, full_proj, preferred_element_type=...]
    unnamed x291 -> x301, local copies, waits for them, and re-layouts: 20.7 us -> 86.2 us
    pallas_call x1 -> x9, Pallas kernels: 7.98 us -> 38.6 us  [local_kernel(): pl.pallas_call(body, out_shape=outs, in_specs=specs or [VMEM] * len(opera...]
    pallas_call x0 -> x5, local copies, waits for them, and re-layouts: none -> 10.9 us  [local_kernel(): pl.pallas_call(body, out_shape=outs, in_specs=specs or [VMEM] * len(opera...]
    slice x6 -> x0, local copies, waits for them, and re-layouts: 9.78 us -> none  [the longest x4 7.18 us: hidden_parts(): piece[2:].reshape(2 * rows, width)]
    ppermute x53 -> x55, waiting for transfers between devices: 113 us -> 105 us  [swap(): lax.ppermute(piece, 'dev', [(number, number ^ mask) for number in range(d...]
    all_gather x3, waiting for transfers between devices: 0.01 us -> 8.03 us  [gather_z(): lax.all_gather(shard, 'dev', axis=0, tiled=False, axis_index_groups=z_gro...]
    concatenate x2 -> x0, local copies, waits for them, and re-layouts: 6.6 us -> none  [shards(): jnp.concatenate([grad_queries.reshape(width, total_rows).astype(low), gra...]
  transfers between devices with their start and end apart: 56 -> 58, of which waited for: 18 -> 18; matrix products, arithmetic and copies ran while one was open for 43% -> 28% of each run, Pallas kernels for 4% -> 10%
where the time goes in v5:
time: 435 us; the launch traced here: 428 us
  local copies, waits for them, and re-layouts  153 us (35%)
  waiting for transfers between devices  114 us (26%)
  starting transfers between devices  46.9 us (11%)
  Pallas kernels  46.1 us (11%)
  other arithmetic  34.5 us (8%)
  matrix products  17.3 us (4%)
  between operations  16.5 us (4%)
    ppermute x55, waiting for transfers between devices, swap(): lax.ppermute(piece, 'dev', [(number, number ^ mask) for number in range(d...  105 us
    unnamed x301, local copies, waits for them, and re-layouts  86.2 us
    ppermute x55, starting transfers between devices, swap(): lax.ppermute(piece, 'dev', [(number, number ^ mask) for number in range(d...  46.8 us
    pallas_call x9, Pallas kernels, local_kernel(): pl.pallas_call(body, out_shape=outs, in_specs=specs or [VMEM] * len(opera...  38.6 us
    ppermute x13, local copies, waits for them, and re-layouts, swap(): lax.ppermute(piece, 'dev', [(number, number ^ mask) for number in range(d...  26.3 us
    pallas_call x5, local copies, waits for them, and re-layouts, local_kernel(): pl.pallas_call(body, out_shape=outs, in_specs=specs or [VMEM] * len(opera...  10.9 us
    dot_general x1, matrix products, shards(): jnp.einsum('fr,fd->rd', grad_features, full_proj, preferred_element_type=...  8.72 us
  transfers between devices with their start and end apart: 58, of which 18 were waited for; matrix products, arithmetic and copies ran while one was open for 28% of the time, Pallas kernels for 10%

profile of v5, /device:TPU:8, one launch (start us, length us, event | category | flops | bytes accessed | tf_op | source)
XLA Modules:
  0.0 428.1 jit_solution(6476911072519574579)
XLA Ops:
  18.8 11.1 %collective-permute-done.1 = bf16[816]{0:T(1024)(128)(2,1)S(1)} collective-permute-done((bf16[816]{0:T(1024)(128)(2,1)S(1)}, bf16[816]{0:T(1024)(128)(2,1)S(1)}, u32[]{:S(2)}, u32[]{:S(2)}) %collective-permute-start.1) | collective-permute-done | bytes 1664 | tf_op jit(solution)/shard_map/ppermute | solution.py:236
  34.1 8.0 %all-gather.7.cloned.1.call-done = bf16[544,1088]{1,0:T(8,128)(2,1)} async-done(((bf16[136,1088]{1,0:T(8,128)(2,1)}), bf16[544,1088]{1,0:T(8,128)(2,1)}) %all-gather.7.cloned.1.call-update) | async-done | bytes 1183760 | tf_op jit(solution)/shard_map/all_gather | solution.py:276
  47.1 2.7 collective-permute-done.4
  50.1 21.3 %collective-permute-done.7.refs_3_ = bf16[4,136,1088]{2,1,0:T(8,128)(2,1)S(1)} collective-permute-done((bf16[4,136,1088]{2,1,0:T(8,128)(2,1)}, bf16[4,136,1088]{2,1,0:T(8,128)(2,1)S(1)}, u32[]{:S(2)}, u32[]{:S(2)}) %collective-permute-start.7) | collective-permute-done | bytes 1183776 | tf_op jit(solution)/shard_map/ppermute | solution.py:236
  80.0 7.4 %collective-permute-done.11.refs_7_ = bf16[2,136,1088]{2,1,0:T(8,128)(2,1)} collective-permute-done((bf16[2,136,1088]{2,1,0:T(8,128)(2,1)}, bf16[2,136,1088]{2,1,0:T(8,128)(2,1)}, u32[]{:S(2)}, u32[]{:S(2)}) %collective-permute-start.11) | collective-permute-done | bytes 591904 | tf_op jit(solution)/shard_map/ppermute | solution.py:236
  87.4 3.1 collective-permute-done.10.refs_6_
  91.7 2.6 copy.54
  95.9 3.8 shard_map.119
  99.8 2.4 fusion.37
  138.5 2.4 pad_maximum_fusion.2.refs_5_
  149.9 3.3 shard_map.121
  154.7 3.7 shard_map.123
  170.9 3.3 shard_map.120
  175.7 3.9 shard_map.122
  188.6 2.3 add_convert_fusion.2
  204.5 4.1 shard_map.124
  211.1 2.4 copy.66
  218.1 2.5 multiply_reduce_fusion
  223.7 8.9 %shard_map.125 = bf16[3,1088,256]{2,1,0:T(8,128)(2,1)S(1)} custom-call(s32[2]{0:T(128)S(1)} %pad_add_fusion.span_ref, bf16[1088,256]{1,0:T(8,128)(2,1)S(1)} %bitcast.72, bf16[1088,256]{1,0:T(8,128)(2,1)S(1)} %copy-done.27, bf16[1088,256]{1,0:T(8,128)(2,1)S(1)} %bitcast.74, bf16[1088,256]{1,0:T(8,128)(2,1)S(1)} %convolution_convert_fusion.do_ref, ...), custom_call_target="tpu_custom_call" | custom-call | flops 713031680 | bytes 3916808 | tf_op jit(solution)/shard_map/pallas_call | solution.py:73
  246.7 3.1 shard_map.129
  273.9 3.1 shard_map.128
  292.6 5.3 %shard_map.126 = (bf16[2,136,1088]{2,1,0:T(8,128)(2,1)}, bf16[2,136,1088]{2,1,0:T(8,128)(2,1)S(1)}, bf16[2,136,1088]{2,1,0:T(8,128)(2,1)S(1)}, f32[2,136,1088]{2...) custom-call(s32[1]{0:T(128)} %bitcast.block_ref, ...), custom_call_target="tpu_custom_call" | custom-call | flops 2424307712 | bytes 13787140 | tf_op jit(solution)/shard_map/pallas_call | solution.py:73
  300.7 8.7 %fusion.36 = (f32[1088]{0:T(1024)}, f32[256,1088]{0,1:T(8,128)}) fusion(bf16[3264,256]{1,0:T(8,128)(2,1)S(1)} %bitcast.70, bf16[3264,1088]{1,0:T(8,128)(2,1)} %bitcast.90), kind=kOutput, calls=%fused_computation.129 | convolution fusion | flops 1818508288 | bytes 9892096 | tf_op jit(solution)/shard_map/fr,fd->rd/dot_general | solution.py:622
  312.2 2.8 copy.79
  315.0 2.4 fusion.17
  344.3 2.7 copy.102
  354.7 9.5 %collective-permute-done.34 = bf16[2,136,1088]{2,1,0:T(8,128)(2,1)S(1)} collective-permute-done((bf16[2,136,1088]{2,1,0:T(8,128)(2,1)S(1)}, bf16[2,136,1088]{2,1,0:T(8,128)(2,1)S(1)}, u32[]{:S(2)}, u32[]{:S(2)}) %collective-permute-start.34) | collective-permute-done | bytes 591904 | tf_op jit(solution)/shard_map/ppermute | solution.py:236
  371.1 10.2 %collective-permute-done.36.refs_5_ = bf16[2,136,1088]{2,1,0:T(8,128)(2,1)S(1)} collective-permute-done((bf16[2,136,1088]{2,1,0:T(8,128)(2,1)S(1)}, bf16[2,136,1088]{2,1,0:T(8,128)(2,1)S(1)}, u32[]{:S(2)}, u32[]{:S(2)}) %collective-permute-start.36) | collective-permute-done | bytes 591904 | tf_op jit(solution)/shard_map/ppermute | solution.py:236
  383.1 6.5 %collective-permute-done.33.refs_2_ = bf16[2,136,1088]{2,1,0:T(8,128)(2,1)S(1)} collective-permute-done((bf16[2,136,1088]{2,1,0:T(8,128)(2,1)S(1)}, bf16[2,136,1088]{2,1,0:T(8,128)(2,1)S(1)}, u32[]{:S(2)}, u32[]{:S(2)}) %collective-permute-start.33) | collective-permute-done | bytes 591904 | tf_op jit(solution)/shard_map/ppermute | solution.py:236
  394.6 16.1 %collective-permute-done.48 = bf16[144,1088]{1,0:T(8,128)(2,1)S(1)} collective-permute-done((bf16[144,1088]{1,0:T(8,128)(2,1)S(1)}, bf16[144,1088]{1,0:T(8,128)(2,1)S(1)}, u32[]{:S(2)}, u32[]{:S(2)}) %collective-permute-start.48) | collective-permute-done | bytes 313376 | tf_op jit(solution)/shard_map/ppermute | solution.py:236
  412.0 3.5 collective-permute-done.37
  415.5 4.9 %collective-permute-done.38 = bf16[136,1088]{1,0:T(8,128)(2,1)S(1)} collective-permute-done((bf16[136,1088]{1,0:T(8,128)(2,1)S(1)}, bf16[136,1088]{1,0:T(8,128)(2,1)S(1)}, u32[]{:S(2)}, u32[]{:S(2)}) %collective-permute-start.38) | collective-permute-done | bytes 295968 | tf_op jit(solution)/shard_map/ppermute | solution.py:236
  (530 shorter events, 233.4 us)
Async XLA Ops:
  7.2 34.9 %all-gather.7.cloned.1.call-start = ((), (), s32[]{:S(2)}) async-start(), calls=%async_computation | async-start | bytes 1566720 | tf_op jit(solution)/shard_map/all_gather | solution.py:276
  8.0 83.7 %all-gather.9.cloned.1.call-start = ((), (), s32[]{:S(2)}) async-start(), calls=%async_computation.1 | async-start | bytes 1474560 | tf_op jit(solution)/shard_map/all_gather | solution.py:276
  9.7 112.8 %all-gather.11.cloned.1.call-start = ((), (), s32[]{:S(2)}) async-start(), calls=%async_computation.2 | async-start | bytes 1658880 | tf_op jit(solution)/shard_map/all_gather | solution.py:276
  14.7 62.5 %collective-permute-start.18 = (bf16[256,1088]{0,1:T(8,128)(2,1)}, bf16[256,1088]{0,1:T(8,128)(2,1)S(1)}, u32[]{:S(2)}, u32[]{:S(2)}) collective-permute-start(bf16[256,1088]{0,1:T(8,128)(2,1)} %copy.45), channel_id=1, source_target_pairs={{0,2},{1,3},{2,0},{3,1},{4,6},{5,7},{6,4},{7,5},{8,10},{9,11},{10,... | collective-permute-start | bytes 1671176 | tf_op jit(solution)/shard_map/ppermute | solution.py:236
  42.1 29.3 %collective-permute-start.7 = (bf16[4,136,1088]{2,1,0:T(8,128)(2,1)}, bf16[4,136,1088]{2,1,0:T(8,128)(2,1)S(1)}, u32[]{:S(2)}, u32[]{:S(2)}) collective-permute-start(bf16[4,136,1088]{2,1,0:T(8,128)(2,1)} %bitcast.75), channel_id=1, source_target_pairs={{0,2},{1,3},{2,0},{3,1},{4,6},{5,7},{6,4},{7,5},{8,10},{9,11},{10,... | collective-permute-start | bytes 3551240 | tf_op jit(solution)/shard_map/ppermute | solution.py:236
  43.6 30.2 %collective-permute-start.6 = (bf16[4,136,1088]{2,1,0:T(8,128)(2,1)}, bf16[4,136,1088]{2,1,0:T(8,128)(2,1)}, u32[]{:S(2)}, u32[]{:S(2)}) collective-permute-start(bf16[4,136,1088]{2,1,0:T(8,128)(2,1)} %bitcast.76), channel_id=1, source_target_pairs={{0,4},{1,5},{2,6},{3,7},{4,0},{5,1},{6,2},{7,3},{8,12},{9,13},{10,... | collective-permute-start | bytes 3551240 | tf_op jit(solution)/shard_map/ppermute | solution.py:236
  50.1 44.2 %collective-permute-start.5 = (bf16[4,136,1088]{2,1,0:T(8,128)(2,1)}, bf16[4,136,1088]{2,1,0:T(8,128)(2,1)}, u32[]{:S(2)}, u32[]{:S(2)}) collective-permute-start(bf16[4,136,1088]{2,1,0:T(8,128)(2,1)} %bitcast.77), channel_id=1, source_target_pairs={{0,1},{1,0},{2,3},{3,2},{4,5},{5,4},{6,7},{7,6},{8,9},{9,8},{10,11... | collective-permute-start | bytes 3551240 | tf_op jit(solution)/shard_map/ppermute | solution.py:236
  94.3 21.3 %collective-permute-start.15 = (bf16[256,1088]{0,1:T(8,128)(2,1)}, bf16[256,1088]{0,1:T(8,128)(2,1)}, u32[]{:S(2)}, u32[]{:S(2)}) collective-permute-start(bf16[256,1088]{0,1:T(8,128)(2,1)} %copy.45), channel_id=1, source_target_pairs={{0,1},{1,0},{2,3},{3,2},{4,5},{5,4},{6,7},{7,6},{8,9},{9,8},{10,11... | collective-permute-start | bytes 1671176 | tf_op jit(solution)/shard_map/ppermute | solution.py:236
  94.8 22.9 %collective-permute-start.29 = (bf16[256,1088]{0,1:T(8,128)(2,1)}, bf16[256,1088]{0,1:T(8,128)(2,1)}, u32[]{:S(2)}, u32[]{:S(2)}) collective-permute-start(bf16[256,1088]{0,1:T(8,128)(2,1)} %copy.75), channel_id=1, source_target_pairs={{0,1},{1,0},{2,3},{3,2},{4,5},{5,4},{6,7},{7,6},{8,9},{9,8},{10,11... | collective-permute-start | bytes 1671176 | tf_op jit(solution)/shard_map/ppermute | solution.py:236
  94.9 24.9 %collective-permute-start.19 = (bf16[256,1088]{0,1:T(8,128)(2,1)}, bf16[256,1088]{0,1:T(8,128)(2,1)}, u32[]{:S(2)}, u32[]{:S(2)}) collective-permute-start(bf16[256,1088]{0,1:T(8,128)(2,1)} %copy-done.131), channel_id=1, source_target_pairs={{0,1},{1,0},{2,3},{3,2},{4,5},{5,4},{6,7},{7,6},{8,9},{9,8},{10,11... | collective-permute-start | bytes 1671176 | tf_op jit(solution)/shard_map/ppermute | solution.py:236
  95.3 34.8 %collective-permute-start.20 = (bf16[4,128,1088]{1,2,0:T(8,128)(2,1)}, bf16[4,128,1088]{1,2,0:T(8,128)(2,1)}, u32[]{:S(2)}, u32[]{:S(2)}) collective-permute-start(bf16[4,128,1088]{1,2,0:T(8,128)(2,1)} %copy.54), channel_id=1, source_target_pairs={{0,4},{1,5},{2,6},{3,7},{4,0},{5,1},{6,2},{7,3},{8,12},{9,13},{10,... | collective-permute-start | bytes 3342344 | tf_op jit(solution)/shard_map/ppermute | solution.py:236
  122.5 32.1 %collective-permute-start.21 = (bf16[4,144,1088]{2,1,0:T(8,128)(2,1)}, bf16[4,144,1088]{2,1,0:T(8,128)(2,1)S(1)}, u32[]{:S(2)}, u32[]{:S(2)}) collective-permute-start(bf16[4,144,1088]{2,1,0:T(8,128)(2,1)} %bitcast.93), channel_id=1, source_target_pairs={{0,4},{1,5},{2,6},{3,7},{4,0},{5,1},{6,2},{7,3},{8,12},{9,13},{10,... | collective-permute-start | bytes 3760136 | tf_op jit(solution)/shard_map/ppermute | solution.py:236
  164.6 21.9 %collective-permute-start.22 = (bf16[256,1088]{0,1:T(8,128)(2,1)}, bf16[256,1088]{0,1:T(8,128)(2,1)}, u32[]{:S(2)}, u32[]{:S(2)}) collective-permute-start(bf16[256,1088]{0,1:T(8,128)(2,1)} %copy.63), channel_id=1, source_target_pairs={{0,1},{1,0},{2,3},{3,2},{4,5},{5,4},{6,7},{7,6},{8,9},{9,8},{10,11... | collective-permute-start | bytes 1671176 | tf_op jit(solution)/shard_map/ppermute | solution.py:236
  186.5 27.2 %collective-permute-start.25 = (bf16[256,1088]{0,1:T(8,128)(2,1)}, bf16[256,1088]{0,1:T(8,128)(2,1)}, u32[]{:S(2)}, u32[]{:S(2)}) collective-permute-start(bf16[256,1088]{0,1:T(8,128)(2,1)} %copy.69), channel_id=1, source_target_pairs={{0,1},{1,0},{2,3},{3,2},{4,5},{5,4},{6,7},{7,6},{8,9},{9,8},{10,11... | collective-permute-start | bytes 1671176 | tf_op jit(solution)/shard_map/ppermute | solution.py:236
  193.0 22.9 %collective-permute-start.26 = (bf16[256,1088]{0,1:T(8,128)(2,1)}, bf16[256,1088]{0,1:T(8,128)(2,1)}, u32[]{:S(2)}, u32[]{:S(2)}) collective-permute-start(bf16[256,1088]{0,1:T(8,128)(2,1)} %copy.71), channel_id=1, source_target_pairs={{0,2},{1,3},{2,0},{3,1},{4,6},{5,7},{6,4},{7,5},{8,10},{9,11},{10,... | collective-permute-start | bytes 1671176 | tf_op jit(solution)/shard_map/ppermute | solution.py:236
  213.5 69.3 %collective-permute-start.23 = (bf16[2,256,1088]{1,2,0:T(8,128)(2,1)}, bf16[2,256,1088]{1,2,0:T(8,128)(2,1)}, u32[]{:S(2)}, u32[]{:S(2)}) collective-permute-start(bf16[2,256,1088]{1,2,0:T(8,128)(2,1)} %copy.66), channel_id=1, source_target_pairs={{0,1},{1,0},{2,3},{3,2},{4,5},{5,4},{6,7},{7,6},{8,9},{9,8},{10,11... | collective-permute-start | bytes 3342344 | tf_op jit(solution)/shard_map/ppermute | solution.py:236
  232.7 58.1 %collective-permute-start.27 = (bf16[3,8,136,256]{3,2,1,0:T(8,128)(2,1)S(1)}, bf16[3,8,136,256]{3,2,1,0:T(8,128)(2,1)}, u32[]{:S(2)}, u32[]{:S(2)}) collective-permute-start(bf16[3,8,136,256]{3,2,1,0:T(8,128)(2,1)S(1)} %bitcast.68), channel_id=1, source_target_pairs={{0,1},{1,0},{2,3},{3,2},{4,5},{5,4},{6,7},{7,6},{8,9},{9,8},{10,11... | collective-permute-start | bytes 5013512 | tf_op jit(solution)/shard_map/ppermute | solution.py:236
  257.3 68.5 %collective-permute-start.41 = (bf16[2,128,1088]{1,2,0:T(8,128)(2,1)}, bf16[2,128,1088]{1,2,0:T(8,128)(2,1)}, u32[]{:S(2)}, u32[]{:S(2)}) collective-permute-start(bf16[2,128,1088]{1,2,0:T(8,128)(2,1)} %copy.93), channel_id=1, source_target_pairs={{0,4},{1,5},{2,6},{3,7},{4,0},{5,1},{6,2},{7,3},{8,12},{9,13},{10,... | collective-permute-start | bytes 1671176 | tf_op jit(solution)/shard_map/ppermute | solution.py:236
  258.8 67.0 %collective-permute-start.40 = (bf16[2,128,1088]{1,2,0:T(8,128)(2,1)}, bf16[2,128,1088]{1,2,0:T(8,128)(2,1)}, u32[]{:S(2)}, u32[]{:S(2)}) collective-permute-start(bf16[2,128,1088]{1,2,0:T(8,128)(2,1)} %copy.92), channel_id=1, source_target_pairs={{0,4},{1,5},{2,6},{3,7},{4,0},{5,1},{6,2},{7,3},{8,12},{9,13},{10,... | collective-permute-start | bytes 1671176 | tf_op jit(solution)/shard_map/ppermute | solution.py:236
  259.4 66.5 %collective-permute-start.45 = (bf16[2,144,1088]{2,1,0:T(8,128)(2,1)}, bf16[2,144,1088]{2,1,0:T(8,128)(2,1)}, u32[]{:S(2)}, u32[]{:S(2)}) collective-permute-start(bf16[2,144,1088]{2,1,0:T(8,128)(2,1)} %copy-done.67), channel_id=1, source_target_pairs={{0,4},{1,5},{2,6},{3,7},{4,0},{5,1},{6,2},{7,3},{8,12},{9,13},{10,... | collective-permute-start | bytes 1880072 | tf_op jit(solution)/shard_map/ppermute | solution.py:236
  290.2 35.6 %collective-permute-start.46 = (bf16[2,144,1088]{2,1,0:T(8,128)(2,1)}, bf16[2,144,1088]{2,1,0:T(8,128)(2,1)}, u32[]{:S(2)}, u32[]{:S(2)}) collective-permute-start(bf16[2,144,1088]{2,1,0:T(8,128)(2,1)} %copy-done.66), channel_id=1, source_target_pairs={{0,4},{1,5},{2,6},{3,7},{4,0},{5,1},{6,2},{7,3},{8,12},{9,13},{10,... | collective-permute-start | bytes 1880072 | tf_op jit(solution)/shard_map/ppermute | solution.py:236
  331.8 34.1 %collective-permute-start.42 = (bf16[128,1088]{1,0:T(8,128)(2,1)}, bf16[128,1088]{1,0:T(8,128)(2,1)S(1)}, u32[]{:S(2)}, u32[]{:S(2)}) collective-permute-start(bf16[128,1088]{1,0:T(8,128)(2,1)} %get-tuple-element.156), channel_id=1, source_target_pairs={{0,16},{1,17},{2,18},{3,19},{4,20},{5,21},{6,22},{7,23},{8,24},{9,... | collective-permute-start | bytes 835592 | tf_op jit(solution)/shard_map/ppermute | solution.py:236
  333.4 33.1 %collective-permute-start.43 = (bf16[128,1088]{1,0:T(8,128)(2,1)}, bf16[128,1088]{1,0:T(8,128)(2,1)}, u32[]{:S(2)}, u32[]{:S(2)}) collective-permute-start(bf16[128,1088]{1,0:T(8,128)(2,1)} %get-tuple-element.157), channel_id=1, source_target_pairs={{0,24},{1,25},{2,26},{3,27},{4,28},{5,29},{6,30},{7,31},{8,16},{9,... | collective-permute-start | bytes 835592 | tf_op jit(solution)/shard_map/ppermute | solution.py:236
  334.5 34.2 %collective-permute-start.44 = (bf16[128,1088]{1,0:T(8,128)(2,1)}, bf16[128,1088]{1,0:T(8,128)(2,1)}, u32[]{:S(2)}, u32[]{:S(2)}) collective-permute-start(bf16[128,1088]{1,0:T(8,128)(2,1)} %get-tuple-element.158), channel_id=1, source_target_pairs={{0,8},{1,9},{2,10},{3,11},{4,12},{5,13},{6,14},{7,15},{8,0},{9,1},... | collective-permute-start | bytes 835592 | tf_op jit(solution)/shard_map/ppermute | solution.py:236
  365.9 23.8 %collective-permute-start.33 = (bf16[2,136,1088]{2,1,0:T(8,128)(2,1)S(1)}, bf16[2,136,1088]{2,1,0:T(8,128)(2,1)S(1)}, u32[]{:S(2)}, u32[]{:S(2)}) collective-permute-start(bf16[2,136,1088]{2,1,0:T(8,128)(2,1)S(1)} %add_convert_fusion.1), channel_id=1, source_target_pairs={{0,4},{1,5},{2,6},{3,7},{4,0},{5,1},{6,2},{7,3},{8,12},{9,13},{10,... | collective-permute-start | bytes 1775624 | tf_op jit(solution)/shard_map/ppermute | solution.py:236
  366.5 23.1 %collective-permute-start.35 = (bf16[2,136,1088]{2,1,0:T(8,128)(2,1)S(1)}, bf16[2,136,1088]{2,1,0:T(8,128)(2,1)S(1)}, u32[]{:S(2)}, u32[]{:S(2)}) collective-permute-start(bf16[2,136,1088]{2,1,0:T(8,128)(2,1)S(1)} %add_convert_fusion), channel_id=1, source_target_pairs={{0,2},{1,3},{2,0},{3,1},{4,6},{5,7},{6,4},{7,5},{8,10},{9,11},{10,... | collective-permute-start | bytes 1775624 | tf_op jit(solution)/shard_map/ppermute | solution.py:236
  368.7 23.6 %collective-permute-start.47 = (bf16[144,1088]{1,0:T(8,128)(2,1)S(1)}, bf16[144,1088]{1,0:T(8,128)(2,1)S(1)}, u32[]{:S(2)}, u32[]{:S(2)}) collective-permute-start(bf16[144,1088]{1,0:T(8,128)(2,1)S(1)} %get-tuple-element.166), channel_id=1, source_target_pairs={{0,16},{1,17},{2,18},{3,19},{4,20},{5,21},{6,22},{7,23},{8,24},{9,... | collective-permute-start | bytes 940040 | tf_op jit(solution)/shard_map/ppermute | solution.py:236
  370.2 40.5 %collective-permute-start.48 = (bf16[144,1088]{1,0:T(8,128)(2,1)S(1)}, bf16[144,1088]{1,0:T(8,128)(2,1)S(1)}, u32[]{:S(2)}, u32[]{:S(2)}) collective-permute-start(bf16[144,1088]{1,0:T(8,128)(2,1)S(1)} %get-tuple-element.167), channel_id=1, source_target_pairs={{0,24},{1,25},{2,26},{3,27},{4,28},{5,29},{6,30},{7,31},{8,16},{9,... | collective-permute-start | bytes 940040 | tf_op jit(solution)/shard_map/ppermute | solution.py:236
  381.3 29.4 %collective-permute-start.49 = (bf16[144,1088]{1,0:T(8,128)(2,1)S(1)}, bf16[144,1088]{1,0:T(8,128)(2,1)S(1)}, u32[]{:S(2)}, u32[]{:S(2)}) collective-permute-start(bf16[144,1088]{1,0:T(8,128)(2,1)S(1)} %get-tuple-element.168), channel_id=1, source_target_pairs={{0,8},{1,9},{2,10},{3,11},{4,12},{5,13},{6,14},{7,15},{8,0},{9,1},... | collective-permute-start | bytes 940040 | tf_op jit(solution)/shard_map/ppermute | solution.py:236
  390.1 25.3 %collective-permute-start.37 = (bf16[136,1088]{1,0:T(8,128)(2,1)S(1)}, bf16[136,1088]{1,0:T(8,128)(2,1)S(1)}, u32[]{:S(2)}, u32[]{:S(2)}) collective-permute-start(bf16[136,1088]{1,0:T(8,128)(2,1)S(1)} %get-tuple-element.138), channel_id=1, source_target_pairs={{0,16},{1,17},{2,18},{3,19},{4,20},{5,21},{6,22},{7,23},{8,24},{9,... | collective-permute-start | bytes 887816 | tf_op jit(solution)/shard_map/ppermute | solution.py:236
  391.2 29.1 %collective-permute-start.38 = (bf16[136,1088]{1,0:T(8,128)(2,1)S(1)}, bf16[136,1088]{1,0:T(8,128)(2,1)S(1)}, u32[]{:S(2)}, u32[]{:S(2)}) collective-permute-start(bf16[136,1088]{1,0:T(8,128)(2,1)S(1)} %get-tuple-element.139), channel_id=1, source_target_pairs={{0,24},{1,25},{2,26},{3,27},{4,28},{5,29},{6,30},{7,31},{8,16},{9,... | collective-permute-start | bytes 887816 | tf_op jit(solution)/shard_map/ppermute | solution.py:236
  392.3 28.0 %collective-permute-start.39 = (bf16[136,1088]{1,0:T(8,128)(2,1)S(1)}, bf16[136,1088]{1,0:T(8,128)(2,1)S(1)}, u32[]{:S(2)}, u32[]{:S(2)}) collective-permute-start(bf16[136,1088]{1,0:T(8,128)(2,1)S(1)} %get-tuple-element.140), channel_id=1, source_target_pairs={{0,8},{1,9},{2,10},{3,11},{4,12},{5,13},{6,14},{7,15},{8,0},{9,1},... | collective-permute-start | bytes 887816 | tf_op jit(solution)/shard_map/ppermute | solution.py:236
  (174 other events, 884.6 us)
Sparse Core Ops, SparseCore 0:
  9.6 32.4 all-gather.6
  44.2 29.5 all-gather.8
  75.4 31.8 all-gather.10

commit v6 on v5

--- a/solution.py
+++ b/solution.py
@@ -2,6 +2,7 @@
 import jax.numpy as jnp
 from jax import lax
 from jax.experimental import pallas as pl
+from jax.experimental.layout import Layout, with_layout_constraint
 from jax.experimental.pallas import tpu as pltpu
 from jax.sharding import PartitionSpec as P
 
@@ -9,7 +10,7 @@
 HEADS = 17
 HEAD_SIZE = 64
 FF = 4352
-VMEM_LIMIT = 32 * 1024 * 1024
+VMEM_LIMIT = 48 * 1024 * 1024
 
 
 epsilon = 1e-05
@@ -63,21 +64,46 @@
     return (mixed, top + jnp.log(total))
 
 
-VMEM = pl.BlockSpec(memory_space=pltpu.VMEM)
-SMEM = pl.BlockSpec(memory_space=pltpu.SMEM)
-
-
-def local_kernel(body, outs, operands, flops, specs=None):
+def local_kernel(body, outs, operands, flops, scalars=(), earlier=()):
     outs = [jax.ShapeDtypeStruct(shape, kind) for shape, kind in outs]
     moved = sum(array.size * array.dtype.itemsize for array in (*outs, *operands))
+    first, count, total = len(scalars), len(operands), len(operands) + len(outs)
+
+    def whole(*refs):
+        scalar_refs, sources = refs[:first], refs[first : first + count]
+        goals = refs[first + count + len(earlier) :][: len(outs)]
+        buffers, sems = refs[-total - 1 : -1], refs[-1]
+        ends = tuple(zip(sources, buffers)) + tuple(zip(buffers[count:], goals))
+        copies = [
+            pltpu.make_async_copy(source, goal, sems.at[number])
+            for number, (source, goal) in enumerate(ends)
+        ]
+        for copy in copies[:count]:
+            copy.start()
+        for copy in copies[:count]:
+            copy.wait()
+        body(*scalar_refs, *buffers)
+        for copy in copies[count:]:
+            copy.start()
+        for copy in copies[count:]:
+            copy.wait()
+
+    anywhere = pl.BlockSpec(memory_space=pl.ANY)
     return pl.pallas_call(
-        body,
+        whole,
         out_shape=outs,
-        in_specs=specs or [VMEM] * len(operands),
-        out_specs=[VMEM] * len(outs),
+        in_specs=[pl.BlockSpec(memory_space=pltpu.SMEM)] * first
+        + [anywhere] * (count + len(earlier)),
+        out_specs=[anywhere] * len(outs),
+        scratch_shapes=[pltpu.VMEM(array.shape, array.dtype) for array in (*operands, *outs)]
+        + [pltpu.SemaphoreType.DMA((total,))],
         compiler_params=pltpu.CompilerParams(vmem_limit_bytes=VMEM_LIMIT),
         cost_estimate=pl.CostEstimate(flops=flops, bytes_accessed=moved, transcendentals=0),
-    )(*operands)
+    )(*scalars, *operands, *earlier)
+
+
+def row_major(values):
+    return with_layout_constraint(values, Layout(major_to_minor=tuple(range(values.ndim))))
 
 
 def product(left, right, left_axis, right_axis):
@@ -117,9 +143,9 @@
     return local_kernel(
         body,
         [((3, width, rows), low)],
-        (span, queries, keys, values, grad_mixed, log_total),
+        (queries, keys, values, grad_mixed, log_total),
         10 * rows * rows * width,
-        [SMEM] + [VMEM] * 5,
+        (span,),
     )[0]
 
 
@@ -170,7 +196,7 @@
     return ([result[3 * place : 3 * place + 3] for place in range(number)], result[sums:])
 
 
-def mlp_weight_grads(blocks, rows, grads, kind):
+def mlp_weight_grads(blocks, rows, grads, kind, earlier):
     width = rows[0].shape[1]
     operands, outs, number = [], [], len(rows)
     for near, far in blocks:
@@ -195,11 +221,11 @@
                 out[...] = total.reshape(out.shape).astype(kind)
 
     flops = sum(16 * rows[0].shape[0] * near[0].shape[2] * width for near, far in blocks)
-    result = local_kernel(body, outs, (*operands, *rows, *grads), flops)
+    result = local_kernel(body, outs, (*operands, *rows, *grads), flops, (), earlier)
     return [tuple(result[2 * place : 2 * place + 2]) for place in range(len(blocks))]
 
 
-def mlp_outputs(blocks, weights):
+def mlp_outputs(blocks, weights, earlier):
     rows, width = blocks[0][0][0].shape[1], weights[0].shape[2]
     number = len(weights)
     operands = [near[0] for near, far in blocks] + [far[0] for near, far in blocks]
@@ -218,7 +244,7 @@
 
     outs = [((2, rows, width), jnp.float32), ((2, rows, width), jnp.bfloat16)]
     flops = 16 * rows * width * sum(weight.shape[1] for weight in weights)
-    return local_kernel(body, outs, (*operands, *weights), flops)
+    return local_kernel(body, outs, (*operands, *weights), flops, (), earlier)
 
 
 def gather_rows(own):
@@ -349,7 +375,7 @@
         ).astype(low)
         share = lax.psum_scatter(product, "dev", scatter_dimension=0, tiled=True)
         return (lambda: share.astype(jnp.float32), grads)
-    pairs = (jnp.stack([first[0], mixed[0]]), jnp.stack([first[1], mixed[1]]))
+    pairs = ((first[0], mixed[0]), (first[1], mixed[1]))
     grads = [part.reshape(-1, 8, width // 8, own) for part in grads]
     diagonal, across, along, mine = attn_products(grads, [swap(part, 1) for part in grads], pairs)
 
@@ -369,14 +395,14 @@
 def attn_products(mine, beside, pairs):
     block = (lax.axis_index("dev") & 7).astype(jnp.int32).reshape(1)
     rows = mine[0].shape[2]
-    width = pairs[0].shape[2]
+    width = pairs[0][0].shape[1]
     low, wide = jnp.bfloat16, jnp.float32
     kinds = (low, low, low, wide, wide, low, wide, wide)
 
     def body(block_ref, *refs):
         (three, last), (three_beside, last_beside) = refs[:2], refs[2:4]
-        pair_ref, other_ref = refs[4:6]
-        outs = refs[6:]
+        pair_refs, other_refs = refs[4:6], refs[6:8]
+        outs = refs[8:]
         for place, mask in enumerate((6, 2, 4, 0)):
             target = block_ref[0] ^ mask
             for half in range(2):
@@ -388,21 +414,21 @@
                         last_beside[0, target] if matrix == 3 else three_beside[matrix, target]
                     )
                     side = 1 if matrix == 3 else 0
-                    value = product(left, pair_ref[side], 1, 0)
-                    value = value + product(left_beside, other_ref[side], 1, 0)
+                    value = product(left, pair_refs[side][...], 1, 0)
+                    value = value + product(left_beside, other_refs[side][...], 1, 0)
                     out[number] = value.astype(out.dtype)
 
     outs = local_kernel(
         body,
         [((2, rows, width), kind) for kind in kinds],
-        (block, *mine, *beside, *pairs),
+        (*mine, *beside, *pairs[0], *pairs[1]),
         64 * rows * mine[0].shape[3] * width,
-        [SMEM] + [VMEM] * 6,
+        (block,),
     )
     return [outs[2 * place : 2 * place + 2] for place in range(4)]
 
 
-def gather_hidden(shard, near_ready):
+def gather_hidden(shard):
     devices = lax.axis_size("dev")
     if devices != 32:
         both = lax.all_gather(
@@ -411,7 +437,6 @@
         return (both, None)
     cut = 128
     one, two = gather_z(shard[:cut]), gather_z(shard[cut:])
-    one = after(one, near_ready)
     return ((one, swap(one, 4)), two)
 
 
@@ -450,14 +475,14 @@
         ).astype(jnp.float32)
     moved = [[swap(part, 4) for part in pair] for pair in others]
     shares = [
-        scatter_z(mine, [(part,) for part in after(other, ready)])
+        scatter_z(mine, [(part,) for part in other], ready)
         for mine, other in zip(own, moved)
     ]
     return jnp.concatenate(shares, axis=0)
 
 
-def scatter_z(own, others):
-    mine, one, two, three = route_z(own, others)
+def scatter_z(own, others, earlier=()):
+    mine, one, two, three = route_z(own, others, earlier)
     wide = jnp.float32
     return (
         mine
@@ -467,7 +492,7 @@
     )
 
 
-def route_z(own, others):
+def route_z(own, others, earlier):
     layer = (lax.axis_index("dev") >> 3).astype(jnp.int32).reshape(1)
     rows, width = own[0].shape[1:]
     count = len(others[0])
@@ -487,18 +512,15 @@
                         total = total + source[number].astype(jnp.float32)
                     out[...] = total.astype(out.dtype)
 
-    vmem = pl.BlockSpec(memory_space=pltpu.VMEM)
     kinds = (jnp.float32, jnp.bfloat16, jnp.bfloat16, jnp.bfloat16)
-    return pl.pallas_call(
+    return local_kernel(
         body,
-        out_shape=[jax.ShapeDtypeStruct((rows, width), kind) for kind in kinds],
-        in_specs=[pl.BlockSpec(memory_space=pltpu.SMEM)] + [vmem] * (2 * count + 2),
-        out_specs=[vmem] * 4,
-        compiler_params=pltpu.CompilerParams(vmem_limit_bytes=VMEM_LIMIT),
-        cost_estimate=pl.CostEstimate(
-            flops=4 * rows * width, bytes_accessed=30 * rows * width, transcendentals=0
-        ),
-    )(layer, own[0], *others[0], own[1], *others[1])
+        [((rows, width), kind) for kind in kinds],
+        (own[0], *others[0], own[1], *others[1]),
+        4 * rows * width,
+        (layer,),
+        earlier,
+    )
 
 
 def shards(
@@ -520,9 +542,9 @@
     head_shape = (total_rows, HEADS, HEAD_SIZE)
 
     full_vec = gather_vectors(vectors)
-    grad_down = jnp.where(live, cotangent, jnp.zeros_like(cotangent))
+    grad_down = row_major(jnp.where(live, cotangent, jnp.zeros_like(cotangent)))
     full_proj, full_out, attn_ready = gather_attn(attn_weight)
-    gathered = gather_hidden(mlp_weight, attn_ready)
+    gathered = gather_hidden(mlp_weight)
     grad_down_rows = gather_rows(grad_down)
 
     (
@@ -541,7 +563,7 @@
 
     inputs = tokens.astype(jnp.float32)
     first_out, normed_one, factor_one = normalize(inputs, gain_one, shift_one)
-    first_low = first_out.astype(low)
+    first_low = row_major(first_out.astype(low))
     first_beside = swap(first_low, 1)
     projected = jnp.einsum(
         "rd,od->ro", first_low, full_proj, preferred_element_type=jnp.float32
@@ -550,7 +572,7 @@
     keys = projected[:, width : 2 * width].astype(low).reshape(head_shape)
     values = (projected[:, 2 * width :] + value_bias).astype(low).reshape(head_shape)
     mixed, log_total = attend(queries, keys, values, allowed, scale)
-    mixed_low = mixed.reshape(total_rows, width).astype(low)
+    mixed_low = row_major(mixed.reshape(total_rows, width).astype(low))
     mixed_beside = swap(mixed_low, 1)
     branch = (
         jnp.einsum(
@@ -560,7 +582,7 @@
     )
     middle = inputs + branch
     second_out, normed_two, factor_two = normalize(middle, gain_two, shift_two)
-    second_own = second_out.astype(low)
+    second_own = row_major(second_out.astype(low))
     near, far = gather_rows(second_own)
     parts = hidden_parts(gathered, here, devices, second_own)
     near_grads, far_grads = grad_down_rows
@@ -582,15 +604,12 @@
     far_total = (far_sum[0] + swap(far_sum[1], 1).astype(jnp.float32)).astype(low)
     near_taken = swap(near_sum[1], 1)
     grad_second = near_sum[0] + near_taken.astype(jnp.float32)
-    sides = after(sides, far_total)
-    grad_second = grad_second + swap(far_total, 2).astype(jnp.float32)
     all_rows, all_grads = near + far, near_grads + far_grads
-    other_grads = [mlp_weight_grads(side, all_rows, all_grads, low) for side in sides[1:]]
-    own_grads = mlp_weight_grads(sides[0], all_rows, all_grads, jnp.float32)
-    down_keep, down_give = mlp_outputs(sum(sides, []), [part[0] for side in parts for part in side])
-    down_taken = swap(down_give, 1).astype(jnp.float32)
-    down = down_keep[0] + down_taken[0]
-    down_far = (down_keep[1] + down_taken[1]).astype(low)
+    other_grads = [
+        mlp_weight_grads(side, all_rows, all_grads, low, (far_total,)) for side in sides[1:]
+    ]
+    far_taken = after(swap(far_total, 2), other_grads)
+    grad_second = grad_second + far_taken.astype(jnp.float32)
 
     grad_down_wide = grad_down.astype(jnp.float32)
     grad_down_bias = jnp.sum(grad_down_wide, axis=0)
@@ -613,10 +632,18 @@
     attn_finish, attn_sent = scatter_attn(
         (grad_features, grad_branch.T), ((first_low, first_beside), (mixed_low, mixed_beside))
     )
+    own_grads = mlp_weight_grads(sides[0], all_rows, all_grads, jnp.float32, attn_sent)
+    down_keep, down_give = mlp_outputs(
+        sum(sides, []),
+        [part[0] for side in parts for part in side],
+        sum(own_grads, ()),
+    )
+    down_taken = swap(down_give, 1).astype(jnp.float32)
+    down = down_keep[0] + down_taken[0]
+    down_far = swap((down_keep[1] + down_taken[1]).astype(low), 2).astype(jnp.float32)
     mlp_share = scatter_hidden(own_grads, sum(other_grads, []), attn_sent)
     attn_share = attn_finish()
     grad_features = after(grad_features, attn_sent).reshape(3 * width, total_rows)
-    down_far = after(swap(down_far, 2), attn_sent).astype(jnp.float32)
     output = jnp.where(live, middle + (down + down_far + down_bias), 0.0).astype(low)
     grad_columns = jnp.sum(grad_features.astype(jnp.float32), axis=1)
     grad_first = jnp.einsum(

time: 435 us -> 526 us (1.21)
  waiting for transfers between devices: 114 us -> 194 us
  local copies, waits for them, and re-layouts: 153 us -> 114 us
  Pallas kernels: 46.1 us -> 84.4 us
  starting transfers between devices: 46.9 us -> 53.3 us
    ppermute x55, waiting for transfers between devices: 105 us -> 173 us  [swap(): lax.ppermute(piece, 'dev', [(number, number ^ mask) for number in range(d...]
    unnamed x301 -> x299, local copies, waits for them, and re-layouts: 86.2 us -> 50.4 us
    pallas_call x12, Pallas kernels: 42.3 us -> 76.7 us  [local_kernel(): pl.pallas_call(whole, out_shape=outs, in_specs=[pl.BlockSpec(memory_space...]
    all_gather x3, waiting for transfers between devices: 8.03 us -> 20.8 us  [gather_z(): lax.all_gather(shard, 'dev', axis=0, tiled=False, axis_index_groups=z_gro...]
    ppermute x55, starting transfers between devices: 46.8 us -> 53.2 us  [swap(): lax.ppermute(piece, 'dev', [(number, number ^ mask) for number in range(d...]
    ppermute x13 -> x15, local copies, waits for them, and re-layouts: 26.3 us -> 27 us  [swap(): lax.ppermute(piece, 'dev', [(number, number ^ mask) for number in range(d...]
  transfers between devices with their start and end apart: 58 -> 58, of which waited for: 18 -> 22; matrix products, arithmetic and copies ran while one was open for 28% -> 23% of each run, Pallas kernels for 10% -> 16%
where the time goes in v6:
time: 526 us; the launch traced here: 516 us
  waiting for transfers between devices  194 us (37%)
  local copies, waits for them, and re-layouts  114 us (22%)
  Pallas kernels  84.4 us (16%)
  starting transfers between devices  53.3 us (10%)
  other arithmetic  35.1 us (7%)
  matrix products  18.3 us (3%)
  between operations  16.8 us (3%)
    ppermute x55, waiting for transfers between devices, swap(): lax.ppermute(piece, 'dev', [(number, number ^ mask) for number in range(d...  173 us
    pallas_call x12, Pallas kernels, local_kernel(): pl.pallas_call(whole, out_shape=outs, in_specs=[pl.BlockSpec(memory_space...  76.7 us
    ppermute x55, starting transfers between devices, swap(): lax.ppermute(piece, 'dev', [(number, number ^ mask) for number in range(d...  53.2 us
    unnamed x299, local copies, waits for them, and re-layouts  50.4 us
    ppermute x15, local copies, waits for them, and re-layouts, swap(): lax.ppermute(piece, 'dev', [(number, number ^ mask) for number in range(d...  27 us
    all_gather x3, waiting for transfers between devices, gather_z(): lax.all_gather(shard, 'dev', axis=0, tiled=False, axis_index_groups=z_gro...  20.8 us
  transfers between devices with their start and end apart: 58, of which 22 were waited for; matrix products, arithmetic and copies ran while one was open for 23% of the time, Pallas kernels for 16%

profile of v6, /device:TPU:8, one launch (start us, length us, event | category | flops | bytes accessed | tf_op | source)
XLA Modules:
  0.0 516.3 jit_solution(1461500688969843092)
XLA Ops:
  21.1 20.8 %all-gather.7.cloned.1.call-done = bf16[544,1088]{1,0:T(8,128)(2,1)} async-done(((bf16[136,1088]{1,0:T(8,128)(2,1)}), bf16[544,1088]{1,0:T(8,128)(2,1)}) %all-gather.7.cloned.1.call-update) | async-done | bytes 1183760 | tf_op jit(solution)/shard_map/all_gather | solution.py:302
  50.5 20.8 %collective-permute-done.6.refs_2_ = bf16[4,136,1088]{2,1,0:T(8,128)(2,1)} collective-permute-done((bf16[4,136,1088]{2,1,0:T(8,128)(2,1)}, bf16[4,136,1088]{2,1,0:T(8,128)(2,1)}, u32[]{:S(2)}, u32[]{:S(2)}) %collective-permute-start.6) | collective-permute-done | bytes 1183776 | tf_op jit(solution)/shard_map/ppermute | solution.py:262
  79.9 8.4 %collective-permute-done.10.refs_6_ = bf16[2,136,1088]{2,1,0:T(8,128)(2,1)} collective-permute-done((bf16[2,136,1088]{2,1,0:T(8,128)(2,1)}, bf16[2,136,1088]{2,1,0:T(8,128)(2,1)}, u32[]{:S(2)}, u32[]{:S(2)}) %collective-permute-start.10) | collective-permute-done | bytes 591904 | tf_op jit(solution)/shard_map/ppermute | solution.py:262
  88.3 3.1 collective-permute-done.11.refs_7_
  93.7 7.8 %shard_map.119 = (bf16[3,8,136,1088]{3,2,1,0:T(8,128)(2,1)}, bf16[8,136,1088]{2,1,0:T(8,128)(2,1)}) custom-call(s32[1]{0:T(128)} %bitcast.block_ref.refs_0_, bf16[4,136,1088]{2,1,0:T(8,128)(2,1)S(1)} %bitcast.80, bf16[4,136,1088]{2,1,0:T(8,128)(2,1)} %collective-permute-done.5.refs_1_, bf16[4,136,1088]{2,1,0:T(8,128)(2,1)} %collective-permute-done.6.refs_2_, ...), custom_call_target="tpu_custom_call" | custom-call | bytes 18939904 | tf_op jit(solution)/shard_map/pallas_call | solution.py:328
  101.5 5.6 %fusion.38 = f32[256,3264]{0,1:T(8,128)S(1)} fusion(bf16[256,1088]{1,0:T(8,128)(2,1)S(1)} %fusion.13.refs_5_, bf16[3264,1088]{1,0:T(8,128)(2,1)} %bitcast.88), kind=kOutput, calls=%fused_computation.130 | convolution fusion | flops 1818230784 | bytes 11001856 | tf_op jit(solution)/shard_map/rd,od->ro/dot_general | solution.py:568
  113.4 3.0 fusion.36
  125.9 7.8 %collective-permute-done.18 = bf16[256,1088]{0,1:T(8,128)(2,1)S(1)} collective-permute-done((bf16[256,1088]{0,1:T(8,128)(2,1)}, bf16[256,1088]{0,1:T(8,128)(2,1)S(1)}, u32[]{:S(2)}, u32[]{:S(2)}) %collective-permute-start.18) | collective-permute-done | bytes 557088 | tf_op jit(solution)/shard_map/ppermute | solution.py:262
  139.0 10.9 %collective-permute-done.16 = bf16[4,128,1088]{1,2,0:T(8,128)(2,1)} collective-permute-done((bf16[4,128,1088]{1,2,0:T(8,128)(2,1)}, bf16[4,128,1088]{1,2,0:T(8,128)(2,1)}, u32[]{:S(2)}, u32[]{:S(2)}) %collective-permute-start.16) | collective-permute-done | bytes 1114144 | tf_op jit(solution)/shard_map/ppermute | solution.py:262
  160.6 6.4 %shard_map.122 = (bf16[2,256,256]{2,1,0:T(8,128)(2,1)S(1)}, bf16[2,256,256]{2,1,0:T(8,128)(2,1)S(1)}, f32[1,256]{1,0:T(1,128)S(1)}, bf16[2,256,288]{2,1,0:T(8,12...) custom-call(bf16[256,1088]{1,0:T(8,128)(2,1)S(1)} %copy-done.13, ...), custom_call_target="tpu_custom_call" | custom-call | flops 1818230784 | bytes 7942400 | tf_op jit(solution)/shard_map/pallas_call | solution.py:92
  167.7 9.5 %collective-permute-done.17.refs_5_.refs_11_ = bf16[4,144,1088]{2,1,0:T(8,128)(2,1)} collective-permute-done((bf16[4,144,1088]{2,1,0:T(8,128)(2,1)}, bf16[4,144,1088]{2,1,0:T(8,128)(2,1)}, u32[]{:S(2)}, u32[]{:S(2)}) %collective-permute-start.17) | collective-permute-done | bytes 1253408 | tf_op jit(solution)/shard_map/ppermute | solution.py:262
  177.3 7.5 %shard_map.123 = (bf16[2,256,256]{2,1,0:T(8,128)(2,1)S(1)}, bf16[2,256,256]{2,1,0:T(8,128)(2,1)S(1)}, f32[1,256]{1,0:T(1,128)S(1)}, bf16[2,256,288]{2,1,0:T(8,12...) custom-call(bf16[256,1088]{1,0:T(8,128)(2,1)S(1)} %copy-done.14, ...), custom_call_target="tpu_custom_call" | custom-call | flops 1818230784 | bytes 9613568 | tf_op jit(solution)/shard_map/pallas_call | solution.py:92
  195.2 6.1 %shard_map.120 = (bf16[2,256,256]{2,1,0:T(8,128)(2,1)S(1)}, bf16[2,256,256]{2,1,0:T(8,128)(2,1)S(1)}, f32[1,256]{1,0:T(1,128)S(1)}, bf16[2,256,288]{2,1,0:T(8,12...) custom-call(bf16[256,1088]{1,0:T(8,128)(2,1)S(1)} %add_convert_fusion.3.refs_0_.refs_8_, ...), custom_call_target="tpu_custom_call" | custom-call | flops 1818230784 | bytes 7942400 | tf_op jit(solution)/shard_map/pallas_call | solution.py:92
  203.6 8.0 %shard_map.121 = (bf16[2,256,256]{2,1,0:T(8,128)(2,1)S(1)}, bf16[2,256,256]{2,1,0:T(8,128)(2,1)S(1)}, f32[1,256]{1,0:T(1,128)S(1)}, bf16[2,256,288]{2,1,0:T(8,12...) custom-call(bf16[256,1088]{1,0:T(8,128)(2,1)S(1)} %add_convert_fusio, ...), custom_call_target="tpu_custom_call" | custom-call | flops 1818230784 | bytes 9613568 | tf_op jit(solution)/shard_map/pallas_call | solution.py:92
  237.9 7.5 %shard_map.124 = (bf16[2,128,1088]{2,1,0:T(8,128)(2,1)S(1)}, bf16[2,128,1088]{2,1,0:T(8,128)(2,1)S(1)}, bf16[2,144,1088]{2,1,0:T(8,128)(2,1)}, bf16[2,144,1088]{2,1,0:T(8,128)(2,1)}) custom-call(bf16[2,256,256]{2,1,0:T(8,128)(2,1)S(1)} %copy-done.74, bf16[2,256,256]{2,1,0:T(8,128)(2,1)S(1)} %copy-done.69, bf16[2,256,256]{2,1,0:T(8,128)(2,1)S(1)} %copy-done.105, ...), custom_call_target="tpu_custom_call" | custom-call | flops 2424307712 | bytes 9052160 | tf_op jit(solution)/shard_map/pallas_call | solution.py:92
  255.7 9.8 %shard_map.125 = bf16[3,1088,256]{2,1,0:T(8,128)(2,1)S(1)} custom-call(s32[2]{0:T(128)S(1)} %copy-done.93, bf16[1088,256]{1,0:T(8,128)(2,1)S(1)} %bitcast.66, bf16[1088,256]{1,0:T(8,128)(2,1)S(1)} %copy-done.35, bf16[1088,256]{1,0:T(8,128)(2,1)S(1)} %bitcast.72, bf16[1088,256]{1,0:T(8,128)(2,1)S(1)} %convolution_convert_fusion.refs_4_, ...), custom_call_target="tpu_custom_call" | custom-call | flops 713031680 | bytes 3916800 | tf_op jit(solution)/shard_map/pallas_call | solution.py:92
  286.0 6.7 %collective-permute-done.40 = bf16[2,128,1088]{1,2,0:T(8,128)(2,1)} collective-permute-done((bf16[2,128,1088]{1,2,0:T(8,128)(2,1)}, bf16[2,128,1088]{1,2,0:T(8,128)(2,1)}, u32[]{:S(2)}, u32[]{:S(2)}) %collective-permute-start.40) | collective-permute-done | bytes 557088 | tf_op jit(solution)/shard_map/ppermute | solution.py:262
  296.2 8.4 %collective-permute-done.41 = bf16[2,128,1088]{1,2,0:T(8,128)(2,1)} collective-permute-done((bf16[2,128,1088]{1,2,0:T(8,128)(2,1)}, bf16[2,128,1088]{1,2,0:T(8,128)(2,1)}, u32[]{:S(2)}, u32[]{:S(2)}) %collective-permute-start.41) | collective-permute-done | bytes 557088 | tf_op jit(solution)/shard_map/ppermute | solution.py:262
  312.2 8.2 %shard_map.126 = (bf16[2,136,1088]{2,1,0:T(8,128)(2,1)}, bf16[2,136,1088]{2,1,0:T(8,128)(2,1)S(1)}, bf16[2,136,1088]{2,1,0:T(8,128)(2,1)}, f32[2,136,1088]{2,1,0...) custom-call(s32[1]{0:T(128)} %bitcast.block_ref.refs_0_, ...), custom_call_target="tpu_custom_call" | custom-call | flops 2424307712 | bytes 13787136 | tf_op jit(solution)/shard_map/pallas_call | solution.py:92
  321.0 6.3 %fusion.37 = (f32[1088]{0:T(1024)S(1)}, f32[256,1088]{0,1:T(8,128)S(1)}) fusion(bf16[3264,256]{1,0:T(8,128)(2,1)S(1)} %bitcast.64, bf16[3264,1088]{1,0:T(8,128)(2,1)} %bitcast.89), kind=kOutput, calls=%fused_computation.128 | convolution fusion | flops 1818508288 | bytes 9892096 | tf_op jit(solution)/shard_map/fr,fd->rd/dot_general | solution.py:649
  340.9 7.5 %shard_map.127 = (f32[2,128,1088]{2,1,0:T(8,128)}, f32[2,128,1088]{2,1,0:T(8,128)}, f32[2,144,1088]{2,1,0:T(8,128)}, f32[2,144,1088]{2,1,0:T(8,128)}) custom-call(bf16[2,256,256]{2,1,0:T(8,128)(2,1)S(1)} %copy-done.50, bf16[2,256,256]{2,1,0:T(8,128)(2,1)S(1)} %copy-done.48, bf16[2,256,256]{2,1,0:T(8,128)(2,1)S(1)} %copy-done.77, ...), custom_call_target="tpu_custom_call" | custom-call | flops 2424307712 | bytes 11419648 | tf_op jit(solution)/shard_map/pallas_call | solution.py:92
  349.8 7.6 %shard_map.128 = (f32[2,256,1088]{2,1,0:T(8,128)}, bf16[2,256,1088]{2,1,0:T(8,128)(2,1)S(1)}) custom-call(bf16[2,256,256]{2,1,0:T(8,128)(2,1)S(1)} %copy-done.50, bf16[2,256,288]{2,1,0:T(8,128)(2,1)S(1)} %copy-done.40, bf16[2,256,256]{2,1,0:T(8,128)(2,1)S(1)} %copy-done.75, bf16[2,256,288]{2,1,0:T(8,128)(2,1)S(1)} %copy-done.65, ...), custom_call_target="tpu_custom_call" | custom-call | flops 2424307712 | bytes 10305536 | tf_op jit(solution)/shard_map/pallas_call | solution.py:92
  373.7 3.1 shard_map.131
  383.5 10.3 %collective-permute-done.44 = bf16[128,1088]{1,0:T(8,128)(2,1)S(1)} collective-permute-done((bf16[128,1088]{1,0:T(8,128)(2,1)S(1)}, bf16[128,1088]{1,0:T(8,128)(2,1)S(1)}, u32[]{:S(2)}, u32[]{:S(2)}) %collective-permute-start.44) | collective-permute-done | bytes 278560 | tf_op jit(solution)/shard_map/ppermute | solution.py:262
  394.2 8.4 %collective-permute-start.47 = (bf16[144,1088]{1,0:T(8,128)(2,1)S(1)}, bf16[144,1088]{1,0:T(8,128)(2,1)S(1)}, u32[]{:S(2)}, u32[]{:S(2)}) collective-permute-start(bf16[144,1088]{1,0:T(8,128)(2,1)S(1)} %get-tuple-element.124), channel_id=1, source_target_pairs={{0,16},{1,17},{2,18},{3,19},{4,20},{5,21},{6,22},{7,23},{8,24},{9,... | collective-permute-start | bytes 940040 | tf_op jit(solution)/shard_map/ppermute | solution.py:262
  403.6 35.9 %collective-permute-done.42 = bf16[128,1088]{1,0:T(8,128)(2,1)S(1)} collective-permute-done((bf16[128,1088]{1,0:T(8,128)(2,1)S(1)}, bf16[128,1088]{1,0:T(8,128)(2,1)S(1)}, u32[]{:S(2)}, u32[]{:S(2)}) %collective-permute-start.42) | collective-permute-done | bytes 278560 | tf_op jit(solution)/shard_map/ppermute | solution.py:262
  449.4 7.3 %collective-permute-done.31.refs_2_ = bf16[2,136,1088]{2,1,0:T(8,128)(2,1)S(1)} collective-permute-done((bf16[2,136,1088]{2,1,0:T(8,128)(2,1)}, bf16[2,136,1088]{2,1,0:T(8,128)(2,1)S(1)}, u32[]{:S(2)}, u32[]{:S(2)}) %collective-permute-start.31) | collective-permute-done | bytes 591904 | tf_op jit(solution)/shard_map/ppermute | solution.py:262
  457.6 12.2 %collective-permute-done.33.refs_3_ = bf16[2,136,1088]{2,1,0:T(8,128)(2,1)S(1)} collective-permute-done((bf16[2,136,1088]{2,1,0:T(8,128)(2,1)}, bf16[2,136,1088]{2,1,0:T(8,128)(2,1)S(1)}, u32[]{:S(2)}, u32[]{:S(2)}) %collective-permute-start.33) | collective-permute-done | bytes 591904 | tf_op jit(solution)/shard_map/ppermute | solution.py:262
  469.7 3.5 shard_map.129
  480.6 4.2 collective-permute-done.39
  484.9 14.8 %collective-permute-done.38 = bf16[136,1088]{1,0:T(8,128)(2,1)} collective-permute-done((bf16[136,1088]{1,0:T(8,128)(2,1)}, bf16[136,1088]{1,0:T(8,128)(2,1)}, u32[]{:S(2)}, u32[]{:S(2)}) %collective-permute-start.38) | collective-permute-done | bytes 295968 | tf_op jit(solution)/shard_map/ppermute | solution.py:262
  499.7 3.3 collective-permute-done.37
  (526 shorter events, 208.9 us)
Async XLA Ops:
  7.2 34.7 %all-gather.7.cloned.1.call-start = ((), (), s32[]{:S(2)}) async-start(), calls=%async_computation | async-start | bytes 1566720 | tf_op jit(solution)/shard_map/all_gather | solution.py:302
  7.9 111.8 %all-gather.9.cloned.1.call-start = ((), (), s32[]{:S(2)}) async-start(), calls=%async_computation.1 | async-start | bytes 1474560 | tf_op jit(solution)/shard_map/all_gather | solution.py:302
  9.7 113.8 %all-gather.11.cloned.1.call-start = ((), (), s32[]{:S(2)}) async-start(), calls=%async_computation.2 | async-start | bytes 1658880 | tf_op jit(solution)/shard_map/all_gather | solution.py:302
  19.6 25.4 %collective-permute-start.2 = (bf16[1632]{0:T(1024)(128)(2,1)S(1)}, bf16[1632]{0:T(1024)(128)(2,1)S(1)}, u32[]{:S(2)}, u32[]{:S(2)}) collective-permute-start(bf16[1632]{0:T(1024)(128)(2,1)S(1)} %pad_maximum_fusion.3), channel_id=1, source_target_pairs={{0,4},{1,5},{2,6},{3,7},{4,0},{5,1},{6,2},{7,3},{8,12},{9,13},{10,... | collective-permute-start | bytes 9800 | tf_op jit(solution)/shard_map/ppermute | solution.py:262
  41.9 29.4 %collective-permute-start.6 = (bf16[4,136,1088]{2,1,0:T(8,128)(2,1)}, bf16[4,136,1088]{2,1,0:T(8,128)(2,1)}, u32[]{:S(2)}, u32[]{:S(2)}) collective-permute-start(bf16[4,136,1088]{2,1,0:T(8,128)(2,1)} %bitcast.77), channel_id=1, source_target_pairs={{0,4},{1,5},{2,6},{3,7},{4,0},{5,1},{6,2},{7,3},{8,12},{9,13},{10,... | collective-permute-start | bytes 3551240 | tf_op jit(solution)/shard_map/ppermute | solution.py:262
  43.4 31.3 %collective-permute-start.7 = (bf16[4,136,1088]{2,1,0:T(8,128)(2,1)}, bf16[4,136,1088]{2,1,0:T(8,128)(2,1)}, u32[]{:S(2)}, u32[]{:S(2)}) collective-permute-start(bf16[4,136,1088]{2,1,0:T(8,128)(2,1)} %bitcast.78), channel_id=1, source_target_pairs={{0,2},{1,3},{2,0},{3,1},{4,6},{5,7},{6,4},{7,5},{8,10},{9,11},{10,... | collective-permute-start | bytes 3551240 | tf_op jit(solution)/shard_map/ppermute | solution.py:262
  49.0 29.2 %collective-permute-start.4 = (bf16[6528]{0:T(1024)(128)(2,1)S(1)}, bf16[6528]{0:T(1024)(128)(2,1)S(1)}, u32[]{:S(2)}, u32[]{:S(2)}) collective-permute-start(bf16[6528]{0:T(1024)(128)(2,1)S(1)} %pad_maximum_fusion.1), channel_id=1, source_target_pairs={{0,16},{1,17},{2,18},{3,19},{4,20},{5,21},{6,22},{7,23},{8,24},{9,... | collective-permute-start | bytes 39176 | tf_op jit(solution)/shard_map/ppermute | solution.py:262
  50.4 42.0 %collective-permute-start.5 = (bf16[4,136,1088]{2,1,0:T(8,128)(2,1)S(1)}, bf16[4,136,1088]{2,1,0:T(8,128)(2,1)}, u32[]{:S(2)}, u32[]{:S(2)}) collective-permute-start(bf16[4,136,1088]{2,1,0:T(8,128)(2,1)S(1)} %bitcast.79), channel_id=1, source_target_pairs={{0,1},{1,0},{2,3},{3,2},{4,5},{5,4},{6,7},{7,6},{8,9},{9,8},{10,11... | collective-permute-start | bytes 3551240 | tf_op jit(solution)/shard_map/ppermute | solution.py:262
  92.4 33.0 %collective-permute-start.20 = (bf16[256,1088]{0,1:T(8,128)(2,1)}, bf16[256,1088]{0,1:T(8,128)(2,1)}, u32[]{:S(2)}, u32[]{:S(2)}) collective-permute-start(bf16[256,1088]{0,1:T(8,128)(2,1)} %copy.46), channel_id=1, source_target_pairs={{0,2},{1,3},{2,0},{3,1},{4,6},{5,7},{6,4},{7,5},{8,10},{9,11},{10,... | collective-permute-start | bytes 1671176 | tf_op jit(solution)/shard_map/ppermute | solution.py:262
  122.1 27.8 %collective-permute-start.16 = (bf16[4,128,1088]{1,2,0:T(8,128)(2,1)}, bf16[4,128,1088]{1,2,0:T(8,128)(2,1)}, u32[]{:S(2)}, u32[]{:S(2)}) collective-permute-start(bf16[4,128,1088]{1,2,0:T(8,128)(2,1)} %copy.49), channel_id=1, source_target_pairs={{0,4},{1,5},{2,6},{3,7},{4,0},{5,1},{6,2},{7,3},{8,12},{9,13},{10,... | collective-permute-start | bytes 3342344 | tf_op jit(solution)/shard_map/ppermute | solution.py:262
  123.5 53.7 %collective-permute-start.17 = (bf16[4,144,1088]{2,1,0:T(8,128)(2,1)}, bf16[4,144,1088]{2,1,0:T(8,128)(2,1)}, u32[]{:S(2)}, u32[]{:S(2)}) collective-permute-start(bf16[4,144,1088]{2,1,0:T(8,128)(2,1)} %bitcast.73), channel_id=1, source_target_pairs={{0,4},{1,5},{2,6},{3,7},{4,0},{5,1},{6,2},{7,3},{8,12},{9,13},{10,... | collective-permute-start | bytes 3760136 | tf_op jit(solution)/shard_map/ppermute | solution.py:262
  136.5 129.1 %collective-permute-start.27 = (bf16[256,1088]{0,1:T(8,128)(2,1)}, bf16[256,1088]{0,1:T(8,128)(2,1)}, u32[]{:S(2)}, u32[]{:S(2)}) collective-permute-start(bf16[256,1088]{0,1:T(8,128)(2,1)} %copy.77), channel_id=1, source_target_pairs={{0,1},{1,0},{2,3},{3,2},{4,5},{5,4},{6,7},{7,6},{8,9},{9,8},{10,11... | collective-permute-start | bytes 1671176 | tf_op jit(solution)/shard_map/ppermute | solution.py:262
  152.2 39.6 %collective-permute-start.14 = (bf16[256,1088]{0,1:T(8,128)(2,1)}, bf16[256,1088]{0,1:T(8,128)(2,1)}, u32[]{:S(2)}, u32[]{:S(2)}) collective-permute-start(bf16[256,1088]{0,1:T(8,128)(2,1)} %copy.44), channel_id=1, source_target_pairs={{0,1},{1,0},{2,3},{3,2},{4,5},{5,4},{6,7},{7,6},{8,9},{9,8},{10,11... | collective-permute-start | bytes 1671176 | tf_op jit(solution)/shard_map/ppermute | solution.py:262
  152.2 118.0 %collective-permute-start.28 = (bf16[256,1088]{0,1:T(8,128)(2,1)}, bf16[256,1088]{0,1:T(8,128)(2,1)}, u32[]{:S(2)}, u32[]{:S(2)}) collective-permute-start(bf16[256,1088]{0,1:T(8,128)(2,1)} %bitcast.7), channel_id=1, source_target_pairs={{0,1},{1,0},{2,3},{3,2},{4,5},{5,4},{6,7},{7,6},{8,9},{9,8},{10,11... | collective-permute-start | bytes 1671176 | tf_op jit(solution)/shard_map/ppermute | solution.py:262
  190.4 28.2 %collective-permute-start.23 = (bf16[256,1088]{0,1:T(8,128)(2,1)}, bf16[256,1088]{0,1:T(8,128)(2,1)}, u32[]{:S(2)}, u32[]{:S(2)}) collective-permute-start(bf16[256,1088]{0,1:T(8,128)(2,1)} %copy.66), channel_id=1, source_target_pairs={{0,1},{1,0},{2,3},{3,2},{4,5},{5,4},{6,7},{7,6},{8,9},{9,8},{10,11... | collective-permute-start | bytes 1671176 | tf_op jit(solution)/shard_map/ppermute | solution.py:262
  224.8 22.3 %collective-permute-start.24 = (bf16[256,1088]{0,1:T(8,128)(2,1)}, bf16[256,1088]{0,1:T(8,128)(2,1)}, u32[]{:S(2)}, u32[]{:S(2)}) collective-permute-start(bf16[256,1088]{0,1:T(8,128)(2,1)} %copy.68), channel_id=1, source_target_pairs={{0,2},{1,3},{2,0},{3,1},{4,6},{5,7},{6,4},{7,5},{8,10},{9,11},{10,... | collective-permute-start | bytes 1671176 | tf_op jit(solution)/shard_map/ppermute | solution.py:262
  265.5 41.3 %collective-permute-start.25 = (bf16[3,8,136,256]{3,2,1,0:T(8,128)(2,1)S(1)}, bf16[3,8,136,256]{3,2,1,0:T(8,128)(2,1)}, u32[]{:S(2)}, u32[]{:S(2)}) collective-permute-start(bf16[3,8,136,256]{3,2,1,0:T(8,128)(2,1)S(1)} %bitcast.62), channel_id=1, source_target_pairs={{0,1},{1,0},{2,3},{3,2},{4,5},{5,4},{6,7},{7,6},{8,9},{9,8},{10,11... | collective-permute-start | bytes 5013512 | tf_op jit(solution)/shard_map/ppermute | solution.py:262
  278.3 26.3 %collective-permute-start.41 = (bf16[2,128,1088]{1,2,0:T(8,128)(2,1)}, bf16[2,128,1088]{1,2,0:T(8,128)(2,1)}, u32[]{:S(2)}, u32[]{:S(2)}) collective-permute-start(bf16[2,128,1088]{1,2,0:T(8,128)(2,1)} %copy.94), channel_id=1, source_target_pairs={{0,4},{1,5},{2,6},{3,7},{4,0},{5,1},{6,2},{7,3},{8,12},{9,13},{10,... | collective-permute-start | bytes 1671176 | tf_op jit(solution)/shard_map/ppermute | solution.py:262
  283.1 23.7 %collective-permute-start.26 = (bf16[1,8,136,256]{3,2,1,0:T(8,128)(2,1)}, bf16[1,8,136,256]{3,2,1,0:T(8,128)(2,1)}, u32[]{:S(2)}, u32[]{:S(2)}) collective-permute-start(bf16[1,8,136,256]{3,2,1,0:T(8,128)(2,1)} %bitcast.81), channel_id=1, source_target_pairs={{0,1},{1,0},{2,3},{3,2},{4,5},{5,4},{6,7},{7,6},{8,9},{9,8},{10,11... | collective-permute-start | bytes 1671176 | tf_op jit(solution)/shard_map/ppermute | solution.py:262
  284.3 87.8 %collective-permute-start.45 = (bf16[2,144,1088]{2,1,0:T(8,128)(2,1)}, bf16[2,144,1088]{2,1,0:T(8,128)(2,1)}, u32[]{:S(2)}, u32[]{:S(2)}) collective-permute-start(bf16[2,144,1088]{2,1,0:T(8,128)(2,1)} %get-tuple-element.97), channel_id=1, source_target_pairs={{0,4},{1,5},{2,6},{3,7},{4,0},{5,1},{6,2},{7,3},{8,12},{9,13},{10,... | collective-permute-start | bytes 1880072 | tf_op jit(solution)/shard_map/ppermute | solution.py:262
  292.6 81.0 %collective-permute-start.46 = (bf16[2,144,1088]{2,1,0:T(8,128)(2,1)}, bf16[2,144,1088]{2,1,0:T(8,128)(2,1)}, u32[]{:S(2)}, u32[]{:S(2)}) collective-permute-start(bf16[2,144,1088]{2,1,0:T(8,128)(2,1)} %get-tuple-element.98), channel_id=1, source_target_pairs={{0,4},{1,5},{2,6},{3,7},{4,0},{5,1},{6,2},{7,3},{8,12},{9,13},{10,... | collective-permute-start | bytes 1880072 | tf_op jit(solution)/shard_map/ppermute | solution.py:262
  358.8 86.7 %collective-permute-start.29 = (bf16[2,256,1088]{1,2,0:T(8,128)(2,1)}, bf16[2,256,1088]{1,2,0:T(8,128)(2,1)}, u32[]{:S(2)}, u32[]{:S(2)}) collective-permute-start(bf16[2,256,1088]{1,2,0:T(8,128)(2,1)} %copy.88), channel_id=1, source_target_pairs={{0,1},{1,0},{2,3},{3,2},{4,5},{5,4},{6,7},{7,6},{8,9},{9,8},{10,11... | collective-permute-start | bytes 3342344 | tf_op jit(solution)/shard_map/ppermute | solution.py:262
  372.1 30.5 %collective-permute-start.34 = (bf16[2,136,1088]{2,1,0:T(8,128)(2,1)S(1)}, bf16[2,136,1088]{2,1,0:T(8,128)(2,1)S(1)}, u32[]{:S(2)}, u32[]{:S(2)}) collective-permute-start(bf16[2,136,1088]{2,1,0:T(8,128)(2,1)S(1)} %copy-done.97), channel_id=1, source_target_pairs={{0,4},{1,5},{2,6},{3,7},{4,0},{5,1},{6,2},{7,3},{8,12},{9,13},{10,... | collective-permute-start | bytes 1775624 | tf_op jit(solution)/shard_map/ppermute | solution.py:262
  376.8 63.7 %collective-permute-start.49 = (bf16[144,1088]{1,0:T(8,128)(2,1)S(1)}, bf16[144,1088]{1,0:T(8,128)(2,1)S(1)}, u32[]{:S(2)}, u32[]{:S(2)}) collective-permute-start(bf16[144,1088]{1,0:T(8,128)(2,1)S(1)} %get-tuple-element.126), channel_id=1, source_target_pairs={{0,8},{1,9},{2,10},{3,11},{4,12},{5,13},{6,14},{7,15},{8,0},{9,1},... | collective-permute-start | bytes 940040 | tf_op jit(solution)/shard_map/ppermute | solution.py:262
  393.8 47.2 %collective-permute-start.48 = (bf16[144,1088]{1,0:T(8,128)(2,1)S(1)}, bf16[144,1088]{1,0:T(8,128)(2,1)S(1)}, u32[]{:S(2)}, u32[]{:S(2)}) collective-permute-start(bf16[144,1088]{1,0:T(8,128)(2,1)S(1)} %get-tuple-element.125), channel_id=1, source_target_pairs={{0,24},{1,25},{2,26},{3,27},{4,28},{5,29},{6,30},{7,31},{8,16},{9,... | collective-permute-start | bytes 940040 | tf_op jit(solution)/shard_map/ppermute | solution.py:262
  394.2 48.3 %collective-permute-start.47 = (bf16[144,1088]{1,0:T(8,128)(2,1)S(1)}, bf16[144,1088]{1,0:T(8,128)(2,1)S(1)}, u32[]{:S(2)}, u32[]{:S(2)}) collective-permute-start(bf16[144,1088]{1,0:T(8,128)(2,1)S(1)} %get-tuple-element.124), channel_id=1, source_target_pairs={{0,16},{1,17},{2,18},{3,19},{4,20},{5,21},{6,22},{7,23},{8,24},{9,... | collective-permute-start | bytes 940040 | tf_op jit(solution)/shard_map/ppermute | solution.py:262
  402.6 36.9 %collective-permute-start.42 = (bf16[128,1088]{1,0:T(8,128)(2,1)S(1)}, bf16[128,1088]{1,0:T(8,128)(2,1)S(1)}, u32[]{:S(2)}, u32[]{:S(2)}) collective-permute-start(bf16[128,1088]{1,0:T(8,128)(2,1)S(1)} %get-tuple-element.120), channel_id=1, source_target_pairs={{0,16},{1,17},{2,18},{3,19},{4,20},{5,21},{6,22},{7,23},{8,24},{9,... | collective-permute-start | bytes 835592 | tf_op jit(solution)/shard_map/ppermute | solution.py:262
  441.1 28.6 %collective-permute-start.33 = (bf16[2,136,1088]{2,1,0:T(8,128)(2,1)}, bf16[2,136,1088]{2,1,0:T(8,128)(2,1)S(1)}, u32[]{:S(2)}, u32[]{:S(2)}) collective-permute-start(bf16[2,136,1088]{2,1,0:T(8,128)(2,1)} %add_convert_fusion.1), channel_id=1, source_target_pairs={{0,4},{1,5},{2,6},{3,7},{4,0},{5,1},{6,2},{7,3},{8,12},{9,13},{10,... | collective-permute-start | bytes 1775624 | tf_op jit(solution)/shard_map/ppermute | solution.py:262
  442.6 27.2 %collective-permute-start.35 = (bf16[2,136,1088]{2,1,0:T(8,128)(2,1)}, bf16[2,136,1088]{2,1,0:T(8,128)(2,1)S(1)}, u32[]{:S(2)}, u32[]{:S(2)}) collective-permute-start(bf16[2,136,1088]{2,1,0:T(8,128)(2,1)} %add_convert_fusion), channel_id=1, source_target_pairs={{0,2},{1,3},{2,0},{3,1},{4,6},{5,7},{6,4},{7,5},{8,10},{9,11},{10,... | collective-permute-start | bytes 1775624 | tf_op jit(solution)/shard_map/ppermute | solution.py:262
  475.6 24.1 %collective-permute-start.38 = (bf16[136,1088]{1,0:T(8,128)(2,1)}, bf16[136,1088]{1,0:T(8,128)(2,1)}, u32[]{:S(2)}, u32[]{:S(2)}) collective-permute-start(bf16[136,1088]{1,0:T(8,128)(2,1)} %get-tuple-element.117), channel_id=1, source_target_pairs={{0,24},{1,25},{2,26},{3,27},{4,28},{5,29},{6,30},{7,31},{8,16},{9,... | collective-permute-start | bytes 887816 | tf_op jit(solution)/shard_map/ppermute | solution.py:262
  477.2 25.8 %collective-permute-start.37 = (bf16[136,1088]{1,0:T(8,128)(2,1)S(1)}, bf16[136,1088]{1,0:T(8,128)(2,1)}, u32[]{:S(2)}, u32[]{:S(2)}) collective-permute-start(bf16[136,1088]{1,0:T(8,128)(2,1)S(1)} %get-tuple-element.116), channel_id=1, source_target_pairs={{0,16},{1,17},{2,18},{3,19},{4,20},{5,21},{6,22},{7,23},{8,24},{9,... | collective-permute-start | bytes 887816 | tf_op jit(solution)/shard_map/ppermute | solution.py:262
  478.4 26.8 %collective-permute-start.30 = (bf16[256,1088]{0,1:T(8,128)(2,1)S(1)}, bf16[256,1088]{0,1:T(8,128)(2,1)}, u32[]{:S(2)}, u32[]{:S(2)}) collective-permute-start(bf16[256,1088]{0,1:T(8,128)(2,1)S(1)} %copy.90), channel_id=1, source_target_pairs={{0,2},{1,3},{2,0},{3,1},{4,6},{5,7},{6,4},{7,5},{8,10},{9,11},{10,... | collective-permute-start | bytes 1671176 | tf_op jit(solution)/shard_map/ppermute | solution.py:262
  (173 other events, 1574.3 us)
Sparse Core Ops, SparseCore 0:
  9.6 32.2 all-gather.6
  43.5 29.5 all-gather.8
  74.7 31.8 all-gather.10

commit v7 on v6

--- a/solution.py
+++ b/solution.py
@@ -2,7 +2,6 @@
 import jax.numpy as jnp
 from jax import lax
 from jax.experimental import pallas as pl
-from jax.experimental.layout import Layout, with_layout_constraint
 from jax.experimental.pallas import tpu as pltpu
 from jax.sharding import PartitionSpec as P
 
@@ -10,7 +9,7 @@
 HEADS = 17
 HEAD_SIZE = 64
 FF = 4352
-VMEM_LIMIT = 48 * 1024 * 1024
+VMEM_LIMIT = 60 * 1024 * 1024
 
 
 epsilon = 1e-05
@@ -80,11 +79,24 @@
         ]
         for copy in copies[:count]:
             copy.start()
-        for copy in copies[:count]:
-            copy.wait()
-        body(*scalar_refs, *buffers)
-        for copy in copies[count:]:
-            copy.start()
+        waiting = list(range(count))
+        unsent = list(range(len(outs)))
+
+        def need(*numbers):
+            for number in numbers or tuple(waiting):
+                if number in waiting:
+                    waiting.remove(number)
+                    copies[number].wait()
+
+        def send(*numbers):
+            for number in numbers:
+                unsent.remove(number)
+                copies[count + number].start()
+
+        body(need, send, *scalar_refs, *buffers)
+        if waiting:
+            need()
+        send(*tuple(unsent))
         for copy in copies[count:]:
             copy.wait()
 
@@ -102,10 +114,6 @@
     )(*scalars, *operands, *earlier)
 
 
-def row_major(values):
-    return with_layout_constraint(values, Layout(major_to_minor=tuple(range(values.ndim))))
-
-
 def product(left, right, left_axis, right_axis):
     return lax.dot_general(
         left, right, (((left_axis,), (right_axis,)), ((), ())), preferred_element_type=jnp.float32
@@ -116,7 +124,8 @@
     width, rows = queries.shape
     low = jnp.bfloat16
 
-    def body(span_ref, q_ref, k_ref, v_ref, do_ref, log_ref, out_ref):
+    def body(need, send, span_ref, q_ref, k_ref, v_ref, do_ref, log_ref, out_ref):
+        need()
         begin, finish = span_ref[0], span_ref[1]
 
         def inside(axis):
@@ -149,88 +158,88 @@
     )[0]
 
 
-def mlp_block(row_pair, grad_pair, weights, biases, before, last):
-    rows, width = row_pair[0].shape
+def mlp_block(row_pair, grad_pair, weights, biases):
+    width, rows = row_pair[0].shape
     low, wide = jnp.bfloat16, jnp.float32
     hidden = [2 * weight.shape[1] for weight in weights]
     outs = []
     for count in hidden:
-        outs += [((2, rows, count), low), ((2, rows, count), low), ((1, count), wide)]
+        outs += [((2, count, rows), low), ((2, count, rows), low), ((count, 1), wide)]
     sums = len(outs)
-    if last:
-        outs += [((rows, width), wide), ((rows, width), low)]
-    else:
-        outs += [((2, rows, width), wide)]
+    outs += [((width, rows), wide), ((width, rows), low)]
     number = len(weights)
 
-    def body(*refs):
+    def body(need, send, *refs):
         row_refs, grad_refs = refs[:2], refs[2:4]
         weight_refs, bias_refs = refs[4 : 4 + number], refs[4 + number : 4 + 2 * number]
         out_refs = refs[-len(outs) :]
-        for side in range(2):
-            total = None if before is None else refs[4 + 2 * number][side]
+        for side in (1, 0):
+            total = None
             for place in range(number):
+                need(side, 2 + side, 4 + place, 4 + number + place)
                 weight, count = weight_refs[place], hidden[place]
                 up = weight[0:2].reshape(count, width)
                 down = weight[2:4].reshape(count, width)
-                up_sum = product(row_refs[side][...], up, 1, 1) + bias_refs[place][...]
+                up_sum = product(up, row_refs[side][...], 1, 0) + bias_refs[place][...]
                 activated, slope = gelu_parts(up_sum)
-                grad_act = product(grad_refs[side][...], down, 1, 1)
+                grad_act = product(down, grad_refs[side][...], 1, 0)
                 grad_up = (grad_act * slope).astype(low)
                 act_ref, up_ref, sum_ref = out_refs[3 * place : 3 * place + 3]
                 act_ref[side] = activated.astype(low)
                 up_ref[side] = grad_up
-                columns = jnp.sum(grad_up.astype(wide), axis=0, keepdims=True)
-                sum_ref[...] = columns if side == 0 else sum_ref[...] + columns
-                term = product(grad_up, up, 1, 0)
+                columns = jnp.sum(grad_up.astype(wide), axis=1, keepdims=True)
+                sum_ref[...] = columns if side == 1 else sum_ref[...] + columns
+                if side == 0:
+                    send(3 * place, 3 * place + 1, 3 * place + 2)
+                term = product(up, grad_up, 0, 0)
                 total = term if total is None else total + term
-            if last:
-                out = out_refs[sums + side]
-                out[...] = total.astype(out.dtype)
-            else:
-                out_refs[sums][side] = total
+            out = out_refs[sums + side]
+            out[...] = total.astype(out.dtype)
+            send(sums + side)
 
     operands = (*row_pair, *grad_pair, *weights, *biases)
-    operands += () if before is None else (before,)
     result = local_kernel(body, outs, operands, 12 * rows * width * sum(hidden))
     return ([result[3 * place : 3 * place + 3] for place in range(number)], result[sums:])
 
 
 def mlp_weight_grads(blocks, rows, grads, kind, earlier):
-    width = rows[0].shape[1]
+    width = rows[0].shape[0]
     operands, outs, number = [], [], len(rows)
+    operands += [*rows, *grads]
     for near, far in blocks:
         operands += [near[0], far[0], near[1], far[1]]
-        count = near[0].shape[2]
+        count = near[0].shape[1]
         outs += [((2, count // 2, width), kind)] * 2
 
-    def body(*refs):
-        row_refs = refs[len(operands) : len(operands) + number]
-        grad_refs = refs[len(operands) + number : len(operands) + 2 * number]
+    def body(need, send, *refs):
+        row_refs, grad_refs = refs[:number], refs[number : 2 * number]
         out_refs = refs[-len(outs) :]
+        need(*range(2 * number))
         for place in range(len(blocks)):
-            sources = refs[4 * place : 4 * place + 4]
-            for out, pair, others in (
-                (out_refs[2 * place], sources[2:], row_refs),
-                (out_refs[2 * place + 1], sources[:2], grad_refs),
-            ):
+            start = 2 * number + 4 * place
+            need(*range(start, start + 4))
+            sources = refs[start : start + 4]
+            for which, pair, others in ((0, sources[2:], row_refs), (1, sources[:2], grad_refs)):
+                out = out_refs[2 * place + which]
                 total = None
-                for which in range(number):
-                    term = product(pair[which // 2][which % 2], others[which][...], 0, 0)
+                for group in range(number):
+                    term = product(pair[group // 2][group % 2], others[group][...], 1, 1)
                     total = term if total is None else total + term
                 out[...] = total.reshape(out.shape).astype(kind)
-
-    flops = sum(16 * rows[0].shape[0] * near[0].shape[2] * width for near, far in blocks)
-    result = local_kernel(body, outs, (*operands, *rows, *grads), flops, (), earlier)
+                send(2 * place + which)
+
+    flops = sum(16 * rows[0].shape[1] * near[0].shape[1] * width for near, far in blocks)
+    result = local_kernel(body, outs, operands, flops, (), earlier)
     return [tuple(result[2 * place : 2 * place + 2]) for place in range(len(blocks))]
 
 
 def mlp_outputs(blocks, weights, earlier):
-    rows, width = blocks[0][0][0].shape[1], weights[0].shape[2]
+    rows, width = blocks[0][0][0].shape[2], weights[0].shape[2]
     number = len(weights)
     operands = [near[0] for near, far in blocks] + [far[0] for near, far in blocks]
 
-    def body(*refs):
+    def body(need, send, *refs):
+        need()
         weight_refs, out_refs = refs[2 * number : 3 * number], refs[-2:]
         for group in range(2):
             for side in range(2):
@@ -238,11 +247,11 @@
                 for place in range(number):
                     weight = weight_refs[place]
                     down = weight[2:4].reshape(2 * weight.shape[1], width)
-                    term = product(refs[group * number + place][side], down, 1, 0)
+                    term = product(down, refs[group * number + place][side], 0, 0)
                     total = term if total is None else total + term
                 out_refs[side][group] = total.astype(out_refs[side].dtype)
 
-    outs = [((2, rows, width), jnp.float32), ((2, rows, width), jnp.bfloat16)]
+    outs = [((2, width, rows), jnp.float32), ((2, width, rows), jnp.bfloat16)]
     flops = 16 * rows * width * sum(weight.shape[1] for weight in weights)
     return local_kernel(body, outs, (*operands, *weights), flops, (), earlier)
 
@@ -335,7 +344,7 @@
         + [pl.BlockSpec(memory_space=pl.ANY)] * len(arrays),
         out_specs=(pl.BlockSpec(memory_space=pltpu.VMEM), pl.BlockSpec(memory_space=pltpu.VMEM)),
         scratch_shapes=[pltpu.SemaphoreType.DMA((count,))],
-        compiler_params=pltpu.CompilerParams(vmem_limit_bytes=VMEM_LIMIT),
+        compiler_params=pltpu.CompilerParams(vmem_limit_bytes=24 * 1024 * 1024),
         cost_estimate=pl.CostEstimate(
             flops=0, bytes_accessed=4 * count * rows * width, transcendentals=0
         ),
@@ -364,12 +373,12 @@
     devices = lax.axis_size("dev")
     low = jnp.bfloat16
     first, mixed = sources
-    own, width = first[0].shape
+    width, own = first[0].shape
     if devices != 32:
         product = jnp.concatenate(
             [
-                jnp.dot(grads[0].reshape(3 * width, own), first[0], preferred_element_type=jnp.float32),
-                jnp.dot(grads[1], mixed[0], preferred_element_type=jnp.float32),
+                jnp.einsum('fr,dr->fd', grads[0].reshape(3 * width, own), first[0], preferred_element_type=jnp.float32),
+                jnp.einsum('fr,dr->fd', grads[1], mixed[0], preferred_element_type=jnp.float32),
             ],
             axis=0,
         ).astype(low)
@@ -395,11 +404,12 @@
 def attn_products(mine, beside, pairs):
     block = (lax.axis_index("dev") & 7).astype(jnp.int32).reshape(1)
     rows = mine[0].shape[2]
-    width = pairs[0][0].shape[1]
+    width = pairs[0][0].shape[0]
     low, wide = jnp.bfloat16, jnp.float32
     kinds = (low, low, low, wide, wide, low, wide, wide)
 
-    def body(block_ref, *refs):
+    def body(need, send, block_ref, *refs):
+        need()
         (three, last), (three_beside, last_beside) = refs[:2], refs[2:4]
         pair_refs, other_refs = refs[4:6], refs[6:8]
         outs = refs[8:]
@@ -414,9 +424,10 @@
                         last_beside[0, target] if matrix == 3 else three_beside[matrix, target]
                     )
                     side = 1 if matrix == 3 else 0
-                    value = product(left, pair_refs[side][...], 1, 0)
-                    value = value + product(left_beside, other_refs[side][...], 1, 0)
+                    value = product(left, pair_refs[side][...], 1, 1)
+                    value = value + product(left_beside, other_refs[side][...], 1, 1)
                     out[number] = value.astype(out.dtype)
+                send(2 * place + half)
 
     outs = local_kernel(
         body,
@@ -435,7 +446,7 @@
             shard, "dev", axis=0, tiled=True, axis_index_groups=same_low(devices)
         )
         return (both, None)
-    cut = 128
+    cut = shard.shape[0] // 2
     one, two = gather_z(shard[:cut]), gather_z(shard[cut:])
     return ((one, swap(one, 4)), two)
 
@@ -497,7 +508,8 @@
     rows, width = own[0].shape[1:]
     count = len(others[0])
 
-    def body(layer_ref, *refs):
+    def body(need, send, layer_ref, *refs):
+        need()
         outs = refs[-4:]
         for mask, out in enumerate(outs):
             goal = layer_ref[0] ^ mask
@@ -542,10 +554,10 @@
     head_shape = (total_rows, HEADS, HEAD_SIZE)
 
     full_vec = gather_vectors(vectors)
-    grad_down = row_major(jnp.where(live, cotangent, jnp.zeros_like(cotangent)))
+    grad_down = jnp.where(live, cotangent, jnp.zeros_like(cotangent))
     full_proj, full_out, attn_ready = gather_attn(attn_weight)
     gathered = gather_hidden(mlp_weight)
-    grad_down_rows = gather_rows(grad_down)
+    grad_down_rows = gather_rows(grad_down.T)
 
     (
         gain_one,
@@ -563,8 +575,8 @@
 
     inputs = tokens.astype(jnp.float32)
     first_out, normed_one, factor_one = normalize(inputs, gain_one, shift_one)
-    first_low = row_major(first_out.astype(low))
-    first_beside = swap(first_low, 1)
+    first_low = first_out.astype(low)
+    first_beside = swap(first_low.T, 1)
     projected = jnp.einsum(
         "rd,od->ro", first_low, full_proj, preferred_element_type=jnp.float32
     )
@@ -572,8 +584,8 @@
     keys = projected[:, width : 2 * width].astype(low).reshape(head_shape)
     values = (projected[:, 2 * width :] + value_bias).astype(low).reshape(head_shape)
     mixed, log_total = attend(queries, keys, values, allowed, scale)
-    mixed_low = row_major(mixed.reshape(total_rows, width).astype(low))
-    mixed_beside = swap(mixed_low, 1)
+    mixed_low = mixed.reshape(total_rows, width).astype(low)
+    mixed_beside = swap(mixed_low.T, 1)
     branch = (
         jnp.einsum(
             "rd,od->ro", mixed_low, full_out, preferred_element_type=jnp.float32
@@ -582,34 +594,29 @@
     )
     middle = inputs + branch
     second_out, normed_two, factor_two = normalize(middle, gain_two, shift_two)
-    second_own = row_major(second_out.astype(low))
+    second_own = second_out.astype(low).T
     near, far = gather_rows(second_own)
-    parts = hidden_parts(gathered, here, devices, second_own)
+    parts = hidden_parts(gathered, here, devices, projected)
     near_grads, far_grads = grad_down_rows
 
-    sides = []
-    near_sum = far_sum = None
+    every = sum(parts, [])
+    weights = [part[0] for part in every]
+    biases = [pick_blocks(up_bias, *part[1:]).reshape(-1, 1) for part in every]
+    far_blocks, far_sum = mlp_block(far, far_grads, weights, biases)
+    near_blocks, near_sum = mlp_block(near, near_grads, weights, biases)
     grad_up_bias = jnp.zeros_like(up_bias)
-    for place, side in enumerate(parts):
-        weights = [part[0] for part in side]
-        biases = [pick_blocks(up_bias, *part[1:]).reshape(1, -1) for part in side]
-        last = place == len(parts) - 1
-        near_blocks, near_sum = mlp_block(near, near_grads, weights, biases, near_sum, last)
-        far_blocks, far_sum = mlp_block(far, far_grads, weights, biases, far_sum, last)
-        if not last:
-            near_sum, far_sum = near_sum[0], far_sum[0]
-        for part, one, two in zip(side, near_blocks, far_blocks):
-            grad_up_bias = put_blocks(grad_up_bias, *part[1:], (one[2] + two[2]).reshape(-1))
-        sides.append([(one[:2], two[:2]) for one, two in zip(near_blocks, far_blocks)])
+    for part, one, two in zip(every, near_blocks, far_blocks):
+        grad_up_bias = put_blocks(grad_up_bias, *part[1:], (one[2] + two[2]).reshape(-1))
+    blocks = [(one[:2], two[:2]) for one, two in zip(near_blocks, far_blocks)]
+    own_count = len(parts[0])
     far_total = (far_sum[0] + swap(far_sum[1], 1).astype(jnp.float32)).astype(low)
-    near_taken = swap(near_sum[1], 1)
-    grad_second = near_sum[0] + near_taken.astype(jnp.float32)
+    grad_second = near_sum[0] + swap(near_sum[1], 1).astype(jnp.float32)
     all_rows, all_grads = near + far, near_grads + far_grads
-    other_grads = [
-        mlp_weight_grads(side, all_rows, all_grads, low, (far_total,)) for side in sides[1:]
-    ]
+    other_grads = []
+    if len(parts) > 1:
+        other_grads = mlp_weight_grads(blocks[own_count:], all_rows, all_grads, low, (far_total,))
     far_taken = after(swap(far_total, 2), other_grads)
-    grad_second = grad_second + far_taken.astype(jnp.float32)
+    grad_second = (grad_second + far_taken.astype(jnp.float32)).T
 
     grad_down_wide = grad_down.astype(jnp.float32)
     grad_down_bias = jnp.sum(grad_down_wide, axis=0)
@@ -630,18 +637,14 @@
         log_total.reshape(HEADS, 1, total_rows),
     )
     attn_finish, attn_sent = scatter_attn(
-        (grad_features, grad_branch.T), ((first_low, first_beside), (mixed_low, mixed_beside))
-    )
-    own_grads = mlp_weight_grads(sides[0], all_rows, all_grads, jnp.float32, attn_sent)
-    down_keep, down_give = mlp_outputs(
-        sum(sides, []),
-        [part[0] for side in parts for part in side],
-        sum(own_grads, ()),
-    )
+        (grad_features, grad_branch.T), ((first_low.T, first_beside), (mixed_low.T, mixed_beside))
+    )
+    own_grads = mlp_weight_grads(blocks[:own_count], all_rows, all_grads, jnp.float32, attn_sent)
+    down_keep, down_give = mlp_outputs(blocks, weights, sum(own_grads, ()))
     down_taken = swap(down_give, 1).astype(jnp.float32)
-    down = down_keep[0] + down_taken[0]
-    down_far = swap((down_keep[1] + down_taken[1]).astype(low), 2).astype(jnp.float32)
-    mlp_share = scatter_hidden(own_grads, sum(other_grads, []), attn_sent)
+    down = (down_keep[0] + down_taken[0]).T
+    down_far = swap((down_keep[1] + down_taken[1]).astype(low), 2).astype(jnp.float32).T
+    mlp_share = scatter_hidden(own_grads, other_grads, attn_sent)
     attn_share = attn_finish()
     grad_features = after(grad_features, attn_sent).reshape(3 * width, total_rows)
     output = jnp.where(live, middle + (down + down_far + down_bias), 0.0).astype(low)

time: 526 us -> 454 us (0.86); the launches traced: 516 us -> 450 us
  local copies, waits for them, and re-layouts: 114 us -> 25.1 us
  waiting for transfers between devices: 194 us -> 222 us
    unnamed x299 -> x121, local copies, waits for them, and re-layouts: 50.4 us -> 8.29 us
    ppermute x15 -> x0, local copies, waits for them, and re-layouts: 27 us -> none  [swap(): lax.ppermute(piece, 'dev', [(number, number ^ mask) for number in range(d...]
    ppermute x55, waiting for transfers between devices: 173 us -> 198 us  [swap(): lax.ppermute(piece, 'dev', [(number, number ^ mask) for number in range(d...]
    pallas_call x12 -> x10, Pallas kernels: 76.7 us -> 85.9 us  [local_kernel(): pl.pallas_call(whole, out_shape=outs, in_specs=[pl.BlockSpec(memory_space...]
    pallas_call x5 -> x0, local copies, waits for them, and re-layouts: 8.92 us -> none  [local_kernel(): pl.pallas_call(whole, out_shape=outs, in_specs=[pl.BlockSpec(memory_space...]
    convert_element_type x4 -> x0, local copies, waits for them, and re-layouts: 5.7 us -> none  [the longest x2 3.38 us: shards(): mixed_low = row_major(mixed.reshape(total_rows, width).astype(low))]
  transfers between devices with their start and end apart: 58 -> 58, of which waited for: 22 -> 22; matrix products, arithmetic and copies ran while one was open for 23% -> 11% of each run, Pallas kernels for 16% -> 14%
where the time goes in v7:
time: 454 us; the launch traced here: 450 us
  waiting for transfers between devices  222 us (49%)
  Pallas kernels  89.1 us (20%)
  starting transfers between devices  48.3 us (11%)
  other arithmetic  32.2 us (7%)
  local copies, waits for them, and re-layouts  25.1 us (6%)
  matrix products  16.9 us (4%)
  between operations  16.2 us (4%)
    ppermute x55, waiting for transfers between devices, swap(): lax.ppermute(piece, 'dev', [(number, number ^ mask) for number in range(d...  198 us
    pallas_call x10, Pallas kernels, local_kernel(): pl.pallas_call(whole, out_shape=outs, in_specs=[pl.BlockSpec(memory_space...  85.9 us
    ppermute x55, starting transfers between devices, swap(): lax.ppermute(piece, 'dev', [(number, number ^ mask) for number in range(d...  48.2 us
    all_gather x3, waiting for transfers between devices, gather_z(): lax.all_gather(shard, 'dev', axis=0, tiled=False, axis_index_groups=z_gro...  23.3 us
  transfers between devices with their start and end apart: 58, of which 22 were waited for; matrix products, arithmetic and copies ran while one was open for 11% of the time, Pallas kernels for 14%

profile of v7, /device:TPU:8, one launch (start us, length us, event | category | flops | bytes accessed | tf_op | source)
XLA Modules:
  0.0 450.0 jit_solution(14420396011649739674)
XLA Ops:
  18.6 23.3 %all-gather.7.cloned.1.call-done = bf16[544,1088]{1,0:T(8,128)(2,1)} async-done(((bf16[136,1088]{1,0:T(8,128)(2,1)}), bf16[544,1088]{1,0:T(8,128)(2,1)}) %all-gather.7.cloned.1.call-update) | async-done | bytes 1183760 | tf_op jit(solution)/shard_map/all_gather | solution.py:311
  50.0 21.2 %collective-permute-done.7.refs_3_ = bf16[4,136,1088]{2,1,0:T(8,128)(2,1)S(1)} collective-permute-done((bf16[4,136,1088]{2,1,0:T(8,128)(2,1)}, bf16[4,136,1088]{2,1,0:T(8,128)(2,1)S(1)}, u32[]{:S(2)}, u32[]{:S(2)}) %collective-permute-start.7) | collective-permute-done | bytes 1183776 | tf_op jit(solution)/shard_map/ppermute | solution.py:271
  79.0 8.1 %collective-permute-done.11.refs_7_ = bf16[2,136,1088]{2,1,0:T(8,128)(2,1)S(1)} collective-permute-done((bf16[2,136,1088]{2,1,0:T(8,128)(2,1)}, bf16[2,136,1088]{2,1,0:T(8,128)(2,1)S(1)}, u32[]{:S(2)}, u32[]{:S(2)}) %collective-permute-start.11) | collective-permute-done | bytes 591904 | tf_op jit(solution)/shard_map/ppermute | solution.py:271
  91.7 3.2 shard_map.119
  115.0 6.8 %collective-permute-done.18.refs_0_.refs_2_ = bf16[1088,256]{1,0:T(8,128)(2,1)S(1)} collective-permute-done((bf16[1088,256]{1,0:T(8,128)(2,1)S(1)}, bf16[1088,256]{1,0:T(8,128)(2,1)S(1)}, u32[]{:S(2)}, u32[]{:S(2)}) %collective-permute-start.18) | collective-permute-done | bytes 557088 | tf_op jit(solution)/shard_map/ppermute | solution.py:271
  125.9 13.0 %collective-permute-done.16.refs_6_.refs_10_ = bf16[4,136,1088]{2,1,0:T(8,128)(2,1)S(1)} collective-permute-done((bf16[4,136,1088]{2,1,0:T(8,128)(2,1)}, bf16[4,136,1088]{2,1,0:T(8,128)(2,1)S(1)}, u32[]{:S(2)}, u32[]{:S(2)}) %collective-permute-start.16) | collective-permute-done | bytes 1183776 | tf_op jit(solution)/shard_map/ppermute | solution.py:271
  138.9 25.9 %collective-permute-done.17.refs_7_.refs_11_ = bf16[4,136,1088]{2,1,0:T(8,128)(2,1)} collective-permute-done((bf16[4,136,1088]{2,1,0:T(8,128)(2,1)}, bf16[4,136,1088]{2,1,0:T(8,128)(2,1)}, u32[]{:S(2)}, u32[]{:S(2)}) %collective-permute-start.17) | collective-permute-done | bytes 1183776 | tf_op jit(solution)/shard_map/ppermute | solution.py:271
  164.8 14.2 %shard_map.121 = (bf16[2,272,256]{2,1,0:T(8,128)(2,1)}, bf16[2,272,256]{2,1,0:T(8,128)(2,1)}, f32[272,1]{1,0:T(8,128)}, bf16[2,272,256]{2,1,0:T(8,128)(2,1)}, bf...) custom-call(bf16[1088,256]{1,0:T(8,128)(2,1)} %copy-done.31, ...), custom_call_target="tpu_custom_call" | custom-call | flops 3636461568 | bytes 10871296 | tf_op jit(solution)/shard_map/pallas_call | solution.py:104
  180.6 13.8 %shard_map.120 = (bf16[2,272,256]{2,1,0:T(8,128)(2,1)}, bf16[2,272,256]{2,1,0:T(8,128)(2,1)}, f32[272,1]{1,0:T(8,128)}, bf16[2,272,256]{2,1,0:T(8,128)(2,1)}, bf...) custom-call(bf16[1088,256]{1,0:T(8,128)(2,1)} %copy-done.16, ...), custom_call_target="tpu_custom_call" | custom-call | flops 3636461568 | bytes 10871296 | tf_op jit(solution)/shard_map/pallas_call | solution.py:104
  198.9 7.3 %shard_map.122 = (bf16[2,136,1088]{2,1,0:T(8,128)(2,1)}, bf16[2,136,1088]{2,1,0:T(8,128)(2,1)}, bf16[2,136,1088]{2,1,0:T(8,128)(2,1)}, bf16[2,136,1088]{2,1,0:T(8,128)(2,1)}) custom-call(bf16[1088,256]{1,0:T(8,128)(2,1)} %copy-done.16, bf16[1088,256]{1,0:T(8,128)(2,1)} %copy-done.32, bf16[1088,256]{1,0:T(8,128)(2,1)} %copy-done.31, ...), custom_call_target="tpu_custom_call" | custom-call | flops 2424307712 | bytes 9052160 | tf_op jit(solution)/shard_map/pallas_call | solution.py:104
  206.2 4.5 collective-permute-done.24
  215.8 2.8 convolution_convert_fusion.refs_4_
  218.7 12.0 %shard_map.123 = bf16[3,1088,256]{2,1,0:T(8,128)(2,1)} custom-call(s32[2]{0:T(128)} %pad_add_fusion.refs_0_, bf16[1088,256]{1,0:T(8,128)(2,1)} %bitcast.98, bf16[1088,256]{1,0:T(8,128)(2,1)} %slice_bitcast_fusion.refs_2_, bf16[1088,256]{1,0:T(8,128)(2,1)} %bitcast.100, bf16[1088,256]{1,0:T(8,128)(2,1)} %convolution_convert_fusion.refs_4_, ...), custom_call_target="tpu_custom_call" | custom-call | flops 713031680 | bytes 3916800 | tf_op jit(solution)/shard_map/pallas_call | solution.py:104
  240.8 10.0 %shard_map.124 = (bf16[2,136,1088]{2,1,0:T(8,128)(2,1)}, bf16[2,136,1088]{2,1,0:T(8,128)(2,1)}, bf16[2,136,1088]{2,1,0:T(8,128)(2,1)}, f32[2,136,1088]{2,1,0:T(8...) custom-call(s32[1]{0:T(128)} %bitcast.block_ref.refs_0_, ...), custom_call_target="tpu_custom_call" | custom-call | flops 2424307712 | bytes 13787136 | tf_op jit(solution)/shard_map/pallas_call | solution.py:104
  253.0 6.6 %fusion.17 = (f32[1088]{0:T(1024)S(1)}, f32[256]{0:T(256)S(1)}, f32[256]{0:T(256)S(1)}, f32[1088]{0:T(1024)S(1)}, f32[256,1088]{0,1:T(8,128)S(1)}) fusion(bf16[256,1088]{0,1:T(8,128)(2,1)S(1)} %copy-done.8, f32[256]{0:T(256)S(1)} %copy-done.49, f32[256]{0:T(256)S(1)} %copy-done.47, f32[1088]{0:T(1024)S(1)} %copy-done.38, ...), kind=kOutput, calls=%fused_computation.30 | convolution fusion | flops 1821013504 | bytes 10461952 | tf_op jit(solution)/shard_map/fr,fd->rd/dot_general | solution.py:652
  263.6 2.8 collective-permute-done.50
  266.9 3.4 collective-permute-done.51
  275.9 7.7 %shard_map.125 = (f32[2,136,1088]{2,1,0:T(8,128)}, f32[2,136,1088]{2,1,0:T(8,128)}, f32[2,136,1088]{2,1,0:T(8,128)}, f32[2,136,1088]{2,1,0:T(8,128)}) custom-call(bf16[1088,256]{1,0:T(8,128)(2,1)} %copy-done.16, bf16[1088,256]{1,0:T(8,128)(2,1)} %copy-done.32, bf16[1088,256]{1,0:T(8,128)(2,1)} %copy-done.31, ...), custom_call_target="tpu_custom_call" | custom-call | flops 2424307712 | bytes 11419648 | tf_op jit(solution)/shard_map/pallas_call | solution.py:104
  283.6 31.5 %collective-permute-done.45.refs_2_ = bf16[2,136,1088]{2,1,0:T(8,128)(2,1)S(1)} collective-permute-done((bf16[2,136,1088]{2,1,0:T(8,128)(2,1)}, bf16[2,136,1088]{2,1,0:T(8,128)(2,1)S(1)}, u32[]{:S(2)}, u32[]{:S(2)}) %collective-permute-start.45) | collective-permute-done | bytes 591904 | tf_op jit(solution)/shard_map/ppermute | solution.py:271
  315.1 10.2 %collective-permute-done.46.refs_4_ = bf16[2,136,1088]{2,1,0:T(8,128)(2,1)} collective-permute-done((bf16[2,136,1088]{2,1,0:T(8,128)(2,1)}, bf16[2,136,1088]{2,1,0:T(8,128)(2,1)}, u32[]{:S(2)}, u32[]{:S(2)}) %collective-permute-start.46) | collective-permute-done | bytes 591904 | tf_op jit(solution)/shard_map/ppermute | solution.py:271
  325.2 3.5 shard_map.129
  331.6 9.8 %shard_map.126 = (f32[2,1088,256]{2,1,0:T(8,128)}, bf16[2,1088,256]{2,1,0:T(8,128)(2,1)}) custom-call(bf16[2,272,256]{2,1,0:T(8,128)(2,1)} %get-tuple-element.71.refs_8_.refs_0_, bf16[2,272,256]{2,1,0:T(8,128)(2,1)} %get-tuple-element.72.refs_12_.refs_1_, bf16[2,272,256]{2,1,0:T(8,128)(2,1)} %get-tuple-element.73.refs_8_.refs_2_, ...), custom_call_target="tpu_custom_call" | custom-call | flops 2424307712 | bytes 10305536 | tf_op jit(solution)/shard_map/pallas_call | solution.py:104
  345.0 3.5 shard_map.128
  353.7 5.0 %collective-permute-done.48 = bf16[136,1088]{1,0:T(8,128)(2,1)S(1)} collective-permute-done((bf16[136,1088]{1,0:T(8,128)(2,1)}, bf16[136,1088]{1,0:T(8,128)(2,1)S(1)}, u32[]{:S(2)}, u32[]{:S(2)}) %collective-permute-start.48) | collective-permute-done | bytes 295968 | tf_op jit(solution)/shard_map/ppermute | solution.py:271
  358.7 6.0 %collective-permute-done.34 = bf16[2,136,1088]{2,1,0:T(8,128)(2,1)S(1)} collective-permute-done((bf16[2,136,1088]{2,1,0:T(8,128)(2,1)}, bf16[2,136,1088]{2,1,0:T(8,128)(2,1)S(1)}, u32[]{:S(2)}, u32[]{:S(2)}) %collective-permute-start.34) | collective-permute-done | bytes 591904 | tf_op jit(solution)/shard_map/ppermute | solution.py:271
  367.0 9.6 %collective-permute-done.42 = bf16[136,1088]{1,0:T(8,128)(2,1)S(1)} collective-permute-done((bf16[136,1088]{1,0:T(8,128)(2,1)}, bf16[136,1088]{1,0:T(8,128)(2,1)S(1)}, u32[]{:S(2)}, u32[]{:S(2)}) %collective-permute-start.42) | collective-permute-done | bytes 295968 | tf_op jit(solution)/shard_map/ppermute | solution.py:271
  378.1 7.1 %collective-permute-done.43 = bf16[136,1088]{1,0:T(8,128)(2,1)S(1)} collective-permute-done((bf16[136,1088]{1,0:T(8,128)(2,1)}, bf16[136,1088]{1,0:T(8,128)(2,1)S(1)}, u32[]{:S(2)}, u32[]{:S(2)}) %collective-permute-start.43) | collective-permute-done | bytes 295968 | tf_op jit(solution)/shard_map/ppermute | solution.py:271
  393.7 12.2 %collective-permute-done.33.refs_3_ = bf16[2,136,1088]{2,1,0:T(8,128)(2,1)S(1)} collective-permute-done((bf16[2,136,1088]{2,1,0:T(8,128)(2,1)S(1)}, bf16[2,136,1088]{2,1,0:T(8,128)(2,1)S(1)}, u32[]{:S(2)}, u32[]{:S(2)}) %collective-permute-start.33) | collective-permute-done | bytes 591904 | tf_op jit(solution)/shard_map/ppermute | solution.py:271
  406.9 4.0 shard_map.127
  410.9 3.3 collective-permute-start.37
  419.7 13.5 %collective-permute-done.37 = bf16[136,1088]{1,0:T(8,128)(2,1)S(1)} collective-permute-done((bf16[136,1088]{1,0:T(8,128)(2,1)}, bf16[136,1088]{1,0:T(8,128)(2,1)S(1)}, u32[]{:S(2)}, u32[]{:S(2)}) %collective-permute-start.37) | collective-permute-done | bytes 295968 | tf_op jit(solution)/shard_map/ppermute | solution.py:271
  433.2 7.9 %collective-permute-done.38 = bf16[136,1088]{1,0:T(8,128)(2,1)S(1)} collective-permute-done((bf16[136,1088]{1,0:T(8,128)(2,1)}, bf16[136,1088]{1,0:T(8,128)(2,1)S(1)}, u32[]{:S(2)}, u32[]{:S(2)}) %collective-permute-start.38) | collective-permute-done | bytes 295968 | tf_op jit(solution)/shard_map/ppermute | solution.py:271
  (315 shorter events, 120.1 us)
Async XLA Ops:
  7.2 34.7 %all-gather.7.cloned.1.call-start = ((), (), s32[]{:S(2)}) async-start(), calls=%async_computation | async-start | bytes 1566720 | tf_op jit(solution)/shard_map/all_gather | solution.py:311
  8.0 100.3 %all-gather.9.cloned.1.call-start = ((), (), s32[]{:S(2)}) async-start(), calls=%async_computation.1 | async-start | bytes 1566720 | tf_op jit(solution)/shard_map/all_gather | solution.py:311
  10.0 98.9 %all-gather.11.cloned.1.call-start = ((), (), s32[]{:S(2)}) async-start(), calls=%async_computation.2 | async-start | bytes 1566720 | tf_op jit(solution)/shard_map/all_gather | solution.py:311
  17.1 27.7 %collective-permute-start.2 = (bf16[1632]{0:T(1024)(128)(2,1)S(1)}, bf16[1632]{0:T(1024)(128)(2,1)S(1)}, u32[]{:S(2)}, u32[]{:S(2)}) collective-permute-start(bf16[1632]{0:T(1024)(128)(2,1)S(1)} %pad_maximum_fusion.3), channel_id=1, source_target_pairs={{0,4},{1,5},{2,6},{3,7},{4,0},{5,1},{6,2},{7,3},{8,12},{9,13},{10,... | collective-permute-start | bytes 9800 | tf_op jit(solution)/shard_map/ppermute | solution.py:271
  41.9 29.3 %collective-permute-start.7 = (bf16[4,136,1088]{2,1,0:T(8,128)(2,1)}, bf16[4,136,1088]{2,1,0:T(8,128)(2,1)S(1)}, u32[]{:S(2)}, u32[]{:S(2)}) collective-permute-start(bf16[4,136,1088]{2,1,0:T(8,128)(2,1)} %bitcast.86), channel_id=1, source_target_pairs={{0,2},{1,3},{2,0},{3,1},{4,6},{5,7},{6,4},{7,5},{8,10},{9,11},{10,... | collective-permute-start | bytes 3551240 | tf_op jit(solution)/shard_map/ppermute | solution.py:271
  43.4 30.2 %collective-permute-start.6 = (bf16[4,136,1088]{2,1,0:T(8,128)(2,1)}, bf16[4,136,1088]{2,1,0:T(8,128)(2,1)S(1)}, u32[]{:S(2)}, u32[]{:S(2)}) collective-permute-start(bf16[4,136,1088]{2,1,0:T(8,128)(2,1)} %bitcast.87), channel_id=1, source_target_pairs={{0,4},{1,5},{2,6},{3,7},{4,0},{5,1},{6,2},{7,3},{8,12},{9,13},{10,... | collective-permute-start | bytes 3551240 | tf_op jit(solution)/shard_map/ppermute | solution.py:271
  48.8 27.1 %collective-permute-start.4 = (bf16[6528]{0:T(1024)(128)(2,1)S(1)}, bf16[6528]{0:T(1024)(128)(2,1)S(1)}, u32[]{:S(2)}, u32[]{:S(2)}) collective-permute-start(bf16[6528]{0:T(1024)(128)(2,1)S(1)} %pad_maximum_fusion.1), channel_id=1, source_target_pairs={{0,16},{1,17},{2,18},{3,19},{4,20},{5,21},{6,22},{7,23},{8,24},{9,... | collective-permute-start | bytes 39176 | tf_op jit(solution)/shard_map/ppermute | solution.py:271
  50.0 40.2 %collective-permute-start.5 = (bf16[4,136,1088]{2,1,0:T(8,128)(2,1)}, bf16[4,136,1088]{2,1,0:T(8,128)(2,1)}, u32[]{:S(2)}, u32[]{:S(2)}) collective-permute-start(bf16[4,136,1088]{2,1,0:T(8,128)(2,1)} %bitcast.88), channel_id=1, source_target_pairs={{0,1},{1,0},{2,3},{3,2},{4,5},{5,4},{6,7},{7,6},{8,9},{9,8},{10,11... | collective-permute-start | bytes 3551240 | tf_op jit(solution)/shard_map/ppermute | solution.py:271
  90.1 24.3 %collective-permute-start.20 = (bf16[1088,256]{1,0:T(8,128)(2,1)}, bf16[1088,256]{1,0:T(8,128)(2,1)}, u32[]{:S(2)}, u32[]{:S(2)}) collective-permute-start(bf16[1088,256]{1,0:T(8,128)(2,1)} %fusion.33.refs_2_.refs_4_), channel_id=1, source_target_pairs={{0,2},{1,3},{2,0},{3,1},{4,6},{5,7},{6,4},{7,5},{8,10},{9,11},{10,... | collective-permute-start | bytes 1671176 | tf_op jit(solution)/shard_map/ppermute | solution.py:271
  108.3 30.6 %collective-permute-start.16 = (bf16[4,136,1088]{2,1,0:T(8,128)(2,1)}, bf16[4,136,1088]{2,1,0:T(8,128)(2,1)S(1)}, u32[]{:S(2)}, u32[]{:S(2)}) collective-permute-start(bf16[4,136,1088]{2,1,0:T(8,128)(2,1)} %bitcast.102), channel_id=1, source_target_pairs={{0,4},{1,5},{2,6},{3,7},{4,0},{5,1},{6,2},{7,3},{8,12},{9,13},{10,... | collective-permute-start | bytes 3551240 | tf_op jit(solution)/shard_map/ppermute | solution.py:271
  108.9 55.9 %collective-permute-start.17 = (bf16[4,136,1088]{2,1,0:T(8,128)(2,1)}, bf16[4,136,1088]{2,1,0:T(8,128)(2,1)}, u32[]{:S(2)}, u32[]{:S(2)}) collective-permute-start(bf16[4,136,1088]{2,1,0:T(8,128)(2,1)} %bitcast.106), channel_id=1, source_target_pairs={{0,4},{1,5},{2,6},{3,7},{4,0},{5,1},{6,2},{7,3},{8,12},{9,13},{10,... | collective-permute-start | bytes 3551240 | tf_op jit(solution)/shard_map/ppermute | solution.py:271
  110.3 69.5 %collective-permute-start.15 = (bf16[1088,256]{1,0:T(8,128)(2,1)}, bf16[1088,256]{1,0:T(8,128)(2,1)}, u32[]{:S(2)}, u32[]{:S(2)}) collective-permute-start(bf16[1088,256]{1,0:T(8,128)(2,1)} %fusion.33.refs_2_.refs_4_), channel_id=1, source_target_pairs={{0,1},{1,0},{2,3},{3,2},{4,5},{5,4},{6,7},{7,6},{8,9},{9,8},{10,11... | collective-permute-start | bytes 1671176 | tf_op jit(solution)/shard_map/ppermute | solution.py:271
  125.4 54.4 %collective-permute-start.14 = (bf16[1088,256]{1,0:T(8,128)(2,1)S(1)}, bf16[1088,256]{1,0:T(8,128)(2,1)S(1)}, u32[]{:S(2)}, u32[]{:S(2)}) collective-permute-start(bf16[1088,256]{1,0:T(8,128)(2,1)S(1)} %fusion.31.refs_0_), channel_id=1, source_target_pairs={{0,1},{1,0},{2,3},{3,2},{4,5},{5,4},{6,7},{7,6},{8,9},{9,8},{10,11... | collective-permute-start | bytes 1671176 | tf_op jit(solution)/shard_map/ppermute | solution.py:271
  271.0 70.5 %collective-permute-start.40 = (bf16[2,136,1088]{2,1,0:T(8,128)(2,1)}, bf16[2,136,1088]{2,1,0:T(8,128)(2,1)S(1)}, u32[]{:S(2)}, u32[]{:S(2)}) collective-permute-start(bf16[2,136,1088]{2,1,0:T(8,128)(2,1)} %get-tuple-element.91), channel_id=1, source_target_pairs={{0,4},{1,5},{2,6},{3,7},{4,0},{5,1},{6,2},{7,3},{8,12},{9,13},{10,... | collective-permute-start | bytes 1775624 | tf_op jit(solution)/shard_map/ppermute | solution.py:271
  272.4 69.1 %collective-permute-start.41 = (bf16[2,136,1088]{2,1,0:T(8,128)(2,1)}, bf16[2,136,1088]{2,1,0:T(8,128)(2,1)S(1)}, u32[]{:S(2)}, u32[]{:S(2)}) collective-permute-start(bf16[2,136,1088]{2,1,0:T(8,128)(2,1)} %get-tuple-element.92), channel_id=1, source_target_pairs={{0,4},{1,5},{2,6},{3,7},{4,0},{5,1},{6,2},{7,3},{8,12},{9,13},{10,... | collective-permute-start | bytes 1775624 | tf_op jit(solution)/shard_map/ppermute | solution.py:271
  273.0 42.1 %collective-permute-start.45 = (bf16[2,136,1088]{2,1,0:T(8,128)(2,1)}, bf16[2,136,1088]{2,1,0:T(8,128)(2,1)S(1)}, u32[]{:S(2)}, u32[]{:S(2)}) collective-permute-start(bf16[2,136,1088]{2,1,0:T(8,128)(2,1)} %get-tuple-element.93), channel_id=1, source_target_pairs={{0,4},{1,5},{2,6},{3,7},{4,0},{5,1},{6,2},{7,3},{8,12},{9,13},{10,... | collective-permute-start | bytes 1775624 | tf_op jit(solution)/shard_map/ppermute | solution.py:271
  274.5 50.8 %collective-permute-start.46 = (bf16[2,136,1088]{2,1,0:T(8,128)(2,1)}, bf16[2,136,1088]{2,1,0:T(8,128)(2,1)}, u32[]{:S(2)}, u32[]{:S(2)}) collective-permute-start(bf16[2,136,1088]{2,1,0:T(8,128)(2,1)} %get-tuple-element.94), channel_id=1, source_target_pairs={{0,4},{1,5},{2,6},{3,7},{4,0},{5,1},{6,2},{7,3},{8,12},{9,13},{10,... | collective-permute-start | bytes 1775624 | tf_op jit(solution)/shard_map/ppermute | solution.py:271
  275.2 56.3 %collective-permute-start.53 = (f32[816]{0:T(1024)S(1)}, f32[816]{0:T(1024)S(1)}, u32[]{:S(2)}, u32[]{:S(2)}) collective-permute-start(f32[816]{0:T(1024)S(1)} %slice_select_fusion.2), channel_id=1, source_target_pairs={{0,2},{1,3},{2,0},{3,1},{4,6},{5,7},{6,4},{7,5},{8,10},{9,11},{10,... | collective-permute-start | bytes 9800 | tf_op jit(solution)/shard_map/ppermute | solution.py:271
  328.7 24.2 %collective-permute-start.47 = (bf16[136,1088]{1,0:T(8,128)(2,1)}, bf16[136,1088]{1,0:T(8,128)(2,1)S(1)}, u32[]{:S(2)}, u32[]{:S(2)}) collective-permute-start(bf16[136,1088]{1,0:T(8,128)(2,1)} %get-tuple-element.120), channel_id=1, source_target_pairs={{0,16},{1,17},{2,18},{3,19},{4,20},{5,21},{6,22},{7,23},{8,24},{9,... | collective-permute-start | bytes 887816 | tf_op jit(solution)/shard_map/ppermute | solution.py:271
  330.7 20.0 %collective-permute-start.32 = (bf16[2,136,1088]{2,1,0:T(8,128)(2,1)}, bf16[2,136,1088]{2,1,0:T(8,128)(2,1)}, u32[]{:S(2)}, u32[]{:S(2)}) collective-permute-start(bf16[2,136,1088]{2,1,0:T(8,128)(2,1)} %get-tuple-element.107), channel_id=1, source_target_pairs={{0,2},{1,3},{2,0},{3,1},{4,6},{5,7},{6,4},{7,5},{8,10},{9,11},{10,... | collective-permute-start | bytes 1775624 | tf_op jit(solution)/shard_map/ppermute | solution.py:271
  342.6 22.4 %collective-permute-start.49 = (bf16[136,1088]{1,0:T(8,128)(2,1)}, bf16[136,1088]{1,0:T(8,128)(2,1)}, u32[]{:S(2)}, u32[]{:S(2)}) collective-permute-start(bf16[136,1088]{1,0:T(8,128)(2,1)} %get-tuple-element.122), channel_id=1, source_target_pairs={{0,8},{1,9},{2,10},{3,11},{4,12},{5,13},{6,14},{7,15},{8,0},{9,1},... | collective-permute-start | bytes 887816 | tf_op jit(solution)/shard_map/ppermute | solution.py:271
  350.7 25.9 %collective-permute-start.42 = (bf16[136,1088]{1,0:T(8,128)(2,1)}, bf16[136,1088]{1,0:T(8,128)(2,1)S(1)}, u32[]{:S(2)}, u32[]{:S(2)}) collective-permute-start(bf16[136,1088]{1,0:T(8,128)(2,1)} %get-tuple-element.116), channel_id=1, source_target_pairs={{0,16},{1,17},{2,18},{3,19},{4,20},{5,21},{6,22},{7,23},{8,24},{9,... | collective-permute-start | bytes 887816 | tf_op jit(solution)/shard_map/ppermute | solution.py:271
  353.0 32.2 %collective-permute-start.43 = (bf16[136,1088]{1,0:T(8,128)(2,1)}, bf16[136,1088]{1,0:T(8,128)(2,1)S(1)}, u32[]{:S(2)}, u32[]{:S(2)}) collective-permute-start(bf16[136,1088]{1,0:T(8,128)(2,1)} %get-tuple-element.117), channel_id=1, source_target_pairs={{0,24},{1,25},{2,26},{3,27},{4,28},{5,29},{6,30},{7,31},{8,16},{9,... | collective-permute-start | bytes 887816 | tf_op jit(solution)/shard_map/ppermute | solution.py:271
  358.7 28.0 %collective-permute-start.44 = (bf16[136,1088]{1,0:T(8,128)(2,1)}, bf16[136,1088]{1,0:T(8,128)(2,1)S(1)}, u32[]{:S(2)}, u32[]{:S(2)}) collective-permute-start(bf16[136,1088]{1,0:T(8,128)(2,1)} %get-tuple-element.118), channel_id=1, source_target_pairs={{0,8},{1,9},{2,10},{3,11},{4,12},{5,13},{6,14},{7,15},{8,0},{9,1},... | collective-permute-start | bytes 887816 | tf_op jit(solution)/shard_map/ppermute | solution.py:271
  364.7 26.1 %collective-permute-start.29 = (bf16[2,1088,256]{2,1,0:T(8,128)(2,1)S(1)}, bf16[2,1088,256]{2,1,0:T(8,128)(2,1)S(1)}, u32[]{:S(2)}, u32[]{:S(2)}) collective-permute-start(bf16[2,1088,256]{2,1,0:T(8,128)(2,1)S(1)} %copy-done.57), channel_id=1, source_target_pairs={{0,1},{1,0},{2,3},{3,2},{4,5},{5,4},{6,7},{7,6},{8,9},{9,8},{10,11... | collective-permute-start | bytes 3342344 | tf_op jit(solution)/shard_map/ppermute | solution.py:271
  365.8 25.2 %collective-permute-start.31 = (bf16[2,136,1088]{2,1,0:T(8,128)(2,1)S(1)}, bf16[2,136,1088]{2,1,0:T(8,128)(2,1)S(1)}, u32[]{:S(2)}, u32[]{:S(2)}) collective-permute-start(bf16[2,136,1088]{2,1,0:T(8,128)(2,1)S(1)} %copy-done.59), channel_id=1, source_target_pairs={{0,2},{1,3},{2,0},{3,1},{4,6},{5,7},{6,4},{7,5},{8,10},{9,11},{10,... | collective-permute-start | bytes 1775624 | tf_op jit(solution)/shard_map/ppermute | solution.py:271
  385.2 20.6 %collective-permute-start.33 = (bf16[2,136,1088]{2,1,0:T(8,128)(2,1)S(1)}, bf16[2,136,1088]{2,1,0:T(8,128)(2,1)S(1)}, u32[]{:S(2)}, u32[]{:S(2)}) collective-permute-start(bf16[2,136,1088]{2,1,0:T(8,128)(2,1)S(1)} %add_convert_fusion.1), channel_id=1, source_target_pairs={{0,4},{1,5},{2,6},{3,7},{4,0},{5,1},{6,2},{7,3},{8,12},{9,13},{10,... | collective-permute-start | bytes 1775624 | tf_op jit(solution)/shard_map/ppermute | solution.py:271
  386.7 19.2 %collective-permute-start.35 = (bf16[2,136,1088]{2,1,0:T(8,128)(2,1)S(1)}, bf16[2,136,1088]{2,1,0:T(8,128)(2,1)S(1)}, u32[]{:S(2)}, u32[]{:S(2)}) collective-permute-start(bf16[2,136,1088]{2,1,0:T(8,128)(2,1)S(1)} %add_convert_fusion), channel_id=1, source_target_pairs={{0,2},{1,3},{2,0},{3,1},{4,6},{5,7},{6,4},{7,5},{8,10},{9,11},{10,... | collective-permute-start | bytes 1775624 | tf_op jit(solution)/shard_map/ppermute | solution.py:271
  410.9 22.2 %collective-permute-start.37 = (bf16[136,1088]{1,0:T(8,128)(2,1)}, bf16[136,1088]{1,0:T(8,128)(2,1)S(1)}, u32[]{:S(2)}, u32[]{:S(2)}) collective-permute-start(bf16[136,1088]{1,0:T(8,128)(2,1)} %get-tuple-element.112), channel_id=1, source_target_pairs={{0,16},{1,17},{2,18},{3,19},{4,20},{5,21},{6,22},{7,23},{8,24},{9,... | collective-permute-start | bytes 887816 | tf_op jit(solution)/shard_map/ppermute | solution.py:271
  414.3 26.8 %collective-permute-start.38 = (bf16[136,1088]{1,0:T(8,128)(2,1)}, bf16[136,1088]{1,0:T(8,128)(2,1)S(1)}, u32[]{:S(2)}, u32[]{:S(2)}) collective-permute-start(bf16[136,1088]{1,0:T(8,128)(2,1)} %get-tuple-element.113), channel_id=1, source_target_pairs={{0,24},{1,25},{2,26},{3,27},{4,28},{5,29},{6,30},{7,31},{8,16},{9,... | collective-permute-start | bytes 887816 | tf_op jit(solution)/shard_map/ppermute | solution.py:271
  415.8 25.3 %collective-permute-start.39 = (bf16[136,1088]{1,0:T(8,128)(2,1)}, bf16[136,1088]{1,0:T(8,128)(2,1)S(1)}, u32[]{:S(2)}, u32[]{:S(2)}) collective-permute-start(bf16[136,1088]{1,0:T(8,128)(2,1)} %get-tuple-element.114), channel_id=1, source_target_pairs={{0,8},{1,9},{2,10},{3,11},{4,12},{5,13},{6,14},{7,15},{8,0},{9,1},... | collective-permute-start | bytes 887816 | tf_op jit(solution)/shard_map/ppermute | solution.py:271
  417.3 24.8 %collective-permute-start.30 = (bf16[1088,256]{1,0:T(8,128)(2,1)S(1)}, bf16[1088,256]{1,0:T(8,128)(2,1)S(1)}, u32[]{:S(2)}, u32[]{:S(2)}) collective-permute-start(bf16[1088,256]{1,0:T(8,128)(2,1)S(1)} %fusion.32), channel_id=1, source_target_pairs={{0,2},{1,3},{2,0},{3,1},{4,6},{5,7},{6,4},{7,5},{8,10},{9,11},{10,... | collective-permute-start | bytes 1671176 | tf_op jit(solution)/shard_map/ppermute | solution.py:271
  (86 other events, 933.9 us)
Sparse Core Ops, SparseCore 0:
  9.6 32.2 all-gather.6
  43.5 30.7 all-gather.8
  76.4 30.7 all-gather.10

commit v8 on v7

--- a/solution.py
+++ b/solution.py
@@ -63,9 +63,8 @@
     return (mixed, top + jnp.log(total))
 
 
-def local_kernel(body, outs, operands, flops, scalars=(), earlier=()):
+def local_kernel(body, outs, operands, scalars=(), earlier=()):
     outs = [jax.ShapeDtypeStruct(shape, kind) for shape, kind in outs]
-    moved = sum(array.size * array.dtype.itemsize for array in (*outs, *operands))
     first, count, total = len(scalars), len(operands), len(operands) + len(outs)
 
     def whole(*refs):
@@ -110,7 +109,7 @@
         scratch_shapes=[pltpu.VMEM(array.shape, array.dtype) for array in (*operands, *outs)]
         + [pltpu.SemaphoreType.DMA((total,))],
         compiler_params=pltpu.CompilerParams(vmem_limit_bytes=VMEM_LIMIT),
-        cost_estimate=pl.CostEstimate(flops=flops, bytes_accessed=moved, transcendentals=0),
+        cost_estimate=pl.CostEstimate(flops=1, bytes_accessed=1, transcendentals=0),
     )(*scalars, *operands, *earlier)
 
 
@@ -136,9 +135,8 @@
         query_pos, query_live = inside(1)
         allowed = (key_pos <= query_pos) & (key_live == query_live)
 
-        @pl.loop(0, HEADS)
-        def _(head):
-            part = pl.ds(pl.multiple_of(head * HEAD_SIZE, HEAD_SIZE), HEAD_SIZE)
+        for head in range(HEADS):
+            part = pl.ds(head * HEAD_SIZE, HEAD_SIZE)
             q, k, v, do = q_ref[part, :], k_ref[part, :], v_ref[part, :], do_ref[part, :]
             scores = jnp.where(allowed, product(k, q, 0, 0) * scale, neg_large)
             probs = jnp.exp(scores - log_ref[head])
@@ -153,107 +151,85 @@
         body,
         [((3, width, rows), low)],
         (queries, keys, values, grad_mixed, log_total),
-        10 * rows * rows * width,
         (span,),
     )[0]
 
 
-def mlp_block(row_pair, grad_pair, weights, biases):
+def mlp_block(row_pair, grad_pair, weights, bias):
     width, rows = row_pair[0].shape
     low, wide = jnp.bfloat16, jnp.float32
-    hidden = [2 * weight.shape[1] for weight in weights]
-    outs = []
-    for count in hidden:
-        outs += [((2, count, rows), low), ((2, count, rows), low), ((count, 1), wide)]
-    sums = len(outs)
-    outs += [((width, rows), wide), ((width, rows), low)]
-    number = len(weights)
+    count = 2 * weights.shape[1]
 
     def body(need, send, *refs):
-        row_refs, grad_refs = refs[:2], refs[2:4]
-        weight_refs, bias_refs = refs[4 : 4 + number], refs[4 + number : 4 + 2 * number]
-        out_refs = refs[-len(outs) :]
+        row_refs, grad_refs, (weight, bias_ref) = refs[:2], refs[2:4], refs[4:6]
+        act_ref, up_ref, sum_ref = refs[6:9]
         for side in (1, 0):
+            need(side, 2 + side, 4, 5)
             total = None
-            for place in range(number):
-                need(side, 2 + side, 4 + place, 4 + number + place)
-                weight, count = weight_refs[place], hidden[place]
-                up = weight[0:2].reshape(count, width)
-                down = weight[2:4].reshape(count, width)
-                up_sum = product(up, row_refs[side][...], 1, 0) + bias_refs[place][...]
+            for part in range(2):
+                span = slice(part * (count // 2), (part + 1) * (count // 2))
+                up, down = weight[part], weight[2 + part]
+                up_sum = product(up, row_refs[side][...], 1, 0) + bias_ref[span, :]
                 activated, slope = gelu_parts(up_sum)
                 grad_act = product(down, grad_refs[side][...], 1, 0)
                 grad_up = (grad_act * slope).astype(low)
-                act_ref, up_ref, sum_ref = out_refs[3 * place : 3 * place + 3]
-                act_ref[side] = activated.astype(low)
-                up_ref[side] = grad_up
+                act_ref[side, span, :] = activated.astype(low)
+                up_ref[side, span, :] = grad_up
                 columns = jnp.sum(grad_up.astype(wide), axis=1, keepdims=True)
-                sum_ref[...] = columns if side == 1 else sum_ref[...] + columns
-                if side == 0:
-                    send(3 * place, 3 * place + 1, 3 * place + 2)
-                term = product(up, grad_up, 0, 0)
+                sum_ref[span, :] = columns if side == 1 else sum_ref[span, :] + columns
+                term = product(grad_up, up, 0, 0)
                 total = term if total is None else total + term
-            out = out_refs[sums + side]
-            out[...] = total.astype(out.dtype)
-            send(sums + side)
-
-    operands = (*row_pair, *grad_pair, *weights, *biases)
-    result = local_kernel(body, outs, operands, 12 * rows * width * sum(hidden))
-    return ([result[3 * place : 3 * place + 3] for place in range(number)], result[sums:])
-
-
-def mlp_weight_grads(blocks, rows, grads, kind, earlier):
-    width = rows[0].shape[0]
-    operands, outs, number = [], [], len(rows)
-    operands += [*rows, *grads]
-    for near, far in blocks:
-        operands += [near[0], far[0], near[1], far[1]]
-        count = near[0].shape[1]
-        outs += [((2, count // 2, width), kind)] * 2
+            out = refs[9 + side]
+            out[...] = total.T.astype(out.dtype)
+            send(3 + side)
+
+    outs = [((2, count, rows), low), ((2, count, rows), low), ((count, 1), wide)]
+    outs += [((width, rows), wide), ((width, rows), low)]
+    result = local_kernel(body, outs, (*row_pair, *grad_pair, weights, bias))
+    return (result[:3], result[3:])
+
+
+def mlp_weight_grads(near, far, rows, grads, earlier):
+    width, number = rows[0].shape[0], len(rows)
+    count = near[0].shape[1]
+    low = jnp.bfloat16
 
     def body(need, send, *refs):
+        need()
         row_refs, grad_refs = refs[:number], refs[number : 2 * number]
-        out_refs = refs[-len(outs) :]
-        need(*range(2 * number))
-        for place in range(len(blocks)):
-            start = 2 * number + 4 * place
-            need(*range(start, start + 4))
-            sources = refs[start : start + 4]
-            for which, pair, others in ((0, sources[2:], row_refs), (1, sources[:2], grad_refs)):
-                out = out_refs[2 * place + which]
+        near_act, far_act, near_up, far_up, out = refs[2 * number :]
+        for which, pair, others in (
+            (0, (near_up, far_up), row_refs),
+            (1, (near_act, far_act), grad_refs),
+        ):
+            for part in range(2):
+                span = slice(part * (count // 2), (part + 1) * (count // 2))
                 total = None
                 for group in range(number):
-                    term = product(pair[group // 2][group % 2], others[group][...], 1, 1)
+                    left = pair[group // 2][group % 2, span, :]
+                    term = product(left, others[group][...], 1, 1)
                     total = term if total is None else total + term
-                out[...] = total.reshape(out.shape).astype(kind)
-                send(2 * place + which)
-
-    flops = sum(16 * rows[0].shape[1] * near[0].shape[1] * width for near, far in blocks)
-    result = local_kernel(body, outs, operands, flops, (), earlier)
-    return [tuple(result[2 * place : 2 * place + 2]) for place in range(len(blocks))]
-
-
-def mlp_outputs(blocks, weights, earlier):
-    rows, width = blocks[0][0][0].shape[2], weights[0].shape[2]
-    number = len(weights)
-    operands = [near[0] for near, far in blocks] + [far[0] for near, far in blocks]
+                start = which * count + part * (count // 2)
+                out[start : start + count // 2, :] = total.astype(low)
+
+    operands = (*rows, *grads, near[0], far[0], near[1], far[1])
+    return local_kernel(body, [((2 * count, width), low)], operands, (), earlier)[0]
+
+
+def mlp_outputs(near, far, weights, earlier):
+    rows, half, width = near.shape[2], weights.shape[1], weights.shape[2]
 
     def body(need, send, *refs):
         need()
-        weight_refs, out_refs = refs[2 * number : 3 * number], refs[-2:]
+        weight, outs = refs[2], refs[3:]
         for group in range(2):
             for side in range(2):
-                total = None
-                for place in range(number):
-                    weight = weight_refs[place]
-                    down = weight[2:4].reshape(2 * weight.shape[1], width)
-                    term = product(down, refs[group * number + place][side], 0, 0)
-                    total = term if total is None else total + term
-                out_refs[side][group] = total.astype(out_refs[side].dtype)
+                total = product(refs[group][side, :half, :], weight[2], 0, 0)
+                total = total + product(refs[group][side, half:, :], weight[3], 0, 0)
+                outs[side][group] = total.T.astype(outs[side].dtype)
 
     outs = [((2, width, rows), jnp.float32), ((2, width, rows), jnp.bfloat16)]
-    flops = 16 * rows * width * sum(weight.shape[1] for weight in weights)
-    return local_kernel(body, outs, (*operands, *weights), flops, (), earlier)
+    return local_kernel(body, outs, (near, far, weights), (), earlier)
 
 
 def gather_rows(own):
@@ -345,9 +321,7 @@
         out_specs=(pl.BlockSpec(memory_space=pltpu.VMEM), pl.BlockSpec(memory_space=pltpu.VMEM)),
         scratch_shapes=[pltpu.SemaphoreType.DMA((count,))],
         compiler_params=pltpu.CompilerParams(vmem_limit_bytes=24 * 1024 * 1024),
-        cost_estimate=pl.CostEstimate(
-            flops=0, bytes_accessed=4 * count * rows * width, transcendentals=0
-        ),
+        cost_estimate=pl.CostEstimate(flops=1, bytes_accessed=1, transcendentals=0),
     )(block, *arrays)
 
 
@@ -396,7 +370,7 @@
     along_upper = swap((along[0] + across_diagonal).astype(low), 4)
 
     def finish():
-        return scatter_z(mine, ((across_upper, along_upper), (across_lower, along_lower)))
+        return add_z(*route_z(mine, ((across_upper, along_upper), (across_lower, along_lower)), ()))
 
     return (finish, (across[1], along[0]))
 
@@ -433,7 +407,6 @@
         body,
         [((2, rows, width), kind) for kind in kinds],
         (*mine, *beside, *pairs[0], *pairs[1]),
-        64 * rows * mine[0].shape[3] * width,
         (block,),
     )
     return [outs[2 * place : 2 * place + 2] for place in range(4)]
@@ -441,59 +414,19 @@
 
 def gather_hidden(shard):
     devices = lax.axis_size("dev")
-    if devices != 32:
-        both = lax.all_gather(
-            shard, "dev", axis=0, tiled=True, axis_index_groups=same_low(devices)
-        )
-        return (both, None)
-    cut = shard.shape[0] // 2
-    one, two = gather_z(shard[:cut]), gather_z(shard[cut:])
-    return ((one, swap(one, 4)), two)
-
-
-def pick_blocks(bias, blocks, start, stop):
-    picked = lax.dynamic_index_in_dim(bias, blocks, 1, False)
-    return picked[:, start:stop].reshape(-1)
-
-
-def put_blocks(bias, blocks, start, stop, values):
-    values = values.reshape(bias.shape[0], 1, stop - start)
-    return lax.dynamic_update_slice(bias, values, (0, blocks, start))
-
-
-def hidden_parts(gathered, here, devices, ready):
-    one, two = gathered
-    if devices != 32:
-        rows = one.shape[0] // 4
-        return [[(one.reshape(4, rows, -1), here & 3, 0, rows // (devices // 16))]]
-    two = after(two, ready)
-    cut, end = one[0].shape[1], one[0].shape[1] + two.shape[1]
-    own, other = here & 7, (here & 7) ^ 4
-    return [
-        [(one[0], own, 0, cut), (two, own, cut, end)],
-        [(one[1], other, 0, cut), (swap(two, 4), other, cut, end)],
-    ]
-
-
-def scatter_hidden(own, others, ready):
+    both = lax.all_gather(shard, "dev", axis=0, tiled=True, axis_index_groups=same_low(devices))
+    return both.reshape(4, -1, both.shape[1])
+
+
+def scatter_hidden(grads):
     devices = lax.axis_size("dev")
-    low = jnp.bfloat16
-    if devices != 32:
-        width = own[0][0].shape[2]
-        both = jnp.concatenate([part.reshape(-1, width) for part in own[0]], axis=0).astype(low)
-        return lax.psum_scatter(
-            both, "dev", scatter_dimension=0, tiled=True, axis_index_groups=same_low(devices)
-        ).astype(jnp.float32)
-    moved = [[swap(part, 4) for part in pair] for pair in others]
-    shares = [
-        scatter_z(mine, [(part,) for part in other], ready)
-        for mine, other in zip(own, moved)
-    ]
-    return jnp.concatenate(shares, axis=0)
-
-
-def scatter_z(own, others, earlier=()):
-    mine, one, two, three = route_z(own, others, earlier)
+    share = lax.psum_scatter(
+        grads, "dev", scatter_dimension=0, tiled=True, axis_index_groups=same_low(devices)
+    )
+    return share.astype(jnp.float32)
+
+
+def add_z(mine, one, two, three):
     wide = jnp.float32
     return (
         mine
@@ -529,7 +462,6 @@
         body,
         [((rows, width), kind) for kind in kinds],
         (own[0], *others[0], own[1], *others[1]),
-        4 * rows * width,
         (layer,),
         earlier,
     )
@@ -556,7 +488,7 @@
     full_vec = gather_vectors(vectors)
     grad_down = jnp.where(live, cotangent, jnp.zeros_like(cotangent))
     full_proj, full_out, attn_ready = gather_attn(attn_weight)
-    gathered = gather_hidden(mlp_weight)
+    weights = gather_hidden(mlp_weight)
     grad_down_rows = gather_rows(grad_down.T)
 
     (
@@ -570,8 +502,7 @@
         down_bias,
         up_bias,
     ) = split_vectors(full_vec)
-    low_count = 8 if devices == 32 else 4
-    up_bias = up_bias.reshape(devices // 2 // low_count, low_count, -1)
+    up_bias = up_bias.reshape(devices // 8, 4, -1)
 
     inputs = tokens.astype(jnp.float32)
     first_out, normed_one, factor_one = normalize(inputs, gain_one, shift_one)
@@ -596,26 +527,20 @@
     second_out, normed_two, factor_two = normalize(middle, gain_two, shift_two)
     second_own = second_out.astype(low).T
     near, far = gather_rows(second_own)
-    parts = hidden_parts(gathered, here, devices, projected)
     near_grads, far_grads = grad_down_rows
-
-    every = sum(parts, [])
-    weights = [part[0] for part in every]
-    biases = [pick_blocks(up_bias, *part[1:]).reshape(-1, 1) for part in every]
-    far_blocks, far_sum = mlp_block(far, far_grads, weights, biases)
-    near_blocks, near_sum = mlp_block(near, near_grads, weights, biases)
-    grad_up_bias = jnp.zeros_like(up_bias)
-    for part, one, two in zip(every, near_blocks, far_blocks):
-        grad_up_bias = put_blocks(grad_up_bias, *part[1:], (one[2] + two[2]).reshape(-1))
-    blocks = [(one[:2], two[:2]) for one, two in zip(near_blocks, far_blocks)]
-    own_count = len(parts[0])
+    mine = here & 3
+    bias = lax.dynamic_index_in_dim(up_bias, mine, 1, False).reshape(-1, 1)
+    far_block, far_sum = mlp_block(far, far_grads, weights, bias)
+    near_block, near_sum = mlp_block(near, near_grads, weights, bias)
+    column_sums = (near_block[2] + far_block[2]).reshape(up_bias.shape[0], 1, -1)
+    grad_up_bias = lax.dynamic_update_slice(jnp.zeros_like(up_bias), column_sums, (0, mine, 0))
     far_total = (far_sum[0] + swap(far_sum[1], 1).astype(jnp.float32)).astype(low)
     grad_second = near_sum[0] + swap(near_sum[1], 1).astype(jnp.float32)
-    all_rows, all_grads = near + far, near_grads + far_grads
-    other_grads = []
-    if len(parts) > 1:
-        other_grads = mlp_weight_grads(blocks[own_count:], all_rows, all_grads, low, (far_total,))
-    far_taken = after(swap(far_total, 2), other_grads)
+    weight_grads = mlp_weight_grads(
+        near_block, far_block, near + far, near_grads + far_grads, (far_total,)
+    )
+    mlp_share = scatter_hidden(weight_grads)
+    far_taken = after(swap(far_total, 2), weight_grads)
     grad_second = (grad_second + far_taken.astype(jnp.float32)).T
 
     grad_down_wide = grad_down.astype(jnp.float32)
@@ -639,12 +564,10 @@
     attn_finish, attn_sent = scatter_attn(
         (grad_features, grad_branch.T), ((first_low.T, first_beside), (mixed_low.T, mixed_beside))
     )
-    own_grads = mlp_weight_grads(blocks[:own_count], all_rows, all_grads, jnp.float32, attn_sent)
-    down_keep, down_give = mlp_outputs(blocks, weights, sum(own_grads, ()))
+    down_keep, down_give = mlp_outputs(near_block[0], far_block[0], weights, attn_sent)
     down_taken = swap(down_give, 1).astype(jnp.float32)
     down = (down_keep[0] + down_taken[0]).T
     down_far = swap((down_keep[1] + down_taken[1]).astype(low), 2).astype(jnp.float32).T
-    mlp_share = scatter_hidden(own_grads, other_grads, attn_sent)
     attn_share = attn_finish()
     grad_features = after(grad_features, attn_sent).reshape(3 * width, total_rows)
     output = jnp.where(live, middle + (down + down_far + down_bias), 0.0).astype(low)

time: 454 us -> 340 us (0.75)
  waiting for transfers between devices: 222 us -> 157 us
  Pallas kernels: 89.1 us -> 70.7 us
  starting transfers between devices: 48.3 us -> 31.8 us
  local copies, waits for them, and re-layouts: 25.1 us -> 12.2 us
    ppermute x55 -> x43, waiting for transfers between devices: 198 us -> 132 us  [swap(): lax.ppermute(piece, 'dev', [(number, number ^ mask) for number in range(d...]
    pallas_call x10 -> x7, Pallas kernels: 85.9 us -> 67.5 us  [local_kernel(): pl.pallas_call(whole, out_shape=outs, in_specs=[pl.BlockSpec(memory_space...]
    ppermute x55 -> x43, starting transfers between devices: 48.2 us -> 31.7 us  [swap(): lax.ppermute(piece, 'dev', [(number, number ^ mask) for number in range(d...]
    add x7 -> x2, other arithmetic: 7.34 us -> 2.29 us  [the longest x1 2.05 us: add_z(): mine + swap(two, 16).astype(wide) + swap(three, 24).astype(wide)]
    another operation x8 -> x0, local copies, waits for them, and re-layouts: 4.97 us -> none  [the longest x4 3.46 us: shards(): biases = [pick_blocks(up_bias, *part[1:]).reshape(-1, 1) for part in every]]
    all_gather x3 -> x1, waiting for transfers between devices: 23.3 us -> 23.7 us  [gather_z(): lax.all_gather(shard, 'dev', axis=0, tiled=False, axis_index_groups=z_gro...]
  transfers between devices with their start and end apart: 58 -> 46, of which waited for: 22 -> 20; matrix products, arithmetic and copies ran while one was open for 11% -> 16% of each run, Pallas kernels for 14% -> 21%
where the time goes in v8:
time: 340 us; the launch traced here: 336 us
  waiting for transfers between devices  157 us (46%)
  Pallas kernels  70.7 us (21%)
  starting transfers between devices  31.8 us (9%)
  other arithmetic  31 us (9%)
  matrix products  17.4 us (5%)
  between operations  15.8 us (5%)
  local copies, waits for them, and re-layouts  12.2 us (4%)
    ppermute x43, waiting for transfers between devices, swap(): lax.ppermute(piece, 'dev', [(number, number ^ mask) for number in range(d...  132 us
    pallas_call x7, Pallas kernels, local_kernel(): pl.pallas_call(whole, out_shape=outs, in_specs=[pl.BlockSpec(memory_space...  67.5 us
    ppermute x43, starting transfers between devices, swap(): lax.ppermute(piece, 'dev', [(number, number ^ mask) for number in range(d...  31.7 us
    all_gather x1, waiting for transfers between devices, gather_z(): lax.all_gather(shard, 'dev', axis=0, tiled=False, axis_index_groups=z_gro...  23.7 us
    dot_general x1, matrix products, shards(): jnp.einsum('fr,fd->rd', grad_features, full_proj, preferred_element_type=...  7.1 us
  transfers between devices with their start and end apart: 46, of which 20 were waited for; matrix products, arithmetic and copies ran while one was open for 16% of the time, Pallas kernels for 21%

profile of v8, /device:TPU:8, one launch (start us, length us, event | category | flops | bytes accessed | tf_op | source)
XLA Modules:
  0.0 335.9 jit_solution(8015651683554617011)
XLA Ops:
  18.2 23.7 %all-gather.6.cloned.1.call-done = bf16[544,1088]{1,0:T(8,128)(2,1)} async-done(((bf16[136,1088]{1,0:T(8,128)(2,1)}), bf16[544,1088]{1,0:T(8,128)(2,1)}) %all-gather.6.cloned.1.call-update) | async-done | bytes 1183760 | tf_op jit(solution)/shard_map/all_gather | solution.py:287
  46.3 2.3 collective-permute-done.3
  49.9 21.2 %collective-permute-done.7.refs_3_ = bf16[4,136,1088]{2,1,0:T(8,128)(2,1)S(1)} collective-permute-done((bf16[4,136,1088]{2,1,0:T(8,128)(2,1)}, bf16[4,136,1088]{2,1,0:T(8,128)(2,1)S(1)}, u32[]{:S(2)}, u32[]{:S(2)}) %collective-permute-start.7) | collective-permute-done | bytes 1183776 | tf_op jit(solution)/shard_map/ppermute | solution.py:247
  73.5 7.2 %collective-permute-done.6.refs_2_ = bf16[4,136,1088]{2,1,0:T(8,128)(2,1)S(1)} collective-permute-done((bf16[4,136,1088]{2,1,0:T(8,128)(2,1)}, bf16[4,136,1088]{2,1,0:T(8,128)(2,1)S(1)}, u32[]{:S(2)}, u32[]{:S(2)}) %collective-permute-start.6) | collective-permute-done | bytes 1183776 | tf_op jit(solution)/shard_map/ppermute | solution.py:247
  85.4 14.9 %collective-permute-done.11.refs_7_ = bf16[2,136,1088]{2,1,0:T(8,128)(2,1)S(1)} collective-permute-done((bf16[2,136,1088]{2,1,0:T(8,128)(2,1)}, bf16[2,136,1088]{2,1,0:T(8,128)(2,1)S(1)}, u32[]{:S(2)}, u32[]{:S(2)}) %collective-permute-start.11) | collective-permute-done | bytes 591904 | tf_op jit(solution)/shard_map/ppermute | solution.py:247
  101.1 2.1 collective-permute-done.13.refs_9_
  103.5 3.2 shard_map.119
  106.7 2.5 fusion.40
  113.3 2.1 fusion.10
  118.2 14.4 %collective-permute-done.16.refs_0_.refs_2_ = bf16[1088,256]{1,0:T(8,128)(2,1)S(1)} collective-permute-done((bf16[1088,256]{1,0:T(8,128)(2,1)S(1)}, bf16[1088,256]{1,0:T(8,128)(2,1)S(1)}, u32[]{:S(2)}, u32[]{:S(2)}) %collective-permute-start.16) | collective-permute-done | bytes 557088 | tf_op jit(solution)/shard_map/ppermute | solution.py:247
  136.2 11.8 %shard_map.121 = (bf16[2,1088,256]{2,1,0:T(8,128)(2,1)}, bf16[2,1088,256]{2,1,0:T(8,128)(2,1)}, f32[1088,1]{1,0:T(8,128)}, f32[1088,256]{1,0:T(8,128)}, bf16[1088,256]{1,0:T(8,128)(2,1)}) custom-call(bf16[1088,256]{1,0:T(8,128)(2,1)} %copy-done.16, bf16[1088,256]{1,0:T(8,128)(2,1)} %copy-done.18, bf16[1088,256]{1,0:T(8,128)(2,1)} %collective-permute-done.18.refs_2_.refs_6_, ...), custom_call_target="tpu_custom_call" | custom-call | flops 1 | bytes 1 | tf_op jit(solution)/shard_map/pallas_call | solution.py:103
  149.6 11.4 %shard_map.120 = (bf16[2,1088,256]{2,1,0:T(8,128)(2,1)}, bf16[2,1088,256]{2,1,0:T(8,128)(2,1)}, f32[1088,1]{1,0:T(8,128)}, f32[1088,256]{1,0:T(8,128)}, bf16[1088,256]{1,0:T(8,128)(2,1)}) custom-call(bf16[1088,256]{1,0:T(8,128)(2,1)} %copy-done.11, bf16[1088,256]{1,0:T(8,128)(2,1)} %collective-permute-done.14.refs_1_, ...), custom_call_target="tpu_custom_call" | custom-call | flops 1 | bytes 1 | tf_op jit(solution)/shard_map/pallas_call | solution.py:103
  162.6 2.1 slice_bitcast_fusion.refs_2_
  164.7 11.9 %shard_map.122 = bf16[2176,1088]{1,0:T(8,128)(2,1)} custom-call(bf16[1088,256]{1,0:T(8,128)(2,1)} %copy-done.11, bf16[1088,256]{1,0:T(8,128)(2,1)} %collective-permute-done.14.refs_1_, bf16[1088,256]{1,0:T(8,128)(2,1)} %copy-done.16, bf16[1088,256]{1,0:T(8,128)(2,1)} %copy-done.18, bf16[1088,256]{1,0:T(8,128)(2,1)} %fusion.33.refs_2_.refs_4_, ...), custom_call_target="tpu_custom_call" | custom-call | flops 1 | bytes 1 | tf_op jit(solution)/shard_map/pallas_call | solution.py:103
  182.5 2.8 convolution_convert_fusion.refs_4_
  185.3 9.0 %shard_map.123 = bf16[3,1088,256]{2,1,0:T(8,128)(2,1)} custom-call(s32[2]{0:T(128)} %pad_add_fusion.refs_0_, bf16[1088,256]{1,0:T(8,128)(2,1)} %bitcast.96, bf16[1088,256]{1,0:T(8,128)(2,1)} %slice_bitcast_fusion.refs_2_, bf16[1088,256]{1,0:T(8,128)(2,1)} %bitcast.98, bf16[1088,256]{1,0:T(8,128)(2,1)} %convolution_convert_fusion.refs_4_, ...), custom_call_target="tpu_custom_call" | custom-call | flops 1 | bytes 1 | tf_op jit(solution)/shard_map/pallas_call | solution.py:103
  200.7 10.0 %shard_map.124 = (bf16[2,136,1088]{2,1,0:T(8,128)(2,1)}, bf16[2,136,1088]{2,1,0:T(8,128)(2,1)}, bf16[2,136,1088]{2,1,0:T(8,128)(2,1)}, f32[2,136,1088]{2,1,0:T(8...) custom-call(s32[1]{0:T(128)} %bitcast.block_ref.refs_0_, ...), custom_call_target="tpu_custom_call" | custom-call | flops 1 | bytes 1 | tf_op jit(solution)/shard_map/pallas_call | solution.py:103
  210.6 7.1 %fusion.17 = (f32[1088]{0:T(1024)S(1)}, f32[256]{0:T(256)S(1)}, f32[256]{0:T(256)S(1)}, f32[1088]{0:T(1024)S(1)}, f32[256,1088]{0,1:T(8,128)S(1)}) fusion(bf16[256,1088]{0,1:T(8,128)(2,1)S(1)} %copy-done.6, f32[256]{0:T(256)S(1)} %add_rsqrt_fusion.1, f32[256]{0:T(256)S(1)} %broadcast_multiply_fusion.5, f32[1088]{0:T(1024)S(1)} %get-tuple-element.91, ...), kind=kOutput, calls=%fused_computation.29 | convolution fusion | flops 1821013504 | bytes 10461952 | tf_op jit(solution)/shard_map/fr,fd->rd/dot_general | solution.py:575
  223.6 3.8 %collective-permute-done.38 = f32[6528]{0:T(1024)S(1)} collective-permute-done((f32[6528]{0:T(1024)S(1)}, f32[6528]{0:T(1024)S(1)}, u32[]{:S(2)}, u32[]{:S(2)}) %collective-permute-start.38) | collective-permute-done | bytes 26144 | tf_op jit(solution)/shard_map/ppermute | solution.py:247
  227.4 2.3 collective-permute-start.39
  231.6 2.2 collective-permute-start.40
  233.8 9.4 %shard_map.125 = (f32[2,1088,256]{2,1,0:T(8,128)}, bf16[2,1088,256]{2,1,0:T(8,128)(2,1)}) custom-call(bf16[2,1088,256]{2,1,0:T(8,128)(2,1)} %get-tuple-element.35.refs_8_.refs_0_, bf16[2,1088,256]{2,1,0:T(8,128)(2,1)} %get-tuple-element.36.refs_9_.refs_1_, bf16[4,544,1088]{2,1,0:T(8,128)(2,1)} %bitcast.91, f32[2,136,1088]{2,1,0:T(8,128)} %get-tuple-element.44.refs_3_, ...), custom_call_target="tpu_custom_call" | custom-call | flops 1 | bytes 1 | tf_op jit(solution)/shard_map/pallas_call | solution.py:103
  248.2 2.0 add_convert_fusion.1
  250.3 18.6 %collective-permute-done.32 = bf16[2,136,1088]{2,1,0:T(8,128)(2,1)S(1)} collective-permute-done((bf16[2,136,1088]{2,1,0:T(8,128)(2,1)}, bf16[2,136,1088]{2,1,0:T(8,128)(2,1)S(1)}, u32[]{:S(2)}, u32[]{:S(2)}) %collective-permute-start.32) | collective-permute-done | bytes 591904 | tf_op jit(solution)/shard_map/ppermute | solution.py:247
  272.5 9.9 %collective-permute-done.34.refs_6_ = bf16[2,136,1088]{2,1,0:T(8,128)(2,1)} collective-permute-done((bf16[2,136,1088]{2,1,0:T(8,128)(2,1)}, bf16[2,136,1088]{2,1,0:T(8,128)(2,1)}, u32[]{:S(2)}, u32[]{:S(2)}) %collective-permute-start.34) | collective-permute-done | bytes 591904 | tf_op jit(solution)/shard_map/ppermute | solution.py:247
  282.4 10.7 %collective-permute-done.31.refs_3_ = bf16[2,136,1088]{2,1,0:T(8,128)(2,1)} collective-permute-done((bf16[2,136,1088]{2,1,0:T(8,128)(2,1)}, bf16[2,136,1088]{2,1,0:T(8,128)(2,1)}, u32[]{:S(2)}, u32[]{:S(2)}) %collective-permute-start.31) | collective-permute-done | bytes 591904 | tf_op jit(solution)/shard_map/ppermute | solution.py:247
  293.2 4.0 %shard_map.126 = (f32[136,1088]{1,0:T(8,128)}, bf16[136,1088]{1,0:T(8,128)(2,1)}, bf16[136,1088]{1,0:T(8,128)(2,1)}, bf16[136,1088]{1,0:T(8,128)(2,1)}) custom-call(s32[1]{0:T(128)} %bitcast.30.refs_0_, f32[2,136,1088]{2,1,0:T(8,128)} %get-tuple-element.49.refs_1_, bf16[2,136,1088]{2,1,0:T(8,128)(2,1)} %collective-permute-done.29.refs_2_, ...), custom_call_target="tpu_custom_call" | custom-call | flops 1 | bytes 1 | tf_op jit(solution)/shard_map/pallas_call | solution.py:103
  299.2 2.5 collective-permute-start.37
  304.3 11.3 %collective-permute-done.35 = bf16[136,1088]{1,0:T(8,128)(2,1)S(1)} collective-permute-done((bf16[136,1088]{1,0:T(8,128)(2,1)}, bf16[136,1088]{1,0:T(8,128)(2,1)S(1)}, u32[]{:S(2)}, u32[]{:S(2)}) %collective-permute-start.35) | collective-permute-done | bytes 295968 | tf_op jit(solution)/shard_map/ppermute | solution.py:247
  315.5 8.3 %collective-permute-done.36 = bf16[136,1088]{1,0:T(8,128)(2,1)S(1)} collective-permute-done((bf16[136,1088]{1,0:T(8,128)(2,1)}, bf16[136,1088]{1,0:T(8,128)(2,1)S(1)}, u32[]{:S(2)}, u32[]{:S(2)}) %collective-permute-start.36) | collective-permute-done | bytes 295968 | tf_op jit(solution)/shard_map/ppermute | solution.py:247
  323.8 2.0 convert_add_fusion.2
  327.0 2.2 convert_element_type.183
  (199 shorter events, 71.0 us)
Async XLA Ops:
  7.2 34.7 %all-gather.6.cloned.1.call-start = ((), (), s32[]{:S(2)}) async-start(), calls=%async_computation.3 | async-start | bytes 1566720 | tf_op jit(solution)/shard_map/all_gather | solution.py:287
  7.9 127.5 %all-gather.4.cloned.1.call-start = ((), (), s32[]{:S(2)}) async-start(), calls=%async_computation.1 | async-start | bytes 5640192 | tf_op jit(solution)/shard_map/all_gather | solution.py:417
  8.7 318.3 %reduce-scatter.2.cloned.1.call-start = ((), (), s32[]{:S(2)}) async-start(), calls=%async_computation.2 | async-start | bytes 5640192 | tf_op jit(solution)/shard_map/reduce_scatter | solution.py:423
  16.6 28.2 %collective-permute-start.2 = (bf16[1632]{0:T(1024)(128)(2,1)S(1)}, bf16[1632]{0:T(1024)(128)(2,1)S(1)}, u32[]{:S(2)}, u32[]{:S(2)}) collective-permute-start(bf16[1632]{0:T(1024)(128)(2,1)S(1)} %pad_maximum_fusion.2), channel_id=1, source_target_pairs={{0,4},{1,5},{2,6},{3,7},{4,0},{5,1},{6,2},{7,3},{8,12},{9,13},{10,... | collective-permute-start | bytes 9800 | tf_op jit(solution)/shard_map/ppermute | solution.py:247
  41.9 29.3 %collective-permute-start.7 = (bf16[4,136,1088]{2,1,0:T(8,128)(2,1)}, bf16[4,136,1088]{2,1,0:T(8,128)(2,1)S(1)}, u32[]{:S(2)}, u32[]{:S(2)}) collective-permute-start(bf16[4,136,1088]{2,1,0:T(8,128)(2,1)} %bitcast.81), channel_id=1, source_target_pairs={{0,2},{1,3},{2,0},{3,1},{4,6},{5,7},{6,4},{7,5},{8,10},{9,11},{10,... | collective-permute-start | bytes 3551240 | tf_op jit(solution)/shard_map/ppermute | solution.py:247
  43.3 37.4 %collective-permute-start.6 = (bf16[4,136,1088]{2,1,0:T(8,128)(2,1)}, bf16[4,136,1088]{2,1,0:T(8,128)(2,1)S(1)}, u32[]{:S(2)}, u32[]{:S(2)}) collective-permute-start(bf16[4,136,1088]{2,1,0:T(8,128)(2,1)} %bitcast.82), channel_id=1, source_target_pairs={{0,4},{1,5},{2,6},{3,7},{4,0},{5,1},{6,2},{7,3},{8,12},{9,13},{10,... | collective-permute-start | bytes 3551240 | tf_op jit(solution)/shard_map/ppermute | solution.py:247
  48.8 33.4 %collective-permute-start.4 = (bf16[6528]{0:T(1024)(128)(2,1)S(1)}, bf16[6528]{0:T(1024)(128)(2,1)S(1)}, u32[]{:S(2)}, u32[]{:S(2)}) collective-permute-start(bf16[6528]{0:T(1024)(128)(2,1)S(1)} %pad_maximum_fusion), channel_id=1, source_target_pairs={{0,16},{1,17},{2,18},{3,19},{4,20},{5,21},{6,22},{7,23},{8,24},{9,... | collective-permute-start | bytes 39176 | tf_op jit(solution)/shard_map/ppermute | solution.py:247
  49.9 51.1 %collective-permute-start.5 = (bf16[4,136,1088]{2,1,0:T(8,128)(2,1)}, bf16[4,136,1088]{2,1,0:T(8,128)(2,1)}, u32[]{:S(2)}, u32[]{:S(2)}) collective-permute-start(bf16[4,136,1088]{2,1,0:T(8,128)(2,1)} %bitcast.83), channel_id=1, source_target_pairs={{0,1},{1,0},{2,3},{3,2},{4,5},{5,4},{6,7},{7,6},{8,9},{9,8},{10,11... | collective-permute-start | bytes 3551240 | tf_op jit(solution)/shard_map/ppermute | solution.py:247
  72.0 28.3 %collective-permute-start.11 = (bf16[2,136,1088]{2,1,0:T(8,128)(2,1)}, bf16[2,136,1088]{2,1,0:T(8,128)(2,1)S(1)}, u32[]{:S(2)}, u32[]{:S(2)}) collective-permute-start(bf16[2,136,1088]{2,1,0:T(8,128)(2,1)} %slice.144), channel_id=1, source_target_pairs={{0,4},{1,5},{2,6},{3,7},{4,0},{5,1},{6,2},{7,3},{8,12},{9,13},{10,... | collective-permute-start | bytes 1775624 | tf_op jit(solution)/shard_map/ppermute | solution.py:247
  81.6 18.7 %collective-permute-start.10 = (bf16[2,136,1088]{2,1,0:T(8,128)(2,1)}, bf16[2,136,1088]{2,1,0:T(8,128)(2,1)}, u32[]{:S(2)}, u32[]{:S(2)}) collective-permute-start(bf16[2,136,1088]{2,1,0:T(8,128)(2,1)} %slice.143), channel_id=1, source_target_pairs={{0,2},{1,3},{2,0},{3,1},{4,6},{5,7},{6,4},{7,5},{8,10},{9,11},{10,... | collective-permute-start | bytes 1775624 | tf_op jit(solution)/shard_map/ppermute | solution.py:247
  82.2 18.9 %collective-permute-start.9 = (bf16[4,136,1088]{2,1,0:T(8,128)(2,1)S(1)}, bf16[4,136,1088]{2,1,0:T(8,128)(2,1)}, u32[]{:S(2)}, u32[]{:S(2)}) collective-permute-start(bf16[4,136,1088]{2,1,0:T(8,128)(2,1)S(1)} %collective-permute-done.7.refs_3_), channel_id=1, source_target_pairs={{0,1},{1,0},{2,3},{3,2},{4,5},{5,4},{6,7},{7,6},{8,9},{9,8},{10,11... | collective-permute-start | bytes 3551240 | tf_op jit(solution)/shard_map/ppermute | solution.py:247
  82.2 18.9 %collective-permute-start.8 = (bf16[4,136,1088]{2,1,0:T(8,128)(2,1)S(1)}, bf16[4,136,1088]{2,1,0:T(8,128)(2,1)}, u32[]{:S(2)}, u32[]{:S(2)}) collective-permute-start(bf16[4,136,1088]{2,1,0:T(8,128)(2,1)S(1)} %collective-permute-done.6.refs_2_), channel_id=1, source_target_pairs={{0,1},{1,0},{2,3},{3,2},{4,5},{5,4},{6,7},{7,6},{8,9},{9,8},{10,11... | collective-permute-start | bytes 3551240 | tf_op jit(solution)/shard_map/ppermute | solution.py:247
  101.1 17.0 %collective-permute-start.18 = (bf16[1088,256]{1,0:T(8,128)(2,1)}, bf16[1088,256]{1,0:T(8,128)(2,1)}, u32[]{:S(2)}, u32[]{:S(2)}) collective-permute-start(bf16[1088,256]{1,0:T(8,128)(2,1)} %fusion.33.refs_2_.refs_4_), channel_id=1, source_target_pairs={{0,2},{1,3},{2,0},{3,1},{4,6},{5,7},{6,4},{7,5},{8,10},{9,11},{10,... | collective-permute-start | bytes 1671176 | tf_op jit(solution)/shard_map/ppermute | solution.py:247
  118.0 16.4 %collective-permute-start.19 = (bf16[1088,256]{1,0:T(8,128)(2,1)}, bf16[1088,256]{1,0:T(8,128)(2,1)S(1)}, u32[]{:S(2)}, u32[]{:S(2)}) collective-permute-start(bf16[1088,256]{1,0:T(8,128)(2,1)} %collective-permute-done.18.refs_2_.refs_6_), channel_id=1, source_target_pairs={{0,1},{1,0},{2,3},{3,2},{4,5},{5,4},{6,7},{7,6},{8,9},{9,8},{10,11... | collective-permute-start | bytes 1671176 | tf_op jit(solution)/shard_map/ppermute | solution.py:247
  132.7 16.9 %collective-permute-start.15 = (bf16[1088,256]{1,0:T(8,128)(2,1)}, bf16[1088,256]{1,0:T(8,128)(2,1)}, u32[]{:S(2)}, u32[]{:S(2)}) collective-permute-start(bf16[1088,256]{1,0:T(8,128)(2,1)} %fusion.33.refs_2_.refs_4_), channel_id=1, source_target_pairs={{0,1},{1,0},{2,3},{3,2},{4,5},{5,4},{6,7},{7,6},{8,9},{9,8},{10,11... | collective-permute-start | bytes 1671176 | tf_op jit(solution)/shard_map/ppermute | solution.py:247
  134.4 15.2 %collective-permute-start.14 = (bf16[1088,256]{1,0:T(8,128)(2,1)S(1)}, bf16[1088,256]{1,0:T(8,128)(2,1)}, u32[]{:S(2)}, u32[]{:S(2)}) collective-permute-start(bf16[1088,256]{1,0:T(8,128)(2,1)S(1)} %fusion.31.refs_0_), channel_id=1, source_target_pairs={{0,1},{1,0},{2,3},{3,2},{4,5},{5,4},{6,7},{7,6},{8,9},{9,8},{10,11... | collective-permute-start | bytes 1671176 | tf_op jit(solution)/shard_map/ppermute | solution.py:247
  161.0 15.6 %collective-permute-start.20 = (bf16[1088,256]{1,0:T(8,128)(2,1)}, bf16[1088,256]{1,0:T(8,128)(2,1)}, u32[]{:S(2)}, u32[]{:S(2)}) collective-permute-start(bf16[1088,256]{1,0:T(8,128)(2,1)} %get-tuple-element.38), channel_id=1, source_target_pairs={{0,1},{1,0},{2,3},{3,2},{4,5},{5,4},{6,7},{7,6},{8,9},{9,8},{10,11... | collective-permute-start | bytes 1671176 | tf_op jit(solution)/shard_map/ppermute | solution.py:247
  161.6 15.0 %collective-permute-start.22 = (bf16[1088,256]{1,0:T(8,128)(2,1)S(1)}, bf16[1088,256]{1,0:T(8,128)(2,1)S(1)}, u32[]{:S(2)}, u32[]{:S(2)}) collective-permute-start(bf16[1088,256]{1,0:T(8,128)(2,1)S(1)} %add_convert_fusion.2.refs_12_), channel_id=1, source_target_pairs={{0,2},{1,3},{2,0},{3,1},{4,6},{5,7},{6,4},{7,5},{8,10},{9,11},{10,... | collective-permute-start | bytes 1671176 | tf_op jit(solution)/shard_map/ppermute | solution.py:247
  229.7 17.4 %collective-permute-start.30 = (bf16[2,136,1088]{2,1,0:T(8,128)(2,1)}, bf16[2,136,1088]{2,1,0:T(8,128)(2,1)}, u32[]{:S(2)}, u32[]{:S(2)}) collective-permute-start(bf16[2,136,1088]{2,1,0:T(8,128)(2,1)} %get-tuple-element.51), channel_id=1, source_target_pairs={{0,2},{1,3},{2,0},{3,1},{4,6},{5,7},{6,4},{7,5},{8,10},{9,11},{10,... | collective-permute-start | bytes 1775624 | tf_op jit(solution)/shard_map/ppermute | solution.py:247
  231.6 15.3 %collective-permute-start.40 = (f32[1632]{0:T(1024)S(1)}, f32[1632]{0:T(1024)S(1)}, u32[]{:S(2)}, u32[]{:S(2)}) collective-permute-start(f32[1632]{0:T(1024)S(1)} %slice_select_fusion.1), channel_id=1, source_target_pairs={{0,4},{1,5},{2,6},{3,7},{4,0},{5,1},{6,2},{7,3},{8,12},{9,13},{10,... | collective-permute-start | bytes 19592 | tf_op jit(solution)/shard_map/ppermute | solution.py:247
  243.2 29.2 %collective-permute-start.29 = (bf16[2,136,1088]{2,1,0:T(8,128)(2,1)}, bf16[2,136,1088]{2,1,0:T(8,128)(2,1)}, u32[]{:S(2)}, u32[]{:S(2)}) collective-permute-start(bf16[2,136,1088]{2,1,0:T(8,128)(2,1)} %get-tuple-element.50), channel_id=1, source_target_pairs={{0,2},{1,3},{2,0},{3,1},{4,6},{5,7},{6,4},{7,5},{8,10},{9,11},{10,... | collective-permute-start | bytes 1775624 | tf_op jit(solution)/shard_map/ppermute | solution.py:247
  244.9 24.0 %collective-permute-start.32 = (bf16[2,136,1088]{2,1,0:T(8,128)(2,1)}, bf16[2,136,1088]{2,1,0:T(8,128)(2,1)S(1)}, u32[]{:S(2)}, u32[]{:S(2)}) collective-permute-start(bf16[2,136,1088]{2,1,0:T(8,128)(2,1)} %get-tuple-element.53), channel_id=1, source_target_pairs={{0,4},{1,5},{2,6},{3,7},{4,0},{5,1},{6,2},{7,3},{8,12},{9,13},{10,... | collective-permute-start | bytes 1775624 | tf_op jit(solution)/shard_map/ppermute | solution.py:247
  245.0 37.4 %collective-permute-start.34 = (bf16[2,136,1088]{2,1,0:T(8,128)(2,1)}, bf16[2,136,1088]{2,1,0:T(8,128)(2,1)}, u32[]{:S(2)}, u32[]{:S(2)}) collective-permute-start(bf16[2,136,1088]{2,1,0:T(8,128)(2,1)} %get-tuple-element.54), channel_id=1, source_target_pairs={{0,4},{1,5},{2,6},{3,7},{4,0},{5,1},{6,2},{7,3},{8,12},{9,13},{10,... | collective-permute-start | bytes 1775624 | tf_op jit(solution)/shard_map/ppermute | solution.py:247
  246.9 23.1 %collective-permute-start.27 = (bf16[2,1088,256]{2,1,0:T(8,128)(2,1)}, bf16[2,1088,256]{2,1,0:T(8,128)(2,1)S(1)}, u32[]{:S(2)}, u32[]{:S(2)}) collective-permute-start(bf16[2,1088,256]{2,1,0:T(8,128)(2,1)} %get-tuple-element.47), channel_id=1, source_target_pairs={{0,1},{1,0},{2,3},{3,2},{4,5},{5,4},{6,7},{7,6},{8,9},{9,8},{10,11... | collective-permute-start | bytes 3342344 | tf_op jit(solution)/shard_map/ppermute | solution.py:247
  247.1 22.8 %collective-permute-start.41 = (f32[816]{0:T(1024)S(1)}, f32[816]{0:T(1024)S(1)}, u32[]{:S(2)}, u32[]{:S(2)}) collective-permute-start(f32[816]{0:T(1024)S(1)} %slice_select_fusion.2), channel_id=1, source_target_pairs={{0,2},{1,3},{2,0},{3,1},{4,6},{5,7},{6,4},{7,5},{8,10},{9,11},{10,... | collective-permute-start | bytes 9800 | tf_op jit(solution)/shard_map/ppermute | solution.py:247
  268.9 24.3 %collective-permute-start.31 = (bf16[2,136,1088]{2,1,0:T(8,128)(2,1)}, bf16[2,136,1088]{2,1,0:T(8,128)(2,1)}, u32[]{:S(2)}, u32[]{:S(2)}) collective-permute-start(bf16[2,136,1088]{2,1,0:T(8,128)(2,1)} %add_convert_fusion.1), channel_id=1, source_target_pairs={{0,4},{1,5},{2,6},{3,7},{4,0},{5,1},{6,2},{7,3},{8,12},{9,13},{10,... | collective-permute-start | bytes 1775624 | tf_op jit(solution)/shard_map/ppermute | solution.py:247
  269.9 23.3 %collective-permute-start.33 = (bf16[2,136,1088]{2,1,0:T(8,128)(2,1)}, bf16[2,136,1088]{2,1,0:T(8,128)(2,1)}, u32[]{:S(2)}, u32[]{:S(2)}) collective-permute-start(bf16[2,136,1088]{2,1,0:T(8,128)(2,1)} %add_convert_fusion), channel_id=1, source_target_pairs={{0,2},{1,3},{2,0},{3,1},{4,6},{5,7},{6,4},{7,5},{8,10},{9,11},{10,... | collective-permute-start | bytes 1775624 | tf_op jit(solution)/shard_map/ppermute | solution.py:247
  271.0 32.6 %collective-permute-start.42 = (f32[408]{0:T(512)S(1)}, f32[408]{0:T(512)S(1)}, u32[]{:S(2)}, u32[]{:S(2)}) collective-permute-start(f32[408]{0:T(512)S(1)} %slice_select_fusion.3), channel_id=1, source_target_pairs={{0,1},{1,0},{2,3},{3,2},{4,5},{5,4},{6,7},{7,6},{8,9},{9,8},{10,11... | collective-permute-start | bytes 4904 | tf_op jit(solution)/shard_map/ppermute | solution.py:247
  297.2 18.3 %collective-permute-start.35 = (bf16[136,1088]{1,0:T(8,128)(2,1)}, bf16[136,1088]{1,0:T(8,128)(2,1)S(1)}, u32[]{:S(2)}, u32[]{:S(2)}) collective-permute-start(bf16[136,1088]{1,0:T(8,128)(2,1)} %get-tuple-element.56), channel_id=1, source_target_pairs={{0,16},{1,17},{2,18},{3,19},{4,20},{5,21},{6,22},{7,23},{8,24},{9,... | collective-permute-start | bytes 887816 | tf_op jit(solution)/shard_map/ppermute | solution.py:247
  297.5 26.4 %collective-permute-start.36 = (bf16[136,1088]{1,0:T(8,128)(2,1)}, bf16[136,1088]{1,0:T(8,128)(2,1)S(1)}, u32[]{:S(2)}, u32[]{:S(2)}) collective-permute-start(bf16[136,1088]{1,0:T(8,128)(2,1)} %get-tuple-element.57), channel_id=1, source_target_pairs={{0,24},{1,25},{2,26},{3,27},{4,28},{5,29},{6,30},{7,31},{8,16},{9,... | collective-permute-start | bytes 887816 | tf_op jit(solution)/shard_map/ppermute | solution.py:247
  299.2 24.6 %collective-permute-start.37 = (bf16[136,1088]{1,0:T(8,128)(2,1)}, bf16[136,1088]{1,0:T(8,128)(2,1)S(1)}, u32[]{:S(2)}, u32[]{:S(2)}) collective-permute-start(bf16[136,1088]{1,0:T(8,128)(2,1)} %get-tuple-element.58), channel_id=1, source_target_pairs={{0,8},{1,9},{2,10},{3,11},{4,12},{5,13},{6,14},{7,15},{8,0},{9,1},... | collective-permute-start | bytes 887816 | tf_op jit(solution)/shard_map/ppermute | solution.py:247
  303.2 22.7 %collective-permute-start.28 = (bf16[1088,256]{1,0:T(8,128)(2,1)S(1)}, bf16[1088,256]{1,0:T(8,128)(2,1)S(1)}, u32[]{:S(2)}, u32[]{:S(2)}) collective-permute-start(bf16[1088,256]{1,0:T(8,128)(2,1)S(1)} %fusion.32), channel_id=1, source_target_pairs={{0,2},{1,3},{2,0},{3,1},{4,6},{5,7},{6,4},{7,5},{8,10},{9,11},{10,... | collective-permute-start | bytes 1671176 | tf_op jit(solution)/shard_map/ppermute | solution.py:247
  (39 other events, 255.1 us)
Sparse Core Ops, SparseCore 0:
  9.6 32.2 all-gather.5
  44.0 91.3 all-gather.3
  176.7 105.4 reduce-scatter.1

commit v9 on v8

--- a/solution.py
+++ b/solution.py
@@ -195,13 +195,16 @@
     low = jnp.bfloat16
 
     def body(need, send, *refs):
-        need()
-        row_refs, grad_refs = refs[:number], refs[number : 2 * number]
-        near_act, far_act, near_up, far_up, out = refs[2 * number :]
+        near_up, far_up = refs[number : number + 2]
+        row_refs, grad_refs = refs[:number], refs[number + 2 : 2 * number + 2]
+        near_act, far_act, out = refs[2 * number + 2 :]
+        need(*range(number + 2))
         for which, pair, others in (
             (0, (near_up, far_up), row_refs),
             (1, (near_act, far_act), grad_refs),
         ):
+            if which:
+                need()
             for part in range(2):
                 span = slice(part * (count // 2), (part + 1) * (count // 2))
                 total = None
@@ -212,7 +215,7 @@
                 start = which * count + part * (count // 2)
                 out[start : start + count // 2, :] = total.astype(low)
 
-    operands = (*rows, *grads, near[0], far[0], near[1], far[1])
+    operands = (*rows, near[1], far[1], *grads, near[0], far[0])
     return local_kernel(body, [((2 * count, width), low)], operands, (), earlier)[0]
 
 

time: 340 us -> 339 us (level)
  transfers between devices with their start and end apart: 46 -> 46, of which waited for: 20 -> 21; matrix products, arithmetic and copies ran while one was open for 16% -> 16% of each run, Pallas kernels for 21% -> 21%
where the time goes in v9:
time: 339 us; the launch traced here: 335 us
  waiting for transfers between devices  158 us (47%)
  Pallas kernels  69.6 us (21%)
  starting transfers between devices  31.2 us (9%)
  other arithmetic  31.1 us (9%)
  matrix products  17.4 us (5%)
  between operations  15.8 us (5%)
  local copies, waits for them, and re-layouts  11.6 us (3%)
    ppermute x43, waiting for transfers between devices, swap(): lax.ppermute(piece, 'dev', [(number, number ^ mask) for number in range(d...  133 us
    pallas_call x7, Pallas kernels, local_kernel(): pl.pallas_call(whole, out_shape=outs, in_specs=[pl.BlockSpec(memory_space...  66.4 us
    ppermute x43, starting transfers between devices, swap(): lax.ppermute(piece, 'dev', [(number, number ^ mask) for number in range(d...  31.1 us
    all_gather x1, waiting for transfers between devices, gather_z(): lax.all_gather(shard, 'dev', axis=0, tiled=False, axis_index_groups=z_gro...  23.7 us
    dot_general x1, matrix products, shards(): jnp.einsum('fr,fd->rd', grad_features, full_proj, preferred_element_type=...  7.09 us
  transfers between devices with their start and end apart: 46, of which 21 were waited for; matrix products, arithmetic and copies ran while one was open for 16% of the time, Pallas kernels for 21%

profile of v9, /device:TPU:8, one launch (start us, length us, event | category | flops | bytes accessed | tf_op | source)
XLA Modules:
  0.0 334.8 jit_solution(17134027314414659045)
XLA Ops:
  18.2 23.7 %all-gather.6.cloned.1.call-done = bf16[544,1088]{1,0:T(8,128)(2,1)} async-done(((bf16[136,1088]{1,0:T(8,128)(2,1)}), bf16[544,1088]{1,0:T(8,128)(2,1)}) %all-gather.6.cloned.1.call-update) | async-done | bytes 1183760 | tf_op jit(solution)/shard_map/all_gather | solution.py:290
  46.3 2.3 collective-permute-done.3
  49.9 21.2 %collective-permute-done.7.refs_3_ = bf16[4,136,1088]{2,1,0:T(8,128)(2,1)S(1)} collective-permute-done((bf16[4,136,1088]{2,1,0:T(8,128)(2,1)}, bf16[4,136,1088]{2,1,0:T(8,128)(2,1)S(1)}, u32[]{:S(2)}, u32[]{:S(2)}) %collective-permute-start.7) | collective-permute-done | bytes 1183776 | tf_op jit(solution)/shard_map/ppermute | solution.py:250
  73.5 7.2 %collective-permute-done.6.refs_2_ = bf16[4,136,1088]{2,1,0:T(8,128)(2,1)S(1)} collective-permute-done((bf16[4,136,1088]{2,1,0:T(8,128)(2,1)}, bf16[4,136,1088]{2,1,0:T(8,128)(2,1)S(1)}, u32[]{:S(2)}, u32[]{:S(2)}) %collective-permute-start.6) | collective-permute-done | bytes 1183776 | tf_op jit(solution)/shard_map/ppermute | solution.py:250
  83.4 2.0 fusion.33.refs_2_.refs_6_
  85.4 14.9 %collective-permute-done.11.refs_7_ = bf16[2,136,1088]{2,1,0:T(8,128)(2,1)S(1)} collective-permute-done((bf16[2,136,1088]{2,1,0:T(8,128)(2,1)}, bf16[2,136,1088]{2,1,0:T(8,128)(2,1)S(1)}, u32[]{:S(2)}, u32[]{:S(2)}) %collective-permute-start.11) | collective-permute-done | bytes 591904 | tf_op jit(solution)/shard_map/ppermute | solution.py:250
  101.1 2.1 collective-permute-done.13.refs_9_
  103.5 3.2 shard_map.119
  106.7 2.5 fusion.40
  113.3 2.1 fusion.10
  118.2 14.4 %collective-permute-done.16.refs_0_.refs_2_ = bf16[1088,256]{1,0:T(8,128)(2,1)S(1)} collective-permute-done((bf16[1088,256]{1,0:T(8,128)(2,1)S(1)}, bf16[1088,256]{1,0:T(8,128)(2,1)S(1)}, u32[]{:S(2)}, u32[]{:S(2)}) %collective-permute-start.16) | collective-permute-done | bytes 557088 | tf_op jit(solution)/shard_map/ppermute | solution.py:250
  136.2 11.8 %shard_map.121 = (bf16[2,1088,256]{2,1,0:T(8,128)(2,1)}, bf16[2,1088,256]{2,1,0:T(8,128)(2,1)}, f32[1088,1]{1,0:T(8,128)}, f32[1088,256]{1,0:T(8,128)}, bf16[1088,256]{1,0:T(8,128)(2,1)}) custom-call(bf16[1088,256]{1,0:T(8,128)(2,1)} %copy-done.16, bf16[1088,256]{1,0:T(8,128)(2,1)} %copy-done.18, bf16[1088,256]{1,0:T(8,128)(2,1)} %collective-permute-done.18.refs_2_.refs_8_, ...), custom_call_target="tpu_custom_call" | custom-call | flops 1 | bytes 1 | tf_op jit(solution)/shard_map/pallas_call | solution.py:103
  149.6 11.4 %shard_map.120 = (bf16[2,1088,256]{2,1,0:T(8,128)(2,1)}, bf16[2,1088,256]{2,1,0:T(8,128)(2,1)}, f32[1088,1]{1,0:T(8,128)}, f32[1088,256]{1,0:T(8,128)}, bf16[1088,256]{1,0:T(8,128)(2,1)}) custom-call(bf16[1088,256]{1,0:T(8,128)(2,1)} %copy-done.11, bf16[1088,256]{1,0:T(8,128)(2,1)} %collective-permute-done.14.refs_1_, ...), custom_call_target="tpu_custom_call" | custom-call | flops 1 | bytes 1 | tf_op jit(solution)/shard_map/pallas_call | solution.py:103
  162.6 2.1 slice_bitcast_fusion.refs_2_
  164.7 10.8 %shard_map.122 = bf16[2176,1088]{1,0:T(8,128)(2,1)} custom-call(bf16[1088,256]{1,0:T(8,128)(2,1)} %copy-done.11, bf16[1088,256]{1,0:T(8,128)(2,1)} %collective-permute-done.14.refs_1_, bf16[1088,256]{1,0:T(8,128)(2,1)} %copy-done.16, bf16[1088,256]{1,0:T(8,128)(2,1)} %copy-done.18, bf16[2,1088,256]{2,1,0:T(8,128)(2,1)} %get-tuple-element.41.refs_4_, ...), custom_call_target="tpu_custom_call" | custom-call | flops 1 | bytes 1 | tf_op jit(solution)/shard_map/pallas_call | solution.py:103
  181.6 2.8 convolution_convert_fusion.refs_4_
  184.4 9.0 %shard_map.123 = bf16[3,1088,256]{2,1,0:T(8,128)(2,1)} custom-call(s32[2]{0:T(128)} %pad_add_fusion.refs_0_, bf16[1088,256]{1,0:T(8,128)(2,1)} %bitcast.96, bf16[1088,256]{1,0:T(8,128)(2,1)} %slice_bitcast_fusion.refs_2_, bf16[1088,256]{1,0:T(8,128)(2,1)} %bitcast.98, bf16[1088,256]{1,0:T(8,128)(2,1)} %convolution_convert_fusion.refs_4_, ...), custom_call_target="tpu_custom_call" | custom-call | flops 1 | bytes 1 | tf_op jit(solution)/shard_map/pallas_call | solution.py:103
  199.8 10.0 %shard_map.124 = (bf16[2,136,1088]{2,1,0:T(8,128)(2,1)}, bf16[2,136,1088]{2,1,0:T(8,128)(2,1)}, bf16[2,136,1088]{2,1,0:T(8,128)(2,1)}, f32[2,136,1088]{2,1,0:T(8...) custom-call(s32[1]{0:T(128)} %bitcast.block_ref.refs_0_, ...), custom_call_target="tpu_custom_call" | custom-call | flops 1 | bytes 1 | tf_op jit(solution)/shard_map/pallas_call | solution.py:103
  209.8 7.1 %fusion.17 = (f32[1088]{0:T(1024)S(1)}, f32[256]{0:T(256)S(1)}, f32[256]{0:T(256)S(1)}, f32[1088]{0:T(1024)S(1)}, f32[256,1088]{0,1:T(8,128)S(1)}) fusion(bf16[256,1088]{0,1:T(8,128)(2,1)S(1)} %copy-done.6, f32[256]{0:T(256)S(1)} %add_rsqrt_fusion.1, f32[256]{0:T(256)S(1)} %broadcast_multiply_fusion.5, f32[1088]{0:T(1024)S(1)} %get-tuple-element.91, ...), kind=kOutput, calls=%fused_computation.29 | convolution fusion | flops 1821013504 | bytes 10461952 | tf_op jit(solution)/shard_map/fr,fd->rd/dot_general | solution.py:578
  222.4 4.2 %collective-permute-done.38 = f32[6528]{0:T(1024)S(1)} collective-permute-done((f32[6528]{0:T(1024)S(1)}, f32[6528]{0:T(1024)S(1)}, u32[]{:S(2)}, u32[]{:S(2)}) %collective-permute-start.38) | collective-permute-done | bytes 26144 | tf_op jit(solution)/shard_map/ppermute | solution.py:250
  230.5 2.3 collective-permute-start.40
  232.8 9.4 %shard_map.125 = (f32[2,1088,256]{2,1,0:T(8,128)}, bf16[2,1088,256]{2,1,0:T(8,128)(2,1)}) custom-call(bf16[2,1088,256]{2,1,0:T(8,128)(2,1)} %get-tuple-element.35.refs_10_.refs_0_, bf16[2,1088,256]{2,1,0:T(8,128)(2,1)} %get-tuple-element.36.refs_11_.refs_1_, bf16[4,544,1088]{2,1,0:T(8,128)(2,1)} %bitcast.91, f32[2,136,1088]{2,1,0:T(8,128)} %get-tuple-element.44.refs_3_, ...), custom_call_target="tpu_custom_call" | custom-call | flops 1 | bytes 1 | tf_op jit(solution)/shard_map/pallas_call | solution.py:103
  247.1 2.0 add_convert_fusion.1
  249.1 18.4 %collective-permute-done.32 = bf16[2,136,1088]{2,1,0:T(8,128)(2,1)S(1)} collective-permute-done((bf16[2,136,1088]{2,1,0:T(8,128)(2,1)}, bf16[2,136,1088]{2,1,0:T(8,128)(2,1)S(1)}, u32[]{:S(2)}, u32[]{:S(2)}) %collective-permute-start.32) | collective-permute-done | bytes 591904 | tf_op jit(solution)/shard_map/ppermute | solution.py:250
  271.2 10.1 %collective-permute-done.34.refs_6_ = bf16[2,136,1088]{2,1,0:T(8,128)(2,1)} collective-permute-done((bf16[2,136,1088]{2,1,0:T(8,128)(2,1)}, bf16[2,136,1088]{2,1,0:T(8,128)(2,1)}, u32[]{:S(2)}, u32[]{:S(2)}) %collective-permute-start.34) | collective-permute-done | bytes 591904 | tf_op jit(solution)/shard_map/ppermute | solution.py:250
  281.3 10.7 %collective-permute-done.31.refs_3_ = bf16[2,136,1088]{2,1,0:T(8,128)(2,1)} collective-permute-done((bf16[2,136,1088]{2,1,0:T(8,128)(2,1)}, bf16[2,136,1088]{2,1,0:T(8,128)(2,1)}, u32[]{:S(2)}, u32[]{:S(2)}) %collective-permute-start.31) | collective-permute-done | bytes 591904 | tf_op jit(solution)/shard_map/ppermute | solution.py:250
  292.1 4.0 %shard_map.126 = (f32[136,1088]{1,0:T(8,128)}, bf16[136,1088]{1,0:T(8,128)(2,1)}, bf16[136,1088]{1,0:T(8,128)(2,1)}, bf16[136,1088]{1,0:T(8,128)(2,1)}) custom-call(s32[1]{0:T(128)} %bitcast.30.refs_0_, f32[2,136,1088]{2,1,0:T(8,128)} %get-tuple-element.49.refs_1_, bf16[2,136,1088]{2,1,0:T(8,128)(2,1)} %collective-permute-done.29.refs_2_, ...), custom_call_target="tpu_custom_call" | custom-call | flops 1 | bytes 1 | tf_op jit(solution)/shard_map/pallas_call | solution.py:103
  298.1 2.5 collective-permute-start.37
  303.3 11.1 %collective-permute-done.35 = bf16[136,1088]{1,0:T(8,128)(2,1)S(1)} collective-permute-done((bf16[136,1088]{1,0:T(8,128)(2,1)}, bf16[136,1088]{1,0:T(8,128)(2,1)S(1)}, u32[]{:S(2)}, u32[]{:S(2)}) %collective-permute-start.35) | collective-permute-done | bytes 295968 | tf_op jit(solution)/shard_map/ppermute | solution.py:250
  314.4 8.3 %collective-permute-done.36 = bf16[136,1088]{1,0:T(8,128)(2,1)S(1)} collective-permute-done((bf16[136,1088]{1,0:T(8,128)(2,1)}, bf16[136,1088]{1,0:T(8,128)(2,1)S(1)}, u32[]{:S(2)}, u32[]{:S(2)}) %collective-permute-start.36) | collective-permute-done | bytes 295968 | tf_op jit(solution)/shard_map/ppermute | solution.py:250
  322.7 2.0 convert_add_fusion.2
  325.9 2.2 convert_element_type.183
  (199 shorter events, 70.9 us)
Async XLA Ops:
  7.2 34.7 %all-gather.6.cloned.1.call-start = ((), (), s32[]{:S(2)}) async-start(), calls=%async_computation.3 | async-start | bytes 1566720 | tf_op jit(solution)/shard_map/all_gather | solution.py:290
  7.9 127.5 %all-gather.4.cloned.1.call-start = ((), (), s32[]{:S(2)}) async-start(), calls=%async_computation.1 | async-start | bytes 5640192 | tf_op jit(solution)/shard_map/all_gather | solution.py:420
  8.7 317.2 %reduce-scatter.2.cloned.1.call-start = ((), (), s32[]{:S(2)}) async-start(), calls=%async_computation.2 | async-start | bytes 5640192 | tf_op jit(solution)/shard_map/reduce_scatter | solution.py:426
  16.6 28.2 %collective-permute-start.2 = (bf16[1632]{0:T(1024)(128)(2,1)S(1)}, bf16[1632]{0:T(1024)(128)(2,1)S(1)}, u32[]{:S(2)}, u32[]{:S(2)}) collective-permute-start(bf16[1632]{0:T(1024)(128)(2,1)S(1)} %pad_maximum_fusion.2), channel_id=1, source_target_pairs={{0,4},{1,5},{2,6},{3,7},{4,0},{5,1},{6,2},{7,3},{8,12},{9,13},{10,... | collective-permute-start | bytes 9800 | tf_op jit(solution)/shard_map/ppermute | solution.py:250
  41.9 29.3 %collective-permute-start.7 = (bf16[4,136,1088]{2,1,0:T(8,128)(2,1)}, bf16[4,136,1088]{2,1,0:T(8,128)(2,1)S(1)}, u32[]{:S(2)}, u32[]{:S(2)}) collective-permute-start(bf16[4,136,1088]{2,1,0:T(8,128)(2,1)} %bitcast.81), channel_id=1, source_target_pairs={{0,2},{1,3},{2,0},{3,1},{4,6},{5,7},{6,4},{7,5},{8,10},{9,11},{10,... | collective-permute-start | bytes 3551240 | tf_op jit(solution)/shard_map/ppermute | solution.py:250
  43.3 37.4 %collective-permute-start.6 = (bf16[4,136,1088]{2,1,0:T(8,128)(2,1)}, bf16[4,136,1088]{2,1,0:T(8,128)(2,1)S(1)}, u32[]{:S(2)}, u32[]{:S(2)}) collective-permute-start(bf16[4,136,1088]{2,1,0:T(8,128)(2,1)} %bitcast.82), channel_id=1, source_target_pairs={{0,4},{1,5},{2,6},{3,7},{4,0},{5,1},{6,2},{7,3},{8,12},{9,13},{10,... | collective-permute-start | bytes 3551240 | tf_op jit(solution)/shard_map/ppermute | solution.py:250
  48.8 33.4 %collective-permute-start.4 = (bf16[6528]{0:T(1024)(128)(2,1)S(1)}, bf16[6528]{0:T(1024)(128)(2,1)S(1)}, u32[]{:S(2)}, u32[]{:S(2)}) collective-permute-start(bf16[6528]{0:T(1024)(128)(2,1)S(1)} %pad_maximum_fusion), channel_id=1, source_target_pairs={{0,16},{1,17},{2,18},{3,19},{4,20},{5,21},{6,22},{7,23},{8,24},{9,... | collective-permute-start | bytes 39176 | tf_op jit(solution)/shard_map/ppermute | solution.py:250
  49.9 51.1 %collective-permute-start.5 = (bf16[4,136,1088]{2,1,0:T(8,128)(2,1)}, bf16[4,136,1088]{2,1,0:T(8,128)(2,1)}, u32[]{:S(2)}, u32[]{:S(2)}) collective-permute-start(bf16[4,136,1088]{2,1,0:T(8,128)(2,1)} %bitcast.83), channel_id=1, source_target_pairs={{0,1},{1,0},{2,3},{3,2},{4,5},{5,4},{6,7},{7,6},{8,9},{9,8},{10,11... | collective-permute-start | bytes 3551240 | tf_op jit(solution)/shard_map/ppermute | solution.py:250
  72.0 28.3 %collective-permute-start.11 = (bf16[2,136,1088]{2,1,0:T(8,128)(2,1)}, bf16[2,136,1088]{2,1,0:T(8,128)(2,1)S(1)}, u32[]{:S(2)}, u32[]{:S(2)}) collective-permute-start(bf16[2,136,1088]{2,1,0:T(8,128)(2,1)} %slice.144), channel_id=1, source_target_pairs={{0,4},{1,5},{2,6},{3,7},{4,0},{5,1},{6,2},{7,3},{8,12},{9,13},{10,... | collective-permute-start | bytes 1775624 | tf_op jit(solution)/shard_map/ppermute | solution.py:250
  81.6 18.7 %collective-permute-start.10 = (bf16[2,136,1088]{2,1,0:T(8,128)(2,1)}, bf16[2,136,1088]{2,1,0:T(8,128)(2,1)}, u32[]{:S(2)}, u32[]{:S(2)}) collective-permute-start(bf16[2,136,1088]{2,1,0:T(8,128)(2,1)} %slice.143), channel_id=1, source_target_pairs={{0,2},{1,3},{2,0},{3,1},{4,6},{5,7},{6,4},{7,5},{8,10},{9,11},{10,... | collective-permute-start | bytes 1775624 | tf_op jit(solution)/shard_map/ppermute | solution.py:250
  82.2 18.9 %collective-permute-start.9 = (bf16[4,136,1088]{2,1,0:T(8,128)(2,1)S(1)}, bf16[4,136,1088]{2,1,0:T(8,128)(2,1)}, u32[]{:S(2)}, u32[]{:S(2)}) collective-permute-start(bf16[4,136,1088]{2,1,0:T(8,128)(2,1)S(1)} %collective-permute-done.7.refs_3_), channel_id=1, source_target_pairs={{0,1},{1,0},{2,3},{3,2},{4,5},{5,4},{6,7},{7,6},{8,9},{9,8},{10,11... | collective-permute-start | bytes 3551240 | tf_op jit(solution)/shard_map/ppermute | solution.py:250
  82.2 18.9 %collective-permute-start.8 = (bf16[4,136,1088]{2,1,0:T(8,128)(2,1)S(1)}, bf16[4,136,1088]{2,1,0:T(8,128)(2,1)}, u32[]{:S(2)}, u32[]{:S(2)}) collective-permute-start(bf16[4,136,1088]{2,1,0:T(8,128)(2,1)S(1)} %collective-permute-done.6.refs_2_), channel_id=1, source_target_pairs={{0,1},{1,0},{2,3},{3,2},{4,5},{5,4},{6,7},{7,6},{8,9},{9,8},{10,11... | collective-permute-start | bytes 3551240 | tf_op jit(solution)/shard_map/ppermute | solution.py:250
  101.1 17.0 %collective-permute-start.18 = (bf16[1088,256]{1,0:T(8,128)(2,1)}, bf16[1088,256]{1,0:T(8,128)(2,1)}, u32[]{:S(2)}, u32[]{:S(2)}) collective-permute-start(bf16[1088,256]{1,0:T(8,128)(2,1)} %fusion.33.refs_2_.refs_6_), channel_id=1, source_target_pairs={{0,2},{1,3},{2,0},{3,1},{4,6},{5,7},{6,4},{7,5},{8,10},{9,11},{10,... | collective-permute-start | bytes 1671176 | tf_op jit(solution)/shard_map/ppermute | solution.py:250
  117.9 14.7 %collective-permute-start.16 = (bf16[1088,256]{1,0:T(8,128)(2,1)S(1)}, bf16[1088,256]{1,0:T(8,128)(2,1)S(1)}, u32[]{:S(2)}, u32[]{:S(2)}) collective-permute-start(bf16[1088,256]{1,0:T(8,128)(2,1)S(1)} %fusion.31.refs_0_), channel_id=1, source_target_pairs={{0,2},{1,3},{2,0},{3,1},{4,6},{5,7},{6,4},{7,5},{8,10},{9,11},{10,... | collective-permute-start | bytes 1671176 | tf_op jit(solution)/shard_map/ppermute | solution.py:250
  118.0 16.4 %collective-permute-start.19 = (bf16[1088,256]{1,0:T(8,128)(2,1)}, bf16[1088,256]{1,0:T(8,128)(2,1)S(1)}, u32[]{:S(2)}, u32[]{:S(2)}) collective-permute-start(bf16[1088,256]{1,0:T(8,128)(2,1)} %collective-permute-done.18.refs_2_.refs_8_), channel_id=1, source_target_pairs={{0,1},{1,0},{2,3},{3,2},{4,5},{5,4},{6,7},{7,6},{8,9},{9,8},{10,11... | collective-permute-start | bytes 1671176 | tf_op jit(solution)/shard_map/ppermute | solution.py:250
  132.7 16.9 %collective-permute-start.15 = (bf16[1088,256]{1,0:T(8,128)(2,1)}, bf16[1088,256]{1,0:T(8,128)(2,1)}, u32[]{:S(2)}, u32[]{:S(2)}) collective-permute-start(bf16[1088,256]{1,0:T(8,128)(2,1)} %fusion.33.refs_2_.refs_6_), channel_id=1, source_target_pairs={{0,1},{1,0},{2,3},{3,2},{4,5},{5,4},{6,7},{7,6},{8,9},{9,8},{10,11... | collective-permute-start | bytes 1671176 | tf_op jit(solution)/shard_map/ppermute | solution.py:250
  134.4 15.2 %collective-permute-start.14 = (bf16[1088,256]{1,0:T(8,128)(2,1)S(1)}, bf16[1088,256]{1,0:T(8,128)(2,1)}, u32[]{:S(2)}, u32[]{:S(2)}) collective-permute-start(bf16[1088,256]{1,0:T(8,128)(2,1)S(1)} %fusion.31.refs_0_), channel_id=1, source_target_pairs={{0,1},{1,0},{2,3},{3,2},{4,5},{5,4},{6,7},{7,6},{8,9},{9,8},{10,11... | collective-permute-start | bytes 1671176 | tf_op jit(solution)/shard_map/ppermute | solution.py:250
  161.0 15.3 %collective-permute-start.20 = (bf16[1088,256]{1,0:T(8,128)(2,1)}, bf16[1088,256]{1,0:T(8,128)(2,1)}, u32[]{:S(2)}, u32[]{:S(2)}) collective-permute-start(bf16[1088,256]{1,0:T(8,128)(2,1)} %get-tuple-element.38), channel_id=1, source_target_pairs={{0,1},{1,0},{2,3},{3,2},{4,5},{5,4},{6,7},{7,6},{8,9},{9,8},{10,11... | collective-permute-start | bytes 1671176 | tf_op jit(solution)/shard_map/ppermute | solution.py:250
  228.6 17.4 %collective-permute-start.30 = (bf16[2,136,1088]{2,1,0:T(8,128)(2,1)}, bf16[2,136,1088]{2,1,0:T(8,128)(2,1)}, u32[]{:S(2)}, u32[]{:S(2)}) collective-permute-start(bf16[2,136,1088]{2,1,0:T(8,128)(2,1)} %get-tuple-element.51), channel_id=1, source_target_pairs={{0,2},{1,3},{2,0},{3,1},{4,6},{5,7},{6,4},{7,5},{8,10},{9,11},{10,... | collective-permute-start | bytes 1775624 | tf_op jit(solution)/shard_map/ppermute | solution.py:250
  230.5 15.3 %collective-permute-start.40 = (f32[1632]{0:T(1024)S(1)}, f32[1632]{0:T(1024)S(1)}, u32[]{:S(2)}, u32[]{:S(2)}) collective-permute-start(f32[1632]{0:T(1024)S(1)} %slice_select_fusion.1), channel_id=1, source_target_pairs={{0,4},{1,5},{2,6},{3,7},{4,0},{5,1},{6,2},{7,3},{8,12},{9,13},{10,... | collective-permute-start | bytes 19592 | tf_op jit(solution)/shard_map/ppermute | solution.py:250
  242.2 29.0 %collective-permute-start.29 = (bf16[2,136,1088]{2,1,0:T(8,128)(2,1)}, bf16[2,136,1088]{2,1,0:T(8,128)(2,1)}, u32[]{:S(2)}, u32[]{:S(2)}) collective-permute-start(bf16[2,136,1088]{2,1,0:T(8,128)(2,1)} %get-tuple-element.50), channel_id=1, source_target_pairs={{0,2},{1,3},{2,0},{3,1},{4,6},{5,7},{6,4},{7,5},{8,10},{9,11},{10,... | collective-permute-start | bytes 1775624 | tf_op jit(solution)/shard_map/ppermute | solution.py:250
  243.8 23.8 %collective-permute-start.32 = (bf16[2,136,1088]{2,1,0:T(8,128)(2,1)}, bf16[2,136,1088]{2,1,0:T(8,128)(2,1)S(1)}, u32[]{:S(2)}, u32[]{:S(2)}) collective-permute-start(bf16[2,136,1088]{2,1,0:T(8,128)(2,1)} %get-tuple-element.53), channel_id=1, source_target_pairs={{0,4},{1,5},{2,6},{3,7},{4,0},{5,1},{6,2},{7,3},{8,12},{9,13},{10,... | collective-permute-start | bytes 1775624 | tf_op jit(solution)/shard_map/ppermute | solution.py:250
  243.9 37.4 %collective-permute-start.34 = (bf16[2,136,1088]{2,1,0:T(8,128)(2,1)}, bf16[2,136,1088]{2,1,0:T(8,128)(2,1)}, u32[]{:S(2)}, u32[]{:S(2)}) collective-permute-start(bf16[2,136,1088]{2,1,0:T(8,128)(2,1)} %get-tuple-element.54), channel_id=1, source_target_pairs={{0,4},{1,5},{2,6},{3,7},{4,0},{5,1},{6,2},{7,3},{8,12},{9,13},{10,... | collective-permute-start | bytes 1775624 | tf_op jit(solution)/shard_map/ppermute | solution.py:250
  245.8 22.9 %collective-permute-start.27 = (bf16[2,1088,256]{2,1,0:T(8,128)(2,1)}, bf16[2,1088,256]{2,1,0:T(8,128)(2,1)S(1)}, u32[]{:S(2)}, u32[]{:S(2)}) collective-permute-start(bf16[2,1088,256]{2,1,0:T(8,128)(2,1)} %get-tuple-element.47), channel_id=1, source_target_pairs={{0,1},{1,0},{2,3},{3,2},{4,5},{5,4},{6,7},{7,6},{8,9},{9,8},{10,11... | collective-permute-start | bytes 3342344 | tf_op jit(solution)/shard_map/ppermute | solution.py:250
  246.0 22.6 %collective-permute-start.41 = (f32[816]{0:T(1024)S(1)}, f32[816]{0:T(1024)S(1)}, u32[]{:S(2)}, u32[]{:S(2)}) collective-permute-start(f32[816]{0:T(1024)S(1)} %slice_select_fusion.2), channel_id=1, source_target_pairs={{0,2},{1,3},{2,0},{3,1},{4,6},{5,7},{6,4},{7,5},{8,10},{9,11},{10,... | collective-permute-start | bytes 9800 | tf_op jit(solution)/shard_map/ppermute | solution.py:250
  267.6 24.5 %collective-permute-start.31 = (bf16[2,136,1088]{2,1,0:T(8,128)(2,1)}, bf16[2,136,1088]{2,1,0:T(8,128)(2,1)}, u32[]{:S(2)}, u32[]{:S(2)}) collective-permute-start(bf16[2,136,1088]{2,1,0:T(8,128)(2,1)} %add_convert_fusion.1), channel_id=1, source_target_pairs={{0,4},{1,5},{2,6},{3,7},{4,0},{5,1},{6,2},{7,3},{8,12},{9,13},{10,... | collective-permute-start | bytes 1775624 | tf_op jit(solution)/shard_map/ppermute | solution.py:250
  268.6 23.5 %collective-permute-start.33 = (bf16[2,136,1088]{2,1,0:T(8,128)(2,1)}, bf16[2,136,1088]{2,1,0:T(8,128)(2,1)}, u32[]{:S(2)}, u32[]{:S(2)}) collective-permute-start(bf16[2,136,1088]{2,1,0:T(8,128)(2,1)} %add_convert_fusion), channel_id=1, source_target_pairs={{0,2},{1,3},{2,0},{3,1},{4,6},{5,7},{6,4},{7,5},{8,10},{9,11},{10,... | collective-permute-start | bytes 1775624 | tf_op jit(solution)/shard_map/ppermute | solution.py:250
  269.8 32.9 %collective-permute-start.42 = (f32[408]{0:T(512)S(1)}, f32[408]{0:T(512)S(1)}, u32[]{:S(2)}, u32[]{:S(2)}) collective-permute-start(f32[408]{0:T(512)S(1)} %slice_select_fusion.3), channel_id=1, source_target_pairs={{0,1},{1,0},{2,3},{3,2},{4,5},{5,4},{6,7},{7,6},{8,9},{9,8},{10,11... | collective-permute-start | bytes 4904 | tf_op jit(solution)/shard_map/ppermute | solution.py:250
  296.1 18.3 %collective-permute-start.35 = (bf16[136,1088]{1,0:T(8,128)(2,1)}, bf16[136,1088]{1,0:T(8,128)(2,1)S(1)}, u32[]{:S(2)}, u32[]{:S(2)}) collective-permute-start(bf16[136,1088]{1,0:T(8,128)(2,1)} %get-tuple-element.56), channel_id=1, source_target_pairs={{0,16},{1,17},{2,18},{3,19},{4,20},{5,21},{6,22},{7,23},{8,24},{9,... | collective-permute-start | bytes 887816 | tf_op jit(solution)/shard_map/ppermute | solution.py:250
  296.4 26.3 %collective-permute-start.36 = (bf16[136,1088]{1,0:T(8,128)(2,1)}, bf16[136,1088]{1,0:T(8,128)(2,1)S(1)}, u32[]{:S(2)}, u32[]{:S(2)}) collective-permute-start(bf16[136,1088]{1,0:T(8,128)(2,1)} %get-tuple-element.57), channel_id=1, source_target_pairs={{0,24},{1,25},{2,26},{3,27},{4,28},{5,29},{6,30},{7,31},{8,16},{9,... | collective-permute-start | bytes 887816 | tf_op jit(solution)/shard_map/ppermute | solution.py:250
  298.1 24.6 %collective-permute-start.37 = (bf16[136,1088]{1,0:T(8,128)(2,1)}, bf16[136,1088]{1,0:T(8,128)(2,1)S(1)}, u32[]{:S(2)}, u32[]{:S(2)}) collective-permute-start(bf16[136,1088]{1,0:T(8,128)(2,1)} %get-tuple-element.58), channel_id=1, source_target_pairs={{0,8},{1,9},{2,10},{3,11},{4,12},{5,13},{6,14},{7,15},{8,0},{9,1},... | collective-permute-start | bytes 887816 | tf_op jit(solution)/shard_map/ppermute | solution.py:250
  302.1 22.7 %collective-permute-start.28 = (bf16[1088,256]{1,0:T(8,128)(2,1)S(1)}, bf16[1088,256]{1,0:T(8,128)(2,1)S(1)}, u32[]{:S(2)}, u32[]{:S(2)}) collective-permute-start(bf16[1088,256]{1,0:T(8,128)(2,1)S(1)} %fusion.32), channel_id=1, source_target_pairs={{0,2},{1,3},{2,0},{3,1},{4,6},{5,7},{6,4},{7,5},{8,10},{9,11},{10,... | collective-permute-start | bytes 1671176 | tf_op jit(solution)/shard_map/ppermute | solution.py:250
  (39 other events, 254.9 us)
Sparse Core Ops, SparseCore 0:
  9.6 32.2 all-gather.5
  44.0 91.3 all-gather.3
  175.6 105.7 reduce-scatter.1
